TPU v7x, 32 devices: a whole 2x2x4 slice. The times are simulated.
32 devices in a mesh: pool: 2 (over y), tgt: 16 (over z, x, core).
Axes of the slice: x: 2, y: 2, z: 4, core: 2. Of those that a mesh axis runs over, the one named last changes fastest.
Arguments:
- pool_table: bfloat16 [8192, 4096], P('pool', 'tgt'), may hold values from -6 to 6
- pool_index: int32 [2048], P('pool'), may hold values from 0 to 8191, as said below
- target_features: bfloat16 [2048, 4096], P('pool', 'tgt'), may hold values from -6 to 6
- posterior_factor: bfloat16 [4096, 4096], P('tgt'), as said below
Outputs:
- scores: float32 [2048], P('pool')
Inputs may be any that keep to these rules, and one draw needn't show every extreme that they name: `pool_index`: pool row r names a row of the table block [(r // 1024) * 4096, (r // 1024 + 1) * 4096); the first row of each block of 1024 pool rows names its table block's first row, and the last names the block's last row; rows may repeat. `posterior_factor`: lower triangular with a positive diagonal.
All inputs are finite; a program needn't handle non-finite values.
Results may differ from a plain program's by a relative error of at most 0.004.
Values may be sent and summed in bfloat16 or wider, within the bound.
No kernel may reach another device: no remote copies, remote signals or barrier semaphores. Data moves between devices by JAX's collectives and lax.ppermute only.
A program may use at most 128 MiB of HBM per device.

v0:
```python
import jax
import jax.numpy as jnp
from jax import lax
from jax.sharding import PartitionSpec as P


def make_term(factor, features):

    def term(start, count):
        return lax.dot_general(
            factor, features, (((0,), (1,)), ((), ())), preferred_element_type=jnp.float32
        )

    return (term, factor.shape[1] // lax.axis_size("tgt"))


def route_targets(target_share):
    moved = lax.all_to_all(target_share, "tgt", split_axis=1, concat_axis=0, tiled=True)
    return lax.all_gather(moved, "pool", axis=1, tiled=True)


def body(pool_table, pool_index, target_features, posterior_factor):
    local_index = pool_index - lax.axis_index("pool") * pool_table.shape[0]
    pool_rows = jnp.take(pool_table, local_index, axis=0)
    pool_fn, share_rows = make_term(posterior_factor, pool_rows)
    pool_share = lax.psum_scatter(
        pool_fn(jnp.int32(0), share_rows * lax.axis_size("tgt")).astype(jnp.bfloat16),
        "tgt",
        scatter_dimension=0,
        tiled=True,
    )
    target_fn, share_rows = make_term(posterior_factor, target_features)
    target_share = lax.psum_scatter(
        target_fn(jnp.int32(0), share_rows * lax.axis_size("tgt")).astype(jnp.bfloat16),
        "tgt",
        scatter_dimension=0,
        tiled=True,
    )
    targets_full = route_targets(target_share)
    piece = lax.all_gather(pool_share, "tgt", axis=0, tiled=True)
    cross = lax.dot_general(
        piece, targets_full, (((0,), (0,)), ((), ())), preferred_element_type=jnp.float32
    )
    squares = jnp.sum(jnp.square(piece.astype(jnp.float32)), axis=0)
    cross, squares = (cross, squares)
    target_var = 1.0 + jnp.sum(jnp.square(targets_full.astype(jnp.float32)), axis=0)
    pool_var = 1.0 + squares
    ratio = jnp.square(cross) / (pool_var[:, None] * target_var[None, :])
    partial_scores = -0.5 * jnp.sum(jnp.log1p(-ratio), axis=1)
    return lax.psum(partial_scores, "tgt")


def solution(mesh):
    in_specs = (P("pool", "tgt"), P("pool"), P("pool", "tgt"), P("tgt", None))
    out_specs = P("pool")
    return jax.shard_map(body, mesh=mesh, in_specs=in_specs, out_specs=out_specs, check_vma=False)
```

profile of v0, /device:TPU:0, one launch (start us, length us, event | category | flops | bytes accessed | tf_op | source)
XLA Modules:
  0.0 381.0 jit_solution(8397117188879038305)
XLA Ops:
  6.5 0.0 copy-start
  6.5 0.0 copy-start.3
  6.5 0.0 reduce-scatter.5.cloned.1.call-start
  6.5 1.6 copy-done
  8.1 6.7 %convolution_convert_fusion = bf16[4096,1024]{1,0:T(8,128)(2,1)} fusion(bf16[256,4096]{1,0:T(8,128)(2,1)S(1)} %copy-done, bf16[1024,256]{1,0:T(8,128)(2,1)} %param.6), kind=kOutput, calls=%fused_computation.3 | convolution fusion | flops 2151677952 | bytes 11010048 | tf_op jit(solution)/shard_map/dot_general | solution.py:10
  14.8 0.0 reduce-scatter.5.cloned.1.call-update
  14.8 0.0 reduce-scatter.3.cloned.1.call-start
  14.9 0.0 copy-done.3
  14.9 5.3 %gather_fusion = bf16[1024,256]{1,0:T(8,128)(2,1)S(1)} fusion(bf16[4096,256]{1,0:T(8,128)(2,1)} %param.4, s32[1024]{0:T(1024)S(1)} %fusion.7), kind=kCustom, calls=%fused_computation | custom fusion | bytes 1052672 | tf_op jit(solution)/shard_map/jit(_take)/gather | solution.py:24
  20.2 5.8 %convert_bitcast_fusion = bf16[4096,1024]{0,1:T(8,128)(2,1)} fusion(bf16[256,4096]{1,0:T(8,128)(2,1)S(1)} %copy-done, bf16[1024,256]{1,0:T(8,128)(2,1)S(1)} %gather_fusion, pred[1024]{0:T(1024)(128)(4,1)S(1)} %compare_and_fusion), kind=kOutput, calls=%fused_computation.2 | convolution fusion | flops 2151940096 | bytes 11011072 | tf_op jit(solution)/shard_map/dot_general | solution.py:10
  26.1 0.0 reduce-scatter.3.cloned.1.call-update
  26.1 0.0 all-gather.5.cloned.1.call-start
  26.1 96.2 %reduce-scatter.5.cloned.1.call-done = bf16[256,1024]{1,0:T(8,128)(2,1)} async-done(((bf16[4096,1024]{1,0:T(8,128)(2,1)}), bf16[256,1024]{1,0:T(8,128)(2,1)}) %reduce-scatter.5.cloned.1.call-update) | async-done | bytes 524304 | tf_op jit(solution)/shard_map/reduce_scatter | solution.py:33
  122.3 1.2 copy.5
  123.6 18.7 %all_to_all.19 = bf16[256,16,64]{0,2,1:T(8,128)(2,1)S(1)} all-to-all(bf16[256,16,64]{0,2,1:T(8,128)(2,1)S(1)} %bitcast.12), channel_id=1, replica_groups=mesh['pool'=2,'tgt'=16] {'tgt'}, dimensions={1} | all-to-all | bytes 1048576 | tf_op jit(solution)/shard_map/all_to_all | solution.py:18
  142.3 0.8 copy.7
  143.1 0.0 all-gather.5.cloned.1.call-update
  143.2 0.0 all-gather.3.cloned.1.call-start
  143.2 87.9 %reduce-scatter.3.cloned.1.call-done = bf16[256,1024]{0,1:T(8,128)(2,1)} async-done(((bf16[4096,1024]{0,1:T(8,128)(2,1)}), bf16[256,1024]{0,1:T(8,128)(2,1)}) %reduce-scatter.3.cloned.1.call-update) | async-done | bytes 524304 | tf_op jit(solution)/shard_map/reduce_scatter | solution.py:26
  231.1 0.0 all-gather.3.cloned.1.call-update
  231.1 22.6 %all-gather.5.cloned.1.call-done = bf16[4096,128]{0,1:T(8,128)(2,1)} async-done(((bf16[4096,64]{0,1:T(8,128)(2,1)}), bf16[4096,128]{0,1:T(8,128)(2,1)}) %all-gather.5.cloned.1.call-update) | async-done | bytes 1048592 | tf_op jit(solution)/shard_map/all_gather | solution.py:19
  253.7 0.0 copy-start.2
  253.7 1.6 multiply_reduce_fusion.1
  255.3 78.5 %all-gather.3.cloned.1.call-done = bf16[4096,1024]{0,1:T(8,128)(2,1)} async-done(((bf16[256,1024]{0,1:T(8,128)(2,1)}), bf16[4096,1024]{0,1:T(8,128)(2,1)}) %all-gather.3.cloned.1.call-update) | async-done | bytes 8388624 | tf_op jit(solution)/shard_map/all_gather | solution.py:40
  333.8 0.0 copy-start.1
  333.8 5.2 %multiply_reduce_fusion = f32[1024]{0:T(1024)S(1)} fusion(bf16[4096,1024]{0,1:T(8,128)(2,1)} %all-gather.3.cloned.1.call-done), kind=kLoop, calls=%fused_computation.1 | loop fusion | flops 12581888 | bytes 8392704 | tf_op jit(solution)/shard_map/reduce_sum | solution.py:44
  339.1 0.0 copy-done.2
  339.1 0.5 copy-done.1
  339.6 3.1 fusion.3
  342.8 31.7 %psum.7 = f32[1024]{0:T(1024)} all-reduce(f32[1024]{0:T(1024)S(1)} %broadcast_multiply_fusion), channel_id=1, replica_groups=mesh['pool'=2,'tgt'=16] {'tgt'}, use_global_device_ids=true, to_apply=%region_5.6 | all-reduce | flops 1024 | bytes 8192 | tf_op jit(solution)/shard_map/psum | solution.py:50
  (5 shorter events, 0.0 us)
Async XLA Ops:
  6.5 1.6 copy-start
  6.5 8.3 %copy-start.3 = (s32[1024]{0:T(1024)S(1)}, s32[1024]{0:T(1024)}, u32[]{:S(2)}) copy-start(s32[1024]{0:T(1024)} %param.5) | copy-start | bytes 12292
  6.5 115.8 %reduce-scatter.5.cloned.1.call-start = ((), (), s32[]{:S(2)}) async-start(), calls=%async_computation.5 | async-start | bytes 8912896 | tf_op jit(solution)/shard_map/reduce_scatter | solution.py:33
  14.8 216.2 %reduce-scatter.3.cloned.1.call-start = ((), (), s32[]{:S(2)}) async-start(), calls=%async_computation.3 | async-start | bytes 8912896 | tf_op jit(solution)/shard_map/reduce_scatter | solution.py:26
  26.1 227.6 %all-gather.5.cloned.1.call-start = ((), (), s32[]{:S(2)}) async-start(), calls=%async_computation.6 | async-start | bytes 1572864 | tf_op jit(solution)/shard_map/all_gather | solution.py:19
  143.2 190.7 %all-gather.3.cloned.1.call-start = ((), (), s32[]{:S(2)}) async-start(), calls=%async_computation.4 | async-start | bytes 8912896 | tf_op jit(solution)/shard_map/all_gather | solution.py:40
  253.7 85.4 %copy-start.2 = (bf16[4096,128]{0,1:T(8,128)(2,1)S(1)}, bf16[4096,128]{0,1:T(8,128)(2,1)}, u32[]{:S(2)}) copy-start(bf16[4096,128]{0,1:T(8,128)(2,1)} %all-gather.5.cloned.1.call-done) | copy-start | bytes 3145732
  333.8 5.8 %copy-start.1 = (bf16[4096,1024]{0,1:T(8,128)(2,1)S(1)}, bf16[4096,1024]{0,1:T(8,128)(2,1)}, u32[]{:S(2)}) copy-start(bf16[4096,1024]{0,1:T(8,128)(2,1)} %all-gather.3.cloned.1.call-done) | copy-start | bytes 25165828
Sparse Core Ops, SparseCore 0:
  14.9 107.3 reduce-scatter.4
  126.4 104.5 reduce-scatter.2
  232.6 21.0 all-gather.4
  255.7 78.0 all-gather.2
where the time goes:
time: 381 us
  waiting for transfers between devices  285 us (75%)
  blocking collectives  50.4 us (13%)
  matrix products  15.6 us (4%)
  between operations  13.2 us (3%)
  local copies, waits for them, and re-layouts  9.51 us (2%)
  other arithmetic  6.86 us (2%)
    reduce_scatter x1, waiting for transfers between devices, body(): lax.psum_scatter(target_fn(jnp.int32(0), share_rows * lax.axis_size('tgt'...  96.2 us
    reduce_scatter x1, waiting for transfers between devices, body(): lax.psum_scatter(pool_fn(jnp.int32(0), share_rows * lax.axis_size('tgt'))...  87.9 us
    all_gather x1, waiting for transfers between devices, body(): piece = lax.all_gather(pool_share, 'tgt', axis=0, tiled=True)  78.5 us
    psum x1, blocking collectives, body(): return lax.psum(partial_scores, 'tgt')  31.7 us
    all_gather x1, waiting for transfers between devices, route_targets(): return lax.all_gather(moved, 'pool', axis=1, tiled=True)  22.6 us
    all_to_all x1, blocking collectives, route_targets(): lax.all_to_all(target_share, 'tgt', split_axis=1, concat_axis=0, tiled=True)  18.7 us
    dot_general x2, matrix products, term(): lax.dot_general(factor, features, (((0,), (1,)), ((), ())), preferred_ele...  12.5 us
  transfers between devices with their start and end apart: 4, of which 4 were waited for; matrix products, arithmetic and copies ran while one was open for 4% of the time, Pallas kernels for 0%

commit v1 on v0

v1 whole, which is shorter than its diff:
```python
import jax
import jax.numpy as jnp
from jax import lax
from jax.sharding import PartitionSpec as P

QUARTERS = 4
CORES = 2
BF = jnp.bfloat16
F32 = jnp.float32


def matmul(a, b):
    return lax.dot_general(a, b, (((1,), (0,)), ((), ())), preferred_element_type=F32)


def matmul_t(a, b):
    return lax.dot_general(a, b, (((1,), (1,)), ((), ())), preferred_element_type=F32)


def token(*arrays):
    width = min(v.shape[-1] for v in arrays)
    rows = [lax.slice_in_dim(v.reshape(-1, v.shape[-1])[:1], 0, width, axis=1) for v in arrays]
    return sum(jnp.minimum(jnp.abs(r.astype(F32)), 0.0) for r in rows)


def behind(value, zeros):
    return value + zeros[:, :value.shape[-1]].astype(value.dtype)


def square_sum(a):
    return jnp.sum(jnp.square(a.astype(F32)), axis=1)


def make_body(n_pool, n_tgt):
    nz = QUARTERS
    nx = n_tgt // (nz * CORES)
    outer = (1, 0, 3, 2)
    middle = (0, 2, 1, 3)
    spread_out = (3, 2, 1, 0)

    def place(z, x, c):
        return (z * nx + x) * CORES + c

    def inner(value, shift, flip):
        pairs = [
            (place(z, x, c), place(z, (x + shift) % nx, c ^ flip))
            for z in range(nz) for x in range(nx) for c in range(CORES)
        ]
        return lax.ppermute(value, "tgt", pairs)

    def along_z(value, to):
        pairs = [
            (place(z, x, c), place(to[z], x, c)) for z in range(nz) for x in range(nx) for c in range(CORES)
        ]
        return lax.ppermute(value, "tgt", pairs)

    def over_pool(value, shift):
        return lax.ppermute(value, "pool", [(p, (p + shift) % n_pool) for p in range(n_pool)])

    def choose(values, z):
        out = jnp.int32(values[0])
        for k in range(1, nz):
            out = jnp.where(z == k, jnp.int32(values[k]), out)
        return out

    def body(pool_table, pool_index, target_features, posterior_factor):
        me = lax.axis_index("tgt")
        core = me % CORES
        x = (me // CORES) % nx
        z = me // (CORES * nx)
        top = z == nz - 1
        width, hidden = posterior_factor.shape
        quarter = hidden // nz

        local_index = pool_index - lax.axis_index("pool") * pool_table.shape[0]
        pool_rows = jnp.take(pool_table, local_index, axis=0)
        count = pool_rows.shape[0] // (nx * CORES)
        count_t = target_features.shape[0] // (nx * CORES)

        rows = jnp.concatenate([
            target_features.reshape(nx, CORES, count_t, width), pool_rows.reshape(nx, CORES, count, width)
        ], axis=2)
        n_rows = count + count_t

        def rows_of(s, f):
            return lax.dynamic_slice(rows, (lax.rem(x + s, nx), core ^ f, 0, 0), (1, 1, n_rows, width))[0, 0]

        def factor_own(choice):
            return lax.dynamic_slice_in_dim(posterior_factor, choose(choice, z) * quarter, quarter, 1)

        def factor_x(own):
            return [inner(own, s, 0) for s in range(1, nx)]

        def partial(pieces):
            total = None
            for f, l in zip(features, pieces):
                term = matmul(f, l)
                total = term if total is None else total + term
            return total

        def factor_flip(same):
            return [inner(v, 0, 1) for v in same]

        order = [(s, 0) for s in range(nx)] + [(s, 1) for s in range(nx)]

        own1 = factor_own([0, 1, 2, 1])
        same1 = [own1] + factor_x(own1)

        done = token(*same1[1:])
        features = [inner(behind(rows_of(s, f), done), s, f) if s or f else rows_of(0, 0) for s, f in order]
        first = partial(same1 + factor_flip(same1))

        start = token(first)
        step1 = along_z(first.astype(BF), outer)
        step2 = along_z(first.astype(BF), middle)
        own2 = behind(factor_own([0, 0, 0, 0]), start)
        own3 = behind(factor_own([1, 1, 1, 2]), start)
        flip2, flip3 = inner(own2, 0, 1), inner(own3, 0, 1)
        moved2, moved3 = factor_x(own2), factor_x(own3)
        done = token(step1, step2, flip2, flip3, *moved2, *moved3)
        moved2, moved3 = [behind(v, done) for v in moved2], [behind(v, done) for v in moved3]
        second = partial([own2] + moved2 + [flip2] + factor_flip(moved2))
        third = partial([own3] + moved3 + [flip3] + factor_flip(moved3))

        start = token(second, third) + done
        step3 = along_z(behind(second, start).astype(BF), outer)
        step4 = along_z((behind(second, start) + step1.astype(F32)).astype(BF), middle)
        white_a = (third + step1.astype(F32) + jnp.where(top, 0.0, step2.astype(F32)) + start).astype(BF)
        own4 = behind(factor_own([3, 3, 3, 3]), start)
        flip4, moved4 = inner(own4, 0, 1), factor_x(own4)
        t_a, p_a = white_a[:count_t], white_a[count_t:]
        t_flip_a = inner(t_a, 0, 1)
        t_moved_a = [inner(t_a, s, 0) for s in range(1, nx)]
        p_moved_a = [over_pool(p_a, s) for s in range(1, n_pool)]
        done = token(step3, step4, flip4, *moved4, t_flip_a, *t_moved_a, *p_moved_a)

        moved4 = [behind(v, done) for v in moved4]
        fourth = partial([own4] + moved4 + [flip4] + factor_flip(moved4))
        t_moved_a = [behind(v, done) for v in t_moved_a]
        white_b = (jnp.where(top, fourth, second + step3.astype(F32) + step4.astype(F32)) + done).astype(BF)
        t_b, p_b = white_b[:count_t], white_b[count_t:]
        t_moved_b = [inner(t_b, s, 0) for s in range(1, nx)]
        p_moved_b = [over_pool(p_b, s) for s in range(1, n_pool)]
        t_flip_b = inner(t_b, 0, 1)

        def spread(t, t_moved, t_flip, p, p_moved):
            low = jnp.concatenate([t] + t_moved, axis=0)
            high = jnp.concatenate([t_flip] + [inner(v, 0, 1) for v in t_moved], axis=0)
            return jnp.where(top, high, low), jnp.where(top, low, high), jnp.concatenate([p] + p_moved, axis=0)

        keep_a, give_a, p_a = spread(t_a, t_moved_a, t_flip_a, p_a, p_moved_a)
        keep_b, give_b, p_b = spread(t_b, t_moved_b, t_flip_b, p_b, p_moved_b)

        given = along_z(matmul_t(give_a, p_a) + matmul_t(give_b, p_b), outer)
        p_squares = square_sum(p_a) + square_sum(p_b)
        n_keep = keep_a.shape[0]
        squares = along_z(jnp.concatenate([square_sum(give_a) + square_sum(give_b), p_squares]), outer)
        target_var = 1.0 + (square_sum(keep_a) + square_sum(keep_b) + squares[:n_keep])
        pool_var = 1.0 + (p_squares + squares[n_keep:])
        cross = matmul_t(keep_a, p_a) + matmul_t(keep_b, p_b) + given
        ratio = jnp.square(cross) / (target_var[:, None] * pool_var[None, :])
        sums = -0.5 * jnp.sum(jnp.log1p(-ratio), axis=0)

        sums = sums + along_z(sums, outer)
        own = sums[:count]
        for s in range(1, n_pool):
            own = own + over_pool(sums[s * count:(s + 1) * count], -s)
        flipped = inner(own, 0, 1)
        both = jnp.where(core == 0, jnp.concatenate([own, flipped]), jnp.concatenate([flipped, own]))
        parts = jnp.stack([both] + [inner(both, s, 0) for s in range(1, nx)])
        if nx == 2:
            scores = jnp.where(x == 0, parts.reshape(-1), parts[::-1].reshape(-1))
        else:
            scores = jnp.take(parts, (x - jnp.arange(nx)) % nx, axis=0).reshape(-1)
        return jnp.where(z >= nz - 2, scores, along_z(scores, spread_out))

    return body


def solution(mesh):
    in_specs = (P("pool", "tgt"), P("pool"), P("pool", "tgt"), P("tgt", None))
    out_specs = P("pool")
    body = make_body(mesh.shape["pool"], mesh.shape["tgt"])
    return jax.shard_map(body, mesh=mesh, in_specs=in_specs, out_specs=out_specs, check_vma=False)
```

time: 381 us -> 159 us (0.42)
  waiting for transfers between devices: 285 us -> 94.7 us
  blocking collectives: 50.4 us -> 0 us
  starting transfers between devices: 0.13 us -> 34.3 us
  between operations: 13.2 us -> 0.43 us
    reduce_scatter x2 -> x0, waiting for transfers between devices: 184 us -> none  [the longest x1 96.2 us: body(): lax.psum_scatter(target_fn(jnp.int32(0), share_rows * lax.axis_size('tgt'...]
    all_gather x2 -> x0, waiting for transfers between devices: 101 us -> none  [the longest x1 78.5 us: body(): piece = lax.all_gather(pool_share, 'tgt', axis=0, tiled=True)]
    ppermute x0 -> x34, waiting for transfers between devices: none -> 94.7 us  [the longest x23 59.2 us: inner(): return lax.ppermute(value, 'tgt', pairs)]
    ppermute x0 -> x34, starting transfers between devices: none -> 34.3 us  [the longest x8 16.3 us: along_z(): return lax.ppermute(value, 'tgt', pairs)]
    psum x1 -> x0, blocking collectives: 31.7 us -> none  [body(): return lax.psum(partial_scores, 'tgt')]
    all_to_all x1 -> x0, blocking collectives: 18.7 us -> none  [route_targets(): lax.all_to_all(target_share, 'tgt', split_axis=1, concat_axis=0, tiled=True)]
    reduce_sum x2 -> x4, other arithmetic: 6.83 us -> 2.44 us  [square_sum(): return jnp.sum(jnp.square(a.astype(F32)), axis=1)]
    dot_general x3 -> x20, matrix products: 15.6 us -> 13.3 us  [the longest x16 9.81 us: matmul(): lax.dot_general(a, b, (((1,), (0,)), ((), ())), preferred_element_type=F32)]
  transfers between devices with their start and end apart: 4 -> 34, of which waited for: 4 -> 22; matrix products, arithmetic and copies ran while one was open for 4% -> 13% of each run, Pallas kernels for 0% -> 0%
where the time goes in v1:
time: 159 us
  waiting for transfers between devices  94.7 us (60%)
  starting transfers between devices  34.3 us (22%)
  matrix products  13.3 us (8%)
  local copies, waits for them, and re-layouts  8.38 us (5%)
  other arithmetic  7.5 us (5%)
    ppermute x23, waiting for transfers between devices, inner(): return lax.ppermute(value, 'tgt', pairs)  59.2 us
    ppermute x8, waiting for transfers between devices, along_z(): return lax.ppermute(value, 'tgt', pairs)  28.3 us
    ppermute x8, starting transfers between devices, along_z(): return lax.ppermute(value, 'tgt', pairs)  16.3 us
    ppermute x23, starting transfers between devices, inner(): return lax.ppermute(value, 'tgt', pairs)  13.3 us
    dot_general x16, matrix products, matmul(): lax.dot_general(a, b, (((1,), (0,)), ((), ())), preferred_element_type=F32)  9.81 us
    ppermute x3, waiting for transfers between devices, over_pool(): lax.ppermute(value, 'pool', [(p, (p + shift) % n_pool) for p in range(n_p...  7.16 us
    gather x1, local copies, waits for them, and re-layouts, body(): pool_rows = jnp.take(pool_table, local_index, axis=0)  4.93 us
    ppermute x3, starting transfers between devices, over_pool(): lax.ppermute(value, 'pool', [(p, (p + shift) % n_pool) for p in range(n_p...  4.71 us
  transfers between devices with their start and end apart: 34, of which 22 were waited for; matrix products, arithmetic and copies ran while one was open for 13% of the time, Pallas kernels for 0%

profile of v1, /device:TPU:0, one launch (start us, length us, event | category | flops | bytes accessed | tf_op | source)
XLA Modules:
  0.0 158.6 jit_solution(15643053895197456239)
XLA Ops:
  0.0 1.2 constant_dynamic-slice_fusion
  1.2 3.0 %collective-permute-start = (bf16[256,1024]{1,0:T(8,128)(2,1)S(1)}, bf16[256,1024]{1,0:T(8,128)(2,1)}, u32[]{:S(2)}, u32[]{:S(2)}) collective-permute-start(bf16[256,1024]{1,0:T(8,128)(2,1)S(1)} %constant_dynamic-slice_fusion), channel_id=1, source_target_pairs={{0,2},{1,3},{2,0},{3,1},{4,6},{5,7},{6,4},{7,5},{8,10},{9,11},{10,... | collective-permute-start | bytes 1572872 | tf_op jit(solution)/shard_map/ppermute | solution.py:49
  5.7 4.9 %gather_fusion = bf16[1024,256]{1,0:T(8,128)(2,1)} fusion(bf16[4096,256]{1,0:T(8,128)(2,1)S(1)} %copy-done, s32[1024]{0:T(1024)S(1)} %fusion.67), kind=kCustom, calls=%fused_computation | custom fusion | bytes 1052672 | tf_op jit(solution)/shard_map/jit(_take)/gather | solution.py:76
  10.6 1.2 broadcast_select_fusion.4
  11.9 4.4 %collective-permute-done = bf16[256,1024]{1,0:T(8,128)(2,1)} collective-permute-done((bf16[256,1024]{1,0:T(8,128)(2,1)S(1)}, bf16[256,1024]{1,0:T(8,128)(2,1)}, u32[]{:S(2)}, u32[]{:S(2)}) %collective-permute-start) | collective-permute-done | bytes 524320 | tf_op jit(solution)/shard_map/ppermute | solution.py:49
  17.2 1.8 %collective-permute-start.1 = (bf16[512,256]{1,0:T(8,128)(2,1)S(1)}, bf16[512,256]{1,0:T(8,128)(2,1)S(1)}, u32[]{:S(2)}, u32[]{:S(2)}) collective-permute-start(bf16[512,256]{1,0:T(8,128)(2,1)S(1)} %get-tuple-element.20), channel_id=1, source_target_pairs={{0,2},{1,3},{2,0},{3,1},{4,6},{5,7},{6,4},{7,5},{8,10},{9,11},{10,... | collective-permute-start | bytes 786440 | tf_op jit(solution)/shard_map/ppermute | solution.py:49
  20.0 6.5 %collective-permute-done.1 = bf16[512,256]{1,0:T(8,128)(2,1)S(1)} collective-permute-done((bf16[512,256]{1,0:T(8,128)(2,1)S(1)}, bf16[512,256]{1,0:T(8,128)(2,1)S(1)}, u32[]{:S(2)}, u32[]{:S(2)}) %collective-permute-start.1) | collective-permute-done | bytes 262176 | tf_op jit(solution)/shard_map/ppermute | solution.py:49
  26.5 1.5 fusion.83
  28.0 1.5 fusion.84
  31.3 1.8 %collective-permute-start.11 = (bf16[256,1024]{1,0:T(8,128)(2,1)S(1)}, bf16[256,1024]{1,0:T(8,128)(2,1)S(1)}, u32[]{:S(2)}, u32[]{:S(2)}) collective-permute-start(bf16[256,1024]{1,0:T(8,128)(2,1)S(1)} %get-tuple-element.17), channel_id=1, source_target_pairs={{0,2},{1,3},{2,0},{3,1},{4,6},{5,7},{6,4},{7,5},{8,10},{9,11},{10,... | collective-permute-start | bytes 1572872 | tf_op jit(solution)/shard_map/ppermute | solution.py:49
  33.1 1.6 collective-permute-start.7
  38.8 7.4 %collective-permute-done.11 = bf16[256,1024]{1,0:T(8,128)(2,1)S(1)} collective-permute-done((bf16[256,1024]{1,0:T(8,128)(2,1)S(1)}, bf16[256,1024]{1,0:T(8,128)(2,1)S(1)}, u32[]{:S(2)}, u32[]{:S(2)}) %collective-permute-start.11) | collective-permute-done | bytes 524320 | tf_op jit(solution)/shard_map/ppermute | solution.py:49
  46.2 9.9 %collective-permute-done.6 = bf16[256,1024]{1,0:T(8,128)(2,1)S(1)} collective-permute-done((bf16[256,1024]{1,0:T(8,128)(2,1)S(1)}, bf16[256,1024]{1,0:T(8,128)(2,1)S(1)}, u32[]{:S(2)}, u32[]{:S(2)}) %collective-permute-start.6) | collective-permute-done | bytes 524320 | tf_op jit(solution)/shard_map/ppermute | solution.py:49
  56.1 2.6 %collective-permute-done.7 = bf16[512,1024]{1,0:T(8,128)(2,1)S(1)} collective-permute-done((bf16[512,1024]{1,0:T(8,128)(2,1)S(1)}, bf16[512,1024]{1,0:T(8,128)(2,1)S(1)}, u32[]{:S(2)}, u32[]{:S(2)}) %collective-permute-start.7) | collective-permute-done | bytes 1048608 | tf_op jit(solution)/shard_map/ppermute | solution.py:55
  63.7 4.8 %collective-permute-start.16 = (bf16[512,1024]{1,0:T(8,128)(2,1)S(1)}, bf16[512,1024]{1,0:T(8,128)(2,1)S(1)}, u32[]{:S(2)}, u32[]{:S(2)}) collective-permute-start(bf16[512,1024]{1,0:T(8,128)(2,1)S(1)} %get-tuple-element.15), channel_id=1, source_target_pairs={{0,4},{1,5},{2,6},{3,7},{4,0},{5,1},{6,2},{7,3},{8,12},{9,13},{10,... | collective-permute-start | bytes 3145736 | tf_op jit(solution)/shard_map/ppermute | solution.py:55
  69.4 1.6 %collective-permute-start.20 = (bf16[256,1024]{1,0:T(8,128)(2,1)S(1)}, bf16[256,1024]{1,0:T(8,128)(2,1)S(1)}, u32[]{:S(2)}, u32[]{:S(2)}) collective-permute-start(bf16[256,1024]{1,0:T(8,128)(2,1)S(1)} %get-tuple-element.26), channel_id=1, source_target_pairs={{0,16},{16,0},{1,17},{17,1},{2,18},{18,2},{3,19},{19,3},{4,20},{20... | collective-permute-start | bytes 1572872 | tf_op jit(solution)/shard_map/ppermute | solution.py:58
  71.1 6.4 %collective-permute-done.15 = bf16[256,1024]{1,0:T(8,128)(2,1)S(1)} collective-permute-done((bf16[256,1024]{1,0:T(8,128)(2,1)S(1)}, bf16[256,1024]{1,0:T(8,128)(2,1)S(1)}, u32[]{:S(2)}, u32[]{:S(2)}) %collective-permute-start.15) | collective-permute-done | bytes 524320 | tf_op jit(solution)/shard_map/ppermute | solution.py:49
  78.3 4.7 %collective-permute-done.20 = bf16[256,1024]{1,0:T(8,128)(2,1)S(1)} collective-permute-done((bf16[256,1024]{1,0:T(8,128)(2,1)S(1)}, bf16[256,1024]{1,0:T(8,128)(2,1)S(1)}, u32[]{:S(2)}, u32[]{:S(2)}) %collective-permute-start.20) | collective-permute-done | bytes 524320 | tf_op jit(solution)/shard_map/ppermute | solution.py:58
  83.1 7.8 %collective-permute-done.19 = bf16[256,1024]{1,0:T(8,128)(2,1)S(1)} collective-permute-done((bf16[256,1024]{1,0:T(8,128)(2,1)S(1)}, bf16[256,1024]{1,0:T(8,128)(2,1)S(1)}, u32[]{:S(2)}, u32[]{:S(2)}) %collective-permute-start.19) | collective-permute-done | bytes 524320 | tf_op jit(solution)/shard_map/ppermute | solution.py:49
  95.1 1.6 collective-permute-start.24
  97.5 1.6 %collective-permute-start.26 = (bf16[256,1024]{1,0:T(8,128)(2,1)S(1)}, bf16[256,1024]{1,0:T(8,128)(2,1)S(1)}, u32[]{:S(2)}, u32[]{:S(2)}) collective-permute-start(bf16[256,1024]{1,0:T(8,128)(2,1)S(1)} %get-tuple-element.24), channel_id=1, source_target_pairs={{0,16},{16,0},{1,17},{17,1},{2,18},{18,2},{3,19},{19,3},{4,20},{20... | collective-permute-start | bytes 1572872 | tf_op jit(solution)/shard_map/ppermute | solution.py:58
  99.1 10.0 %collective-permute-done.24 = bf16[256,1024]{1,0:T(8,128)(2,1)S(1)} collective-permute-done((bf16[256,1024]{1,0:T(8,128)(2,1)S(1)}, bf16[256,1024]{1,0:T(8,128)(2,1)S(1)}, u32[]{:S(2)}, u32[]{:S(2)}) %collective-permute-start.24) | collective-permute-done | bytes 524320 | tf_op jit(solution)/shard_map/ppermute | solution.py:49
  112.2 3.7 %collective-permute-start.27 = (f32[512,512]{1,0:T(8,128)S(1)}, f32[512,512]{1,0:T(8,128)S(1)}, u32[]{:S(2)}, u32[]{:S(2)}) collective-permute-start(f32[512,512]{1,0:T(8,128)S(1)} %convolution_add_fusion), channel_id=1, source_target_pairs={{0,4},{1,5},{2,6},{3,7},{4,0},{5,1},{6,2},{7,3},{8,12},{9,13},{10,... | collective-permute-start | bytes 3145736 | tf_op jit(solution)/shard_map/ppermute | solution.py:55
  119.0 20.1 %collective-permute-done.28 = f32[1024]{0:T(1024)S(1)} collective-permute-done((f32[1024]{0:T(1024)S(1)}, f32[1024]{0:T(1024)S(1)}, u32[]{:S(2)}, u32[]{:S(2)}) %collective-permute-start.28) | collective-permute-done | bytes 4128 | tf_op jit(solution)/shard_map/ppermute | solution.py:55
  140.3 1.8 %collective-permute-start.29 = (f32[512]{0:T(512)S(1)}, f32[512]{0:T(512)S(1)}, u32[]{:S(2)}, u32[]{:S(2)}) collective-permute-start(f32[512]{0:T(512)S(1)} %broadcast_multiply_fusion), channel_id=1, source_target_pairs={{0,4},{1,5},{2,6},{3,7},{4,0},{5,1},{6,2},{7,3},{8,12},{9,13},{10,... | collective-permute-start | bytes 6152 | tf_op jit(solution)/shard_map/ppermute | solution.py:55
  142.1 1.9 %collective-permute-done.29 = f32[512]{0:T(512)S(1)} collective-permute-done((f32[512]{0:T(512)S(1)}, f32[512]{0:T(512)S(1)}, u32[]{:S(2)}, u32[]{:S(2)}) %collective-permute-start.29) | collective-permute-done | bytes 2080 | tf_op jit(solution)/shard_map/ppermute | solution.py:55
  144.0 1.5 collective-permute-start.30
  145.5 2.0 %collective-permute-done.30 = f32[256]{0:T(256)S(1)} collective-permute-done((f32[256]{0:T(256)S(1)}, f32[256]{0:T(256)S(1)}, u32[]{:S(2)}, u32[]{:S(2)}) %collective-permute-start.30) | collective-permute-done | bytes 1056 | tf_op jit(solution)/shard_map/ppermute | solution.py:58
  148.7 1.5 collective-permute-start.32
  150.2 2.1 %collective-permute-done.32 = f32[512]{0:T(512)S(1)} collective-permute-done((f32[512]{0:T(512)S(1)}, f32[512]{0:T(512)S(1)}, u32[]{:S(2)}, u32[]{:S(2)}) %collective-permute-start.32) | collective-permute-done | bytes 2080 | tf_op jit(solution)/shard_map/ppermute | solution.py:49
  152.5 2.7 %collective-permute-start.33 = (f32[1024]{0:T(1024)S(1)}, f32[1024]{0:T(1024)S(1)}, u32[]{:S(2)}, u32[]{:S(2)}) collective-permute-start(f32[1024]{0:T(1024)S(1)} %bitcast.61), channel_id=1, source_target_pairs={{0,12},{1,13},{2,14},{3,15},{4,8},{5,9},{6,10},{7,11},{8,4},{9,5},... | collective-permute-start | bytes 12296 | tf_op jit(solution)/shard_map/ppermute | solution.py:55
  155.2 2.8 %collective-permute-done.33 = f32[1024]{0:T(1024)S(1)} collective-permute-done((f32[1024]{0:T(1024)S(1)}, f32[1024]{0:T(1024)S(1)}, u32[]{:S(2)}, u32[]{:S(2)}) %collective-permute-start.33) | collective-permute-done | bytes 4128 | tf_op jit(solution)/shard_map/ppermute | solution.py:55
  (108 shorter events, 30.3 us)
Async XLA Ops:
  1.2 15.0 %collective-permute-start = (bf16[256,1024]{1,0:T(8,128)(2,1)S(1)}, bf16[256,1024]{1,0:T(8,128)(2,1)}, u32[]{:S(2)}, u32[]{:S(2)}) collective-permute-start(bf16[256,1024]{1,0:T(8,128)(2,1)S(1)} %constant_dynamic-slice_fusion), channel_id=1, source_target_pairs={{0,2},{1,3},{2,0},{3,1},{4,6},{5,7},{6,4},{7,5},{8,10},{9,11},{10,... | collective-permute-start | bytes 1572872 | tf_op jit(solution)/shard_map/ppermute | solution.py:49
  4.2 23.7 %collective-permute-start.3 = (bf16[256,1024]{1,0:T(8,128)(2,1)S(1)}, bf16[256,1024]{1,0:T(8,128)(2,1)}, u32[]{:S(2)}, u32[]{:S(2)}) collective-permute-start(bf16[256,1024]{1,0:T(8,128)(2,1)S(1)} %constant_dynamic-slice_fusion), channel_id=1, source_target_pairs={{0,1},{1,0},{2,3},{3,2},{4,5},{5,4},{6,7},{7,6},{8,9},{9,8},{10,11... | collective-permute-start | bytes 1572872 | tf_op jit(solution)/shard_map/ppermute | solution.py:49
  17.2 9.3 %collective-permute-start.1 = (bf16[512,256]{1,0:T(8,128)(2,1)S(1)}, bf16[512,256]{1,0:T(8,128)(2,1)S(1)}, u32[]{:S(2)}, u32[]{:S(2)}) collective-permute-start(bf16[512,256]{1,0:T(8,128)(2,1)S(1)} %get-tuple-element.20), channel_id=1, source_target_pairs={{0,2},{1,3},{2,0},{3,1},{4,6},{5,7},{6,4},{7,5},{8,10},{9,11},{10,... | collective-permute-start | bytes 786440 | tf_op jit(solution)/shard_map/ppermute | solution.py:49
  19.4 8.6 %collective-permute-start.2 = (bf16[512,256]{1,0:T(8,128)(2,1)S(1)}, bf16[512,256]{1,0:T(8,128)(2,1)S(1)}, u32[]{:S(2)}, u32[]{:S(2)}) collective-permute-start(bf16[512,256]{1,0:T(8,128)(2,1)S(1)} %get-tuple-element.21), channel_id=1, source_target_pairs={{0,1},{1,0},{2,3},{3,2},{4,5},{5,4},{6,7},{7,6},{8,9},{9,8},{10,11... | collective-permute-start | bytes 786440 | tf_op jit(solution)/shard_map/ppermute | solution.py:49
  19.5 10.0 %collective-permute-start.4 = (bf16[512,256]{1,0:T(8,128)(2,1)S(1)}, bf16[512,256]{1,0:T(8,128)(2,1)S(1)}, u32[]{:S(2)}, u32[]{:S(2)}) collective-permute-start(bf16[512,256]{1,0:T(8,128)(2,1)S(1)} %get-tuple-element.22), channel_id=1, source_target_pairs={{0,3},{1,2},{2,1},{3,0},{4,7},{5,6},{6,5},{7,4},{8,11},{9,10},{10,... | collective-permute-start | bytes 786440 | tf_op jit(solution)/shard_map/ppermute | solution.py:49
  19.9 9.6 %collective-permute-start.5 = (bf16[256,1024]{1,0:T(8,128)(2,1)}, bf16[256,1024]{1,0:T(8,128)(2,1)S(1)}, u32[]{:S(2)}, u32[]{:S(2)}) collective-permute-start(bf16[256,1024]{1,0:T(8,128)(2,1)} %collective-permute-done), channel_id=1, source_target_pairs={{0,1},{1,0},{2,3},{3,2},{4,5},{5,4},{6,7},{7,6},{8,9},{9,8},{10,11... | collective-permute-start | bytes 1572872 | tf_op jit(solution)/shard_map/ppermute | solution.py:49
  31.3 14.9 %collective-permute-start.11 = (bf16[256,1024]{1,0:T(8,128)(2,1)S(1)}, bf16[256,1024]{1,0:T(8,128)(2,1)S(1)}, u32[]{:S(2)}, u32[]{:S(2)}) collective-permute-start(bf16[256,1024]{1,0:T(8,128)(2,1)S(1)} %get-tuple-element.17), channel_id=1, source_target_pairs={{0,2},{1,3},{2,0},{3,1},{4,6},{5,7},{6,4},{7,5},{8,10},{9,11},{10,... | collective-permute-start | bytes 1572872 | tf_op jit(solution)/shard_map/ppermute | solution.py:49
  33.1 5.3 %collective-permute-start.9 = (bf16[256,1024]{1,0:T(8,128)(2,1)S(1)}, bf16[256,1024]{1,0:T(8,128)(2,1)S(1)}, u32[]{:S(2)}, u32[]{:S(2)}) collective-permute-start(bf16[256,1024]{1,0:T(8,128)(2,1)S(1)} %get-tuple-element.17), channel_id=1, source_target_pairs={{0,1},{1,0},{2,3},{3,2},{4,5},{5,4},{6,7},{7,6},{8,9},{9,8},{10,11... | collective-permute-start | bytes 1572872 | tf_op jit(solution)/shard_map/ppermute | solution.py:49
  33.1 25.6 %collective-permute-start.7 = (bf16[512,1024]{1,0:T(8,128)(2,1)S(1)}, bf16[512,1024]{1,0:T(8,128)(2,1)S(1)}, u32[]{:S(2)}, u32[]{:S(2)}) collective-permute-start(bf16[512,1024]{1,0:T(8,128)(2,1)S(1)} %add_add_fusion.2), channel_id=1, source_target_pairs={{0,4},{1,5},{2,6},{3,7},{4,0},{5,1},{6,2},{7,3},{8,12},{9,13},{10,... | collective-permute-start | bytes 3145736 | tf_op jit(solution)/shard_map/ppermute | solution.py:55
  34.7 24.0 %collective-permute-start.8 = (bf16[512,1024]{1,0:T(8,128)(2,1)S(1)}, bf16[512,1024]{1,0:T(8,128)(2,1)S(1)}, u32[]{:S(2)}, u32[]{:S(2)}) collective-permute-start(bf16[512,1024]{1,0:T(8,128)(2,1)S(1)} %add_add_fusion.2), channel_id=1, source_target_pairs={{0,0},{1,1},{2,2},{3,3},{4,8},{5,9},{6,10},{7,11},{8,4},{9,5},{10,... | collective-permute-start | bytes 3145736 | tf_op jit(solution)/shard_map/ppermute | solution.py:55
  35.4 2.0 %collective-permute-start.10 = (bf16[256,1024]{1,0:T(8,128)(2,1)S(1)}, bf16[256,1024]{1,0:T(8,128)(2,1)S(1)}, u32[]{:S(2)}, u32[]{:S(2)}) collective-permute-start(bf16[256,1024]{1,0:T(8,128)(2,1)S(1)} %get-tuple-element.18), channel_id=1, source_target_pairs={{0,1},{1,0},{2,3},{3,2},{4,5},{5,4},{6,7},{7,6},{8,9},{9,8},{10,11... | collective-permute-start | bytes 1572872 | tf_op jit(solution)/shard_map/ppermute | solution.py:49
  37.4 18.7 %collective-permute-start.6 = (bf16[256,1024]{1,0:T(8,128)(2,1)S(1)}, bf16[256,1024]{1,0:T(8,128)(2,1)S(1)}, u32[]{:S(2)}, u32[]{:S(2)}) collective-permute-start(bf16[256,1024]{1,0:T(8,128)(2,1)S(1)} %get-tuple-element.18), channel_id=1, source_target_pairs={{0,2},{1,3},{2,0},{3,1},{4,6},{5,7},{6,4},{7,5},{8,10},{9,11},{10,... | collective-permute-start | bytes 1572872 | tf_op jit(solution)/shard_map/ppermute | solution.py:49
  58.8 2.0 %collective-permute-start.12 = (bf16[256,1024]{1,0:T(8,128)(2,1)S(1)}, bf16[256,1024]{1,0:T(8,128)(2,1)S(1)}, u32[]{:S(2)}, u32[]{:S(2)}) collective-permute-start(bf16[256,1024]{1,0:T(8,128)(2,1)S(1)} %get-tuple-element.32), channel_id=1, source_target_pairs={{0,1},{1,0},{2,3},{3,2},{4,5},{5,4},{6,7},{7,6},{8,9},{9,8},{10,11... | collective-permute-start | bytes 1572872 | tf_op jit(solution)/shard_map/ppermute | solution.py:49
  58.9 2.6 %collective-permute-start.13 = (bf16[256,1024]{1,0:T(8,128)(2,1)S(1)}, bf16[256,1024]{1,0:T(8,128)(2,1)S(1)}, u32[]{:S(2)}, u32[]{:S(2)}) collective-permute-start(bf16[256,1024]{1,0:T(8,128)(2,1)S(1)} %get-tuple-element.31), channel_id=1, source_target_pairs={{0,1},{1,0},{2,3},{3,2},{4,5},{5,4},{6,7},{7,6},{8,9},{9,8},{10,11... | collective-permute-start | bytes 1572872 | tf_op jit(solution)/shard_map/ppermute | solution.py:49
  63.1 7.9 %collective-permute-start.14 = (bf16[256,1024]{1,0:T(8,128)(2,1)S(1)}, bf16[256,1024]{1,0:T(8,128)(2,1)S(1)}, u32[]{:S(2)}, u32[]{:S(2)}) collective-permute-start(bf16[256,1024]{1,0:T(8,128)(2,1)S(1)} %get-tuple-element.25), channel_id=1, source_target_pairs={{0,1},{1,0},{2,3},{3,2},{4,5},{5,4},{6,7},{7,6},{8,9},{9,8},{10,11... | collective-permute-start | bytes 1572872 | tf_op jit(solution)/shard_map/ppermute | solution.py:49
  63.3 14.2 %collective-permute-start.15 = (bf16[256,1024]{1,0:T(8,128)(2,1)S(1)}, bf16[256,1024]{1,0:T(8,128)(2,1)S(1)}, u32[]{:S(2)}, u32[]{:S(2)}) collective-permute-start(bf16[256,1024]{1,0:T(8,128)(2,1)S(1)} %get-tuple-element.25), channel_id=1, source_target_pairs={{0,2},{1,3},{2,0},{3,1},{4,6},{5,7},{6,4},{7,5},{8,10},{9,11},{10,... | collective-permute-start | bytes 1572872 | tf_op jit(solution)/shard_map/ppermute | solution.py:49
  63.7 28.2 %collective-permute-start.16 = (bf16[512,1024]{1,0:T(8,128)(2,1)S(1)}, bf16[512,1024]{1,0:T(8,128)(2,1)S(1)}, u32[]{:S(2)}, u32[]{:S(2)}) collective-permute-start(bf16[512,1024]{1,0:T(8,128)(2,1)S(1)} %get-tuple-element.15), channel_id=1, source_target_pairs={{0,4},{1,5},{2,6},{3,7},{4,0},{5,1},{6,2},{7,3},{8,12},{9,13},{10,... | collective-permute-start | bytes 3145736 | tf_op jit(solution)/shard_map/ppermute | solution.py:55
  68.5 23.4 %collective-permute-start.17 = (bf16[512,1024]{1,0:T(8,128)(2,1)S(1)}, bf16[512,1024]{1,0:T(8,128)(2,1)S(1)}, u32[]{:S(2)}, u32[]{:S(2)}) collective-permute-start(bf16[512,1024]{1,0:T(8,128)(2,1)S(1)} %get-tuple-element.16), channel_id=1, source_target_pairs={{0,0},{1,1},{2,2},{3,3},{4,8},{5,9},{6,10},{7,11},{8,4},{9,5},{10,... | collective-permute-start | bytes 3145736 | tf_op jit(solution)/shard_map/ppermute | solution.py:55
  69.4 13.7 %collective-permute-start.20 = (bf16[256,1024]{1,0:T(8,128)(2,1)S(1)}, bf16[256,1024]{1,0:T(8,128)(2,1)S(1)}, u32[]{:S(2)}, u32[]{:S(2)}) collective-permute-start(bf16[256,1024]{1,0:T(8,128)(2,1)S(1)} %get-tuple-element.26), channel_id=1, source_target_pairs={{0,16},{16,0},{1,17},{17,1},{2,18},{18,2},{3,19},{19,3},{4,20},{20... | collective-permute-start | bytes 1572872 | tf_op jit(solution)/shard_map/ppermute | solution.py:58
  71.0 12.1 %collective-permute-start.18 = (bf16[256,1024]{1,0:T(8,128)(2,1)S(1)}, bf16[256,1024]{1,0:T(8,128)(2,1)S(1)}, u32[]{:S(2)}, u32[]{:S(2)}) collective-permute-start(bf16[256,1024]{1,0:T(8,128)(2,1)S(1)} %slice_add_fusion), channel_id=1, source_target_pairs={{0,1},{1,0},{2,3},{3,2},{4,5},{5,4},{6,7},{7,6},{8,9},{9,8},{10,11... | collective-permute-start | bytes 1572872 | tf_op jit(solution)/shard_map/ppermute | solution.py:49
  77.5 13.4 %collective-permute-start.19 = (bf16[256,1024]{1,0:T(8,128)(2,1)S(1)}, bf16[256,1024]{1,0:T(8,128)(2,1)S(1)}, u32[]{:S(2)}, u32[]{:S(2)}) collective-permute-start(bf16[256,1024]{1,0:T(8,128)(2,1)S(1)} %slice_add_fusion), channel_id=1, source_target_pairs={{0,2},{1,3},{2,0},{3,1},{4,6},{5,7},{6,4},{7,5},{8,10},{9,11},{10,... | collective-permute-start | bytes 1572872 | tf_op jit(solution)/shard_map/ppermute | solution.py:49
  92.0 2.0 %collective-permute-start.22 = (bf16[256,1024]{1,0:T(8,128)(2,1)S(1)}, bf16[256,1024]{1,0:T(8,128)(2,1)S(1)}, u32[]{:S(2)}, u32[]{:S(2)}) collective-permute-start(bf16[256,1024]{1,0:T(8,128)(2,1)S(1)} %get-tuple-element.29), channel_id=1, source_target_pairs={{0,1},{1,0},{2,3},{3,2},{4,5},{5,4},{6,7},{7,6},{8,9},{9,8},{10,11... | collective-permute-start | bytes 1572872 | tf_op jit(solution)/shard_map/ppermute | solution.py:49
  95.1 14.0 %collective-permute-start.24 = (bf16[256,1024]{1,0:T(8,128)(2,1)S(1)}, bf16[256,1024]{1,0:T(8,128)(2,1)S(1)}, u32[]{:S(2)}, u32[]{:S(2)}) collective-permute-start(bf16[256,1024]{1,0:T(8,128)(2,1)S(1)} %get-tuple-element.23), channel_id=1, source_target_pairs={{0,2},{1,3},{2,0},{3,1},{4,6},{5,7},{6,4},{7,5},{8,10},{9,11},{10,... | collective-permute-start | bytes 1572872 | tf_op jit(solution)/shard_map/ppermute | solution.py:49
  96.7 12.5 %collective-permute-start.21 = (bf16[256,1024]{1,0:T(8,128)(2,1)S(1)}, bf16[256,1024]{1,0:T(8,128)(2,1)S(1)}, u32[]{:S(2)}, u32[]{:S(2)}) collective-permute-start(bf16[256,1024]{1,0:T(8,128)(2,1)S(1)} %get-tuple-element.30), channel_id=1, source_target_pairs={{0,1},{1,0},{2,3},{3,2},{4,5},{5,4},{6,7},{7,6},{8,9},{9,8},{10,11... | collective-permute-start | bytes 1572872 | tf_op jit(solution)/shard_map/ppermute | solution.py:49
  96.9 13.0 %collective-permute-start.23 = (bf16[256,1024]{1,0:T(8,128)(2,1)S(1)}, bf16[256,1024]{1,0:T(8,128)(2,1)S(1)}, u32[]{:S(2)}, u32[]{:S(2)}) collective-permute-start(bf16[256,1024]{1,0:T(8,128)(2,1)S(1)} %get-tuple-element.23), channel_id=1, source_target_pairs={{0,1},{1,0},{2,3},{3,2},{4,5},{5,4},{6,7},{7,6},{8,9},{9,8},{10,11... | collective-permute-start | bytes 1572872 | tf_op jit(solution)/shard_map/ppermute | solution.py:49
  97.5 13.9 %collective-permute-start.26 = (bf16[256,1024]{1,0:T(8,128)(2,1)S(1)}, bf16[256,1024]{1,0:T(8,128)(2,1)S(1)}, u32[]{:S(2)}, u32[]{:S(2)}) collective-permute-start(bf16[256,1024]{1,0:T(8,128)(2,1)S(1)} %get-tuple-element.24), channel_id=1, source_target_pairs={{0,16},{16,0},{1,17},{17,1},{2,18},{18,2},{3,19},{19,3},{4,20},{20... | collective-permute-start | bytes 1572872 | tf_op jit(solution)/shard_map/ppermute | solution.py:58
  112.2 26.9 %collective-permute-start.27 = (f32[512,512]{1,0:T(8,128)S(1)}, f32[512,512]{1,0:T(8,128)S(1)}, u32[]{:S(2)}, u32[]{:S(2)}) collective-permute-start(f32[512,512]{1,0:T(8,128)S(1)} %convolution_add_fusion), channel_id=1, source_target_pairs={{0,4},{1,5},{2,6},{3,7},{4,0},{5,1},{6,2},{7,3},{8,12},{9,13},{10,... | collective-permute-start | bytes 3145736 | tf_op jit(solution)/shard_map/ppermute | solution.py:55
  118.1 21.0 %collective-permute-start.28 = (f32[1024]{0:T(1024)S(1)}, f32[1024]{0:T(1024)S(1)}, u32[]{:S(2)}, u32[]{:S(2)}) collective-permute-start(f32[1024]{0:T(1024)S(1)} %pad_maximum_fusion.8), channel_id=1, source_target_pairs={{0,4},{1,5},{2,6},{3,7},{4,0},{5,1},{6,2},{7,3},{8,12},{9,13},{10,... | collective-permute-start | bytes 12296 | tf_op jit(solution)/shard_map/ppermute | solution.py:55
  140.3 3.7 %collective-permute-start.29 = (f32[512]{0:T(512)S(1)}, f32[512]{0:T(512)S(1)}, u32[]{:S(2)}, u32[]{:S(2)}) collective-permute-start(f32[512]{0:T(512)S(1)} %broadcast_multiply_fusion), channel_id=1, source_target_pairs={{0,4},{1,5},{2,6},{3,7},{4,0},{5,1},{6,2},{7,3},{8,12},{9,13},{10,... | collective-permute-start | bytes 6152 | tf_op jit(solution)/shard_map/ppermute | solution.py:55
  144.0 3.6 %collective-permute-start.30 = (f32[256]{0:T(256)S(1)}, f32[256]{0:T(256)S(1)}, u32[]{:S(2)}, u32[]{:S(2)}) collective-permute-start(f32[256]{0:T(256)S(1)} %slice.108), channel_id=1, source_target_pairs={{0,16},{16,0},{1,17},{17,1},{2,18},{18,2},{3,19},{19,3},{4,20},{20... | collective-permute-start | bytes 3080 | tf_op jit(solution)/shard_map/ppermute | solution.py:58
  148.7 3.6 %collective-permute-start.32 = (f32[512]{0:T(512)S(1)}, f32[512]{0:T(512)S(1)}, u32[]{:S(2)}, u32[]{:S(2)}) collective-permute-start(f32[512]{0:T(512)S(1)} %maximum_select_fusion), channel_id=1, source_target_pairs={{0,2},{1,3},{2,0},{3,1},{4,6},{5,7},{6,4},{7,5},{8,10},{9,11},{10,... | collective-permute-start | bytes 6152 | tf_op jit(solution)/shard_map/ppermute | solution.py:49
  152.5 5.5 %collective-permute-start.33 = (f32[1024]{0:T(1024)S(1)}, f32[1024]{0:T(1024)S(1)}, u32[]{:S(2)}, u32[]{:S(2)}) collective-permute-start(f32[1024]{0:T(1024)S(1)} %bitcast.61), channel_id=1, source_target_pairs={{0,12},{1,13},{2,14},{3,15},{4,8},{5,9},{6,10},{7,11},{8,4},{9,5},... | collective-permute-start | bytes 12296 | tf_op jit(solution)/shard_map/ppermute | solution.py:55
  (6 other events, 35.9 us)

commit v2 on v1

--- a/solution.py
+++ b/solution.py
@@ -24,7 +24,8 @@
 
 
 def behind(value, zeros):
-    return value + zeros[:, :value.shape[-1]].astype(value.dtype)
+    zeros = zeros if zeros.shape[-1] == 1 else zeros[:, :value.shape[-1]]
+    return value + zeros.astype(value.dtype)
 
 
 def square_sum(a):
@@ -36,7 +37,7 @@
     nx = n_tgt // (nz * CORES)
     outer = (1, 0, 3, 2)
     middle = (0, 2, 1, 3)
-    spread_out = (3, 2, 1, 0)
+    mirror = (3, 2, 1, 0)
 
     def place(z, x, c):
         return (z * nx + x) * CORES + c
@@ -54,8 +55,21 @@
         ]
         return lax.ppermute(value, "tgt", pairs)
 
-    def over_pool(value, shift):
-        return lax.ppermute(value, "pool", [(p, (p + shift) % n_pool) for p in range(n_pool)])
+    def over_pool(value, shift, flip=0, to=None):
+        to = to or range(nz)
+        pairs = [
+            (p * n_tgt + place(z, x, c), ((p + shift) % n_pool) * n_tgt + place(to[z], x, c ^ flip))
+            for p in range(n_pool) for z in range(nz) for x in range(nx) for c in range(CORES)
+        ]
+        return lax.ppermute(value, ("pool", "tgt"), pairs)
+
+    def in_order(pieces, index):
+        n = len(pieces)
+        if n == 2:
+            low = index == 0
+            return jnp.concatenate([jnp.where(low, pieces[0], pieces[1]), jnp.where(low, pieces[1], pieces[0])], axis=0)
+        stacked = jnp.take(jnp.stack(pieces), (index - jnp.arange(n)) % n, axis=0)
+        return stacked.reshape((-1,) + stacked.shape[2:])
 
     def choose(values, z):
         out = jnp.int32(values[0])
@@ -73,7 +87,7 @@
         quarter = hidden // nz
 
         local_index = pool_index - lax.axis_index("pool") * pool_table.shape[0]
-        pool_rows = jnp.take(pool_table, local_index, axis=0)
+        pool_rows = pool_table.at[local_index].get(mode="promise_in_bounds")
         count = pool_rows.shape[0] // (nx * CORES)
         count_t = target_features.shape[0] // (nx * CORES)
 
@@ -103,16 +117,27 @@
 
         order = [(s, 0) for s in range(nx)] + [(s, 1) for s in range(nx)]
 
+        pool = lax.axis_index("pool")
+        part_rows = width // n_pool
         own1 = factor_own([0, 1, 2, 1])
-        same1 = [own1] + factor_x(own1)
-
-        done = token(*same1[1:])
+        mine1 = lax.dynamic_slice_in_dim(own1, pool * part_rows, part_rows, 0)
+        parts1 = [inner(mine1, s, 0) for s in range(1, nx)]
+
+        done = token(*parts1)
         features = [inner(behind(rows_of(s, f), done), s, f) if s or f else rows_of(0, 0) for s, f in order]
-        first = partial(same1 + factor_flip(same1))
+        flip1 = inner(own1, 0, 1)
+        near1, far1 = [], []
+        for v in parts1:
+            v = behind(v, done)
+            near1.append([v] + [over_pool(v, r) for r in range(1, n_pool)])
+            far1.append([inner(v, 0, 1)] + [over_pool(v, r, 1) for r in range(1, n_pool)])
+        done = token(*[v for (s, _), v in zip(order, features) if s])
+        near1, far1 = [[in_order([behind(v, done[:, :1]) for v in u], pool) for u in w] for w in (near1, far1)]
+        first = partial([own1] + near1 + [flip1] + far1).astype(BF)
 
         start = token(first)
-        step1 = along_z(first.astype(BF), outer)
-        step2 = along_z(first.astype(BF), middle)
+        step1 = along_z(first, outer)
+        step2 = along_z(first, middle)
         own2 = behind(factor_own([0, 0, 0, 0]), start)
         own3 = behind(factor_own([1, 1, 1, 2]), start)
         flip2, flip3 = inner(own2, 0, 1), inner(own3, 0, 1)
@@ -143,36 +168,51 @@
         p_moved_b = [over_pool(p_b, s) for s in range(1, n_pool)]
         t_flip_b = inner(t_b, 0, 1)
 
-        def spread(t, t_moved, t_flip, p, p_moved):
-            low = jnp.concatenate([t] + t_moved, axis=0)
-            high = jnp.concatenate([t_flip] + [inner(v, 0, 1) for v in t_moved], axis=0)
-            return jnp.where(top, high, low), jnp.where(top, low, high), jnp.concatenate([p] + p_moved, axis=0)
-
-        keep_a, give_a, p_a = spread(t_a, t_moved_a, t_flip_a, p_a, p_moved_a)
-        keep_b, give_b, p_b = spread(t_b, t_moved_b, t_flip_b, p_b, p_moved_b)
-
-        given = along_z(matmul_t(give_a, p_a) + matmul_t(give_b, p_b), outer)
-        p_squares = square_sum(p_a) + square_sum(p_b)
-        n_keep = keep_a.shape[0]
-        squares = along_z(jnp.concatenate([square_sum(give_a) + square_sum(give_b), p_squares]), outer)
-        target_var = 1.0 + (square_sum(keep_a) + square_sum(keep_b) + squares[:n_keep])
-        pool_var = 1.0 + (p_squares + squares[n_keep:])
-        cross = matmul_t(keep_a, p_a) + matmul_t(keep_b, p_b) + given
-        ratio = jnp.square(cross) / (target_var[:, None] * pool_var[None, :])
-        sums = -0.5 * jnp.sum(jnp.log1p(-ratio), axis=0)
-
-        sums = sums + along_z(sums, outer)
-        own = sums[:count]
+        def groups(t, t_moved, t_flip):
+            far, far_flip = jnp.concatenate(t_moved, axis=0), jnp.concatenate([inner(v, 0, 1) for v in t_moved], axis=0)
+            keep = jnp.where(top, t_flip, t), jnp.where(top, far_flip, far)
+            give = jnp.where(top, t, t_flip), jnp.where(top, far, far_flip)
+            return keep, give
+
+        keep_a, give_a = groups(t_a, t_moved_a, t_flip_a)
+        keep_b, give_b = groups(t_b, t_moved_b, t_flip_b)
+        p_far_a, p_far_b = jnp.concatenate(p_moved_a, axis=0), jnp.concatenate(p_moved_b, axis=0)
+        p_all_a, p_all_b = jnp.concatenate([p_a, p_far_a], axis=0), jnp.concatenate([p_b, p_far_b], axis=0)
+
+        given_near = along_z(matmul_t(give_a[0], p_a) + matmul_t(give_b[0], p_b), outer)
+        swapped = token(given_near)[:, :1]
+        give_side = behind(matmul_t(give_a[0], p_far_a) + matmul_t(give_b[0], p_far_b), swapped)
+        give_far = behind(matmul_t(give_a[1], p_all_a) + matmul_t(give_b[1], p_all_b), swapped)
+        if nx == 2:
+            given = along_z(jnp.concatenate([give_side, give_far], axis=1), outer)
+            given_side, given_far = given[:, :give_side.shape[1]], given[:, give_side.shape[1]:]
+        else:
+            given_side, given_far = along_z(give_side, outer), along_z(give_far, outer)
+
+        p_squares = square_sum(p_all_a) + square_sum(p_all_b)
+        sizes = [p_squares.shape[0], keep_a[0].shape[0], keep_a[1].shape[0]]
+        squares = along_z(jnp.concatenate(
+            [p_squares] + [square_sum(a) + square_sum(b) for a, b in zip(give_a, give_b)]
+        ), outer)
+        pool_var = 1.0 + (p_squares + squares[:sizes[0]])
+
+        def log_sums(group, given, offset):
+            a, b = keep_a[group], keep_b[group]
+            target_var = 1.0 + (square_sum(a) + square_sum(b) + squares[offset:offset + sizes[1 + group]])
+            cross = matmul_t(a, p_all_a) + matmul_t(b, p_all_b) + given
+            ratio = jnp.square(cross) / (target_var[:, None] * pool_var[None, :])
+            return -0.5 * jnp.sum(jnp.log1p(-ratio), axis=0)
+
+        sums = log_sums(0, jnp.concatenate([given_near, given_side], axis=1), sizes[0])
+        sums = sums + log_sums(1, given_far, sizes[0] + sizes[1])
+
+        blocks = [sums[s * count:(s + 1) * count] for s in range(n_pool)]
+        own = blocks[0] + along_z(blocks[0], outer)
         for s in range(1, n_pool):
-            own = own + over_pool(sums[s * count:(s + 1) * count], -s)
-        flipped = inner(own, 0, 1)
-        both = jnp.where(core == 0, jnp.concatenate([own, flipped]), jnp.concatenate([flipped, own]))
-        parts = jnp.stack([both] + [inner(both, s, 0) for s in range(1, nx)])
-        if nx == 2:
-            scores = jnp.where(x == 0, parts.reshape(-1), parts[::-1].reshape(-1))
-        else:
-            scores = jnp.take(parts, (x - jnp.arange(nx)) % nx, axis=0).reshape(-1)
-        return jnp.where(z >= nz - 2, scores, along_z(scores, spread_out))
+            own = own + (over_pool(blocks[s], -s) + over_pool(blocks[s], -s, 0, outer))
+        rows = [in_order([own if s == 0 else inner(own, s, 0), inner(own, s, 1)], core) for s in range(nx)]
+        scores = in_order(rows, x)
+        return jnp.where(z >= nz - 2, scores, along_z(scores, mirror))
 
     return body
 

time: 159 us -> 157 us (0.987)
  waiting for transfers between devices: 94.7 us -> 85 us
  local copies, waits for them, and re-layouts: 8.38 us -> 10.5 us
  between operations: 0.43 us -> 2.48 us
  other arithmetic: 7.5 us -> 9.28 us
    ppermute x23 -> x24, waiting for transfers between devices: 59.2 us -> 50 us  [inner(): return lax.ppermute(value, 'tgt', pairs)]
    ppermute x8 -> x9, waiting for transfers between devices: 28.3 us -> 25.4 us  [along_z(): return lax.ppermute(value, 'tgt', pairs)]
    ppermute x3 -> x6, waiting for transfers between devices: 7.16 us -> 9.55 us  [over_pool(): return lax.ppermute(value, ('pool', 'tgt'), pairs)]
    dynamic_slice x0 -> x1, local copies, waits for them, and re-layouts: none -> 1.97 us  [body(): mine1 = lax.dynamic_slice_in_dim(own1, pool * part_rows, part_rows, 0)]
    add x10 -> x13, other arithmetic: 0.6 us -> 2.39 us  [the longest x6 2.34 us: behind(): return value + zeros.astype(value.dtype)]
    dot_general x4 -> x10, matrix products: 3.49 us -> 4.69 us  [matmul_t(): lax.dot_general(a, b, (((1,), (1,)), ((), ())), preferred_element_type=F32)]
    ppermute x3 -> x6, starting transfers between devices: 4.71 us -> 5.8 us  [over_pool(): return lax.ppermute(value, ('pool', 'tgt'), pairs)]
    ppermute x23 -> x24, starting transfers between devices: 13.3 us -> 13 us  [inner(): return lax.ppermute(value, 'tgt', pairs)]
  transfers between devices with their start and end apart: 34 -> 39, of which waited for: 22 -> 20; matrix products, arithmetic and copies ran while one was open for 13% -> 17% of each run, Pallas kernels for 0% -> 0%
where the time goes in v2:
time: 157 us
  waiting for transfers between devices  85 us (54%)
  starting transfers between devices  35 us (22%)
  matrix products  14.6 us (9%)
  local copies, waits for them, and re-layouts  10.5 us (7%)
  other arithmetic  9.28 us (6%)
  between operations  2.48 us (2%)
    ppermute x24, waiting for transfers between devices, inner(): return lax.ppermute(value, 'tgt', pairs)  50 us
    ppermute x9, waiting for transfers between devices, along_z(): return lax.ppermute(value, 'tgt', pairs)  25.4 us
    ppermute x9, starting transfers between devices, along_z(): return lax.ppermute(value, 'tgt', pairs)  16.2 us
    ppermute x24, starting transfers between devices, inner(): return lax.ppermute(value, 'tgt', pairs)  13 us
    dot_general x16, matrix products, matmul(): lax.dot_general(a, b, (((1,), (0,)), ((), ())), preferred_element_type=F32)  9.89 us
    ppermute x6, waiting for transfers between devices, over_pool(): return lax.ppermute(value, ('pool', 'tgt'), pairs)  9.55 us
    ppermute x6, starting transfers between devices, over_pool(): return lax.ppermute(value, ('pool', 'tgt'), pairs)  5.8 us
    dot_general x10, matrix products, matmul_t(): lax.dot_general(a, b, (((1,), (1,)), ((), ())), preferred_element_type=F32)  4.69 us
  transfers between devices with their start and end apart: 39, of which 20 were waited for; matrix products, arithmetic and copies ran while one was open for 17% of the time, Pallas kernels for 0%

profile of v2, /device:TPU:0, one launch (start us, length us, event | category | flops | bytes accessed | tf_op | source)
XLA Modules:
  0.0 156.9 jit_solution(16960350146080717517)
XLA Ops:
  0.0 2.0 %dynamic_slice.31 = bf16[128,1024]{1,0:T(8,128)(2,1)} dynamic-slice(bf16[256,4096]{1,0:T(8,128)(2,1)} %param.7, s32[]{:T(128)S(6)} %select_n.201, s32[]{:T(128)S(6)} %select_n.202), dynamic_slice_sizes={128,1024} | dynamic-slice | bytes 524292 | tf_op jit(solution)/shard_map/dynamic_slice | solution.py:123
  2.0 2.9 %collective-permute-start = (bf16[128,1024]{1,0:T(8,128)(2,1)}, bf16[128,1024]{1,0:T(8,128)(2,1)}, u32[]{:S(2)}, u32[]{:S(2)}) collective-permute-start(bf16[128,1024]{1,0:T(8,128)(2,1)} %dynamic_slice.31), channel_id=1, source_target_pairs={{0,2},{1,3},{2,0},{3,1},{4,6},{5,7},{6,4},{7,5},{8,10},{9,11},{10,... | collective-permute-start | bytes 786440 | tf_op jit(solution)/shard_map/ppermute | solution.py:50
  4.9 1.9 %constant_dynamic-slice_fusion = bf16[256,1024]{1,0:T(8,128)(2,1)} fusion(bf16[256,4096]{1,0:T(8,128)(2,1)} %param.7, s32[]{:T(128)S(6)} %select_n.198), kind=kLoop, calls=%fused_computation.166 | loop fusion | bytes 1048580 | tf_op jit(solution)/shard_map/dynamic_slice | solution.py:103
  7.5 3.9 %gather_fusion = bf16[1024,256]{1,0:T(8,128)(2,1)S(1)} fusion(bf16[4096,256]{1,0:T(8,128)(2,1)S(1)} %copy-done, s32[1024]{0:T(1024)S(1)} %fusion.42), kind=kCustom, calls=%fused_computation | custom fusion | bytes 1052672 | tf_op jit(solution)/shard_map/gather | solution.py:90
  13.7 1.3 collective-permute-start.1
  15.1 1.5 fusion.108
  17.6 1.8 %collective-permute-start.3 = (bf16[128,1024]{1,0:T(8,128)(2,1)S(1)}, bf16[128,1024]{1,0:T(8,128)(2,1)S(1)}, u32[]{:S(2)}, u32[]{:S(2)}) collective-permute-start(bf16[128,1024]{1,0:T(8,128)(2,1)S(1)} %broadcast_add_fusion.4), channel_id=1, source_target_pairs={{0,16},{1,17},{2,18},{3,19},{4,20},{5,21},{6,22},{7,23},{8,24},{9,... | collective-permute-start | bytes 786440 | tf_op jit(solution)/shard_map/ppermute | solution.py:64
  19.4 3.7 %collective-permute-done.1 = bf16[512,256]{1,0:T(8,128)(2,1)S(1)} collective-permute-done((bf16[512,256]{1,0:T(8,128)(2,1)}, bf16[512,256]{1,0:T(8,128)(2,1)S(1)}, u32[]{:S(2)}, u32[]{:S(2)}) %collective-permute-start.1) | collective-permute-done | bytes 262176 | tf_op jit(solution)/shard_map/ppermute | solution.py:50
  24.3 2.9 %collective-permute-done.2 = bf16[512,256]{1,0:T(8,128)(2,1)S(1)} collective-permute-done((bf16[512,256]{1,0:T(8,128)(2,1)}, bf16[512,256]{1,0:T(8,128)(2,1)S(1)}, u32[]{:S(2)}, u32[]{:S(2)}) %collective-permute-start.2) | collective-permute-done | bytes 262176 | tf_op jit(solution)/shard_map/ppermute | solution.py:50
  29.1 1.5 fusion.109
  30.6 1.0 broadcast_select_fusion.11
  34.0 1.8 %collective-permute-start.8 = (bf16[256,1024]{1,0:T(8,128)(2,1)S(1)}, bf16[256,1024]{1,0:T(8,128)(2,1)S(1)}, u32[]{:S(2)}, u32[]{:S(2)}) collective-permute-start(bf16[256,1024]{1,0:T(8,128)(2,1)S(1)} %get-tuple-element.23), channel_id=1, source_target_pairs={{0,2},{1,3},{2,0},{3,1},{4,6},{5,7},{6,4},{7,5},{8,10},{9,11},{10,... | collective-permute-start | bytes 1572872 | tf_op jit(solution)/shard_map/ppermute | solution.py:50
  36.5 4.4 %collective-permute-start.9 = (bf16[512,1024]{1,0:T(8,128)(2,1)S(1)}, bf16[512,1024]{1,0:T(8,128)(2,1)S(1)}, u32[]{:S(2)}, u32[]{:S(2)}) collective-permute-start(bf16[512,1024]{1,0:T(8,128)(2,1)S(1)} %add_convert_fusion.1), channel_id=1, source_target_pairs={{0,4},{1,5},{2,6},{3,7},{4,0},{5,1},{6,2},{7,3},{8,12},{9,13},{10,... | collective-permute-start | bytes 3145736 | tf_op jit(solution)/shard_map/ppermute | solution.py:56
  41.8 1.0 collective-permute-done.11
  44.3 4.6 %collective-permute-done.8 = bf16[256,1024]{1,0:T(8,128)(2,1)S(1)} collective-permute-done((bf16[256,1024]{1,0:T(8,128)(2,1)S(1)}, bf16[256,1024]{1,0:T(8,128)(2,1)S(1)}, u32[]{:S(2)}, u32[]{:S(2)}) %collective-permute-start.8) | collective-permute-done | bytes 524320 | tf_op jit(solution)/shard_map/ppermute | solution.py:50
  48.8 10.3 %collective-permute-done.13 = bf16[256,1024]{1,0:T(8,128)(2,1)S(1)} collective-permute-done((bf16[256,1024]{1,0:T(8,128)(2,1)S(1)}, bf16[256,1024]{1,0:T(8,128)(2,1)S(1)}, u32[]{:S(2)}, u32[]{:S(2)}) %collective-permute-start.13) | collective-permute-done | bytes 524320 | tf_op jit(solution)/shard_map/ppermute | solution.py:50
  59.1 5.3 %collective-permute-done.9 = bf16[512,1024]{1,0:T(8,128)(2,1)S(1)} collective-permute-done((bf16[512,1024]{1,0:T(8,128)(2,1)S(1)}, bf16[512,1024]{1,0:T(8,128)(2,1)S(1)}, u32[]{:S(2)}, u32[]{:S(2)}) %collective-permute-start.9) | collective-permute-done | bytes 1048608 | tf_op jit(solution)/shard_map/ppermute | solution.py:56
  69.1 1.6 %collective-permute-start.17 = (bf16[256,1024]{1,0:T(8,128)(2,1)S(1)}, bf16[256,1024]{1,0:T(8,128)(2,1)S(1)}, u32[]{:S(2)}, u32[]{:S(2)}) collective-permute-start(bf16[256,1024]{1,0:T(8,128)(2,1)S(1)} %get-tuple-element.34), channel_id=1, source_target_pairs={{0,16},{1,17},{2,18},{3,19},{4,20},{5,21},{6,22},{7,23},{8,24},{9,... | collective-permute-start | bytes 1572872 | tf_op jit(solution)/shard_map/ppermute | solution.py:64
  71.6 3.4 %collective-permute-start.19 = (bf16[512,1024]{1,0:T(8,128)(2,1)S(1)}, bf16[512,1024]{1,0:T(8,128)(2,1)S(1)}, u32[]{:S(2)}, u32[]{:S(2)}) collective-permute-start(bf16[512,1024]{1,0:T(8,128)(2,1)S(1)} %get-tuple-element.21), channel_id=1, source_target_pairs={{0,4},{1,5},{2,6},{3,7},{4,0},{5,1},{6,2},{7,3},{8,12},{9,13},{10,... | collective-permute-start | bytes 3145736 | tf_op jit(solution)/shard_map/ppermute | solution.py:56
  75.6 7.8 %collective-permute-done.17 = bf16[256,1024]{1,0:T(8,128)(2,1)S(1)} collective-permute-done((bf16[256,1024]{1,0:T(8,128)(2,1)S(1)}, bf16[256,1024]{1,0:T(8,128)(2,1)S(1)}, u32[]{:S(2)}, u32[]{:S(2)}) %collective-permute-start.17) | collective-permute-done | bytes 524320 | tf_op jit(solution)/shard_map/ppermute | solution.py:64
  85.1 4.8 %collective-permute-done.22 = bf16[256,1024]{1,0:T(8,128)(2,1)S(1)} collective-permute-done((bf16[256,1024]{1,0:T(8,128)(2,1)S(1)}, bf16[256,1024]{1,0:T(8,128)(2,1)S(1)}, u32[]{:S(2)}, u32[]{:S(2)}) %collective-permute-start.22) | collective-permute-done | bytes 524320 | tf_op jit(solution)/shard_map/ppermute | solution.py:50
  89.9 9.7 %collective-permute-done.18 = bf16[256,1024]{1,0:T(8,128)(2,1)S(1)} collective-permute-done((bf16[256,1024]{1,0:T(8,128)(2,1)S(1)}, bf16[256,1024]{1,0:T(8,128)(2,1)S(1)}, u32[]{:S(2)}, u32[]{:S(2)}) %collective-permute-start.18) | collective-permute-done | bytes 524320 | tf_op jit(solution)/shard_map/ppermute | solution.py:50
  107.2 10.0 %collective-permute-done.28 = bf16[256,1024]{1,0:T(8,128)(2,1)S(1)} collective-permute-done((bf16[256,1024]{1,0:T(8,128)(2,1)S(1)}, bf16[256,1024]{1,0:T(8,128)(2,1)S(1)}, u32[]{:S(2)}, u32[]{:S(2)}) %collective-permute-start.28) | collective-permute-done | bytes 524320 | tf_op jit(solution)/shard_map/ppermute | solution.py:50
  121.2 1.7 %collective-permute-start.31 = (f32[1024]{0:T(1024)S(1)}, f32[1024]{0:T(1024)S(1)}, u32[]{:S(2)}, u32[]{:S(2)}) collective-permute-start(f32[1024]{0:T(1024)S(1)} %pad_maximum_fusion.3), channel_id=1, source_target_pairs={{0,4},{1,5},{2,6},{3,7},{4,0},{5,1},{6,2},{7,3},{8,12},{9,13},{10,... | collective-permute-start | bytes 12296 | tf_op jit(solution)/shard_map/ppermute | solution.py:56
  123.4 16.7 %collective-permute-done.31 = f32[1024]{0:T(1024)S(1)} collective-permute-done((f32[1024]{0:T(1024)S(1)}, f32[1024]{0:T(1024)S(1)}, u32[]{:S(2)}, u32[]{:S(2)}) %collective-permute-start.31) | collective-permute-done | bytes 4128 | tf_op jit(solution)/shard_map/ppermute | solution.py:56
  142.2 1.3 collective-permute-start.34
  143.5 1.7 %collective-permute-start.32 = (f32[256]{0:T(256)S(1)}, f32[256]{0:T(256)S(1)}, u32[]{:S(2)}, u32[]{:S(2)}) collective-permute-start(f32[256]{0:T(256)S(1)} %get-tuple-element.47), channel_id=1, source_target_pairs={{0,4},{1,5},{2,6},{3,7},{4,0},{5,1},{6,2},{7,3},{8,12},{9,13},{10,... | collective-permute-start | bytes 3080 | tf_op jit(solution)/shard_map/ppermute | solution.py:56
  145.3 1.4 collective-permute-done.34
  147.7 1.3 collective-permute-start.37
  149.0 1.8 %collective-permute-done.36 = f32[256]{0:T(256)S(1)} collective-permute-done((f32[256]{0:T(256)S(1)}, f32[256]{0:T(256)S(1)}, u32[]{:S(2)}, u32[]{:S(2)}) %collective-permute-start.36) | collective-permute-done | bytes 1056 | tf_op jit(solution)/shard_map/ppermute | solution.py:50
  150.8 2.5 %collective-permute-start.38 = (f32[1024]{0:T(1024)S(1)}, f32[1024]{0:T(1024)S(1)}, u32[]{:S(2)}, u32[]{:S(2)}) collective-permute-start(f32[1024]{0:T(1024)S(1)} %pad_maximum_fusion.4), channel_id=1, source_target_pairs={{0,12},{1,13},{2,14},{3,15},{4,8},{5,9},{6,10},{7,11},{8,4},{9,5},... | collective-permute-start | bytes 12296 | tf_op jit(solution)/shard_map/ppermute | solution.py:56
  153.3 2.9 %collective-permute-done.38 = f32[1024]{0:T(1024)S(1)} collective-permute-done((f32[1024]{0:T(1024)S(1)}, f32[1024]{0:T(1024)S(1)}, u32[]{:S(2)}, u32[]{:S(2)}) %collective-permute-start.38) | collective-permute-done | bytes 4128 | tf_op jit(solution)/shard_map/ppermute | solution.py:56
  (127 shorter events, 33.9 us)
Async XLA Ops:
  2.0 9.6 %collective-permute-start = (bf16[128,1024]{1,0:T(8,128)(2,1)}, bf16[128,1024]{1,0:T(8,128)(2,1)}, u32[]{:S(2)}, u32[]{:S(2)}) collective-permute-start(bf16[128,1024]{1,0:T(8,128)(2,1)} %dynamic_slice.31), channel_id=1, source_target_pairs={{0,2},{1,3},{2,0},{3,1},{4,6},{5,7},{6,4},{7,5},{8,10},{9,11},{10,... | collective-permute-start | bytes 786440 | tf_op jit(solution)/shard_map/ppermute | solution.py:50
  6.8 22.3 %collective-permute-start.5 = (bf16[256,1024]{1,0:T(8,128)(2,1)}, bf16[256,1024]{1,0:T(8,128)(2,1)}, u32[]{:S(2)}, u32[]{:S(2)}) collective-permute-start(bf16[256,1024]{1,0:T(8,128)(2,1)} %constant_dynamic-slice_fusion), channel_id=1, source_target_pairs={{0,1},{1,0},{2,3},{3,2},{4,5},{5,4},{6,7},{7,6},{8,9},{9,8},{10,11... | collective-permute-start | bytes 1572872 | tf_op jit(solution)/shard_map/ppermute | solution.py:50
  13.2 15.8 %collective-permute-start.4 = (bf16[512,256]{1,0:T(8,128)(2,1)}, bf16[512,256]{1,0:T(8,128)(2,1)S(1)}, u32[]{:S(2)}, u32[]{:S(2)}) collective-permute-start(bf16[512,256]{1,0:T(8,128)(2,1)} %get-tuple-element.29), channel_id=1, source_target_pairs={{0,1},{1,0},{2,3},{3,2},{4,5},{5,4},{6,7},{7,6},{8,9},{9,8},{10,11... | collective-permute-start | bytes 786440 | tf_op jit(solution)/shard_map/ppermute | solution.py:50
  13.7 9.4 %collective-permute-start.1 = (bf16[512,256]{1,0:T(8,128)(2,1)}, bf16[512,256]{1,0:T(8,128)(2,1)S(1)}, u32[]{:S(2)}, u32[]{:S(2)}) collective-permute-start(bf16[512,256]{1,0:T(8,128)(2,1)} %get-tuple-element.30), channel_id=1, source_target_pairs={{0,2},{1,3},{2,0},{3,1},{4,6},{5,7},{6,4},{7,5},{8,10},{9,11},{10,... | collective-permute-start | bytes 786440 | tf_op jit(solution)/shard_map/ppermute | solution.py:50
  15.0 12.2 %collective-permute-start.2 = (bf16[512,256]{1,0:T(8,128)(2,1)}, bf16[512,256]{1,0:T(8,128)(2,1)S(1)}, u32[]{:S(2)}, u32[]{:S(2)}) collective-permute-start(bf16[512,256]{1,0:T(8,128)(2,1)} %get-tuple-element.28), channel_id=1, source_target_pairs={{0,3},{1,2},{2,1},{3,0},{4,7},{5,6},{6,5},{7,4},{8,11},{9,10},{10,... | collective-permute-start | bytes 786440 | tf_op jit(solution)/shard_map/ppermute | solution.py:50
  17.6 13.0 %collective-permute-start.3 = (bf16[128,1024]{1,0:T(8,128)(2,1)S(1)}, bf16[128,1024]{1,0:T(8,128)(2,1)S(1)}, u32[]{:S(2)}, u32[]{:S(2)}) collective-permute-start(bf16[128,1024]{1,0:T(8,128)(2,1)S(1)} %broadcast_add_fusion.4), channel_id=1, source_target_pairs={{0,16},{1,17},{2,18},{3,19},{4,20},{5,21},{6,22},{7,23},{8,24},{9,... | collective-permute-start | bytes 786440 | tf_op jit(solution)/shard_map/ppermute | solution.py:64
  23.1 9.0 %collective-permute-start.7 = (bf16[128,1024]{1,0:T(8,128)(2,1)S(1)}, bf16[128,1024]{1,0:T(8,128)(2,1)S(1)}, u32[]{:S(2)}, u32[]{:S(2)}) collective-permute-start(bf16[128,1024]{1,0:T(8,128)(2,1)S(1)} %broadcast_add_fusion.4), channel_id=1, source_target_pairs={{0,17},{1,16},{2,19},{3,18},{4,21},{5,20},{6,23},{7,22},{8,25},{9,... | collective-permute-start | bytes 786440 | tf_op jit(solution)/shard_map/ppermute | solution.py:64
  27.2 4.9 %collective-permute-start.6 = (bf16[128,1024]{1,0:T(8,128)(2,1)S(1)}, bf16[128,1024]{1,0:T(8,128)(2,1)S(1)}, u32[]{:S(2)}, u32[]{:S(2)}) collective-permute-start(bf16[128,1024]{1,0:T(8,128)(2,1)S(1)} %broadcast_add_fusion.4), channel_id=1, source_target_pairs={{0,1},{1,0},{2,3},{3,2},{4,5},{5,4},{6,7},{7,6},{8,9},{9,8},{10,11... | collective-permute-start | bytes 786440 | tf_op jit(solution)/shard_map/ppermute | solution.py:50
  34.0 14.9 %collective-permute-start.8 = (bf16[256,1024]{1,0:T(8,128)(2,1)S(1)}, bf16[256,1024]{1,0:T(8,128)(2,1)S(1)}, u32[]{:S(2)}, u32[]{:S(2)}) collective-permute-start(bf16[256,1024]{1,0:T(8,128)(2,1)S(1)} %get-tuple-element.23), channel_id=1, source_target_pairs={{0,2},{1,3},{2,0},{3,1},{4,6},{5,7},{6,4},{7,5},{8,10},{9,11},{10,... | collective-permute-start | bytes 1572872 | tf_op jit(solution)/shard_map/ppermute | solution.py:50
  35.8 8.0 %collective-permute-start.12 = (bf16[256,1024]{1,0:T(8,128)(2,1)S(1)}, bf16[256,1024]{1,0:T(8,128)(2,1)S(1)}, u32[]{:S(2)}, u32[]{:S(2)}) collective-permute-start(bf16[256,1024]{1,0:T(8,128)(2,1)S(1)} %get-tuple-element.23), channel_id=1, source_target_pairs={{0,1},{1,0},{2,3},{3,2},{4,5},{5,4},{6,7},{7,6},{8,9},{9,8},{10,11... | collective-permute-start | bytes 1572872 | tf_op jit(solution)/shard_map/ppermute | solution.py:50
  35.8 23.3 %collective-permute-start.10 = (bf16[512,1024]{1,0:T(8,128)(2,1)S(1)}, bf16[512,1024]{1,0:T(8,128)(2,1)S(1)}, u32[]{:S(2)}, u32[]{:S(2)}) collective-permute-start(bf16[512,1024]{1,0:T(8,128)(2,1)S(1)} %add_convert_fusion.1), channel_id=1, source_target_pairs={{0,0},{1,1},{2,2},{3,3},{4,8},{5,9},{6,10},{7,11},{8,4},{9,5},{10,... | collective-permute-start | bytes 3145736 | tf_op jit(solution)/shard_map/ppermute | solution.py:56
  36.5 27.9 %collective-permute-start.9 = (bf16[512,1024]{1,0:T(8,128)(2,1)S(1)}, bf16[512,1024]{1,0:T(8,128)(2,1)S(1)}, u32[]{:S(2)}, u32[]{:S(2)}) collective-permute-start(bf16[512,1024]{1,0:T(8,128)(2,1)S(1)} %add_convert_fusion.1), channel_id=1, source_target_pairs={{0,4},{1,5},{2,6},{3,7},{4,0},{5,1},{6,2},{7,3},{8,12},{9,13},{10,... | collective-permute-start | bytes 3145736 | tf_op jit(solution)/shard_map/ppermute | solution.py:56
  42.8 16.3 %collective-permute-start.13 = (bf16[256,1024]{1,0:T(8,128)(2,1)S(1)}, bf16[256,1024]{1,0:T(8,128)(2,1)S(1)}, u32[]{:S(2)}, u32[]{:S(2)}) collective-permute-start(bf16[256,1024]{1,0:T(8,128)(2,1)S(1)} %get-tuple-element.24), channel_id=1, source_target_pairs={{0,2},{1,3},{2,0},{3,1},{4,6},{5,7},{6,4},{7,5},{8,10},{9,11},{10,... | collective-permute-start | bytes 1572872 | tf_op jit(solution)/shard_map/ppermute | solution.py:50
  67.9 7.7 %collective-permute-start.21 = (bf16[256,1024]{1,0:T(8,128)(2,1)S(1)}, bf16[256,1024]{1,0:T(8,128)(2,1)S(1)}, u32[]{:S(2)}, u32[]{:S(2)}) collective-permute-start(bf16[256,1024]{1,0:T(8,128)(2,1)S(1)} %slice_add_fusion), channel_id=1, source_target_pairs={{0,1},{1,0},{2,3},{3,2},{4,5},{5,4},{6,7},{7,6},{8,9},{9,8},{10,11... | collective-permute-start | bytes 1572872 | tf_op jit(solution)/shard_map/ppermute | solution.py:50
  69.1 14.3 %collective-permute-start.17 = (bf16[256,1024]{1,0:T(8,128)(2,1)S(1)}, bf16[256,1024]{1,0:T(8,128)(2,1)S(1)}, u32[]{:S(2)}, u32[]{:S(2)}) collective-permute-start(bf16[256,1024]{1,0:T(8,128)(2,1)S(1)} %get-tuple-element.34), channel_id=1, source_target_pairs={{0,16},{1,17},{2,18},{3,19},{4,20},{5,21},{6,22},{7,23},{8,24},{9,... | collective-permute-start | bytes 1572872 | tf_op jit(solution)/shard_map/ppermute | solution.py:64
  70.7 28.9 %collective-permute-start.20 = (bf16[512,1024]{1,0:T(8,128)(2,1)S(1)}, bf16[512,1024]{1,0:T(8,128)(2,1)S(1)}, u32[]{:S(2)}, u32[]{:S(2)}) collective-permute-start(bf16[512,1024]{1,0:T(8,128)(2,1)S(1)} %get-tuple-element.22), channel_id=1, source_target_pairs={{0,0},{1,1},{2,2},{3,3},{4,8},{5,9},{6,10},{7,11},{8,4},{9,5},{10,... | collective-permute-start | bytes 3145736 | tf_op jit(solution)/shard_map/ppermute | solution.py:56
  71.6 28.0 %collective-permute-start.19 = (bf16[512,1024]{1,0:T(8,128)(2,1)S(1)}, bf16[512,1024]{1,0:T(8,128)(2,1)S(1)}, u32[]{:S(2)}, u32[]{:S(2)}) collective-permute-start(bf16[512,1024]{1,0:T(8,128)(2,1)S(1)} %get-tuple-element.21), channel_id=1, source_target_pairs={{0,4},{1,5},{2,6},{3,7},{4,0},{5,1},{6,2},{7,3},{8,12},{9,13},{10,... | collective-permute-start | bytes 3145736 | tf_op jit(solution)/shard_map/ppermute | solution.py:56
  75.1 14.9 %collective-permute-start.22 = (bf16[256,1024]{1,0:T(8,128)(2,1)S(1)}, bf16[256,1024]{1,0:T(8,128)(2,1)S(1)}, u32[]{:S(2)}, u32[]{:S(2)}) collective-permute-start(bf16[256,1024]{1,0:T(8,128)(2,1)S(1)} %get-tuple-element.33), channel_id=1, source_target_pairs={{0,2},{1,3},{2,0},{3,1},{4,6},{5,7},{6,4},{7,5},{8,10},{9,11},{10,... | collective-permute-start | bytes 1572872 | tf_op jit(solution)/shard_map/ppermute | solution.py:50
  75.6 14.3 %collective-permute-start.16 = (bf16[256,1024]{1,0:T(8,128)(2,1)S(1)}, bf16[256,1024]{1,0:T(8,128)(2,1)S(1)}, u32[]{:S(2)}, u32[]{:S(2)}) collective-permute-start(bf16[256,1024]{1,0:T(8,128)(2,1)S(1)} %get-tuple-element.33), channel_id=1, source_target_pairs={{0,1},{1,0},{2,3},{3,2},{4,5},{5,4},{6,7},{7,6},{8,9},{9,8},{10,11... | collective-permute-start | bytes 1572872 | tf_op jit(solution)/shard_map/ppermute | solution.py:50
  83.4 16.2 %collective-permute-start.18 = (bf16[256,1024]{1,0:T(8,128)(2,1)S(1)}, bf16[256,1024]{1,0:T(8,128)(2,1)S(1)}, u32[]{:S(2)}, u32[]{:S(2)}) collective-permute-start(bf16[256,1024]{1,0:T(8,128)(2,1)S(1)} %slice_add_fusion), channel_id=1, source_target_pairs={{0,2},{1,3},{2,0},{3,1},{4,6},{5,7},{6,4},{7,5},{8,10},{9,11},{10,... | collective-permute-start | bytes 1572872 | tf_op jit(solution)/shard_map/ppermute | solution.py:50
  100.4 3.8 %collective-permute-start.27 = (bf16[256,1024]{1,0:T(8,128)(2,1)S(1)}, bf16[256,1024]{1,0:T(8,128)(2,1)S(1)}, u32[]{:S(2)}, u32[]{:S(2)}) collective-permute-start(bf16[256,1024]{1,0:T(8,128)(2,1)S(1)} %get-tuple-element.49), channel_id=1, source_target_pairs={{0,1},{1,0},{2,3},{3,2},{4,5},{5,4},{6,7},{7,6},{8,9},{9,8},{10,11... | collective-permute-start | bytes 1572872 | tf_op jit(solution)/shard_map/ppermute | solution.py:50
  103.1 14.2 %collective-permute-start.28 = (bf16[256,1024]{1,0:T(8,128)(2,1)S(1)}, bf16[256,1024]{1,0:T(8,128)(2,1)S(1)}, u32[]{:S(2)}, u32[]{:S(2)}) collective-permute-start(bf16[256,1024]{1,0:T(8,128)(2,1)S(1)} %get-tuple-element.32), channel_id=1, source_target_pairs={{0,2},{1,3},{2,0},{3,1},{4,6},{5,7},{6,4},{7,5},{8,10},{9,11},{10,... | collective-permute-start | bytes 1572872 | tf_op jit(solution)/shard_map/ppermute | solution.py:50
  103.6 13.9 %collective-permute-start.25 = (bf16[256,1024]{1,0:T(8,128)(2,1)S(1)}, bf16[256,1024]{1,0:T(8,128)(2,1)S(1)}, u32[]{:S(2)}, u32[]{:S(2)}) collective-permute-start(bf16[256,1024]{1,0:T(8,128)(2,1)S(1)} %get-tuple-element.31), channel_id=1, source_target_pairs={{0,16},{1,17},{2,18},{3,19},{4,20},{5,21},{6,22},{7,23},{8,24},{9,... | collective-permute-start | bytes 1572872 | tf_op jit(solution)/shard_map/ppermute | solution.py:64
  106.8 11.4 %collective-permute-start.26 = (f32[256,256]{1,0:T(8,128)S(1)}, f32[256,256]{1,0:T(8,128)S(1)}, u32[]{:S(2)}, u32[]{:S(2)}) collective-permute-start(f32[256,256]{1,0:T(8,128)S(1)} %convolution_add_fusion.4), channel_id=1, source_target_pairs={{0,4},{1,5},{2,6},{3,7},{4,0},{5,1},{6,2},{7,3},{8,12},{9,13},{10,... | collective-permute-start | bytes 786440 | tf_op jit(solution)/shard_map/ppermute | solution.py:56
  120.3 19.9 %collective-permute-start.30 = (f32[256,768]{1,0:T(8,128)S(1)}, f32[256,768]{1,0:T(8,128)S(1)}, u32[]{:S(2)}, u32[]{:S(2)}) collective-permute-start(f32[256,768]{1,0:T(8,128)S(1)} %pad_maximum_fusion.2), channel_id=1, source_target_pairs={{0,4},{1,5},{2,6},{3,7},{4,0},{5,1},{6,2},{7,3},{8,12},{9,13},{10,... | collective-permute-start | bytes 2359304 | tf_op jit(solution)/shard_map/ppermute | solution.py:56
  121.2 18.9 %collective-permute-start.31 = (f32[1024]{0:T(1024)S(1)}, f32[1024]{0:T(1024)S(1)}, u32[]{:S(2)}, u32[]{:S(2)}) collective-permute-start(f32[1024]{0:T(1024)S(1)} %pad_maximum_fusion.3), channel_id=1, source_target_pairs={{0,4},{1,5},{2,6},{3,7},{4,0},{5,1},{6,2},{7,3},{8,12},{9,13},{10,... | collective-permute-start | bytes 12296 | tf_op jit(solution)/shard_map/ppermute | solution.py:56
  141.6 3.6 %collective-permute-start.33 = (f32[256]{0:T(256)S(1)}, f32[256]{0:T(256)S(1)}, u32[]{:S(2)}, u32[]{:S(2)}) collective-permute-start(f32[256]{0:T(256)S(1)} %get-tuple-element.48), channel_id=1, source_target_pairs={{0,16},{1,17},{2,18},{3,19},{4,20},{5,21},{6,22},{7,23},{8,24},{9,... | collective-permute-start | bytes 3080 | tf_op jit(solution)/shard_map/ppermute | solution.py:64
  142.2 4.5 %collective-permute-start.34 = (f32[256]{0:T(256)S(1)}, f32[256]{0:T(256)S(1)}, u32[]{:S(2)}, u32[]{:S(2)}) collective-permute-start(f32[256]{0:T(256)S(1)} %get-tuple-element.48), channel_id=1, source_target_pairs={{0,20},{1,21},{2,22},{3,23},{4,16},{5,17},{6,18},{7,19},{8,28},{9,... | collective-permute-start | bytes 3080 | tf_op jit(solution)/shard_map/ppermute | solution.py:64
  143.5 3.6 %collective-permute-start.32 = (f32[256]{0:T(256)S(1)}, f32[256]{0:T(256)S(1)}, u32[]{:S(2)}, u32[]{:S(2)}) collective-permute-start(f32[256]{0:T(256)S(1)} %get-tuple-element.47), channel_id=1, source_target_pairs={{0,4},{1,5},{2,6},{3,7},{4,0},{5,1},{6,2},{7,3},{8,12},{9,13},{10,... | collective-permute-start | bytes 3080 | tf_op jit(solution)/shard_map/ppermute | solution.py:56
  147.1 3.6 %collective-permute-start.36 = (f32[256]{0:T(256)S(1)}, f32[256]{0:T(256)S(1)}, u32[]{:S(2)}, u32[]{:S(2)}) collective-permute-start(f32[256]{0:T(256)S(1)} %add_add_fusion.3), channel_id=1, source_target_pairs={{0,2},{1,3},{2,0},{3,1},{4,6},{5,7},{6,4},{7,5},{8,10},{9,11},{10,... | collective-permute-start | bytes 3080 | tf_op jit(solution)/shard_map/ppermute | solution.py:50
  147.7 3.0 %collective-permute-start.37 = (f32[256]{0:T(256)S(1)}, f32[256]{0:T(256)S(1)}, u32[]{:S(2)}, u32[]{:S(2)}) collective-permute-start(f32[256]{0:T(256)S(1)} %add_add_fusion.3), channel_id=1, source_target_pairs={{0,3},{1,2},{2,1},{3,0},{4,7},{5,6},{6,5},{7,4},{8,11},{9,10},{10,... | collective-permute-start | bytes 3080 | tf_op jit(solution)/shard_map/ppermute | solution.py:50
  150.8 5.5 %collective-permute-start.38 = (f32[1024]{0:T(1024)S(1)}, f32[1024]{0:T(1024)S(1)}, u32[]{:S(2)}, u32[]{:S(2)}) collective-permute-start(f32[1024]{0:T(1024)S(1)} %pad_maximum_fusion.4), channel_id=1, source_target_pairs={{0,12},{1,13},{2,14},{3,15},{4,8},{5,9},{6,10},{7,11},{8,4},{9,5},... | collective-permute-start | bytes 12296 | tf_op jit(solution)/shard_map/ppermute | solution.py:56
  (11 other events, 44.6 us)

commit v3 on v2

--- a/solution.py
+++ b/solution.py
@@ -21,6 +21,12 @@
     width = min(v.shape[-1] for v in arrays)
     rows = [lax.slice_in_dim(v.reshape(-1, v.shape[-1])[:1], 0, width, axis=1) for v in arrays]
     return sum(jnp.minimum(jnp.abs(r.astype(F32)), 0.0) for r in rows)
+
+
+def fence(swap, middle, others):
+    done = lax.optimization_barrier(token(swap))
+    done = lax.optimization_barrier(token(middle) + done)
+    return token(*others) + done
 
 
 def behind(value, zeros):
@@ -37,7 +43,7 @@
     nx = n_tgt // (nz * CORES)
     outer = (1, 0, 3, 2)
     middle = (0, 2, 1, 3)
-    mirror = (3, 2, 1, 0)
+    skip = (2, 3, 0, 1)
 
     def place(z, x, c):
         return (z * nx + x) * CORES + c
@@ -119,7 +125,7 @@
 
         pool = lax.axis_index("pool")
         part_rows = width // n_pool
-        own1 = factor_own([0, 1, 2, 1])
+        own1 = lax.optimization_barrier(factor_own([0, 1, 2, 1]))
         mine1 = lax.dynamic_slice_in_dim(own1, pool * part_rows, part_rows, 0)
         parts1 = [inner(mine1, s, 0) for s in range(1, nx)]
 
@@ -128,10 +134,9 @@
         flip1 = inner(own1, 0, 1)
         near1, far1 = [], []
         for v in parts1:
-            v = behind(v, done)
             near1.append([v] + [over_pool(v, r) for r in range(1, n_pool)])
             far1.append([inner(v, 0, 1)] + [over_pool(v, r, 1) for r in range(1, n_pool)])
-        done = token(*[v for (s, _), v in zip(order, features) if s])
+        done = token(*features[1:nx])
         near1, far1 = [[in_order([behind(v, done[:, :1]) for v in u], pool) for u in w] for w in (near1, far1)]
         first = partial([own1] + near1 + [flip1] + far1).astype(BF)
 
@@ -142,7 +147,7 @@
         own3 = behind(factor_own([1, 1, 1, 2]), start)
         flip2, flip3 = inner(own2, 0, 1), inner(own3, 0, 1)
         moved2, moved3 = factor_x(own2), factor_x(own3)
-        done = token(step1, step2, flip2, flip3, *moved2, *moved3)
+        done = fence(step1, step2, [flip2, flip3, *moved2, *moved3])
         moved2, moved3 = [behind(v, done) for v in moved2], [behind(v, done) for v in moved3]
         second = partial([own2] + moved2 + [flip2] + factor_flip(moved2))
         third = partial([own3] + moved3 + [flip3] + factor_flip(moved3))
@@ -157,7 +162,7 @@
         t_flip_a = inner(t_a, 0, 1)
         t_moved_a = [inner(t_a, s, 0) for s in range(1, nx)]
         p_moved_a = [over_pool(p_a, s) for s in range(1, n_pool)]
-        done = token(step3, step4, flip4, *moved4, t_flip_a, *t_moved_a, *p_moved_a)
+        done = fence(step3, step4, [flip4, *moved4, t_flip_a, *t_moved_a, *p_moved_a])
 
         moved4 = [behind(v, done) for v in moved4]
         fourth = partial([own4] + moved4 + [flip4] + factor_flip(moved4))
@@ -180,9 +185,8 @@
         p_all_a, p_all_b = jnp.concatenate([p_a, p_far_a], axis=0), jnp.concatenate([p_b, p_far_b], axis=0)
 
         given_near = along_z(matmul_t(give_a[0], p_a) + matmul_t(give_b[0], p_b), outer)
-        swapped = token(given_near)[:, :1]
-        give_side = behind(matmul_t(give_a[0], p_far_a) + matmul_t(give_b[0], p_far_b), swapped)
-        give_far = behind(matmul_t(give_a[1], p_all_a) + matmul_t(give_b[1], p_all_b), swapped)
+        give_side = behind(matmul_t(give_a[0], p_far_a) + matmul_t(give_b[0], p_far_b), token(given_near)[:, :1] if n_pool > 2 else token(given_near))
+        give_far = matmul_t(give_a[1], p_all_a) + matmul_t(give_b[1], p_all_b)
         if nx == 2:
             given = along_z(jnp.concatenate([give_side, give_far], axis=1), outer)
             given_side, given_far = given[:, :give_side.shape[1]], given[:, give_side.shape[1]:]
@@ -212,7 +216,7 @@
             own = own + (over_pool(blocks[s], -s) + over_pool(blocks[s], -s, 0, outer))
         rows = [in_order([own if s == 0 else inner(own, s, 0), inner(own, s, 1)], core) for s in range(nx)]
         scores = in_order(rows, x)
-        return jnp.where(z >= nz - 2, scores, along_z(scores, mirror))
+        return jnp.where(z >= nz - 2, scores, along_z(scores, skip))
 
     return body
 

time: 157 us -> 153 us (0.975)
  local copies, waits for them, and re-layouts: 10.5 us -> 6.57 us
  starting transfers between devices: 35 us -> 37.2 us
    ppermute x24, waiting for transfers between devices: 50 us -> 27.2 us  [inner(): return lax.ppermute(value, 'tgt', pairs)]
    ppermute x9, waiting for transfers between devices: 25.4 us -> 42.6 us  [along_z(): return lax.ppermute(value, 'tgt', pairs)]
    ppermute x6, waiting for transfers between devices: 9.55 us -> 16.6 us  [over_pool(): return lax.ppermute(value, ('pool', 'tgt'), pairs)]
    ppermute x24, starting transfers between devices: 13 us -> 16.9 us  [inner(): return lax.ppermute(value, 'tgt', pairs)]
  transfers between devices with their start and end apart: 39 -> 39, of which waited for: 20 -> 21; matrix products, arithmetic and copies ran while one was open for 17% -> 14% of each run, Pallas kernels for 0% -> 0%
where the time goes in v3:
time: 153 us
  waiting for transfers between devices  86.4 us (56%)
  starting transfers between devices  37.2 us (24%)
  matrix products  13.4 us (9%)
  other arithmetic  7.86 us (5%)
  local copies, waits for them, and re-layouts  6.57 us (4%)
    ppermute x9, waiting for transfers between devices, along_z(): return lax.ppermute(value, 'tgt', pairs)  42.6 us
    ppermute x24, waiting for transfers between devices, inner(): return lax.ppermute(value, 'tgt', pairs)  27.2 us
    ppermute x24, starting transfers between devices, inner(): return lax.ppermute(value, 'tgt', pairs)  16.9 us
    ppermute x6, waiting for transfers between devices, over_pool(): return lax.ppermute(value, ('pool', 'tgt'), pairs)  16.6 us
    ppermute x9, starting transfers between devices, along_z(): return lax.ppermute(value, 'tgt', pairs)  15.1 us
    dot_general x16, matrix products, matmul(): lax.dot_general(a, b, (((1,), (0,)), ((), ())), preferred_element_type=F32)  8.76 us
    ppermute x6, starting transfers between devices, over_pool(): return lax.ppermute(value, ('pool', 'tgt'), pairs)  5.09 us
    dot_general x10, matrix products, matmul_t(): lax.dot_general(a, b, (((1,), (1,)), ((), ())), preferred_element_type=F32)  4.68 us
  transfers between devices with their start and end apart: 39, of which 21 were waited for; matrix products, arithmetic and copies ran while one was open for 14% of the time, Pallas kernels for 0%

profile of v3, /device:TPU:0, one launch (start us, length us, event | category | flops | bytes accessed | tf_op | source)
XLA Modules:
  0.0 152.7 jit_solution(12216441327962715195)
XLA Ops:
  2.5 2.5 %collective-permute-start = (bf16[128,1024]{1,0:T(8,128)(2,1)}, bf16[128,1024]{1,0:T(8,128)(2,1)S(1)}, u32[]{:S(2)}, u32[]{:S(2)}) collective-permute-start(bf16[128,1024]{1,0:T(8,128)(2,1)} %constant_dynamic-slice_fusion), channel_id=1, source_target_pairs={{0,2},{1,3},{2,0},{3,1},{4,6},{5,7},{6,4},{7,5},{8,10},{9,11},{10,... | collective-permute-start | bytes 786440 | tf_op jit(solution)/shard_map/ppermute | solution.py:56
  5.7 3.9 %gather_fusion = bf16[1024,256]{1,0:T(8,128)(2,1)S(1)} fusion(bf16[4096,256]{1,0:T(8,128)(2,1)S(1)} %copy-done, s32[1024]{0:T(1024)S(1)} %fusion.41), kind=kCustom, calls=%fused_computation | custom fusion | bytes 1052672 | tf_op jit(solution)/shard_map/gather | solution.py:96
  10.6 1.6 %collective-permute-done = bf16[128,1024]{1,0:T(8,128)(2,1)S(1)} collective-permute-done((bf16[128,1024]{1,0:T(8,128)(2,1)}, bf16[128,1024]{1,0:T(8,128)(2,1)S(1)}, u32[]{:S(2)}, u32[]{:S(2)}) %collective-permute-start) | collective-permute-done | bytes 262176 | tf_op jit(solution)/shard_map/ppermute | solution.py:56
  13.4 1.8 %collective-permute-start.1 = (bf16[512,256]{1,0:T(8,128)(2,1)S(1)}, bf16[512,256]{1,0:T(8,128)(2,1)S(1)}, u32[]{:S(2)}, u32[]{:S(2)}) collective-permute-start(bf16[512,256]{1,0:T(8,128)(2,1)S(1)} %get-tuple-element.28), channel_id=1, source_target_pairs={{0,2},{1,3},{2,0},{3,1},{4,6},{5,7},{6,4},{7,5},{8,10},{9,11},{10,... | collective-permute-start | bytes 786440 | tf_op jit(solution)/shard_map/ppermute | solution.py:56
  15.8 1.8 %collective-permute-start.2 = (bf16[128,1024]{1,0:T(8,128)(2,1)S(1)}, bf16[128,1024]{1,0:T(8,128)(2,1)S(1)}, u32[]{:S(2)}, u32[]{:S(2)}) collective-permute-start(bf16[128,1024]{1,0:T(8,128)(2,1)S(1)} %collective-permute-done), channel_id=1, source_target_pairs={{0,16},{1,17},{2,18},{3,19},{4,20},{5,21},{6,22},{7,23},{8,24},{9,... | collective-permute-start | bytes 786440 | tf_op jit(solution)/shard_map/ppermute | solution.py:70
  17.6 5.0 %collective-permute-done.1 = bf16[512,256]{1,0:T(8,128)(2,1)S(1)} collective-permute-done((bf16[512,256]{1,0:T(8,128)(2,1)S(1)}, bf16[512,256]{1,0:T(8,128)(2,1)S(1)}, u32[]{:S(2)}, u32[]{:S(2)}) %collective-permute-start.1) | collective-permute-done | bytes 262176 | tf_op jit(solution)/shard_map/ppermute | solution.py:56
  24.4 1.4 collective-permute-start.6
  25.8 1.5 fusion.108
  27.7 3.1 %collective-permute-done.7 = bf16[128,1024]{1,0:T(8,128)(2,1)S(1)} collective-permute-done((bf16[128,1024]{1,0:T(8,128)(2,1)S(1)}, bf16[128,1024]{1,0:T(8,128)(2,1)S(1)}, u32[]{:S(2)}, u32[]{:S(2)}) %collective-permute-start.7) | collective-permute-done | bytes 262176 | tf_op jit(solution)/shard_map/ppermute | solution.py:70
  31.5 2.1 %collective-permute-start.13 = (bf16[512,1024]{1,0:T(8,128)(2,1)S(1)}, bf16[512,1024]{1,0:T(8,128)(2,1)S(1)}, u32[]{:S(2)}, u32[]{:S(2)}) collective-permute-start(bf16[512,1024]{1,0:T(8,128)(2,1)S(1)} %add_convert_fusion.1), channel_id=1, source_target_pairs={{0,4},{1,5},{2,6},{3,7},{4,0},{5,1},{6,2},{7,3},{8,12},{9,13},{10,... | collective-permute-start | bytes 3145736 | tf_op jit(solution)/shard_map/ppermute | solution.py:62
  34.6 1.6 %collective-permute-start.8 = (bf16[256,1024]{1,0:T(8,128)(2,1)S(1)}, bf16[256,1024]{1,0:T(8,128)(2,1)S(1)}, u32[]{:S(2)}, u32[]{:S(2)}) collective-permute-start(bf16[256,1024]{1,0:T(8,128)(2,1)S(1)} %get-tuple-element.21), channel_id=1, source_target_pairs={{0,2},{1,3},{2,0},{3,1},{4,6},{5,7},{6,4},{7,5},{8,10},{9,11},{10,... | collective-permute-start | bytes 1572872 | tf_op jit(solution)/shard_map/ppermute | solution.py:56
  37.6 1.3 collective-permute-done.9
  40.3 16.8 %collective-permute-done.13 = bf16[512,1024]{1,0:T(8,128)(2,1)S(1)} collective-permute-done((bf16[512,1024]{1,0:T(8,128)(2,1)S(1)}, bf16[512,1024]{1,0:T(8,128)(2,1)S(1)}, u32[]{:S(2)}, u32[]{:S(2)}) %collective-permute-start.13) | collective-permute-done | bytes 1048608 | tf_op jit(solution)/shard_map/ppermute | solution.py:62
  57.1 2.5 %collective-permute-done.11 = bf16[256,1024]{1,0:T(8,128)(2,1)S(1)} collective-permute-done((bf16[256,1024]{1,0:T(8,128)(2,1)S(1)}, bf16[256,1024]{1,0:T(8,128)(2,1)S(1)}, u32[]{:S(2)}, u32[]{:S(2)}) %collective-permute-start.11) | collective-permute-done | bytes 524320 | tf_op jit(solution)/shard_map/ppermute | solution.py:56
  63.9 4.1 %collective-permute-start.22 = (bf16[512,1024]{1,0:T(8,128)(2,1)S(1)}, bf16[512,1024]{1,0:T(8,128)(2,1)S(1)}, u32[]{:S(2)}, u32[]{:S(2)}) collective-permute-start(bf16[512,1024]{1,0:T(8,128)(2,1)S(1)} %get-tuple-element.19), channel_id=1, source_target_pairs={{0,4},{1,5},{2,6},{3,7},{4,0},{5,1},{6,2},{7,3},{8,12},{9,13},{10,... | collective-permute-start | bytes 3145736 | tf_op jit(solution)/shard_map/ppermute | solution.py:62
  69.6 1.6 %collective-permute-start.20 = (bf16[256,1024]{1,0:T(8,128)(2,1)S(1)}, bf16[256,1024]{1,0:T(8,128)(2,1)S(1)}, u32[]{:S(2)}, u32[]{:S(2)}) collective-permute-start(bf16[256,1024]{1,0:T(8,128)(2,1)S(1)} %get-tuple-element.31), channel_id=1, source_target_pairs={{0,2},{1,3},{2,0},{3,1},{4,6},{5,7},{6,4},{7,5},{8,10},{9,11},{10,... | collective-permute-start | bytes 1572872 | tf_op jit(solution)/shard_map/ppermute | solution.py:56
  71.7 10.9 %collective-permute-done.17 = bf16[256,1024]{1,0:T(8,128)(2,1)S(1)} collective-permute-done((bf16[256,1024]{1,0:T(8,128)(2,1)S(1)}, bf16[256,1024]{1,0:T(8,128)(2,1)S(1)}, u32[]{:S(2)}, u32[]{:S(2)}) %collective-permute-start.17) | collective-permute-done | bytes 524320 | tf_op jit(solution)/shard_map/ppermute | solution.py:70
  82.6 1.5 collective-permute-start.18
  84.8 6.7 %collective-permute-done.22 = bf16[512,1024]{1,0:T(8,128)(2,1)S(1)} collective-permute-done((bf16[512,1024]{1,0:T(8,128)(2,1)S(1)}, bf16[512,1024]{1,0:T(8,128)(2,1)S(1)}, u32[]{:S(2)}, u32[]{:S(2)}) %collective-permute-start.22) | collective-permute-done | bytes 1048608 | tf_op jit(solution)/shard_map/ppermute | solution.py:62
  91.6 4.6 %collective-permute-done.18 = bf16[256,1024]{1,0:T(8,128)(2,1)S(1)} collective-permute-done((bf16[256,1024]{1,0:T(8,128)(2,1)S(1)}, bf16[256,1024]{1,0:T(8,128)(2,1)S(1)}, u32[]{:S(2)}, u32[]{:S(2)}) %collective-permute-start.18) | collective-permute-done | bytes 524320 | tf_op jit(solution)/shard_map/ppermute | solution.py:56
  99.6 1.5 collective-permute-start.28
  104.2 1.3 collective-permute-start.26
  105.5 8.3 %collective-permute-done.28 = bf16[256,1024]{1,0:T(8,128)(2,1)S(1)} collective-permute-done((bf16[256,1024]{1,0:T(8,128)(2,1)S(1)}, bf16[256,1024]{1,0:T(8,128)(2,1)S(1)}, u32[]{:S(2)}, u32[]{:S(2)}) %collective-permute-start.28) | collective-permute-done | bytes 524320 | tf_op jit(solution)/shard_map/ppermute | solution.py:56
  117.2 2.1 %collective-permute-start.31 = (f32[1024]{0:T(1024)S(1)}, f32[1024]{0:T(1024)S(1)}, u32[]{:S(2)}, u32[]{:S(2)}) collective-permute-start(f32[1024]{0:T(1024)S(1)} %pad_maximum_fusion.3), channel_id=1, source_target_pairs={{0,4},{1,5},{2,6},{3,7},{4,0},{5,1},{6,2},{7,3},{8,12},{9,13},{10,... | collective-permute-start | bytes 12296 | tf_op jit(solution)/shard_map/ppermute | solution.py:62
  119.8 16.3 %collective-permute-done.31 = f32[1024]{0:T(1024)S(1)} collective-permute-done((f32[1024]{0:T(1024)S(1)}, f32[1024]{0:T(1024)S(1)}, u32[]{:S(2)}, u32[]{:S(2)}) %collective-permute-start.31) | collective-permute-done | bytes 4128 | tf_op jit(solution)/shard_map/ppermute | solution.py:62
  138.0 1.3 collective-permute-start.34
  139.3 1.7 %collective-permute-start.32 = (f32[256]{0:T(256)S(1)}, f32[256]{0:T(256)S(1)}, u32[]{:S(2)}, u32[]{:S(2)}) collective-permute-start(f32[256]{0:T(256)S(1)} %get-tuple-element.45), channel_id=1, source_target_pairs={{0,4},{1,5},{2,6},{3,7},{4,0},{5,1},{6,2},{7,3},{8,12},{9,13},{10,... | collective-permute-start | bytes 3080 | tf_op jit(solution)/shard_map/ppermute | solution.py:62
  141.2 1.3 collective-permute-done.34
  142.9 1.5 %collective-permute-start.36 = (f32[256]{0:T(256)S(1)}, f32[256]{0:T(256)S(1)}, u32[]{:S(2)}, u32[]{:S(2)}) collective-permute-start(f32[256]{0:T(256)S(1)} %add_add_fusion.3), channel_id=1, source_target_pairs={{0,2},{1,3},{2,0},{3,1},{4,6},{5,7},{6,4},{7,5},{8,10},{9,11},{10,... | collective-permute-start | bytes 3080 | tf_op jit(solution)/shard_map/ppermute | solution.py:56
  144.8 1.8 %collective-permute-done.36 = f32[256]{0:T(256)S(1)} collective-permute-done((f32[256]{0:T(256)S(1)}, f32[256]{0:T(256)S(1)}, u32[]{:S(2)}, u32[]{:S(2)}) %collective-permute-start.36) | collective-permute-done | bytes 1056 | tf_op jit(solution)/shard_map/ppermute | solution.py:56
  147.5 2.1 %collective-permute-start.38 = (f32[1024]{0:T(1024)S(1)}, f32[1024]{0:T(1024)S(1)}, u32[]{:S(2)}, u32[]{:S(2)}) collective-permute-start(f32[1024]{0:T(1024)S(1)} %pad_maximum_fusion.4), channel_id=1, source_target_pairs={{0,8},{1,9},{2,10},{3,11},{4,12},{5,13},{6,14},{7,15},{8,0},{9,1},... | collective-permute-start | bytes 12296 | tf_op jit(solution)/shard_map/ppermute | solution.py:62
  149.6 2.5 %collective-permute-done.38 = f32[1024]{0:T(1024)S(1)} collective-permute-done((f32[1024]{0:T(1024)S(1)}, f32[1024]{0:T(1024)S(1)}, u32[]{:S(2)}, u32[]{:S(2)}) %collective-permute-start.38) | collective-permute-done | bytes 4128 | tf_op jit(solution)/shard_map/ppermute | solution.py:62
  (127 shorter events, 33.6 us)
Async XLA Ops:
  1.2 24.5 %collective-permute-start.4 = (bf16[256,1024]{1,0:T(8,128)(2,1)S(1)}, bf16[256,1024]{1,0:T(8,128)(2,1)}, u32[]{:S(2)}, u32[]{:S(2)}) collective-permute-start(bf16[256,1024]{1,0:T(8,128)(2,1)S(1)} %constant_dynamic-slice_fusion.1), channel_id=1, source_target_pairs={{0,1},{1,0},{2,3},{3,2},{4,5},{5,4},{6,7},{7,6},{8,9},{9,8},{10,11... | collective-permute-start | bytes 1572872 | tf_op jit(solution)/shard_map/ppermute | solution.py:56
  2.5 9.7 %collective-permute-start = (bf16[128,1024]{1,0:T(8,128)(2,1)}, bf16[128,1024]{1,0:T(8,128)(2,1)S(1)}, u32[]{:S(2)}, u32[]{:S(2)}) collective-permute-start(bf16[128,1024]{1,0:T(8,128)(2,1)} %constant_dynamic-slice_fusion), channel_id=1, source_target_pairs={{0,2},{1,3},{2,0},{3,1},{4,6},{5,7},{6,4},{7,5},{8,10},{9,11},{10,... | collective-permute-start | bytes 786440 | tf_op jit(solution)/shard_map/ppermute | solution.py:56
  13.4 11.0 %collective-permute-start.3 = (bf16[512,256]{1,0:T(8,128)(2,1)S(1)}, bf16[512,256]{1,0:T(8,128)(2,1)S(1)}, u32[]{:S(2)}, u32[]{:S(2)}) collective-permute-start(bf16[512,256]{1,0:T(8,128)(2,1)S(1)} %get-tuple-element.27), channel_id=1, source_target_pairs={{0,1},{1,0},{2,3},{3,2},{4,5},{5,4},{6,7},{7,6},{8,9},{9,8},{10,11... | collective-permute-start | bytes 786440 | tf_op jit(solution)/shard_map/ppermute | solution.py:56
  13.4 9.2 %collective-permute-start.1 = (bf16[512,256]{1,0:T(8,128)(2,1)S(1)}, bf16[512,256]{1,0:T(8,128)(2,1)S(1)}, u32[]{:S(2)}, u32[]{:S(2)}) collective-permute-start(bf16[512,256]{1,0:T(8,128)(2,1)S(1)} %get-tuple-element.28), channel_id=1, source_target_pairs={{0,2},{1,3},{2,0},{3,1},{4,6},{5,7},{6,4},{7,5},{8,10},{9,11},{10,... | collective-permute-start | bytes 786440 | tf_op jit(solution)/shard_map/ppermute | solution.py:56
  15.7 15.3 %collective-permute-start.5 = (bf16[512,256]{1,0:T(8,128)(2,1)S(1)}, bf16[512,256]{1,0:T(8,128)(2,1)S(1)}, u32[]{:S(2)}, u32[]{:S(2)}) collective-permute-start(bf16[512,256]{1,0:T(8,128)(2,1)S(1)} %get-tuple-element.26), channel_id=1, source_target_pairs={{0,3},{1,2},{2,1},{3,0},{4,7},{5,6},{6,5},{7,4},{8,11},{9,10},{10,... | collective-permute-start | bytes 786440 | tf_op jit(solution)/shard_map/ppermute | solution.py:56
  15.8 11.4 %collective-permute-start.2 = (bf16[128,1024]{1,0:T(8,128)(2,1)S(1)}, bf16[128,1024]{1,0:T(8,128)(2,1)S(1)}, u32[]{:S(2)}, u32[]{:S(2)}) collective-permute-start(bf16[128,1024]{1,0:T(8,128)(2,1)S(1)} %collective-permute-done), channel_id=1, source_target_pairs={{0,16},{1,17},{2,18},{3,19},{4,20},{5,21},{6,22},{7,23},{8,24},{9,... | collective-permute-start | bytes 786440 | tf_op jit(solution)/shard_map/ppermute | solution.py:70
  22.6 8.3 %collective-permute-start.7 = (bf16[128,1024]{1,0:T(8,128)(2,1)S(1)}, bf16[128,1024]{1,0:T(8,128)(2,1)S(1)}, u32[]{:S(2)}, u32[]{:S(2)}) collective-permute-start(bf16[128,1024]{1,0:T(8,128)(2,1)S(1)} %collective-permute-done), channel_id=1, source_target_pairs={{0,17},{1,16},{2,19},{3,18},{4,21},{5,20},{6,23},{7,22},{8,25},{9,... | collective-permute-start | bytes 786440 | tf_op jit(solution)/shard_map/ppermute | solution.py:70
  24.4 6.5 %collective-permute-start.6 = (bf16[128,1024]{1,0:T(8,128)(2,1)S(1)}, bf16[128,1024]{1,0:T(8,128)(2,1)S(1)}, u32[]{:S(2)}, u32[]{:S(2)}) collective-permute-start(bf16[128,1024]{1,0:T(8,128)(2,1)S(1)} %collective-permute-done), channel_id=1, source_target_pairs={{0,1},{1,0},{2,3},{3,2},{4,5},{5,4},{6,7},{7,6},{8,9},{9,8},{10,11... | collective-permute-start | bytes 786440 | tf_op jit(solution)/shard_map/ppermute | solution.py:56
  31.5 25.6 %collective-permute-start.13 = (bf16[512,1024]{1,0:T(8,128)(2,1)S(1)}, bf16[512,1024]{1,0:T(8,128)(2,1)S(1)}, u32[]{:S(2)}, u32[]{:S(2)}) collective-permute-start(bf16[512,1024]{1,0:T(8,128)(2,1)S(1)} %add_convert_fusion.1), channel_id=1, source_target_pairs={{0,4},{1,5},{2,6},{3,7},{4,0},{5,1},{6,2},{7,3},{8,12},{9,13},{10,... | collective-permute-start | bytes 3145736 | tf_op jit(solution)/shard_map/ppermute | solution.py:62
  33.6 23.4 %collective-permute-start.12 = (bf16[512,1024]{1,0:T(8,128)(2,1)S(1)}, bf16[512,1024]{1,0:T(8,128)(2,1)S(1)}, u32[]{:S(2)}, u32[]{:S(2)}) collective-permute-start(bf16[512,1024]{1,0:T(8,128)(2,1)S(1)} %add_convert_fusion.1), channel_id=1, source_target_pairs={{0,0},{1,1},{2,2},{3,3},{4,8},{5,9},{6,10},{7,11},{8,4},{9,5},{10,... | collective-permute-start | bytes 3145736 | tf_op jit(solution)/shard_map/ppermute | solution.py:62
  34.6 22.5 %collective-permute-start.8 = (bf16[256,1024]{1,0:T(8,128)(2,1)S(1)}, bf16[256,1024]{1,0:T(8,128)(2,1)S(1)}, u32[]{:S(2)}, u32[]{:S(2)}) collective-permute-start(bf16[256,1024]{1,0:T(8,128)(2,1)S(1)} %get-tuple-element.21), channel_id=1, source_target_pairs={{0,2},{1,3},{2,0},{3,1},{4,6},{5,7},{6,4},{7,5},{8,10},{9,11},{10,... | collective-permute-start | bytes 1572872 | tf_op jit(solution)/shard_map/ppermute | solution.py:56
  36.2 3.6 %collective-permute-start.10 = (bf16[256,1024]{1,0:T(8,128)(2,1)S(1)}, bf16[256,1024]{1,0:T(8,128)(2,1)S(1)}, u32[]{:S(2)}, u32[]{:S(2)}) collective-permute-start(bf16[256,1024]{1,0:T(8,128)(2,1)S(1)} %get-tuple-element.21), channel_id=1, source_target_pairs={{0,1},{1,0},{2,3},{3,2},{4,5},{5,4},{6,7},{7,6},{8,9},{9,8},{10,11... | collective-permute-start | bytes 1572872 | tf_op jit(solution)/shard_map/ppermute | solution.py:56
  38.8 20.7 %collective-permute-start.11 = (bf16[256,1024]{1,0:T(8,128)(2,1)S(1)}, bf16[256,1024]{1,0:T(8,128)(2,1)S(1)}, u32[]{:S(2)}, u32[]{:S(2)}) collective-permute-start(bf16[256,1024]{1,0:T(8,128)(2,1)S(1)} %get-tuple-element.22), channel_id=1, source_target_pairs={{0,2},{1,3},{2,0},{3,1},{4,6},{5,7},{6,4},{7,5},{8,10},{9,11},{10,... | collective-permute-start | bytes 1572872 | tf_op jit(solution)/shard_map/ppermute | solution.py:56
  63.9 27.6 %collective-permute-start.22 = (bf16[512,1024]{1,0:T(8,128)(2,1)S(1)}, bf16[512,1024]{1,0:T(8,128)(2,1)S(1)}, u32[]{:S(2)}, u32[]{:S(2)}) collective-permute-start(bf16[512,1024]{1,0:T(8,128)(2,1)S(1)} %get-tuple-element.19), channel_id=1, source_target_pairs={{0,4},{1,5},{2,6},{3,7},{4,0},{5,1},{6,2},{7,3},{8,12},{9,13},{10,... | collective-permute-start | bytes 3145736 | tf_op jit(solution)/shard_map/ppermute | solution.py:62
  68.1 3.6 %collective-permute-start.19 = (bf16[256,1024]{1,0:T(8,128)(2,1)S(1)}, bf16[256,1024]{1,0:T(8,128)(2,1)S(1)}, u32[]{:S(2)}, u32[]{:S(2)}) collective-permute-start(bf16[256,1024]{1,0:T(8,128)(2,1)S(1)} %slice_add_fusion), channel_id=1, source_target_pairs={{0,1},{1,0},{2,3},{3,2},{4,5},{5,4},{6,7},{7,6},{8,9},{9,8},{10,11... | collective-permute-start | bytes 1572872 | tf_op jit(solution)/shard_map/ppermute | solution.py:56
  68.2 14.4 %collective-permute-start.17 = (bf16[256,1024]{1,0:T(8,128)(2,1)S(1)}, bf16[256,1024]{1,0:T(8,128)(2,1)S(1)}, u32[]{:S(2)}, u32[]{:S(2)}) collective-permute-start(bf16[256,1024]{1,0:T(8,128)(2,1)S(1)} %get-tuple-element.32), channel_id=1, source_target_pairs={{0,16},{1,17},{2,18},{3,19},{4,20},{5,21},{6,22},{7,23},{8,24},{9,... | collective-permute-start | bytes 1572872 | tf_op jit(solution)/shard_map/ppermute | solution.py:70
  68.7 22.8 %collective-permute-start.21 = (bf16[512,1024]{1,0:T(8,128)(2,1)S(1)}, bf16[512,1024]{1,0:T(8,128)(2,1)S(1)}, u32[]{:S(2)}, u32[]{:S(2)}) collective-permute-start(bf16[512,1024]{1,0:T(8,128)(2,1)S(1)} %get-tuple-element.20), channel_id=1, source_target_pairs={{0,0},{1,1},{2,2},{3,3},{4,8},{5,9},{6,10},{7,11},{8,4},{9,5},{10,... | collective-permute-start | bytes 3145736 | tf_op jit(solution)/shard_map/ppermute | solution.py:62
  69.6 21.9 %collective-permute-start.20 = (bf16[256,1024]{1,0:T(8,128)(2,1)S(1)}, bf16[256,1024]{1,0:T(8,128)(2,1)S(1)}, u32[]{:S(2)}, u32[]{:S(2)}) collective-permute-start(bf16[256,1024]{1,0:T(8,128)(2,1)S(1)} %get-tuple-element.31), channel_id=1, source_target_pairs={{0,2},{1,3},{2,0},{3,1},{4,6},{5,7},{6,4},{7,5},{8,10},{9,11},{10,... | collective-permute-start | bytes 1572872 | tf_op jit(solution)/shard_map/ppermute | solution.py:56
  71.6 19.9 %collective-permute-start.16 = (bf16[256,1024]{1,0:T(8,128)(2,1)S(1)}, bf16[256,1024]{1,0:T(8,128)(2,1)S(1)}, u32[]{:S(2)}, u32[]{:S(2)}) collective-permute-start(bf16[256,1024]{1,0:T(8,128)(2,1)S(1)} %get-tuple-element.31), channel_id=1, source_target_pairs={{0,1},{1,0},{2,3},{3,2},{4,5},{5,4},{6,7},{7,6},{8,9},{9,8},{10,11... | collective-permute-start | bytes 1572872 | tf_op jit(solution)/shard_map/ppermute | solution.py:56
  82.6 13.5 %collective-permute-start.18 = (bf16[256,1024]{1,0:T(8,128)(2,1)S(1)}, bf16[256,1024]{1,0:T(8,128)(2,1)S(1)}, u32[]{:S(2)}, u32[]{:S(2)}) collective-permute-start(bf16[256,1024]{1,0:T(8,128)(2,1)S(1)} %slice_add_fusion), channel_id=1, source_target_pairs={{0,2},{1,3},{2,0},{3,1},{4,6},{5,7},{6,4},{7,5},{8,10},{9,11},{10,... | collective-permute-start | bytes 1572872 | tf_op jit(solution)/shard_map/ppermute | solution.py:56
  96.9 4.6 %collective-permute-start.27 = (bf16[256,1024]{1,0:T(8,128)(2,1)S(1)}, bf16[256,1024]{1,0:T(8,128)(2,1)S(1)}, u32[]{:S(2)}, u32[]{:S(2)}) collective-permute-start(bf16[256,1024]{1,0:T(8,128)(2,1)S(1)} %get-tuple-element.47), channel_id=1, source_target_pairs={{0,1},{1,0},{2,3},{3,2},{4,5},{5,4},{6,7},{7,6},{8,9},{9,8},{10,11... | collective-permute-start | bytes 1572872 | tf_op jit(solution)/shard_map/ppermute | solution.py:56
  99.4 3.6 %collective-permute-start.24 = (bf16[256,1024]{1,0:T(8,128)(2,1)S(1)}, bf16[256,1024]{1,0:T(8,128)(2,1)S(1)}, u32[]{:S(2)}, u32[]{:S(2)}) collective-permute-start(bf16[256,1024]{1,0:T(8,128)(2,1)S(1)} %get-tuple-element.30), channel_id=1, source_target_pairs={{0,1},{1,0},{2,3},{3,2},{4,5},{5,4},{6,7},{7,6},{8,9},{9,8},{10,11... | collective-permute-start | bytes 1572872 | tf_op jit(solution)/shard_map/ppermute | solution.py:56
  99.6 14.2 %collective-permute-start.28 = (bf16[256,1024]{1,0:T(8,128)(2,1)S(1)}, bf16[256,1024]{1,0:T(8,128)(2,1)S(1)}, u32[]{:S(2)}, u32[]{:S(2)}) collective-permute-start(bf16[256,1024]{1,0:T(8,128)(2,1)S(1)} %get-tuple-element.30), channel_id=1, source_target_pairs={{0,2},{1,3},{2,0},{3,1},{4,6},{5,7},{6,4},{7,5},{8,10},{9,11},{10,... | collective-permute-start | bytes 1572872 | tf_op jit(solution)/shard_map/ppermute | solution.py:56
  101.1 13.9 %collective-permute-start.25 = (bf16[256,1024]{1,0:T(8,128)(2,1)S(1)}, bf16[256,1024]{1,0:T(8,128)(2,1)S(1)}, u32[]{:S(2)}, u32[]{:S(2)}) collective-permute-start(bf16[256,1024]{1,0:T(8,128)(2,1)S(1)} %get-tuple-element.29), channel_id=1, source_target_pairs={{0,16},{1,17},{2,18},{3,19},{4,20},{5,21},{6,22},{7,23},{8,24},{9,... | collective-permute-start | bytes 1572872 | tf_op jit(solution)/shard_map/ppermute | solution.py:70
  104.2 11.4 %collective-permute-start.26 = (f32[256,256]{1,0:T(8,128)S(1)}, f32[256,256]{1,0:T(8,128)S(1)}, u32[]{:S(2)}, u32[]{:S(2)}) collective-permute-start(f32[256,256]{1,0:T(8,128)S(1)} %convolution_add_fusion.4), channel_id=1, source_target_pairs={{0,4},{1,5},{2,6},{3,7},{4,0},{5,1},{6,2},{7,3},{8,12},{9,13},{10,... | collective-permute-start | bytes 786440 | tf_op jit(solution)/shard_map/ppermute | solution.py:62
  116.6 19.4 %collective-permute-start.30 = (f32[256,768]{1,0:T(8,128)S(1)}, f32[256,768]{1,0:T(8,128)S(1)}, u32[]{:S(2)}, u32[]{:S(2)}) collective-permute-start(f32[256,768]{1,0:T(8,128)S(1)} %pad_maximum_fusion.2), channel_id=1, source_target_pairs={{0,4},{1,5},{2,6},{3,7},{4,0},{5,1},{6,2},{7,3},{8,12},{9,13},{10,... | collective-permute-start | bytes 2359304 | tf_op jit(solution)/shard_map/ppermute | solution.py:62
  117.2 18.8 %collective-permute-start.31 = (f32[1024]{0:T(1024)S(1)}, f32[1024]{0:T(1024)S(1)}, u32[]{:S(2)}, u32[]{:S(2)}) collective-permute-start(f32[1024]{0:T(1024)S(1)} %pad_maximum_fusion.3), channel_id=1, source_target_pairs={{0,4},{1,5},{2,6},{3,7},{4,0},{5,1},{6,2},{7,3},{8,12},{9,13},{10,... | collective-permute-start | bytes 12296 | tf_op jit(solution)/shard_map/ppermute | solution.py:62
  137.5 3.6 %collective-permute-start.33 = (f32[256]{0:T(256)S(1)}, f32[256]{0:T(256)S(1)}, u32[]{:S(2)}, u32[]{:S(2)}) collective-permute-start(f32[256]{0:T(256)S(1)} %get-tuple-element.46), channel_id=1, source_target_pairs={{0,16},{1,17},{2,18},{3,19},{4,20},{5,21},{6,22},{7,23},{8,24},{9,... | collective-permute-start | bytes 3080 | tf_op jit(solution)/shard_map/ppermute | solution.py:70
  138.0 4.5 %collective-permute-start.34 = (f32[256]{0:T(256)S(1)}, f32[256]{0:T(256)S(1)}, u32[]{:S(2)}, u32[]{:S(2)}) collective-permute-start(f32[256]{0:T(256)S(1)} %get-tuple-element.46), channel_id=1, source_target_pairs={{0,20},{1,21},{2,22},{3,23},{4,16},{5,17},{6,18},{7,19},{8,28},{9,... | collective-permute-start | bytes 3080 | tf_op jit(solution)/shard_map/ppermute | solution.py:70
  139.3 3.6 %collective-permute-start.32 = (f32[256]{0:T(256)S(1)}, f32[256]{0:T(256)S(1)}, u32[]{:S(2)}, u32[]{:S(2)}) collective-permute-start(f32[256]{0:T(256)S(1)} %get-tuple-element.45), channel_id=1, source_target_pairs={{0,4},{1,5},{2,6},{3,7},{4,0},{5,1},{6,2},{7,3},{8,12},{9,13},{10,... | collective-permute-start | bytes 3080 | tf_op jit(solution)/shard_map/ppermute | solution.py:62
  142.9 3.6 %collective-permute-start.36 = (f32[256]{0:T(256)S(1)}, f32[256]{0:T(256)S(1)}, u32[]{:S(2)}, u32[]{:S(2)}) collective-permute-start(f32[256]{0:T(256)S(1)} %add_add_fusion.3), channel_id=1, source_target_pairs={{0,2},{1,3},{2,0},{3,1},{4,6},{5,7},{6,4},{7,5},{8,10},{9,11},{10,... | collective-permute-start | bytes 3080 | tf_op jit(solution)/shard_map/ppermute | solution.py:56
  147.5 4.6 %collective-permute-start.38 = (f32[1024]{0:T(1024)S(1)}, f32[1024]{0:T(1024)S(1)}, u32[]{:S(2)}, u32[]{:S(2)}) collective-permute-start(f32[1024]{0:T(1024)S(1)} %pad_maximum_fusion.4), channel_id=1, source_target_pairs={{0,8},{1,9},{2,10},{3,11},{4,12},{5,13},{6,14},{7,15},{8,0},{9,1},... | collective-permute-start | bytes 12296 | tf_op jit(solution)/shard_map/ppermute | solution.py:62
  (10 other events, 41.3 us)

commit v4 on v3

--- a/solution.py
+++ b/solution.py
@@ -23,9 +23,9 @@
     return sum(jnp.minimum(jnp.abs(r.astype(F32)), 0.0) for r in rows)
 
 
-def fence(swap, middle, others):
-    done = lax.optimization_barrier(token(swap))
-    done = lax.optimization_barrier(token(middle) + done)
+def fence(middle, swap, others):
+    done = lax.optimization_barrier(token(middle))
+    done = lax.optimization_barrier(token(swap) + done)
     return token(*others) + done
 
 
@@ -137,7 +137,10 @@
             near1.append([v] + [over_pool(v, r) for r in range(1, n_pool)])
             far1.append([inner(v, 0, 1)] + [over_pool(v, r, 1) for r in range(1, n_pool)])
         done = token(*features[1:nx])
-        near1, far1 = [[in_order([behind(v, done[:, :1]) for v in u], pool) for u in w] for w in (near1, far1)]
+        crossed = token(*features[nx + 1:])[:, :1]
+        joined = lax.optimization_barrier(token(*[v for u in far1 for v in u]) + crossed)
+        near1 = [in_order([behind(v, done[:, :1]) for v in u], pool) for u in near1]
+        far1 = [in_order([behind(v, joined) for v in u], pool) for u in far1]
         first = partial([own1] + near1 + [flip1] + far1).astype(BF)
 
         start = token(first)
@@ -147,7 +150,7 @@
         own3 = behind(factor_own([1, 1, 1, 2]), start)
         flip2, flip3 = inner(own2, 0, 1), inner(own3, 0, 1)
         moved2, moved3 = factor_x(own2), factor_x(own3)
-        done = fence(step1, step2, [flip2, flip3, *moved2, *moved3])
+        done = fence(step2, step1, [flip2, flip3, *moved2, *moved3])
         moved2, moved3 = [behind(v, done) for v in moved2], [behind(v, done) for v in moved3]
         second = partial([own2] + moved2 + [flip2] + factor_flip(moved2))
         third = partial([own3] + moved3 + [flip3] + factor_flip(moved3))
@@ -162,12 +165,14 @@
         t_flip_a = inner(t_a, 0, 1)
         t_moved_a = [inner(t_a, s, 0) for s in range(1, nx)]
         p_moved_a = [over_pool(p_a, s) for s in range(1, n_pool)]
-        done = fence(step3, step4, [flip4, *moved4, t_flip_a, *t_moved_a, *p_moved_a])
+        done = fence(step4, step3, [flip4, *moved4, t_flip_a, *t_moved_a, *p_moved_a])
 
         moved4 = [behind(v, done) for v in moved4]
         fourth = partial([own4] + moved4 + [flip4] + factor_flip(moved4))
-        t_moved_a = [behind(v, done) for v in t_moved_a]
         white_b = (jnp.where(top, fourth, second + step3.astype(F32) + step4.astype(F32)) + done).astype(BF)
+        later = token(white_b) + done
+        t_a, t_flip_a = behind(t_a, later), behind(t_flip_a, later)
+        t_moved_a = [behind(v, later) for v in t_moved_a]
         t_b, p_b = white_b[:count_t], white_b[count_t:]
         t_moved_b = [inner(t_b, s, 0) for s in range(1, nx)]
         p_moved_b = [over_pool(p_b, s) for s in range(1, n_pool)]

time: 153 us -> 157 us (1.026)
  other arithmetic: 7.86 us -> 11.4 us
  starting transfers between devices: 37.2 us -> 34.7 us
  waiting for transfers between devices: 86.4 us -> 88 us
    ppermute x9, waiting for transfers between devices: 42.6 us -> 47.3 us  [along_z(): return lax.ppermute(value, 'tgt', pairs)]
    ppermute x6, waiting for transfers between devices: 16.6 us -> 12.8 us  [over_pool(): return lax.ppermute(value, ('pool', 'tgt'), pairs)]
    ppermute x24, starting transfers between devices: 16.9 us -> 13.5 us  [inner(): return lax.ppermute(value, 'tgt', pairs)]
    select_n x5, other arithmetic: 0.11 us -> 2.17 us  [in_order(): jnp.where(low, pieces[0], pieces[1])]
    ppermute x6, starting transfers between devices: 5.09 us -> 7.06 us  [over_pool(): return lax.ppermute(value, ('pool', 'tgt'), pairs)]
  transfers between devices with their start and end apart: 39 -> 39, of which waited for: 21 -> 20; matrix products, arithmetic and copies ran while one was open for 14% -> 13% of each run, Pallas kernels for 0% -> 0%
where the time goes in v4:
time: 157 us; the launch traced here: 156 us
  waiting for transfers between devices  88 us (56%)
  starting transfers between devices  34.7 us (22%)
  matrix products  12.5 us (8%)
  other arithmetic  11.4 us (7%)
  local copies, waits for them, and re-layouts  7.83 us (5%)
  between operations  1.85 us (1%)
    ppermute x9, waiting for transfers between devices, along_z(): return lax.ppermute(value, 'tgt', pairs)  47.3 us
    ppermute x24, waiting for transfers between devices, inner(): return lax.ppermute(value, 'tgt', pairs)  27.9 us
    ppermute x9, starting transfers between devices, along_z(): return lax.ppermute(value, 'tgt', pairs)  14.1 us
    ppermute x24, starting transfers between devices, inner(): return lax.ppermute(value, 'tgt', pairs)  13.5 us
    ppermute x6, waiting for transfers between devices, over_pool(): return lax.ppermute(value, ('pool', 'tgt'), pairs)  12.8 us
    dot_general x16, matrix products, matmul(): lax.dot_general(a, b, (((1,), (0,)), ((), ())), preferred_element_type=F32)  7.81 us
    ppermute x6, starting transfers between devices, over_pool(): return lax.ppermute(value, ('pool', 'tgt'), pairs)  7.06 us
    dot_general x10, matrix products, matmul_t(): lax.dot_general(a, b, (((1,), (1,)), ((), ())), preferred_element_type=F32)  4.69 us
  transfers between devices with their start and end apart: 39, of which 20 were waited for; matrix products, arithmetic and copies ran while one was open for 13% of the time, Pallas kernels for 0%

profile of v4, /device:TPU:0, one launch (start us, length us, event | category | flops | bytes accessed | tf_op | source)
XLA Modules:
  0.0 156.3 jit_solution(12381954894453468381)
XLA Ops:
  0.0 1.2 constant_dynamic-slice_fusion.1
  2.0 2.9 %collective-permute-start = (bf16[128,1024]{1,0:T(8,128)(2,1)}, bf16[128,1024]{1,0:T(8,128)(2,1)}, u32[]{:S(2)}, u32[]{:S(2)}) collective-permute-start(bf16[128,1024]{1,0:T(8,128)(2,1)} %constant_dynamic-slice_fusion), channel_id=1, source_target_pairs={{0,2},{1,3},{2,0},{3,1},{4,6},{5,7},{6,4},{7,5},{8,10},{9,11},{10,... | collective-permute-start | bytes 786440 | tf_op jit(solution)/shard_map/ppermute | solution.py:56
  5.6 3.9 %gather_fusion = bf16[1024,256]{1,0:T(8,128)(2,1)S(1)} fusion(bf16[4096,256]{1,0:T(8,128)(2,1)S(1)} %copy-done, s32[1024]{0:T(1024)S(1)} %fusion.41), kind=kCustom, calls=%fused_computation | custom fusion | bytes 1052672 | tf_op jit(solution)/shard_map/gather | solution.py:96
  10.5 1.0 collective-permute-done
  12.3 2.0 %fusion.29 = (bf16[512,256]{1,0:T(8,128)(2,1)}, bf16[512,256]{1,0:T(8,128)(2,1)}, bf16[512,256]{1,0:T(8,128)(2,1)}) fusion(s32[]{:T(128)S(6)} %select_n.195, s32[]{:T(128)S(6)} %select_n.200, bf16[2,2,256,256]{3,2,1,0:T(8,128)(2,1)} %bitcast.61, bf16[2,2,256,256]{3,2,1,0:T(8,128)(2,1)S(1)} %bitcast.59, bf16[256]{0:T(256)(128)(2,1)S(1)} %fusion.102, ...), kind=kLoop, calls=%fused_computation.72 | loop fusion | flops 2883584 | bytes 1835536 | tf_op jit(solution)/shard_map/add | solution.py:34
  14.2 1.7 %collective-permute-start.1 = (bf16[512,256]{1,0:T(8,128)(2,1)}, bf16[512,256]{1,0:T(8,128)(2,1)S(1)}, u32[]{:S(2)}, u32[]{:S(2)}) collective-permute-start(bf16[512,256]{1,0:T(8,128)(2,1)} %get-tuple-element.28), channel_id=1, source_target_pairs={{0,2},{1,3},{2,0},{3,1},{4,6},{5,7},{6,4},{7,5},{8,10},{9,11},{10,... | collective-permute-start | bytes 786440 | tf_op jit(solution)/shard_map/ppermute | solution.py:56
  16.0 1.5 collective-permute-start.2
  18.6 5.1 %collective-permute-done.1 = bf16[512,256]{1,0:T(8,128)(2,1)S(1)} collective-permute-done((bf16[512,256]{1,0:T(8,128)(2,1)}, bf16[512,256]{1,0:T(8,128)(2,1)S(1)}, u32[]{:S(2)}, u32[]{:S(2)}) %collective-permute-start.1) | collective-permute-done | bytes 262176 | tf_op jit(solution)/shard_map/ppermute | solution.py:56
  24.9 1.7 %collective-permute-done.5 = bf16[512,256]{1,0:T(8,128)(2,1)S(1)} collective-permute-done((bf16[512,256]{1,0:T(8,128)(2,1)}, bf16[512,256]{1,0:T(8,128)(2,1)S(1)}, u32[]{:S(2)}, u32[]{:S(2)}) %collective-permute-start.5) | collective-permute-done | bytes 262176 | tf_op jit(solution)/shard_map/ppermute | solution.py:56
  26.6 1.2 collective-permute-start.3
  29.0 1.1 collective-permute-done.7
  30.9 1.1 broadcast_select_fusion.11
  32.4 1.1 broadcast_select_fusion.9
  35.4 4.8 %collective-permute-start.12 = (bf16[512,1024]{1,0:T(8,128)(2,1)S(1)}, bf16[512,1024]{1,0:T(8,128)(2,1)S(1)}, u32[]{:S(2)}, u32[]{:S(2)}) collective-permute-start(bf16[512,1024]{1,0:T(8,128)(2,1)S(1)} %add_convert_fusion.1), channel_id=1, source_target_pairs={{0,4},{1,5},{2,6},{3,7},{4,0},{5,1},{6,2},{7,3},{8,12},{9,13},{10,... | collective-permute-start | bytes 3145736 | tf_op jit(solution)/shard_map/ppermute | solution.py:62
  40.5 1.2 collective-permute-start.11
  43.1 1.3 collective-permute-done.10
  46.1 17.2 %collective-permute-done.12 = bf16[512,1024]{1,0:T(8,128)(2,1)S(1)} collective-permute-done((bf16[512,1024]{1,0:T(8,128)(2,1)S(1)}, bf16[512,1024]{1,0:T(8,128)(2,1)S(1)}, u32[]{:S(2)}, u32[]{:S(2)}) %collective-permute-start.12) | collective-permute-done | bytes 1048608 | tf_op jit(solution)/shard_map/ppermute | solution.py:62
  63.4 1.8 %collective-permute-done.8 = bf16[256,1024]{1,0:T(8,128)(2,1)S(1)} collective-permute-done((bf16[256,1024]{1,0:T(8,128)(2,1)S(1)}, bf16[256,1024]{1,0:T(8,128)(2,1)S(1)}, u32[]{:S(2)}, u32[]{:S(2)}) %collective-permute-start.8) | collective-permute-done | bytes 524320 | tf_op jit(solution)/shard_map/ppermute | solution.py:56
  70.5 1.6 %collective-permute-start.20 = (bf16[256,1024]{1,0:T(8,128)(2,1)S(1)}, bf16[256,1024]{1,0:T(8,128)(2,1)S(1)}, u32[]{:S(2)}, u32[]{:S(2)}) collective-permute-start(bf16[256,1024]{1,0:T(8,128)(2,1)S(1)} %get-tuple-element.32), channel_id=1, source_target_pairs={{0,16},{1,17},{2,18},{3,19},{4,20},{5,21},{6,22},{7,23},{8,24},{9,... | collective-permute-start | bytes 1572872 | tf_op jit(solution)/shard_map/ppermute | solution.py:70
  72.1 1.9 %collective-permute-start.21 = (bf16[512,1024]{1,0:T(8,128)(2,1)S(1)}, bf16[512,1024]{1,0:T(8,128)(2,1)S(1)}, u32[]{:S(2)}, u32[]{:S(2)}) collective-permute-start(bf16[512,1024]{1,0:T(8,128)(2,1)S(1)} %get-tuple-element.19), channel_id=1, source_target_pairs={{0,4},{1,5},{2,6},{3,7},{4,0},{5,1},{6,2},{7,3},{8,12},{9,13},{10,... | collective-permute-start | bytes 3145736 | tf_op jit(solution)/shard_map/ppermute | solution.py:62
  74.6 9.9 %collective-permute-done.20 = bf16[256,1024]{1,0:T(8,128)(2,1)S(1)} collective-permute-done((bf16[256,1024]{1,0:T(8,128)(2,1)S(1)}, bf16[256,1024]{1,0:T(8,128)(2,1)S(1)}, u32[]{:S(2)}, u32[]{:S(2)}) %collective-permute-start.20) | collective-permute-done | bytes 524320 | tf_op jit(solution)/shard_map/ppermute | solution.py:70
  85.9 11.2 %collective-permute-done.21 = bf16[512,1024]{1,0:T(8,128)(2,1)S(1)} collective-permute-done((bf16[512,1024]{1,0:T(8,128)(2,1)S(1)}, bf16[512,1024]{1,0:T(8,128)(2,1)S(1)}, u32[]{:S(2)}, u32[]{:S(2)}) %collective-permute-start.21) | collective-permute-done | bytes 1048608 | tf_op jit(solution)/shard_map/ppermute | solution.py:62
  97.1 2.5 %collective-permute-done.17 = bf16[256,1024]{1,0:T(8,128)(2,1)S(1)} collective-permute-done((bf16[256,1024]{1,0:T(8,128)(2,1)S(1)}, bf16[256,1024]{1,0:T(8,128)(2,1)S(1)}, u32[]{:S(2)}, u32[]{:S(2)}) %collective-permute-start.17) | collective-permute-done | bytes 524320 | tf_op jit(solution)/shard_map/ppermute | solution.py:56
  106.5 10.8 %collective-permute-done.28 = bf16[256,1024]{1,0:T(8,128)(2,1)S(1)} collective-permute-done((bf16[256,1024]{1,0:T(8,128)(2,1)S(1)}, bf16[256,1024]{1,0:T(8,128)(2,1)S(1)}, u32[]{:S(2)}, u32[]{:S(2)}) %collective-permute-start.28) | collective-permute-done | bytes 524320 | tf_op jit(solution)/shard_map/ppermute | solution.py:56
  121.0 2.0 %collective-permute-start.31 = (f32[1024]{0:T(1024)S(1)}, f32[1024]{0:T(1024)S(1)}, u32[]{:S(2)}, u32[]{:S(2)}) collective-permute-start(f32[1024]{0:T(1024)S(1)} %pad_maximum_fusion.3), channel_id=1, source_target_pairs={{0,4},{1,5},{2,6},{3,7},{4,0},{5,1},{6,2},{7,3},{8,12},{9,13},{10,... | collective-permute-start | bytes 12296 | tf_op jit(solution)/shard_map/ppermute | solution.py:62
  123.5 17.0 %collective-permute-done.31 = f32[1024]{0:T(1024)S(1)} collective-permute-done((f32[1024]{0:T(1024)S(1)}, f32[1024]{0:T(1024)S(1)}, u32[]{:S(2)}, u32[]{:S(2)}) %collective-permute-start.31) | collective-permute-done | bytes 4128 | tf_op jit(solution)/shard_map/ppermute | solution.py:62
  142.9 2.6 %collective-permute-start.34 = (f32[256]{0:T(256)S(1)}, f32[256]{0:T(256)S(1)}, u32[]{:S(2)}, u32[]{:S(2)}) collective-permute-start(f32[256]{0:T(256)S(1)} %get-tuple-element.46), channel_id=1, source_target_pairs={{0,20},{1,21},{2,22},{3,23},{4,16},{5,17},{6,18},{7,19},{8,28},{9,... | collective-permute-start | bytes 3080 | tf_op jit(solution)/shard_map/ppermute | solution.py:70
  145.8 1.5 collective-permute-done.34
  148.0 1.2 collective-permute-start.37
  149.3 1.8 %collective-permute-done.36 = f32[256]{0:T(256)S(1)} collective-permute-done((f32[256]{0:T(256)S(1)}, f32[256]{0:T(256)S(1)}, u32[]{:S(2)}, u32[]{:S(2)}) %collective-permute-start.36) | collective-permute-done | bytes 1056 | tf_op jit(solution)/shard_map/ppermute | solution.py:56
  151.1 2.7 %collective-permute-start.38 = (f32[1024]{0:T(1024)S(1)}, f32[1024]{0:T(1024)S(1)}, u32[]{:S(2)}, u32[]{:S(2)}) collective-permute-start(f32[1024]{0:T(1024)S(1)} %pad_maximum_fusion.4), channel_id=1, source_target_pairs={{0,8},{1,9},{2,10},{3,11},{4,12},{5,13},{6,14},{7,15},{8,0},{9,1},... | collective-permute-start | bytes 12296 | tf_op jit(solution)/shard_map/ppermute | solution.py:62
  153.8 1.9 %collective-permute-done.38 = f32[1024]{0:T(1024)S(1)} collective-permute-done((f32[1024]{0:T(1024)S(1)}, f32[1024]{0:T(1024)S(1)}, u32[]{:S(2)}, u32[]{:S(2)}) %collective-permute-start.38) | collective-permute-done | bytes 4128 | tf_op jit(solution)/shard_map/ppermute | solution.py:62
  (132 shorter events, 33.9 us)
Async XLA Ops:
  2.0 9.6 %collective-permute-start = (bf16[128,1024]{1,0:T(8,128)(2,1)}, bf16[128,1024]{1,0:T(8,128)(2,1)}, u32[]{:S(2)}, u32[]{:S(2)}) collective-permute-start(bf16[128,1024]{1,0:T(8,128)(2,1)} %constant_dynamic-slice_fusion), channel_id=1, source_target_pairs={{0,2},{1,3},{2,0},{3,1},{4,6},{5,7},{6,4},{7,5},{8,10},{9,11},{10,... | collective-permute-start | bytes 786440 | tf_op jit(solution)/shard_map/ppermute | solution.py:56
  14.2 9.5 %collective-permute-start.1 = (bf16[512,256]{1,0:T(8,128)(2,1)}, bf16[512,256]{1,0:T(8,128)(2,1)S(1)}, u32[]{:S(2)}, u32[]{:S(2)}) collective-permute-start(bf16[512,256]{1,0:T(8,128)(2,1)} %get-tuple-element.28), channel_id=1, source_target_pairs={{0,2},{1,3},{2,0},{3,1},{4,6},{5,7},{6,4},{7,5},{8,10},{9,11},{10,... | collective-permute-start | bytes 786440 | tf_op jit(solution)/shard_map/ppermute | solution.py:56
  16.0 10.6 %collective-permute-start.5 = (bf16[512,256]{1,0:T(8,128)(2,1)}, bf16[512,256]{1,0:T(8,128)(2,1)S(1)}, u32[]{:S(2)}, u32[]{:S(2)}) collective-permute-start(bf16[512,256]{1,0:T(8,128)(2,1)} %get-tuple-element.26), channel_id=1, source_target_pairs={{0,3},{1,2},{2,1},{3,0},{4,7},{5,6},{6,5},{7,4},{8,11},{9,10},{10,... | collective-permute-start | bytes 786440 | tf_op jit(solution)/shard_map/ppermute | solution.py:56
  16.0 14.9 %collective-permute-start.2 = (bf16[128,1024]{1,0:T(8,128)(2,1)}, bf16[128,1024]{1,0:T(8,128)(2,1)}, u32[]{:S(2)}, u32[]{:S(2)}) collective-permute-start(bf16[128,1024]{1,0:T(8,128)(2,1)} %collective-permute-done), channel_id=1, source_target_pairs={{0,16},{1,17},{2,18},{3,19},{4,20},{5,21},{6,22},{7,23},{8,24},{9,... | collective-permute-start | bytes 786440 | tf_op jit(solution)/shard_map/ppermute | solution.py:70
  17.5 11.5 %collective-permute-start.6 = (bf16[128,1024]{1,0:T(8,128)(2,1)}, bf16[128,1024]{1,0:T(8,128)(2,1)}, u32[]{:S(2)}, u32[]{:S(2)}) collective-permute-start(bf16[128,1024]{1,0:T(8,128)(2,1)} %collective-permute-done), channel_id=1, source_target_pairs={{0,1},{1,0},{2,3},{3,2},{4,5},{5,4},{6,7},{7,6},{8,9},{9,8},{10,11... | collective-permute-start | bytes 786440 | tf_op jit(solution)/shard_map/ppermute | solution.py:56
  17.9 12.2 %collective-permute-start.7 = (bf16[128,1024]{1,0:T(8,128)(2,1)}, bf16[128,1024]{1,0:T(8,128)(2,1)}, u32[]{:S(2)}, u32[]{:S(2)}) collective-permute-start(bf16[128,1024]{1,0:T(8,128)(2,1)} %collective-permute-done), channel_id=1, source_target_pairs={{0,17},{1,16},{2,19},{3,18},{4,21},{5,20},{6,23},{7,22},{8,25},{9,... | collective-permute-start | bytes 786440 | tf_op jit(solution)/shard_map/ppermute | solution.py:70
  23.7 9.8 %collective-permute-start.4 = (bf16[256,1024]{1,0:T(8,128)(2,1)S(1)}, bf16[256,1024]{1,0:T(8,128)(2,1)S(1)}, u32[]{:S(2)}, u32[]{:S(2)}) collective-permute-start(bf16[256,1024]{1,0:T(8,128)(2,1)S(1)} %constant_dynamic-slice_fusion.1), channel_id=1, source_target_pairs={{0,1},{1,0},{2,3},{3,2},{4,5},{5,4},{6,7},{7,6},{8,9},{9,8},{10,11... | collective-permute-start | bytes 1572872 | tf_op jit(solution)/shard_map/ppermute | solution.py:56
  26.6 6.9 %collective-permute-start.3 = (bf16[512,256]{1,0:T(8,128)(2,1)}, bf16[512,256]{1,0:T(8,128)(2,1)S(1)}, u32[]{:S(2)}, u32[]{:S(2)}) collective-permute-start(bf16[512,256]{1,0:T(8,128)(2,1)} %get-tuple-element.27), channel_id=1, source_target_pairs={{0,1},{1,0},{2,3},{3,2},{4,5},{5,4},{6,7},{7,6},{8,9},{9,8},{10,11... | collective-permute-start | bytes 786440 | tf_op jit(solution)/shard_map/ppermute | solution.py:56
  34.5 11.6 %collective-permute-start.13 = (bf16[512,1024]{1,0:T(8,128)(2,1)S(1)}, bf16[512,1024]{1,0:T(8,128)(2,1)S(1)}, u32[]{:S(2)}, u32[]{:S(2)}) collective-permute-start(bf16[512,1024]{1,0:T(8,128)(2,1)S(1)} %add_convert_fusion.1), channel_id=1, source_target_pairs={{0,0},{1,1},{2,2},{3,3},{4,8},{5,9},{6,10},{7,11},{8,4},{9,5},{10,... | collective-permute-start | bytes 3145736 | tf_op jit(solution)/shard_map/ppermute | solution.py:62
  35.4 28.0 %collective-permute-start.12 = (bf16[512,1024]{1,0:T(8,128)(2,1)S(1)}, bf16[512,1024]{1,0:T(8,128)(2,1)S(1)}, u32[]{:S(2)}, u32[]{:S(2)}) collective-permute-start(bf16[512,1024]{1,0:T(8,128)(2,1)S(1)} %add_convert_fusion.1), channel_id=1, source_target_pairs={{0,4},{1,5},{2,6},{3,7},{4,0},{5,1},{6,2},{7,3},{8,12},{9,13},{10,... | collective-permute-start | bytes 3145736 | tf_op jit(solution)/shard_map/ppermute | solution.py:62
  40.5 22.9 %collective-permute-start.11 = (bf16[256,1024]{1,0:T(8,128)(2,1)S(1)}, bf16[256,1024]{1,0:T(8,128)(2,1)S(1)}, u32[]{:S(2)}, u32[]{:S(2)}) collective-permute-start(bf16[256,1024]{1,0:T(8,128)(2,1)S(1)} %get-tuple-element.22), channel_id=1, source_target_pairs={{0,2},{1,3},{2,0},{3,1},{4,6},{5,7},{6,4},{7,5},{8,10},{9,11},{10,... | collective-permute-start | bytes 1572872 | tf_op jit(solution)/shard_map/ppermute | solution.py:56
  41.7 4.0 %collective-permute-start.9 = (bf16[256,1024]{1,0:T(8,128)(2,1)S(1)}, bf16[256,1024]{1,0:T(8,128)(2,1)S(1)}, u32[]{:S(2)}, u32[]{:S(2)}) collective-permute-start(bf16[256,1024]{1,0:T(8,128)(2,1)S(1)} %get-tuple-element.22), channel_id=1, source_target_pairs={{0,1},{1,0},{2,3},{3,2},{4,5},{5,4},{6,7},{7,6},{8,9},{9,8},{10,11... | collective-permute-start | bytes 1572872 | tf_op jit(solution)/shard_map/ppermute | solution.py:56
  44.4 20.8 %collective-permute-start.8 = (bf16[256,1024]{1,0:T(8,128)(2,1)S(1)}, bf16[256,1024]{1,0:T(8,128)(2,1)S(1)}, u32[]{:S(2)}, u32[]{:S(2)}) collective-permute-start(bf16[256,1024]{1,0:T(8,128)(2,1)S(1)} %get-tuple-element.21), channel_id=1, source_target_pairs={{0,2},{1,3},{2,0},{3,1},{4,6},{5,7},{6,4},{7,5},{8,10},{9,11},{10,... | collective-permute-start | bytes 1572872 | tf_op jit(solution)/shard_map/ppermute | solution.py:56
  69.5 15.6 %collective-permute-start.22 = (bf16[512,1024]{1,0:T(8,128)(2,1)S(1)}, bf16[512,1024]{1,0:T(8,128)(2,1)S(1)}, u32[]{:S(2)}, u32[]{:S(2)}) collective-permute-start(bf16[512,1024]{1,0:T(8,128)(2,1)S(1)} %get-tuple-element.20), channel_id=1, source_target_pairs={{0,0},{1,1},{2,2},{3,3},{4,8},{5,9},{6,10},{7,11},{8,4},{9,5},{10,... | collective-permute-start | bytes 3145736 | tf_op jit(solution)/shard_map/ppermute | solution.py:62
  70.5 14.0 %collective-permute-start.20 = (bf16[256,1024]{1,0:T(8,128)(2,1)S(1)}, bf16[256,1024]{1,0:T(8,128)(2,1)S(1)}, u32[]{:S(2)}, u32[]{:S(2)}) collective-permute-start(bf16[256,1024]{1,0:T(8,128)(2,1)S(1)} %get-tuple-element.32), channel_id=1, source_target_pairs={{0,16},{1,17},{2,18},{3,19},{4,20},{5,21},{6,22},{7,23},{8,24},{9,... | collective-permute-start | bytes 1572872 | tf_op jit(solution)/shard_map/ppermute | solution.py:70
  72.1 24.9 %collective-permute-start.21 = (bf16[512,1024]{1,0:T(8,128)(2,1)S(1)}, bf16[512,1024]{1,0:T(8,128)(2,1)S(1)}, u32[]{:S(2)}, u32[]{:S(2)}) collective-permute-start(bf16[512,1024]{1,0:T(8,128)(2,1)S(1)} %get-tuple-element.19), channel_id=1, source_target_pairs={{0,4},{1,5},{2,6},{3,7},{4,0},{5,1},{6,2},{7,3},{8,12},{9,13},{10,... | collective-permute-start | bytes 3145736 | tf_op jit(solution)/shard_map/ppermute | solution.py:62
  74.0 23.0 %collective-permute-start.16 = (bf16[256,1024]{1,0:T(8,128)(2,1)S(1)}, bf16[256,1024]{1,0:T(8,128)(2,1)S(1)}, u32[]{:S(2)}, u32[]{:S(2)}) collective-permute-start(bf16[256,1024]{1,0:T(8,128)(2,1)S(1)} %get-tuple-element.31), channel_id=1, source_target_pairs={{0,1},{1,0},{2,3},{3,2},{4,5},{5,4},{6,7},{7,6},{8,9},{9,8},{10,11... | collective-permute-start | bytes 1572872 | tf_op jit(solution)/shard_map/ppermute | solution.py:56
  74.0 23.0 %collective-permute-start.19 = (bf16[256,1024]{1,0:T(8,128)(2,1)S(1)}, bf16[256,1024]{1,0:T(8,128)(2,1)S(1)}, u32[]{:S(2)}, u32[]{:S(2)}) collective-permute-start(bf16[256,1024]{1,0:T(8,128)(2,1)S(1)} %get-tuple-element.31), channel_id=1, source_target_pairs={{0,2},{1,3},{2,0},{3,1},{4,6},{5,7},{6,4},{7,5},{8,10},{9,11},{10,... | collective-permute-start | bytes 1572872 | tf_op jit(solution)/shard_map/ppermute | solution.py:56
  84.5 15.1 %collective-permute-start.17 = (bf16[256,1024]{1,0:T(8,128)(2,1)S(1)}, bf16[256,1024]{1,0:T(8,128)(2,1)S(1)}, u32[]{:S(2)}, u32[]{:S(2)}) collective-permute-start(bf16[256,1024]{1,0:T(8,128)(2,1)S(1)} %slice_add_fusion), channel_id=1, source_target_pairs={{0,2},{1,3},{2,0},{3,1},{4,6},{5,7},{6,4},{7,5},{8,10},{9,11},{10,... | collective-permute-start | bytes 1572872 | tf_op jit(solution)/shard_map/ppermute | solution.py:56
  85.1 14.5 %collective-permute-start.18 = (bf16[256,1024]{1,0:T(8,128)(2,1)S(1)}, bf16[256,1024]{1,0:T(8,128)(2,1)S(1)}, u32[]{:S(2)}, u32[]{:S(2)}) collective-permute-start(bf16[256,1024]{1,0:T(8,128)(2,1)S(1)} %slice_add_fusion), channel_id=1, source_target_pairs={{0,1},{1,0},{2,3},{3,2},{4,5},{5,4},{6,7},{7,6},{8,9},{9,8},{10,11... | collective-permute-start | bytes 1572872 | tf_op jit(solution)/shard_map/ppermute | solution.py:56
  103.0 14.3 %collective-permute-start.28 = (bf16[256,1024]{1,0:T(8,128)(2,1)S(1)}, bf16[256,1024]{1,0:T(8,128)(2,1)S(1)}, u32[]{:S(2)}, u32[]{:S(2)}) collective-permute-start(bf16[256,1024]{1,0:T(8,128)(2,1)S(1)} %get-tuple-element.30), channel_id=1, source_target_pairs={{0,2},{1,3},{2,0},{3,1},{4,6},{5,7},{6,4},{7,5},{8,10},{9,11},{10,... | collective-permute-start | bytes 1572872 | tf_op jit(solution)/shard_map/ppermute | solution.py:56
  103.7 13.6 %collective-permute-start.27 = (bf16[256,1024]{1,0:T(8,128)(2,1)S(1)}, bf16[256,1024]{1,0:T(8,128)(2,1)S(1)}, u32[]{:S(2)}, u32[]{:S(2)}) collective-permute-start(bf16[256,1024]{1,0:T(8,128)(2,1)S(1)} %broadcast_add_fusion), channel_id=1, source_target_pairs={{0,1},{1,0},{2,3},{3,2},{4,5},{5,4},{6,7},{7,6},{8,9},{9,8},{10,11... | collective-permute-start | bytes 1572872 | tf_op jit(solution)/shard_map/ppermute | solution.py:56
  103.8 14.4 %collective-permute-start.25 = (bf16[256,1024]{1,0:T(8,128)(2,1)S(1)}, bf16[256,1024]{1,0:T(8,128)(2,1)S(1)}, u32[]{:S(2)}, u32[]{:S(2)}) collective-permute-start(bf16[256,1024]{1,0:T(8,128)(2,1)S(1)} %get-tuple-element.29), channel_id=1, source_target_pairs={{0,16},{1,17},{2,18},{3,19},{4,20},{5,21},{6,22},{7,23},{8,24},{9,... | collective-permute-start | bytes 1572872 | tf_op jit(solution)/shard_map/ppermute | solution.py:70
  106.0 13.4 %collective-permute-start.26 = (f32[256,256]{1,0:T(8,128)S(1)}, f32[256,256]{1,0:T(8,128)S(1)}, u32[]{:S(2)}, u32[]{:S(2)}) collective-permute-start(f32[256,256]{1,0:T(8,128)S(1)} %convolution_add_fusion.4), channel_id=1, source_target_pairs={{0,4},{1,5},{2,6},{3,7},{4,0},{5,1},{6,2},{7,3},{8,12},{9,13},{10,... | collective-permute-start | bytes 786440 | tf_op jit(solution)/shard_map/ppermute | solution.py:62
  120.3 20.1 %collective-permute-start.30 = (f32[256,768]{1,0:T(8,128)S(1)}, f32[256,768]{1,0:T(8,128)S(1)}, u32[]{:S(2)}, u32[]{:S(2)}) collective-permute-start(f32[256,768]{1,0:T(8,128)S(1)} %pad_maximum_fusion.2), channel_id=1, source_target_pairs={{0,4},{1,5},{2,6},{3,7},{4,0},{5,1},{6,2},{7,3},{8,12},{9,13},{10,... | collective-permute-start | bytes 2359304 | tf_op jit(solution)/shard_map/ppermute | solution.py:62
  121.0 19.4 %collective-permute-start.31 = (f32[1024]{0:T(1024)S(1)}, f32[1024]{0:T(1024)S(1)}, u32[]{:S(2)}, u32[]{:S(2)}) collective-permute-start(f32[1024]{0:T(1024)S(1)} %pad_maximum_fusion.3), channel_id=1, source_target_pairs={{0,4},{1,5},{2,6},{3,7},{4,0},{5,1},{6,2},{7,3},{8,12},{9,13},{10,... | collective-permute-start | bytes 12296 | tf_op jit(solution)/shard_map/ppermute | solution.py:62
  141.9 3.6 %collective-permute-start.32 = (f32[256]{0:T(256)S(1)}, f32[256]{0:T(256)S(1)}, u32[]{:S(2)}, u32[]{:S(2)}) collective-permute-start(f32[256]{0:T(256)S(1)} %get-tuple-element.45), channel_id=1, source_target_pairs={{0,4},{1,5},{2,6},{3,7},{4,0},{5,1},{6,2},{7,3},{8,12},{9,13},{10,... | collective-permute-start | bytes 3080 | tf_op jit(solution)/shard_map/ppermute | solution.py:62
  142.3 3.6 %collective-permute-start.33 = (f32[256]{0:T(256)S(1)}, f32[256]{0:T(256)S(1)}, u32[]{:S(2)}, u32[]{:S(2)}) collective-permute-start(f32[256]{0:T(256)S(1)} %get-tuple-element.46), channel_id=1, source_target_pairs={{0,16},{1,17},{2,18},{3,19},{4,20},{5,21},{6,22},{7,23},{8,24},{9,... | collective-permute-start | bytes 3080 | tf_op jit(solution)/shard_map/ppermute | solution.py:70
  142.9 4.5 %collective-permute-start.34 = (f32[256]{0:T(256)S(1)}, f32[256]{0:T(256)S(1)}, u32[]{:S(2)}, u32[]{:S(2)}) collective-permute-start(f32[256]{0:T(256)S(1)} %get-tuple-element.46), channel_id=1, source_target_pairs={{0,20},{1,21},{2,22},{3,23},{4,16},{5,17},{6,18},{7,19},{8,28},{9,... | collective-permute-start | bytes 3080 | tf_op jit(solution)/shard_map/ppermute | solution.py:70
  147.4 3.6 %collective-permute-start.36 = (f32[256]{0:T(256)S(1)}, f32[256]{0:T(256)S(1)}, u32[]{:S(2)}, u32[]{:S(2)}) collective-permute-start(f32[256]{0:T(256)S(1)} %add_add_fusion.3), channel_id=1, source_target_pairs={{0,2},{1,3},{2,0},{3,1},{4,6},{5,7},{6,4},{7,5},{8,10},{9,11},{10,... | collective-permute-start | bytes 3080 | tf_op jit(solution)/shard_map/ppermute | solution.py:56
  148.0 3.0 %collective-permute-start.37 = (f32[256]{0:T(256)S(1)}, f32[256]{0:T(256)S(1)}, u32[]{:S(2)}, u32[]{:S(2)}) collective-permute-start(f32[256]{0:T(256)S(1)} %add_add_fusion.3), channel_id=1, source_target_pairs={{0,3},{1,2},{2,1},{3,0},{4,7},{5,6},{6,5},{7,4},{8,11},{9,10},{10,... | collective-permute-start | bytes 3080 | tf_op jit(solution)/shard_map/ppermute | solution.py:56
  151.1 4.6 %collective-permute-start.38 = (f32[1024]{0:T(1024)S(1)}, f32[1024]{0:T(1024)S(1)}, u32[]{:S(2)}, u32[]{:S(2)}) collective-permute-start(f32[1024]{0:T(1024)S(1)} %pad_maximum_fusion.4), channel_id=1, source_target_pairs={{0,8},{1,9},{2,10},{3,11},{4,12},{5,13},{6,14},{7,15},{8,0},{9,1},... | collective-permute-start | bytes 12296 | tf_op jit(solution)/shard_map/ppermute | solution.py:62
  (10 other events, 42.6 us)

commit v5 on v3

--- a/solution.py
+++ b/solution.py
@@ -23,9 +23,9 @@
     return sum(jnp.minimum(jnp.abs(r.astype(F32)), 0.0) for r in rows)
 
 
-def fence(swap, middle, others):
-    done = lax.optimization_barrier(token(swap))
-    done = lax.optimization_barrier(token(middle) + done)
+def fence(first, second, others):
+    done = lax.optimization_barrier(token(*first))
+    done = lax.optimization_barrier(token(*second) + done)
     return token(*others) + done
 
 
@@ -105,6 +105,9 @@
         def rows_of(s, f):
             return lax.dynamic_slice(rows, (lax.rem(x + s, nx), core ^ f, 0, 0), (1, 1, n_rows, width))[0, 0]
 
+        def rows_of_both(s):
+            return lax.dynamic_index_in_dim(rows, lax.rem(x + s, nx), 0, keepdims=False)
+
         def factor_own(choice):
             return lax.dynamic_slice_in_dim(posterior_factor, choose(choice, z) * quarter, quarter, 1)
 
@@ -130,15 +133,14 @@
         parts1 = [inner(mine1, s, 0) for s in range(1, nx)]
 
         done = token(*parts1)
-        features = [inner(behind(rows_of(s, f), done), s, f) if s or f else rows_of(0, 0) for s, f in order]
-        flip1 = inner(own1, 0, 1)
-        near1, far1 = [], []
-        for v in parts1:
-            near1.append([v] + [over_pool(v, r) for r in range(1, n_pool)])
-            far1.append([inner(v, 0, 1)] + [over_pool(v, r, 1) for r in range(1, n_pool)])
-        done = token(*features[1:nx])
-        near1, far1 = [[in_order([behind(v, done[:, :1]) for v in u], pool) for u in w] for w in (near1, far1)]
-        first = partial([own1] + near1 + [flip1] + far1).astype(BF)
+        features, other = [rows_of(0, 0)], [rows_of(0, 1)]
+        for s in range(1, nx):
+            both = inner(behind(rows_of_both(s), done), s, 0)
+            features.append(lax.dynamic_index_in_dim(both, core, 0, keepdims=False))
+            other.append(lax.dynamic_index_in_dim(both, 1 - core, 0, keepdims=False))
+        features += [inner(v, 0, 1) for v in other]
+        near1 = [in_order([v] + [over_pool(v, r) for r in range(1, n_pool)], pool) for v in parts1]
+        first = partial([own1] + near1 + [inner(v, 0, 1) for v in [own1] + near1]).astype(BF)
 
         start = token(first)
         step1 = along_z(first, outer)
@@ -147,7 +149,7 @@
         own3 = behind(factor_own([1, 1, 1, 2]), start)
         flip2, flip3 = inner(own2, 0, 1), inner(own3, 0, 1)
         moved2, moved3 = factor_x(own2), factor_x(own3)
-        done = fence(step1, step2, [flip2, flip3, *moved2, *moved3])
+        done = fence([step2], [step1], [flip2, flip3, *moved2, *moved3])
         moved2, moved3 = [behind(v, done) for v in moved2], [behind(v, done) for v in moved3]
         second = partial([own2] + moved2 + [flip2] + factor_flip(moved2))
         third = partial([own3] + moved3 + [flip3] + factor_flip(moved3))
@@ -162,7 +164,7 @@
         t_flip_a = inner(t_a, 0, 1)
         t_moved_a = [inner(t_a, s, 0) for s in range(1, nx)]
         p_moved_a = [over_pool(p_a, s) for s in range(1, n_pool)]
-        done = fence(step3, step4, [flip4, *moved4, t_flip_a, *t_moved_a, *p_moved_a])
+        done = fence([step3, *moved4], [step4], [flip4, t_flip_a, *t_moved_a, *p_moved_a])
 
         moved4 = [behind(v, done) for v in moved4]
         fourth = partial([own4] + moved4 + [flip4] + factor_flip(moved4))

time: 153 us -> 156 us (1.020)
  local copies, waits for them, and re-layouts: 6.57 us -> 8.55 us
    ppermute x9, waiting for transfers between devices: 42.6 us -> 46.7 us  [along_z(): return lax.ppermute(value, 'tgt', pairs)]
    ppermute x24, waiting for transfers between devices: 27.2 us -> 23.4 us  [inner(): return lax.ppermute(value, 'tgt', pairs)]
    ppermute x24, starting transfers between devices: 16.9 us -> 14.5 us  [inner(): return lax.ppermute(value, 'tgt', pairs)]
    ppermute x6 -> x5, starting transfers between devices: 5.09 us -> 7 us  [over_pool(): return lax.ppermute(value, ('pool', 'tgt'), pairs)]
    ppermute x6 -> x5, waiting for transfers between devices: 16.6 us -> 16.7 us  [over_pool(): return lax.ppermute(value, ('pool', 'tgt'), pairs)]
  transfers between devices with their start and end apart: 39 -> 38, of which waited for: 21 -> 22; matrix products, arithmetic and copies ran while one was open for 14% -> 16% of each run, Pallas kernels for 0% -> 0%
where the time goes in v5:
time: 156 us
  waiting for transfers between devices  86.8 us (56%)
  starting transfers between devices  36 us (23%)
  matrix products  14.5 us (9%)
  other arithmetic  9.22 us (6%)
  local copies, waits for them, and re-layouts  8.55 us (5%)
    ppermute x9, waiting for transfers between devices, along_z(): return lax.ppermute(value, 'tgt', pairs)  46.7 us
    ppermute x24, waiting for transfers between devices, inner(): return lax.ppermute(value, 'tgt', pairs)  23.4 us
    ppermute x5, waiting for transfers between devices, over_pool(): return lax.ppermute(value, ('pool', 'tgt'), pairs)  16.7 us
    ppermute x24, starting transfers between devices, inner(): return lax.ppermute(value, 'tgt', pairs)  14.5 us
    ppermute x9, starting transfers between devices, along_z(): return lax.ppermute(value, 'tgt', pairs)  14.5 us
    dot_general x16, matrix products, matmul(): lax.dot_general(a, b, (((1,), (0,)), ((), ())), preferred_element_type=F32)  9.81 us
    ppermute x5, starting transfers between devices, over_pool(): return lax.ppermute(value, ('pool', 'tgt'), pairs)  7 us
    dot_general x10, matrix products, matmul_t(): lax.dot_general(a, b, (((1,), (1,)), ((), ())), preferred_element_type=F32)  4.72 us
  transfers between devices with their start and end apart: 38, of which 22 were waited for; matrix products, arithmetic and copies ran while one was open for 16% of the time, Pallas kernels for 0%

profile of v5, /device:TPU:0, one launch (start us, length us, event | category | flops | bytes accessed | tf_op | source)
XLA Modules:
  0.0 155.7 jit_solution(3689568811695012816)
XLA Ops:
  0.0 2.0 %constant_dynamic-slice_fusion.1 = bf16[256,1024]{1,0:T(8,128)(2,1)} fusion(bf16[256,4096]{1,0:T(8,128)(2,1)} %param.7, s32[]{:T(128)S(6)} %select_n.189), kind=kLoop, calls=%fused_computation.163 | loop fusion | bytes 1048580 | tf_op jit(solution)/shard_map/dynamic_slice | solution.py:112
  2.5 1.7 %constant_dynamic-slice_fusion = bf16[128,1024]{1,0:T(8,128)(2,1)} fusion(bf16[256,1024]{1,0:T(8,128)(2,1)} %constant_dynamic-slice_fusion.1, s32[]{:T(128)S(6)} %select_n.191), kind=kLoop, calls=%fused_computation.162 | loop fusion | bytes 524292 | tf_op jit(solution)/shard_map/dynamic_slice | solution.py:132
  4.1 2.5 %collective-permute-start = (bf16[128,1024]{1,0:T(8,128)(2,1)}, bf16[128,1024]{1,0:T(8,128)(2,1)}, u32[]{:S(2)}, u32[]{:S(2)}) collective-permute-start(bf16[128,1024]{1,0:T(8,128)(2,1)} %constant_dynamic-slice_fusion), channel_id=1, source_target_pairs={{0,2},{1,3},{2,0},{3,1},{4,6},{5,7},{6,4},{7,5},{8,10},{9,11},{10,... | collective-permute-start | bytes 786440 | tf_op jit(solution)/shard_map/ppermute | solution.py:56
  7.3 3.9 %gather_fusion = bf16[1024,256]{1,0:T(8,128)(2,1)S(1)} fusion(bf16[4096,256]{1,0:T(8,128)(2,1)S(1)} %copy-done, s32[1024]{0:T(1024)S(1)} %fusion.39), kind=kCustom, calls=%fused_computation | custom fusion | bytes 1052672 | tf_op jit(solution)/shard_map/gather | solution.py:96
  12.3 1.7 %collective-permute-done = bf16[128,1024]{1,0:T(8,128)(2,1)} collective-permute-done((bf16[128,1024]{1,0:T(8,128)(2,1)}, bf16[128,1024]{1,0:T(8,128)(2,1)}, u32[]{:S(2)}, u32[]{:S(2)}) %collective-permute-start) | collective-permute-done | bytes 262176 | tf_op jit(solution)/shard_map/ppermute | solution.py:56
  14.7 1.9 %fusion.19 = bf16[2,512,256]{2,1,0:T(8,128)(2,1)} fusion(s32[]{:T(128)S(6)} %select_n.190, bf16[2,2,256,256]{3,2,1,0:T(8,128)(2,1)} %bitcast.59, bf16[2,2,256,256]{3,2,1,0:T(8,128)(2,1)S(1)} %bitcast.58, bf16[256]{0:T(256)(128)(2,1)S(1)} %fusion.95), kind=kLoop, calls=%fused_computation.51 | loop fusion | flops 2097152 | bytes 1573380 | tf_op jit(solution)/shard_map/add | solution.py:34
  16.5 1.7 %collective-permute-start.1 = (bf16[2,512,256]{2,1,0:T(8,128)(2,1)}, bf16[2,512,256]{2,1,0:T(8,128)(2,1)S(1)}, u32[]{:S(2)}, u32[]{:S(2)}) collective-permute-start(bf16[2,512,256]{2,1,0:T(8,128)(2,1)} %fusion.19), channel_id=1, source_target_pairs={{0,2},{1,3},{2,0},{3,1},{4,6},{5,7},{6,4},{7,5},{8,10},{9,11},{10,... | collective-permute-start | bytes 1572872 | tf_op jit(solution)/shard_map/ppermute | solution.py:56
  18.3 1.5 collective-permute-start.2
  19.8 1.5 fusion.107
  21.3 4.8 %collective-permute-done.2 = bf16[128,1024]{1,0:T(8,128)(2,1)S(1)} collective-permute-done((bf16[128,1024]{1,0:T(8,128)(2,1)}, bf16[128,1024]{1,0:T(8,128)(2,1)S(1)}, u32[]{:S(2)}, u32[]{:S(2)}) %collective-permute-start.2) | collective-permute-done | bytes 262176 | tf_op jit(solution)/shard_map/ppermute | solution.py:70
  27.3 3.2 %collective-permute-done.1 = bf16[2,512,256]{2,1,0:T(8,128)(2,1)S(1)} collective-permute-done((bf16[2,512,256]{2,1,0:T(8,128)(2,1)}, bf16[2,512,256]{2,1,0:T(8,128)(2,1)S(1)}, u32[]{:S(2)}, u32[]{:S(2)}) %collective-permute-start.1) | collective-permute-done | bytes 524320 | tf_op jit(solution)/shard_map/ppermute | solution.py:56
  30.6 1.5 fusion.108
  34.0 4.4 %collective-permute-start.11 = (bf16[512,1024]{1,0:T(8,128)(2,1)S(1)}, bf16[512,1024]{1,0:T(8,128)(2,1)S(1)}, u32[]{:S(2)}, u32[]{:S(2)}) collective-permute-start(bf16[512,1024]{1,0:T(8,128)(2,1)S(1)} %add_convert_fusion.1), channel_id=1, source_target_pairs={{0,4},{1,5},{2,6},{3,7},{4,0},{5,1},{6,2},{7,3},{8,12},{9,13},{10,... | collective-permute-start | bytes 3145736 | tf_op jit(solution)/shard_map/ppermute | solution.py:62
  38.7 1.4 collective-permute-start.7
  44.4 17.6 %collective-permute-done.11 = bf16[512,1024]{1,0:T(8,128)(2,1)S(1)} collective-permute-done((bf16[512,1024]{1,0:T(8,128)(2,1)S(1)}, bf16[512,1024]{1,0:T(8,128)(2,1)S(1)}, u32[]{:S(2)}, u32[]{:S(2)}) %collective-permute-start.11) | collective-permute-done | bytes 1048608 | tf_op jit(solution)/shard_map/ppermute | solution.py:62
  62.0 1.8 %collective-permute-done.10 = bf16[256,1024]{1,0:T(8,128)(2,1)S(1)} collective-permute-done((bf16[256,1024]{1,0:T(8,128)(2,1)S(1)}, bf16[256,1024]{1,0:T(8,128)(2,1)S(1)}, u32[]{:S(2)}, u32[]{:S(2)}) %collective-permute-start.10) | collective-permute-done | bytes 524320 | tf_op jit(solution)/shard_map/ppermute | solution.py:56
  68.7 1.6 %collective-permute-start.16 = (bf16[256,1024]{1,0:T(8,128)(2,1)S(1)}, bf16[256,1024]{1,0:T(8,128)(2,1)S(1)}, u32[]{:S(2)}, u32[]{:S(2)}) collective-permute-start(bf16[256,1024]{1,0:T(8,128)(2,1)S(1)} %get-tuple-element.29), channel_id=1, source_target_pairs={{0,16},{1,17},{2,18},{3,19},{4,20},{5,21},{6,22},{7,23},{8,24},{9,... | collective-permute-start | bytes 1572872 | tf_op jit(solution)/shard_map/ppermute | solution.py:70
  71.2 1.4 collective-permute-start.17
  73.8 9.3 %collective-permute-done.16 = bf16[256,1024]{1,0:T(8,128)(2,1)S(1)} collective-permute-done((bf16[256,1024]{1,0:T(8,128)(2,1)S(1)}, bf16[256,1024]{1,0:T(8,128)(2,1)S(1)}, u32[]{:S(2)}, u32[]{:S(2)}) %collective-permute-start.16) | collective-permute-done | bytes 524320 | tf_op jit(solution)/shard_map/ppermute | solution.py:70
  83.8 2.2 %collective-permute-done.17 = bf16[256,1024]{1,0:T(8,128)(2,1)S(1)} collective-permute-done((bf16[256,1024]{1,0:T(8,128)(2,1)S(1)}, bf16[256,1024]{1,0:T(8,128)(2,1)S(1)}, u32[]{:S(2)}, u32[]{:S(2)}) %collective-permute-start.17) | collective-permute-done | bytes 524320 | tf_op jit(solution)/shard_map/ppermute | solution.py:56
  86.0 7.4 %collective-permute-done.21 = bf16[512,1024]{1,0:T(8,128)(2,1)S(1)} collective-permute-done((bf16[512,1024]{1,0:T(8,128)(2,1)S(1)}, bf16[512,1024]{1,0:T(8,128)(2,1)S(1)}, u32[]{:S(2)}, u32[]{:S(2)}) %collective-permute-start.21) | collective-permute-done | bytes 1048608 | tf_op jit(solution)/shard_map/ppermute | solution.py:62
  93.4 3.1 %collective-permute-done.19 = bf16[256,1024]{1,0:T(8,128)(2,1)S(1)} collective-permute-done((bf16[256,1024]{1,0:T(8,128)(2,1)S(1)}, bf16[256,1024]{1,0:T(8,128)(2,1)S(1)}, u32[]{:S(2)}, u32[]{:S(2)}) %collective-permute-start.19) | collective-permute-done | bytes 524320 | tf_op jit(solution)/shard_map/ppermute | solution.py:56
  104.6 3.0 %collective-permute-start.25 = (f32[256,256]{1,0:T(8,128)S(1)}, f32[256,256]{1,0:T(8,128)S(1)}, u32[]{:S(2)}, u32[]{:S(2)}) collective-permute-start(f32[256,256]{1,0:T(8,128)S(1)} %convolution_add_fusion.4), channel_id=1, source_target_pairs={{0,4},{1,5},{2,6},{3,7},{4,0},{5,1},{6,2},{7,3},{8,12},{9,13},{10,... | collective-permute-start | bytes 786440 | tf_op jit(solution)/shard_map/ppermute | solution.py:62
  107.6 6.5 %collective-permute-done.27 = bf16[256,1024]{1,0:T(8,128)(2,1)S(1)} collective-permute-done((bf16[256,1024]{1,0:T(8,128)(2,1)S(1)}, bf16[256,1024]{1,0:T(8,128)(2,1)S(1)}, u32[]{:S(2)}, u32[]{:S(2)}) %collective-permute-start.27) | collective-permute-done | bytes 524320 | tf_op jit(solution)/shard_map/ppermute | solution.py:56
  116.8 3.2 %collective-permute-start.29 = (f32[256,768]{1,0:T(8,128)S(1)}, f32[256,768]{1,0:T(8,128)S(1)}, u32[]{:S(2)}, u32[]{:S(2)}) collective-permute-start(f32[256,768]{1,0:T(8,128)S(1)} %pad_maximum_fusion.2), channel_id=1, source_target_pairs={{0,4},{1,5},{2,6},{3,7},{4,0},{5,1},{6,2},{7,3},{8,12},{9,13},{10,... | collective-permute-start | bytes 2359304 | tf_op jit(solution)/shard_map/ppermute | solution.py:62
  121.0 16.6 %collective-permute-done.30 = f32[1024]{0:T(1024)S(1)} collective-permute-done((f32[1024]{0:T(1024)S(1)}, f32[1024]{0:T(1024)S(1)}, u32[]{:S(2)}, u32[]{:S(2)}) %collective-permute-start.30) | collective-permute-done | bytes 4128 | tf_op jit(solution)/shard_map/ppermute | solution.py:62
  139.8 2.7 %collective-permute-start.33 = (f32[256]{0:T(256)S(1)}, f32[256]{0:T(256)S(1)}, u32[]{:S(2)}, u32[]{:S(2)}) collective-permute-start(f32[256]{0:T(256)S(1)} %get-tuple-element.43), channel_id=1, source_target_pairs={{0,20},{1,21},{2,22},{3,23},{4,16},{5,17},{6,18},{7,19},{8,28},{9,... | collective-permute-start | bytes 3080 | tf_op jit(solution)/shard_map/ppermute | solution.py:70
  142.8 1.4 collective-permute-done.33
  144.2 1.8 %collective-permute-done.31 = f32[256]{0:T(256)S(1)} collective-permute-done((f32[256]{0:T(256)S(1)}, f32[256]{0:T(256)S(1)}, u32[]{:S(2)}, u32[]{:S(2)}) %collective-permute-start.31) | collective-permute-done | bytes 1056 | tf_op jit(solution)/shard_map/ppermute | solution.py:62
  146.0 1.4 collective-permute-start.35
  147.9 1.8 %collective-permute-done.35 = f32[256]{0:T(256)S(1)} collective-permute-done((f32[256]{0:T(256)S(1)}, f32[256]{0:T(256)S(1)}, u32[]{:S(2)}, u32[]{:S(2)}) %collective-permute-start.35) | collective-permute-done | bytes 1056 | tf_op jit(solution)/shard_map/ppermute | solution.py:56
  151.8 3.2 %collective-permute-done.37 = f32[1024]{0:T(1024)S(1)} collective-permute-done((f32[1024]{0:T(1024)S(1)}, f32[1024]{0:T(1024)S(1)}, u32[]{:S(2)}, u32[]{:S(2)}) %collective-permute-start.37) | collective-permute-done | bytes 4128 | tf_op jit(solution)/shard_map/ppermute | solution.py:62
  (127 shorter events, 35.3 us)
Async XLA Ops:
  2.0 28.6 %collective-permute-start.4 = (bf16[256,1024]{1,0:T(8,128)(2,1)}, bf16[256,1024]{1,0:T(8,128)(2,1)}, u32[]{:S(2)}, u32[]{:S(2)}) collective-permute-start(bf16[256,1024]{1,0:T(8,128)(2,1)} %constant_dynamic-slice_fusion.1), channel_id=1, source_target_pairs={{0,1},{1,0},{2,3},{3,2},{4,5},{5,4},{6,7},{7,6},{8,9},{9,8},{10,11... | collective-permute-start | bytes 1572872 | tf_op jit(solution)/shard_map/ppermute | solution.py:56
  4.1 9.8 %collective-permute-start = (bf16[128,1024]{1,0:T(8,128)(2,1)}, bf16[128,1024]{1,0:T(8,128)(2,1)}, u32[]{:S(2)}, u32[]{:S(2)}) collective-permute-start(bf16[128,1024]{1,0:T(8,128)(2,1)} %constant_dynamic-slice_fusion), channel_id=1, source_target_pairs={{0,2},{1,3},{2,0},{3,1},{4,6},{5,7},{6,4},{7,5},{8,10},{9,11},{10,... | collective-permute-start | bytes 786440 | tf_op jit(solution)/shard_map/ppermute | solution.py:56
  12.0 18.6 %collective-permute-start.3 = (bf16[512,256]{1,0:T(8,128)(2,1)}, bf16[512,256]{1,0:T(8,128)(2,1)S(1)}, u32[]{:S(2)}, u32[]{:S(2)}) collective-permute-start(bf16[512,256]{1,0:T(8,128)(2,1)} %get-tuple-element.31), channel_id=1, source_target_pairs={{0,1},{1,0},{2,3},{3,2},{4,5},{5,4},{6,7},{7,6},{8,9},{9,8},{10,11... | collective-permute-start | bytes 786440 | tf_op jit(solution)/shard_map/ppermute | solution.py:56
  16.5 14.0 %collective-permute-start.1 = (bf16[2,512,256]{2,1,0:T(8,128)(2,1)}, bf16[2,512,256]{2,1,0:T(8,128)(2,1)S(1)}, u32[]{:S(2)}, u32[]{:S(2)}) collective-permute-start(bf16[2,512,256]{2,1,0:T(8,128)(2,1)} %fusion.19), channel_id=1, source_target_pairs={{0,2},{1,3},{2,0},{3,1},{4,6},{5,7},{6,4},{7,5},{8,10},{9,11},{10,... | collective-permute-start | bytes 1572872 | tf_op jit(solution)/shard_map/ppermute | solution.py:56
  18.3 7.9 %collective-permute-start.2 = (bf16[128,1024]{1,0:T(8,128)(2,1)}, bf16[128,1024]{1,0:T(8,128)(2,1)S(1)}, u32[]{:S(2)}, u32[]{:S(2)}) collective-permute-start(bf16[128,1024]{1,0:T(8,128)(2,1)} %collective-permute-done), channel_id=1, source_target_pairs={{0,16},{1,17},{2,18},{3,19},{4,20},{5,21},{6,22},{7,23},{8,24},{9,... | collective-permute-start | bytes 786440 | tf_op jit(solution)/shard_map/ppermute | solution.py:70
  27.2 5.4 %collective-permute-start.6 = (bf16[256,1024]{1,0:T(8,128)(2,1)S(1)}, bf16[256,1024]{1,0:T(8,128)(2,1)S(1)}, u32[]{:S(2)}, u32[]{:S(2)}) collective-permute-start(bf16[256,1024]{1,0:T(8,128)(2,1)S(1)} %pad_maximum_fusion.3), channel_id=1, source_target_pairs={{0,1},{1,0},{2,3},{3,2},{4,5},{5,4},{6,7},{7,6},{8,9},{9,8},{10,11... | collective-permute-start | bytes 1572872 | tf_op jit(solution)/shard_map/ppermute | solution.py:56
  33.2 11.2 %collective-permute-start.12 = (bf16[512,1024]{1,0:T(8,128)(2,1)S(1)}, bf16[512,1024]{1,0:T(8,128)(2,1)S(1)}, u32[]{:S(2)}, u32[]{:S(2)}) collective-permute-start(bf16[512,1024]{1,0:T(8,128)(2,1)S(1)} %add_convert_fusion.1), channel_id=1, source_target_pairs={{0,0},{1,1},{2,2},{3,3},{4,8},{5,9},{6,10},{7,11},{8,4},{9,5},{10,... | collective-permute-start | bytes 3145736 | tf_op jit(solution)/shard_map/ppermute | solution.py:62
  34.0 28.0 %collective-permute-start.11 = (bf16[512,1024]{1,0:T(8,128)(2,1)S(1)}, bf16[512,1024]{1,0:T(8,128)(2,1)S(1)}, u32[]{:S(2)}, u32[]{:S(2)}) collective-permute-start(bf16[512,1024]{1,0:T(8,128)(2,1)S(1)} %add_convert_fusion.1), channel_id=1, source_target_pairs={{0,4},{1,5},{2,6},{3,7},{4,0},{5,1},{6,2},{7,3},{8,12},{9,13},{10,... | collective-permute-start | bytes 3145736 | tf_op jit(solution)/shard_map/ppermute | solution.py:62
  38.7 23.3 %collective-permute-start.7 = (bf16[256,1024]{1,0:T(8,128)(2,1)S(1)}, bf16[256,1024]{1,0:T(8,128)(2,1)S(1)}, u32[]{:S(2)}, u32[]{:S(2)}) collective-permute-start(bf16[256,1024]{1,0:T(8,128)(2,1)S(1)} %get-tuple-element.21), channel_id=1, source_target_pairs={{0,2},{1,3},{2,0},{3,1},{4,6},{5,7},{6,4},{7,5},{8,10},{9,11},{10,... | collective-permute-start | bytes 1572872 | tf_op jit(solution)/shard_map/ppermute | solution.py:56
  40.2 3.8 %collective-permute-start.9 = (bf16[256,1024]{1,0:T(8,128)(2,1)S(1)}, bf16[256,1024]{1,0:T(8,128)(2,1)S(1)}, u32[]{:S(2)}, u32[]{:S(2)}) collective-permute-start(bf16[256,1024]{1,0:T(8,128)(2,1)S(1)} %get-tuple-element.21), channel_id=1, source_target_pairs={{0,1},{1,0},{2,3},{3,2},{4,5},{5,4},{6,7},{7,6},{8,9},{9,8},{10,11... | collective-permute-start | bytes 1572872 | tf_op jit(solution)/shard_map/ppermute | solution.py:56
  40.2 2.7 %collective-permute-start.8 = (bf16[256,1024]{1,0:T(8,128)(2,1)S(1)}, bf16[256,1024]{1,0:T(8,128)(2,1)S(1)}, u32[]{:S(2)}, u32[]{:S(2)}) collective-permute-start(bf16[256,1024]{1,0:T(8,128)(2,1)S(1)} %get-tuple-element.22), channel_id=1, source_target_pairs={{0,1},{1,0},{2,3},{3,2},{4,5},{5,4},{6,7},{7,6},{8,9},{9,8},{10,11... | collective-permute-start | bytes 1572872 | tf_op jit(solution)/shard_map/ppermute | solution.py:56
  42.8 21.0 %collective-permute-start.10 = (bf16[256,1024]{1,0:T(8,128)(2,1)S(1)}, bf16[256,1024]{1,0:T(8,128)(2,1)S(1)}, u32[]{:S(2)}, u32[]{:S(2)}) collective-permute-start(bf16[256,1024]{1,0:T(8,128)(2,1)S(1)} %get-tuple-element.22), channel_id=1, source_target_pairs={{0,2},{1,3},{2,0},{3,1},{4,6},{5,7},{6,4},{7,5},{8,10},{9,11},{10,... | collective-permute-start | bytes 1572872 | tf_op jit(solution)/shard_map/ppermute | solution.py:56
  68.1 25.3 %collective-permute-start.21 = (bf16[512,1024]{1,0:T(8,128)(2,1)S(1)}, bf16[512,1024]{1,0:T(8,128)(2,1)S(1)}, u32[]{:S(2)}, u32[]{:S(2)}) collective-permute-start(bf16[512,1024]{1,0:T(8,128)(2,1)S(1)} %get-tuple-element.19), channel_id=1, source_target_pairs={{0,4},{1,5},{2,6},{3,7},{4,0},{5,1},{6,2},{7,3},{8,12},{9,13},{10,... | collective-permute-start | bytes 3145736 | tf_op jit(solution)/shard_map/ppermute | solution.py:62
  68.5 4.5 %collective-permute-start.18 = (bf16[256,1024]{1,0:T(8,128)(2,1)S(1)}, bf16[256,1024]{1,0:T(8,128)(2,1)S(1)}, u32[]{:S(2)}, u32[]{:S(2)}) collective-permute-start(bf16[256,1024]{1,0:T(8,128)(2,1)S(1)} %slice_add_fusion), channel_id=1, source_target_pairs={{0,1},{1,0},{2,3},{3,2},{4,5},{5,4},{6,7},{7,6},{8,9},{9,8},{10,11... | collective-permute-start | bytes 1572872 | tf_op jit(solution)/shard_map/ppermute | solution.py:56
  68.7 14.4 %collective-permute-start.16 = (bf16[256,1024]{1,0:T(8,128)(2,1)S(1)}, bf16[256,1024]{1,0:T(8,128)(2,1)S(1)}, u32[]{:S(2)}, u32[]{:S(2)}) collective-permute-start(bf16[256,1024]{1,0:T(8,128)(2,1)S(1)} %get-tuple-element.29), channel_id=1, source_target_pairs={{0,16},{1,17},{2,18},{3,19},{4,20},{5,21},{6,22},{7,23},{8,24},{9,... | collective-permute-start | bytes 1572872 | tf_op jit(solution)/shard_map/ppermute | solution.py:70
  70.3 23.1 %collective-permute-start.20 = (bf16[512,1024]{1,0:T(8,128)(2,1)S(1)}, bf16[512,1024]{1,0:T(8,128)(2,1)S(1)}, u32[]{:S(2)}, u32[]{:S(2)}) collective-permute-start(bf16[512,1024]{1,0:T(8,128)(2,1)S(1)} %get-tuple-element.20), channel_id=1, source_target_pairs={{0,0},{1,1},{2,2},{3,3},{4,8},{5,9},{6,10},{7,11},{8,4},{9,5},{10,... | collective-permute-start | bytes 3145736 | tf_op jit(solution)/shard_map/ppermute | solution.py:62
  71.2 14.8 %collective-permute-start.17 = (bf16[256,1024]{1,0:T(8,128)(2,1)S(1)}, bf16[256,1024]{1,0:T(8,128)(2,1)S(1)}, u32[]{:S(2)}, u32[]{:S(2)}) collective-permute-start(bf16[256,1024]{1,0:T(8,128)(2,1)S(1)} %slice_add_fusion), channel_id=1, source_target_pairs={{0,2},{1,3},{2,0},{3,1},{4,6},{5,7},{6,4},{7,5},{8,10},{9,11},{10,... | collective-permute-start | bytes 1572872 | tf_op jit(solution)/shard_map/ppermute | solution.py:56
  73.1 23.5 %collective-permute-start.19 = (bf16[256,1024]{1,0:T(8,128)(2,1)S(1)}, bf16[256,1024]{1,0:T(8,128)(2,1)S(1)}, u32[]{:S(2)}, u32[]{:S(2)}) collective-permute-start(bf16[256,1024]{1,0:T(8,128)(2,1)S(1)} %get-tuple-element.28), channel_id=1, source_target_pairs={{0,2},{1,3},{2,0},{3,1},{4,6},{5,7},{6,4},{7,5},{8,10},{9,11},{10,... | collective-permute-start | bytes 1572872 | tf_op jit(solution)/shard_map/ppermute | solution.py:56
  83.1 13.4 %collective-permute-start.15 = (bf16[256,1024]{1,0:T(8,128)(2,1)S(1)}, bf16[256,1024]{1,0:T(8,128)(2,1)S(1)}, u32[]{:S(2)}, u32[]{:S(2)}) collective-permute-start(bf16[256,1024]{1,0:T(8,128)(2,1)S(1)} %get-tuple-element.28), channel_id=1, source_target_pairs={{0,1},{1,0},{2,3},{3,2},{4,5},{5,4},{6,7},{7,6},{8,9},{9,8},{10,11... | collective-permute-start | bytes 1572872 | tf_op jit(solution)/shard_map/ppermute | solution.py:56
  97.2 4.7 %collective-permute-start.26 = (bf16[256,1024]{1,0:T(8,128)(2,1)S(1)}, bf16[256,1024]{1,0:T(8,128)(2,1)S(1)}, u32[]{:S(2)}, u32[]{:S(2)}) collective-permute-start(bf16[256,1024]{1,0:T(8,128)(2,1)S(1)} %get-tuple-element.44), channel_id=1, source_target_pairs={{0,1},{1,0},{2,3},{3,2},{4,5},{5,4},{6,7},{7,6},{8,9},{9,8},{10,11... | collective-permute-start | bytes 1572872 | tf_op jit(solution)/shard_map/ppermute | solution.py:56
  99.7 3.7 %collective-permute-start.23 = (bf16[256,1024]{1,0:T(8,128)(2,1)S(1)}, bf16[256,1024]{1,0:T(8,128)(2,1)S(1)}, u32[]{:S(2)}, u32[]{:S(2)}) collective-permute-start(bf16[256,1024]{1,0:T(8,128)(2,1)S(1)} %get-tuple-element.27), channel_id=1, source_target_pairs={{0,1},{1,0},{2,3},{3,2},{4,5},{5,4},{6,7},{7,6},{8,9},{9,8},{10,11... | collective-permute-start | bytes 1572872 | tf_op jit(solution)/shard_map/ppermute | solution.py:56
  99.9 14.2 %collective-permute-start.27 = (bf16[256,1024]{1,0:T(8,128)(2,1)S(1)}, bf16[256,1024]{1,0:T(8,128)(2,1)S(1)}, u32[]{:S(2)}, u32[]{:S(2)}) collective-permute-start(bf16[256,1024]{1,0:T(8,128)(2,1)S(1)} %get-tuple-element.27), channel_id=1, source_target_pairs={{0,2},{1,3},{2,0},{3,1},{4,6},{5,7},{6,4},{7,5},{8,10},{9,11},{10,... | collective-permute-start | bytes 1572872 | tf_op jit(solution)/shard_map/ppermute | solution.py:56
  101.3 13.9 %collective-permute-start.24 = (bf16[256,1024]{1,0:T(8,128)(2,1)S(1)}, bf16[256,1024]{1,0:T(8,128)(2,1)S(1)}, u32[]{:S(2)}, u32[]{:S(2)}) collective-permute-start(bf16[256,1024]{1,0:T(8,128)(2,1)S(1)} %get-tuple-element.26), channel_id=1, source_target_pairs={{0,16},{1,17},{2,18},{3,19},{4,20},{5,21},{6,22},{7,23},{8,24},{9,... | collective-permute-start | bytes 1572872 | tf_op jit(solution)/shard_map/ppermute | solution.py:70
  104.6 11.2 %collective-permute-start.25 = (f32[256,256]{1,0:T(8,128)S(1)}, f32[256,256]{1,0:T(8,128)S(1)}, u32[]{:S(2)}, u32[]{:S(2)}) collective-permute-start(f32[256,256]{1,0:T(8,128)S(1)} %convolution_add_fusion.4), channel_id=1, source_target_pairs={{0,4},{1,5},{2,6},{3,7},{4,0},{5,1},{6,2},{7,3},{8,12},{9,13},{10,... | collective-permute-start | bytes 786440 | tf_op jit(solution)/shard_map/ppermute | solution.py:62
  116.8 20.9 %collective-permute-start.29 = (f32[256,768]{1,0:T(8,128)S(1)}, f32[256,768]{1,0:T(8,128)S(1)}, u32[]{:S(2)}, u32[]{:S(2)}) collective-permute-start(f32[256,768]{1,0:T(8,128)S(1)} %pad_maximum_fusion.2), channel_id=1, source_target_pairs={{0,4},{1,5},{2,6},{3,7},{4,0},{5,1},{6,2},{7,3},{8,12},{9,13},{10,... | collective-permute-start | bytes 2359304 | tf_op jit(solution)/shard_map/ppermute | solution.py:62
  120.4 17.2 %collective-permute-start.30 = (f32[1024]{0:T(1024)S(1)}, f32[1024]{0:T(1024)S(1)}, u32[]{:S(2)}, u32[]{:S(2)}) collective-permute-start(f32[1024]{0:T(1024)S(1)} %pad_maximum_fusion.4), channel_id=1, source_target_pairs={{0,4},{1,5},{2,6},{3,7},{4,0},{5,1},{6,2},{7,3},{8,12},{9,13},{10,... | collective-permute-start | bytes 12296 | tf_op jit(solution)/shard_map/ppermute | solution.py:62
  139.2 3.6 %collective-permute-start.32 = (f32[256]{0:T(256)S(1)}, f32[256]{0:T(256)S(1)}, u32[]{:S(2)}, u32[]{:S(2)}) collective-permute-start(f32[256]{0:T(256)S(1)} %get-tuple-element.43), channel_id=1, source_target_pairs={{0,16},{1,17},{2,18},{3,19},{4,20},{5,21},{6,22},{7,23},{8,24},{9,... | collective-permute-start | bytes 3080 | tf_op jit(solution)/shard_map/ppermute | solution.py:70
  139.8 4.5 %collective-permute-start.33 = (f32[256]{0:T(256)S(1)}, f32[256]{0:T(256)S(1)}, u32[]{:S(2)}, u32[]{:S(2)}) collective-permute-start(f32[256]{0:T(256)S(1)} %get-tuple-element.43), channel_id=1, source_target_pairs={{0,20},{1,21},{2,22},{3,23},{4,16},{5,17},{6,18},{7,19},{8,28},{9,... | collective-permute-start | bytes 3080 | tf_op jit(solution)/shard_map/ppermute | solution.py:70
  142.4 3.6 %collective-permute-start.31 = (f32[256]{0:T(256)S(1)}, f32[256]{0:T(256)S(1)}, u32[]{:S(2)}, u32[]{:S(2)}) collective-permute-start(f32[256]{0:T(256)S(1)} %get-tuple-element.42), channel_id=1, source_target_pairs={{0,4},{1,5},{2,6},{3,7},{4,0},{5,1},{6,2},{7,3},{8,12},{9,13},{10,... | collective-permute-start | bytes 3080 | tf_op jit(solution)/shard_map/ppermute | solution.py:62
  146.0 3.6 %collective-permute-start.35 = (f32[256]{0:T(256)S(1)}, f32[256]{0:T(256)S(1)}, u32[]{:S(2)}, u32[]{:S(2)}) collective-permute-start(f32[256]{0:T(256)S(1)} %add_add_fusion.3), channel_id=1, source_target_pairs={{0,2},{1,3},{2,0},{3,1},{4,6},{5,7},{6,4},{7,5},{8,10},{9,11},{10,... | collective-permute-start | bytes 3080 | tf_op jit(solution)/shard_map/ppermute | solution.py:56
  147.5 3.0 %collective-permute-start.36 = (f32[256]{0:T(256)S(1)}, f32[256]{0:T(256)S(1)}, u32[]{:S(2)}, u32[]{:S(2)}) collective-permute-start(f32[256]{0:T(256)S(1)} %add_add_fusion.3), channel_id=1, source_target_pairs={{0,3},{1,2},{2,1},{3,0},{4,7},{5,6},{6,5},{7,4},{8,11},{9,10},{10,... | collective-permute-start | bytes 3080 | tf_op jit(solution)/shard_map/ppermute | solution.py:56
  150.5 4.6 %collective-permute-start.37 = (f32[1024]{0:T(1024)S(1)}, f32[1024]{0:T(1024)S(1)}, u32[]{:S(2)}, u32[]{:S(2)}) collective-permute-start(f32[1024]{0:T(1024)S(1)} %pad_maximum_fusion.5), channel_id=1, source_target_pairs={{0,8},{1,9},{2,10},{3,11},{4,12},{5,13},{6,14},{7,15},{8,0},{9,1},... | collective-permute-start | bytes 12296 | tf_op jit(solution)/shard_map/ppermute | solution.py:62
  (10 other events, 47.1 us)

commit v6 on v3

--- a/solution.py
+++ b/solution.py
@@ -23,9 +23,9 @@
     return sum(jnp.minimum(jnp.abs(r.astype(F32)), 0.0) for r in rows)
 
 
-def fence(swap, middle, others):
-    done = lax.optimization_barrier(token(swap))
-    done = lax.optimization_barrier(token(middle) + done)
+def fence(first, second, others):
+    done = lax.optimization_barrier(token(first))
+    done = lax.optimization_barrier(token(second) + done)
     return token(*others) + done
 
 
@@ -123,22 +123,12 @@
 
         order = [(s, 0) for s in range(nx)] + [(s, 1) for s in range(nx)]
 
-        pool = lax.axis_index("pool")
-        part_rows = width // n_pool
-        own1 = lax.optimization_barrier(factor_own([0, 1, 2, 1]))
-        mine1 = lax.dynamic_slice_in_dim(own1, pool * part_rows, part_rows, 0)
-        parts1 = [inner(mine1, s, 0) for s in range(1, nx)]
-
-        done = token(*parts1)
+        own1 = factor_own([0, 1, 2, 1])
+        same1 = [own1] + factor_x(own1)
+
+        done = token(*same1[1:])
         features = [inner(behind(rows_of(s, f), done), s, f) if s or f else rows_of(0, 0) for s, f in order]
-        flip1 = inner(own1, 0, 1)
-        near1, far1 = [], []
-        for v in parts1:
-            near1.append([v] + [over_pool(v, r) for r in range(1, n_pool)])
-            far1.append([inner(v, 0, 1)] + [over_pool(v, r, 1) for r in range(1, n_pool)])
-        done = token(*features[1:nx])
-        near1, far1 = [[in_order([behind(v, done[:, :1]) for v in u], pool) for u in w] for w in (near1, far1)]
-        first = partial([own1] + near1 + [flip1] + far1).astype(BF)
+        first = partial(same1 + factor_flip(same1)).astype(BF)
 
         start = token(first)
         step1 = along_z(first, outer)
@@ -147,7 +137,7 @@
         own3 = behind(factor_own([1, 1, 1, 2]), start)
         flip2, flip3 = inner(own2, 0, 1), inner(own3, 0, 1)
         moved2, moved3 = factor_x(own2), factor_x(own3)
-        done = fence(step1, step2, [flip2, flip3, *moved2, *moved3])
+        done = fence(step2, step1, [flip2, flip3, *moved2, *moved3])
         moved2, moved3 = [behind(v, done) for v in moved2], [behind(v, done) for v in moved3]
         second = partial([own2] + moved2 + [flip2] + factor_flip(moved2))
         third = partial([own3] + moved3 + [flip3] + factor_flip(moved3))

time: 153 us -> 154 us (level)
  waiting for transfers between devices: 86.4 us -> 89.4 us
  matrix products: 13.4 us -> 15.5 us
  other arithmetic: 7.86 us -> 5.84 us
  starting transfers between devices: 37.2 us -> 35.5 us
    ppermute x9, waiting for transfers between devices: 42.6 us -> 47.6 us  [along_z(): return lax.ppermute(value, 'tgt', pairs)]
    ppermute x6 -> x4, waiting for transfers between devices: 16.6 us -> 12.5 us  [over_pool(): return lax.ppermute(value, ('pool', 'tgt'), pairs)]
    ppermute x24, waiting for transfers between devices: 27.2 us -> 29.3 us  [inner(): return lax.ppermute(value, 'tgt', pairs)]
    dot_general x16, matrix products: 8.76 us -> 10.8 us  [matmul(): lax.dot_general(a, b, (((1,), (0,)), ((), ())), preferred_element_type=F32)]
    ppermute x9, starting transfers between devices: 15.1 us -> 13.2 us  [along_z(): return lax.ppermute(value, 'tgt', pairs)]
    ppermute x6 -> x4, starting transfers between devices: 5.09 us -> 6.38 us  [over_pool(): return lax.ppermute(value, ('pool', 'tgt'), pairs)]
  transfers between devices with their start and end apart: 39 -> 37, of which waited for: 21 -> 21; matrix products, arithmetic and copies ran while one was open for 14% -> 14% of each run, Pallas kernels for 0% -> 0%
where the time goes in v6:
time: 154 us
  waiting for transfers between devices  89.4 us (58%)
  starting transfers between devices  35.5 us (23%)
  matrix products  15.5 us (10%)
  local copies, waits for them, and re-layouts  6.85 us (4%)
  other arithmetic  5.84 us (4%)
    ppermute x9, waiting for transfers between devices, along_z(): return lax.ppermute(value, 'tgt', pairs)  47.6 us
    ppermute x24, waiting for transfers between devices, inner(): return lax.ppermute(value, 'tgt', pairs)  29.3 us
    ppermute x24, starting transfers between devices, inner(): return lax.ppermute(value, 'tgt', pairs)  15.9 us
    ppermute x9, starting transfers between devices, along_z(): return lax.ppermute(value, 'tgt', pairs)  13.2 us
    ppermute x4, waiting for transfers between devices, over_pool(): return lax.ppermute(value, ('pool', 'tgt'), pairs)  12.5 us
    dot_general x16, matrix products, matmul(): lax.dot_general(a, b, (((1,), (0,)), ((), ())), preferred_element_type=F32)  10.8 us
    ppermute x4, starting transfers between devices, over_pool(): return lax.ppermute(value, ('pool', 'tgt'), pairs)  6.38 us
    dot_general x10, matrix products, matmul_t(): lax.dot_general(a, b, (((1,), (1,)), ((), ())), preferred_element_type=F32)  4.68 us
  transfers between devices with their start and end apart: 37, of which 21 were waited for; matrix products, arithmetic and copies ran while one was open for 14% of the time, Pallas kernels for 0%

profile of v6, /device:TPU:0, one launch (start us, length us, event | category | flops | bytes accessed | tf_op | source)
XLA Modules:
  0.0 153.6 jit_solution(10535294050509599475)
XLA Ops:
  0.0 2.0 %constant_dynamic-slice_fusion = bf16[256,1024]{1,0:T(8,128)(2,1)} fusion(bf16[256,4096]{1,0:T(8,128)(2,1)} %param.7, s32[]{:T(128)S(6)} %select_n.171), kind=kLoop, calls=%fused_computation.148 | loop fusion | bytes 1048580 | tf_op jit(solution)/shard_map/dynamic_slice | solution.py:109
  2.0 2.9 %collective-permute-start = (bf16[256,1024]{1,0:T(8,128)(2,1)}, bf16[256,1024]{1,0:T(8,128)(2,1)}, u32[]{:S(2)}, u32[]{:S(2)}) collective-permute-start(bf16[256,1024]{1,0:T(8,128)(2,1)} %constant_dynamic-slice_fusion), channel_id=1, source_target_pairs={{0,2},{1,3},{2,0},{3,1},{4,6},{5,7},{6,4},{7,5},{8,10},{9,11},{10,... | collective-permute-start | bytes 1572872 | tf_op jit(solution)/shard_map/ppermute | solution.py:56
  5.7 3.9 %gather_fusion = bf16[1024,256]{1,0:T(8,128)(2,1)S(1)} fusion(bf16[4096,256]{1,0:T(8,128)(2,1)S(1)} %copy-done, s32[1024]{0:T(1024)S(1)} %fusion.31), kind=kCustom, calls=%fused_computation | custom fusion | bytes 1052672 | tf_op jit(solution)/shard_map/gather | solution.py:96
  9.7 7.5 %collective-permute-done = bf16[256,1024]{1,0:T(8,128)(2,1)} collective-permute-done((bf16[256,1024]{1,0:T(8,128)(2,1)}, bf16[256,1024]{1,0:T(8,128)(2,1)}, u32[]{:S(2)}, u32[]{:S(2)}) %collective-permute-start) | collective-permute-done | bytes 524320 | tf_op jit(solution)/shard_map/ppermute | solution.py:56
  18.1 1.8 %collective-permute-start.1 = (bf16[512,256]{1,0:T(8,128)(2,1)S(1)}, bf16[512,256]{1,0:T(8,128)(2,1)S(1)}, u32[]{:S(2)}, u32[]{:S(2)}) collective-permute-start(bf16[512,256]{1,0:T(8,128)(2,1)S(1)} %get-tuple-element.28), channel_id=1, source_target_pairs={{0,2},{1,3},{2,0},{3,1},{4,6},{5,7},{6,4},{7,5},{8,10},{9,11},{10,... | collective-permute-start | bytes 786440 | tf_op jit(solution)/shard_map/ppermute | solution.py:56
  19.9 1.5 fusion.95
  22.0 4.8 %collective-permute-done.1 = bf16[512,256]{1,0:T(8,128)(2,1)S(1)} collective-permute-done((bf16[512,256]{1,0:T(8,128)(2,1)S(1)}, bf16[512,256]{1,0:T(8,128)(2,1)S(1)}, u32[]{:S(2)}, u32[]{:S(2)}) %collective-permute-start.1) | collective-permute-done | bytes 262176 | tf_op jit(solution)/shard_map/ppermute | solution.py:56
  26.7 1.5 fusion.96
  28.2 1.5 fusion.97
  31.5 4.4 %collective-permute-start.10 = (bf16[512,1024]{1,0:T(8,128)(2,1)S(1)}, bf16[512,1024]{1,0:T(8,128)(2,1)S(1)}, u32[]{:S(2)}, u32[]{:S(2)}) collective-permute-start(bf16[512,1024]{1,0:T(8,128)(2,1)S(1)} %add_convert_fusion.1), channel_id=1, source_target_pairs={{0,4},{1,5},{2,6},{3,7},{4,0},{5,1},{6,2},{7,3},{8,12},{9,13},{10,... | collective-permute-start | bytes 3145736 | tf_op jit(solution)/shard_map/ppermute | solution.py:62
  36.1 2.0 %collective-permute-start.6 = (bf16[256,1024]{1,0:T(8,128)(2,1)S(1)}, bf16[256,1024]{1,0:T(8,128)(2,1)S(1)}, u32[]{:S(2)}, u32[]{:S(2)}) collective-permute-start(bf16[256,1024]{1,0:T(8,128)(2,1)S(1)} %get-tuple-element.21), channel_id=1, source_target_pairs={{0,2},{1,3},{2,0},{3,1},{4,6},{5,7},{6,4},{7,5},{8,10},{9,11},{10,... | collective-permute-start | bytes 1572872 | tf_op jit(solution)/shard_map/ppermute | solution.py:56
  41.8 17.9 %collective-permute-done.10 = bf16[512,1024]{1,0:T(8,128)(2,1)S(1)} collective-permute-done((bf16[512,1024]{1,0:T(8,128)(2,1)S(1)}, bf16[512,1024]{1,0:T(8,128)(2,1)S(1)}, u32[]{:S(2)}, u32[]{:S(2)}) %collective-permute-start.10) | collective-permute-done | bytes 1048608 | tf_op jit(solution)/shard_map/ppermute | solution.py:62
  59.8 1.8 %collective-permute-done.9 = bf16[256,1024]{1,0:T(8,128)(2,1)S(1)} collective-permute-done((bf16[256,1024]{1,0:T(8,128)(2,1)S(1)}, bf16[256,1024]{1,0:T(8,128)(2,1)S(1)}, u32[]{:S(2)}, u32[]{:S(2)}) %collective-permute-start.9) | collective-permute-done | bytes 524320 | tf_op jit(solution)/shard_map/ppermute | solution.py:56
  66.4 1.6 %collective-permute-start.15 = (bf16[256,1024]{1,0:T(8,128)(2,1)S(1)}, bf16[256,1024]{1,0:T(8,128)(2,1)S(1)}, u32[]{:S(2)}, u32[]{:S(2)}) collective-permute-start(bf16[256,1024]{1,0:T(8,128)(2,1)S(1)} %get-tuple-element.32), channel_id=1, source_target_pairs={{0,16},{1,17},{2,18},{3,19},{4,20},{5,21},{6,22},{7,23},{8,24},{9,... | collective-permute-start | bytes 1572872 | tf_op jit(solution)/shard_map/ppermute | solution.py:70
  68.9 1.6 %collective-permute-start.18 = (bf16[256,1024]{1,0:T(8,128)(2,1)S(1)}, bf16[256,1024]{1,0:T(8,128)(2,1)S(1)}, u32[]{:S(2)}, u32[]{:S(2)}) collective-permute-start(bf16[256,1024]{1,0:T(8,128)(2,1)S(1)} %get-tuple-element.31), channel_id=1, source_target_pairs={{0,2},{1,3},{2,0},{3,1},{4,6},{5,7},{6,4},{7,5},{8,10},{9,11},{10,... | collective-permute-start | bytes 1572872 | tf_op jit(solution)/shard_map/ppermute | solution.py:56
  71.0 9.8 %collective-permute-done.15 = bf16[256,1024]{1,0:T(8,128)(2,1)S(1)} collective-permute-done((bf16[256,1024]{1,0:T(8,128)(2,1)S(1)}, bf16[256,1024]{1,0:T(8,128)(2,1)S(1)}, u32[]{:S(2)}, u32[]{:S(2)}) %collective-permute-start.15) | collective-permute-done | bytes 524320 | tf_op jit(solution)/shard_map/ppermute | solution.py:70
  80.8 1.5 collective-permute-start.16
  83.0 8.1 %collective-permute-done.20 = bf16[512,1024]{1,0:T(8,128)(2,1)S(1)} collective-permute-done((bf16[512,1024]{1,0:T(8,128)(2,1)S(1)}, bf16[512,1024]{1,0:T(8,128)(2,1)S(1)}, u32[]{:S(2)}, u32[]{:S(2)}) %collective-permute-start.20) | collective-permute-done | bytes 1048608 | tf_op jit(solution)/shard_map/ppermute | solution.py:62
  91.2 3.2 %collective-permute-done.16 = bf16[256,1024]{1,0:T(8,128)(2,1)S(1)} collective-permute-done((bf16[256,1024]{1,0:T(8,128)(2,1)S(1)}, bf16[256,1024]{1,0:T(8,128)(2,1)S(1)}, u32[]{:S(2)}, u32[]{:S(2)}) %collective-permute-start.16) | collective-permute-done | bytes 524320 | tf_op jit(solution)/shard_map/ppermute | solution.py:56
  97.8 1.5 collective-permute-start.26
  99.3 1.5 collective-permute-start.23
  103.5 2.1 %collective-permute-start.24 = (f32[256,256]{1,0:T(8,128)S(1)}, f32[256,256]{1,0:T(8,128)S(1)}, u32[]{:S(2)}, u32[]{:S(2)}) collective-permute-start(f32[256,256]{1,0:T(8,128)S(1)} %convolution_add_fusion.4), channel_id=1, source_target_pairs={{0,4},{1,5},{2,6},{3,7},{4,0},{5,1},{6,2},{7,3},{8,12},{9,13},{10,... | collective-permute-start | bytes 786440 | tf_op jit(solution)/shard_map/ppermute | solution.py:62
  105.6 6.5 %collective-permute-done.26 = bf16[256,1024]{1,0:T(8,128)(2,1)S(1)} collective-permute-done((bf16[256,1024]{1,0:T(8,128)(2,1)S(1)}, bf16[256,1024]{1,0:T(8,128)(2,1)S(1)}, u32[]{:S(2)}, u32[]{:S(2)}) %collective-permute-start.26) | collective-permute-done | bytes 524320 | tf_op jit(solution)/shard_map/ppermute | solution.py:56
  114.8 3.1 %collective-permute-start.28 = (f32[256,768]{1,0:T(8,128)S(1)}, f32[256,768]{1,0:T(8,128)S(1)}, u32[]{:S(2)}, u32[]{:S(2)}) collective-permute-start(f32[256,768]{1,0:T(8,128)S(1)} %pad_maximum_fusion.2), channel_id=1, source_target_pairs={{0,4},{1,5},{2,6},{3,7},{4,0},{5,1},{6,2},{7,3},{8,12},{9,13},{10,... | collective-permute-start | bytes 2359304 | tf_op jit(solution)/shard_map/ppermute | solution.py:62
  118.9 16.5 %collective-permute-done.29 = f32[1024]{0:T(1024)S(1)} collective-permute-done((f32[1024]{0:T(1024)S(1)}, f32[1024]{0:T(1024)S(1)}, u32[]{:S(2)}, u32[]{:S(2)}) %collective-permute-start.29) | collective-permute-done | bytes 4128 | tf_op jit(solution)/shard_map/ppermute | solution.py:62
  137.6 2.7 %collective-permute-start.32 = (f32[256]{0:T(256)S(1)}, f32[256]{0:T(256)S(1)}, u32[]{:S(2)}, u32[]{:S(2)}) collective-permute-start(f32[256]{0:T(256)S(1)} %get-tuple-element.42), channel_id=1, source_target_pairs={{0,20},{1,21},{2,22},{3,23},{4,16},{5,17},{6,18},{7,19},{8,28},{9,... | collective-permute-start | bytes 3080 | tf_op jit(solution)/shard_map/ppermute | solution.py:70
  140.6 1.4 collective-permute-done.32
  142.0 1.8 %collective-permute-done.30 = f32[256]{0:T(256)S(1)} collective-permute-done((f32[256]{0:T(256)S(1)}, f32[256]{0:T(256)S(1)}, u32[]{:S(2)}, u32[]{:S(2)}) %collective-permute-start.30) | collective-permute-done | bytes 1056 | tf_op jit(solution)/shard_map/ppermute | solution.py:62
  143.8 1.6 %collective-permute-start.34 = (f32[256]{0:T(256)S(1)}, f32[256]{0:T(256)S(1)}, u32[]{:S(2)}, u32[]{:S(2)}) collective-permute-start(f32[256]{0:T(256)S(1)} %add_add_fusion.3), channel_id=1, source_target_pairs={{0,2},{1,3},{2,0},{3,1},{4,6},{5,7},{6,4},{7,5},{8,10},{9,11},{10,... | collective-permute-start | bytes 3080 | tf_op jit(solution)/shard_map/ppermute | solution.py:56
  145.7 1.8 %collective-permute-done.34 = f32[256]{0:T(256)S(1)} collective-permute-done((f32[256]{0:T(256)S(1)}, f32[256]{0:T(256)S(1)}, u32[]{:S(2)}, u32[]{:S(2)}) %collective-permute-start.34) | collective-permute-done | bytes 1056 | tf_op jit(solution)/shard_map/ppermute | solution.py:56
  148.4 1.3 collective-permute-start.36
  149.7 3.2 %collective-permute-done.36 = f32[1024]{0:T(1024)S(1)} collective-permute-done((f32[1024]{0:T(1024)S(1)}, f32[1024]{0:T(1024)S(1)}, u32[]{:S(2)}, u32[]{:S(2)}) %collective-permute-start.36) | collective-permute-done | bytes 4128 | tf_op jit(solution)/shard_map/ppermute | solution.py:62
  (121 shorter events, 28.9 us)
Async XLA Ops:
  2.0 15.2 %collective-permute-start = (bf16[256,1024]{1,0:T(8,128)(2,1)}, bf16[256,1024]{1,0:T(8,128)(2,1)}, u32[]{:S(2)}, u32[]{:S(2)}) collective-permute-start(bf16[256,1024]{1,0:T(8,128)(2,1)} %constant_dynamic-slice_fusion), channel_id=1, source_target_pairs={{0,2},{1,3},{2,0},{3,1},{4,6},{5,7},{6,4},{7,5},{8,10},{9,11},{10,... | collective-permute-start | bytes 1572872 | tf_op jit(solution)/shard_map/ppermute | solution.py:56
  4.9 23.3 %collective-permute-start.3 = (bf16[256,1024]{1,0:T(8,128)(2,1)}, bf16[256,1024]{1,0:T(8,128)(2,1)}, u32[]{:S(2)}, u32[]{:S(2)}) collective-permute-start(bf16[256,1024]{1,0:T(8,128)(2,1)} %constant_dynamic-slice_fusion), channel_id=1, source_target_pairs={{0,1},{1,0},{2,3},{3,2},{4,5},{5,4},{6,7},{7,6},{8,9},{9,8},{10,11... | collective-permute-start | bytes 1572872 | tf_op jit(solution)/shard_map/ppermute | solution.py:56
  18.1 8.6 %collective-permute-start.1 = (bf16[512,256]{1,0:T(8,128)(2,1)S(1)}, bf16[512,256]{1,0:T(8,128)(2,1)S(1)}, u32[]{:S(2)}, u32[]{:S(2)}) collective-permute-start(bf16[512,256]{1,0:T(8,128)(2,1)S(1)} %get-tuple-element.28), channel_id=1, source_target_pairs={{0,2},{1,3},{2,0},{3,1},{4,6},{5,7},{6,4},{7,5},{8,10},{9,11},{10,... | collective-permute-start | bytes 786440 | tf_op jit(solution)/shard_map/ppermute | solution.py:56
  21.4 6.8 %collective-permute-start.2 = (bf16[512,256]{1,0:T(8,128)(2,1)S(1)}, bf16[512,256]{1,0:T(8,128)(2,1)S(1)}, u32[]{:S(2)}, u32[]{:S(2)}) collective-permute-start(bf16[512,256]{1,0:T(8,128)(2,1)S(1)} %get-tuple-element.27), channel_id=1, source_target_pairs={{0,1},{1,0},{2,3},{3,2},{4,5},{5,4},{6,7},{7,6},{8,9},{9,8},{10,11... | collective-permute-start | bytes 786440 | tf_op jit(solution)/shard_map/ppermute | solution.py:56
  21.5 8.8 %collective-permute-start.4 = (bf16[512,256]{1,0:T(8,128)(2,1)S(1)}, bf16[512,256]{1,0:T(8,128)(2,1)S(1)}, u32[]{:S(2)}, u32[]{:S(2)}) collective-permute-start(bf16[512,256]{1,0:T(8,128)(2,1)S(1)} %get-tuple-element.26), channel_id=1, source_target_pairs={{0,3},{1,2},{2,1},{3,0},{4,7},{5,6},{6,5},{7,4},{8,11},{9,10},{10,... | collective-permute-start | bytes 786440 | tf_op jit(solution)/shard_map/ppermute | solution.py:56
  21.9 8.4 %collective-permute-start.5 = (bf16[256,1024]{1,0:T(8,128)(2,1)}, bf16[256,1024]{1,0:T(8,128)(2,1)S(1)}, u32[]{:S(2)}, u32[]{:S(2)}) collective-permute-start(bf16[256,1024]{1,0:T(8,128)(2,1)} %collective-permute-done), channel_id=1, source_target_pairs={{0,1},{1,0},{2,3},{3,2},{4,5},{5,4},{6,7},{7,6},{8,9},{9,8},{10,11... | collective-permute-start | bytes 1572872 | tf_op jit(solution)/shard_map/ppermute | solution.py:56
  30.7 11.1 %collective-permute-start.11 = (bf16[512,1024]{1,0:T(8,128)(2,1)S(1)}, bf16[512,1024]{1,0:T(8,128)(2,1)S(1)}, u32[]{:S(2)}, u32[]{:S(2)}) collective-permute-start(bf16[512,1024]{1,0:T(8,128)(2,1)S(1)} %add_convert_fusion.1), channel_id=1, source_target_pairs={{0,0},{1,1},{2,2},{3,3},{4,8},{5,9},{6,10},{7,11},{8,4},{9,5},{10,... | collective-permute-start | bytes 3145736 | tf_op jit(solution)/shard_map/ppermute | solution.py:62
  31.5 28.3 %collective-permute-start.10 = (bf16[512,1024]{1,0:T(8,128)(2,1)S(1)}, bf16[512,1024]{1,0:T(8,128)(2,1)S(1)}, u32[]{:S(2)}, u32[]{:S(2)}) collective-permute-start(bf16[512,1024]{1,0:T(8,128)(2,1)S(1)} %add_convert_fusion.1), channel_id=1, source_target_pairs={{0,4},{1,5},{2,6},{3,7},{4,0},{5,1},{6,2},{7,3},{8,12},{9,13},{10,... | collective-permute-start | bytes 3145736 | tf_op jit(solution)/shard_map/ppermute | solution.py:62
  36.1 23.6 %collective-permute-start.6 = (bf16[256,1024]{1,0:T(8,128)(2,1)S(1)}, bf16[256,1024]{1,0:T(8,128)(2,1)S(1)}, u32[]{:S(2)}, u32[]{:S(2)}) collective-permute-start(bf16[256,1024]{1,0:T(8,128)(2,1)S(1)} %get-tuple-element.21), channel_id=1, source_target_pairs={{0,2},{1,3},{2,0},{3,1},{4,6},{5,7},{6,4},{7,5},{8,10},{9,11},{10,... | collective-permute-start | bytes 1572872 | tf_op jit(solution)/shard_map/ppermute | solution.py:56
  38.2 3.2 %collective-permute-start.8 = (bf16[256,1024]{1,0:T(8,128)(2,1)S(1)}, bf16[256,1024]{1,0:T(8,128)(2,1)S(1)}, u32[]{:S(2)}, u32[]{:S(2)}) collective-permute-start(bf16[256,1024]{1,0:T(8,128)(2,1)S(1)} %get-tuple-element.21), channel_id=1, source_target_pairs={{0,1},{1,0},{2,3},{3,2},{4,5},{5,4},{6,7},{7,6},{8,9},{9,8},{10,11... | collective-permute-start | bytes 1572872 | tf_op jit(solution)/shard_map/ppermute | solution.py:56
  38.2 2.7 %collective-permute-start.7 = (bf16[256,1024]{1,0:T(8,128)(2,1)S(1)}, bf16[256,1024]{1,0:T(8,128)(2,1)S(1)}, u32[]{:S(2)}, u32[]{:S(2)}) collective-permute-start(bf16[256,1024]{1,0:T(8,128)(2,1)S(1)} %get-tuple-element.22), channel_id=1, source_target_pairs={{0,1},{1,0},{2,3},{3,2},{4,5},{5,4},{6,7},{7,6},{8,9},{9,8},{10,11... | collective-permute-start | bytes 1572872 | tf_op jit(solution)/shard_map/ppermute | solution.py:56
  40.8 20.7 %collective-permute-start.9 = (bf16[256,1024]{1,0:T(8,128)(2,1)S(1)}, bf16[256,1024]{1,0:T(8,128)(2,1)S(1)}, u32[]{:S(2)}, u32[]{:S(2)}) collective-permute-start(bf16[256,1024]{1,0:T(8,128)(2,1)S(1)} %get-tuple-element.22), channel_id=1, source_target_pairs={{0,2},{1,3},{2,0},{3,1},{4,6},{5,7},{6,4},{7,5},{8,10},{9,11},{10,... | collective-permute-start | bytes 1572872 | tf_op jit(solution)/shard_map/ppermute | solution.py:56
  65.9 25.3 %collective-permute-start.20 = (bf16[512,1024]{1,0:T(8,128)(2,1)S(1)}, bf16[512,1024]{1,0:T(8,128)(2,1)S(1)}, u32[]{:S(2)}, u32[]{:S(2)}) collective-permute-start(bf16[512,1024]{1,0:T(8,128)(2,1)S(1)} %get-tuple-element.19), channel_id=1, source_target_pairs={{0,4},{1,5},{2,6},{3,7},{4,0},{5,1},{6,2},{7,3},{8,12},{9,13},{10,... | collective-permute-start | bytes 3145736 | tf_op jit(solution)/shard_map/ppermute | solution.py:62
  66.3 4.6 %collective-permute-start.17 = (bf16[256,1024]{1,0:T(8,128)(2,1)S(1)}, bf16[256,1024]{1,0:T(8,128)(2,1)S(1)}, u32[]{:S(2)}, u32[]{:S(2)}) collective-permute-start(bf16[256,1024]{1,0:T(8,128)(2,1)S(1)} %slice_add_fusion), channel_id=1, source_target_pairs={{0,1},{1,0},{2,3},{3,2},{4,5},{5,4},{6,7},{7,6},{8,9},{9,8},{10,11... | collective-permute-start | bytes 1572872 | tf_op jit(solution)/shard_map/ppermute | solution.py:56
  66.4 14.4 %collective-permute-start.15 = (bf16[256,1024]{1,0:T(8,128)(2,1)S(1)}, bf16[256,1024]{1,0:T(8,128)(2,1)S(1)}, u32[]{:S(2)}, u32[]{:S(2)}) collective-permute-start(bf16[256,1024]{1,0:T(8,128)(2,1)S(1)} %get-tuple-element.32), channel_id=1, source_target_pairs={{0,16},{1,17},{2,18},{3,19},{4,20},{5,21},{6,22},{7,23},{8,24},{9,... | collective-permute-start | bytes 1572872 | tf_op jit(solution)/shard_map/ppermute | solution.py:70
  68.0 23.1 %collective-permute-start.19 = (bf16[512,1024]{1,0:T(8,128)(2,1)S(1)}, bf16[512,1024]{1,0:T(8,128)(2,1)S(1)}, u32[]{:S(2)}, u32[]{:S(2)}) collective-permute-start(bf16[512,1024]{1,0:T(8,128)(2,1)S(1)} %get-tuple-element.20), channel_id=1, source_target_pairs={{0,0},{1,1},{2,2},{3,3},{4,8},{5,9},{6,10},{7,11},{8,4},{9,5},{10,... | collective-permute-start | bytes 3145736 | tf_op jit(solution)/shard_map/ppermute | solution.py:62
  68.9 22.2 %collective-permute-start.18 = (bf16[256,1024]{1,0:T(8,128)(2,1)S(1)}, bf16[256,1024]{1,0:T(8,128)(2,1)S(1)}, u32[]{:S(2)}, u32[]{:S(2)}) collective-permute-start(bf16[256,1024]{1,0:T(8,128)(2,1)S(1)} %get-tuple-element.31), channel_id=1, source_target_pairs={{0,2},{1,3},{2,0},{3,1},{4,6},{5,7},{6,4},{7,5},{8,10},{9,11},{10,... | collective-permute-start | bytes 1572872 | tf_op jit(solution)/shard_map/ppermute | solution.py:56
  70.9 20.2 %collective-permute-start.14 = (bf16[256,1024]{1,0:T(8,128)(2,1)S(1)}, bf16[256,1024]{1,0:T(8,128)(2,1)S(1)}, u32[]{:S(2)}, u32[]{:S(2)}) collective-permute-start(bf16[256,1024]{1,0:T(8,128)(2,1)S(1)} %get-tuple-element.31), channel_id=1, source_target_pairs={{0,1},{1,0},{2,3},{3,2},{4,5},{5,4},{6,7},{7,6},{8,9},{9,8},{10,11... | collective-permute-start | bytes 1572872 | tf_op jit(solution)/shard_map/ppermute | solution.py:56
  80.8 13.5 %collective-permute-start.16 = (bf16[256,1024]{1,0:T(8,128)(2,1)S(1)}, bf16[256,1024]{1,0:T(8,128)(2,1)S(1)}, u32[]{:S(2)}, u32[]{:S(2)}) collective-permute-start(bf16[256,1024]{1,0:T(8,128)(2,1)S(1)} %slice_add_fusion), channel_id=1, source_target_pairs={{0,2},{1,3},{2,0},{3,1},{4,6},{5,7},{6,4},{7,5},{8,10},{9,11},{10,... | collective-permute-start | bytes 1572872 | tf_op jit(solution)/shard_map/ppermute | solution.py:56
  95.1 5.7 %collective-permute-start.25 = (bf16[256,1024]{1,0:T(8,128)(2,1)S(1)}, bf16[256,1024]{1,0:T(8,128)(2,1)S(1)}, u32[]{:S(2)}, u32[]{:S(2)}) collective-permute-start(bf16[256,1024]{1,0:T(8,128)(2,1)S(1)} %get-tuple-element.43), channel_id=1, source_target_pairs={{0,1},{1,0},{2,3},{3,2},{4,5},{5,4},{6,7},{7,6},{8,9},{9,8},{10,11... | collective-permute-start | bytes 1572872 | tf_op jit(solution)/shard_map/ppermute | solution.py:56
  97.6 4.7 %collective-permute-start.22 = (bf16[256,1024]{1,0:T(8,128)(2,1)S(1)}, bf16[256,1024]{1,0:T(8,128)(2,1)S(1)}, u32[]{:S(2)}, u32[]{:S(2)}) collective-permute-start(bf16[256,1024]{1,0:T(8,128)(2,1)S(1)} %get-tuple-element.30), channel_id=1, source_target_pairs={{0,1},{1,0},{2,3},{3,2},{4,5},{5,4},{6,7},{7,6},{8,9},{9,8},{10,11... | collective-permute-start | bytes 1572872 | tf_op jit(solution)/shard_map/ppermute | solution.py:56
  97.8 14.2 %collective-permute-start.26 = (bf16[256,1024]{1,0:T(8,128)(2,1)S(1)}, bf16[256,1024]{1,0:T(8,128)(2,1)S(1)}, u32[]{:S(2)}, u32[]{:S(2)}) collective-permute-start(bf16[256,1024]{1,0:T(8,128)(2,1)S(1)} %get-tuple-element.30), channel_id=1, source_target_pairs={{0,2},{1,3},{2,0},{3,1},{4,6},{5,7},{6,4},{7,5},{8,10},{9,11},{10,... | collective-permute-start | bytes 1572872 | tf_op jit(solution)/shard_map/ppermute | solution.py:56
  99.3 13.9 %collective-permute-start.23 = (bf16[256,1024]{1,0:T(8,128)(2,1)S(1)}, bf16[256,1024]{1,0:T(8,128)(2,1)S(1)}, u32[]{:S(2)}, u32[]{:S(2)}) collective-permute-start(bf16[256,1024]{1,0:T(8,128)(2,1)S(1)} %get-tuple-element.29), channel_id=1, source_target_pairs={{0,16},{1,17},{2,18},{3,19},{4,20},{5,21},{6,22},{7,23},{8,24},{9,... | collective-permute-start | bytes 1572872 | tf_op jit(solution)/shard_map/ppermute | solution.py:70
  103.5 10.4 %collective-permute-start.24 = (f32[256,256]{1,0:T(8,128)S(1)}, f32[256,256]{1,0:T(8,128)S(1)}, u32[]{:S(2)}, u32[]{:S(2)}) collective-permute-start(f32[256,256]{1,0:T(8,128)S(1)} %convolution_add_fusion.4), channel_id=1, source_target_pairs={{0,4},{1,5},{2,6},{3,7},{4,0},{5,1},{6,2},{7,3},{8,12},{9,13},{10,... | collective-permute-start | bytes 786440 | tf_op jit(solution)/shard_map/ppermute | solution.py:62
  114.8 20.7 %collective-permute-start.28 = (f32[256,768]{1,0:T(8,128)S(1)}, f32[256,768]{1,0:T(8,128)S(1)}, u32[]{:S(2)}, u32[]{:S(2)}) collective-permute-start(f32[256,768]{1,0:T(8,128)S(1)} %pad_maximum_fusion.2), channel_id=1, source_target_pairs={{0,4},{1,5},{2,6},{3,7},{4,0},{5,1},{6,2},{7,3},{8,12},{9,13},{10,... | collective-permute-start | bytes 2359304 | tf_op jit(solution)/shard_map/ppermute | solution.py:62
  118.4 17.1 %collective-permute-start.29 = (f32[1024]{0:T(1024)S(1)}, f32[1024]{0:T(1024)S(1)}, u32[]{:S(2)}, u32[]{:S(2)}) collective-permute-start(f32[1024]{0:T(1024)S(1)} %pad_maximum_fusion.3), channel_id=1, source_target_pairs={{0,4},{1,5},{2,6},{3,7},{4,0},{5,1},{6,2},{7,3},{8,12},{9,13},{10,... | collective-permute-start | bytes 12296 | tf_op jit(solution)/shard_map/ppermute | solution.py:62
  137.0 3.6 %collective-permute-start.31 = (f32[256]{0:T(256)S(1)}, f32[256]{0:T(256)S(1)}, u32[]{:S(2)}, u32[]{:S(2)}) collective-permute-start(f32[256]{0:T(256)S(1)} %get-tuple-element.42), channel_id=1, source_target_pairs={{0,16},{1,17},{2,18},{3,19},{4,20},{5,21},{6,22},{7,23},{8,24},{9,... | collective-permute-start | bytes 3080 | tf_op jit(solution)/shard_map/ppermute | solution.py:70
  137.6 4.5 %collective-permute-start.32 = (f32[256]{0:T(256)S(1)}, f32[256]{0:T(256)S(1)}, u32[]{:S(2)}, u32[]{:S(2)}) collective-permute-start(f32[256]{0:T(256)S(1)} %get-tuple-element.42), channel_id=1, source_target_pairs={{0,20},{1,21},{2,22},{3,23},{4,16},{5,17},{6,18},{7,19},{8,28},{9,... | collective-permute-start | bytes 3080 | tf_op jit(solution)/shard_map/ppermute | solution.py:70
  140.2 3.6 %collective-permute-start.30 = (f32[256]{0:T(256)S(1)}, f32[256]{0:T(256)S(1)}, u32[]{:S(2)}, u32[]{:S(2)}) collective-permute-start(f32[256]{0:T(256)S(1)} %get-tuple-element.41), channel_id=1, source_target_pairs={{0,4},{1,5},{2,6},{3,7},{4,0},{5,1},{6,2},{7,3},{8,12},{9,13},{10,... | collective-permute-start | bytes 3080 | tf_op jit(solution)/shard_map/ppermute | solution.py:62
  143.8 3.6 %collective-permute-start.34 = (f32[256]{0:T(256)S(1)}, f32[256]{0:T(256)S(1)}, u32[]{:S(2)}, u32[]{:S(2)}) collective-permute-start(f32[256]{0:T(256)S(1)} %add_add_fusion.3), channel_id=1, source_target_pairs={{0,2},{1,3},{2,0},{3,1},{4,6},{5,7},{6,4},{7,5},{8,10},{9,11},{10,... | collective-permute-start | bytes 3080 | tf_op jit(solution)/shard_map/ppermute | solution.py:56
  145.4 3.0 %collective-permute-start.35 = (f32[256]{0:T(256)S(1)}, f32[256]{0:T(256)S(1)}, u32[]{:S(2)}, u32[]{:S(2)}) collective-permute-start(f32[256]{0:T(256)S(1)} %add_add_fusion.3), channel_id=1, source_target_pairs={{0,3},{1,2},{2,1},{3,0},{4,7},{5,6},{6,5},{7,4},{8,11},{9,10},{10,... | collective-permute-start | bytes 3080 | tf_op jit(solution)/shard_map/ppermute | solution.py:56
  148.4 4.6 %collective-permute-start.36 = (f32[1024]{0:T(1024)S(1)}, f32[1024]{0:T(1024)S(1)}, u32[]{:S(2)}, u32[]{:S(2)}) collective-permute-start(f32[1024]{0:T(1024)S(1)} %pad_maximum_fusion.4), channel_id=1, source_target_pairs={{0,8},{1,9},{2,10},{3,11},{4,12},{5,13},{6,14},{7,15},{8,0},{9,1},... | collective-permute-start | bytes 12296 | tf_op jit(solution)/shard_map/ppermute | solution.py:62
  (9 other events, 43.9 us)

commit v7 on v6

--- a/solution.py
+++ b/solution.py
@@ -42,6 +42,7 @@
     nz = QUARTERS
     nx = n_tgt // (nz * CORES)
     outer = (1, 0, 3, 2)
+    owners = (0, 1, 3, 2)
     middle = (0, 2, 1, 3)
     skip = (2, 3, 0, 1)
 
@@ -143,7 +144,7 @@
         third = partial([own3] + moved3 + [flip3] + factor_flip(moved3))
 
         start = token(second, third) + done
-        step3 = along_z(behind(second, start).astype(BF), outer)
+        step3 = along_z(behind(second, start).astype(BF), owners)
         step4 = along_z((behind(second, start) + step1.astype(F32)).astype(BF), middle)
         white_a = (third + step1.astype(F32) + jnp.where(top, 0.0, step2.astype(F32)) + start).astype(BF)
         own4 = behind(factor_own([3, 3, 3, 3]), start)
@@ -174,20 +175,20 @@
         p_far_a, p_far_b = jnp.concatenate(p_moved_a, axis=0), jnp.concatenate(p_moved_b, axis=0)
         p_all_a, p_all_b = jnp.concatenate([p_a, p_far_a], axis=0), jnp.concatenate([p_b, p_far_b], axis=0)
 
-        given_near = along_z(matmul_t(give_a[0], p_a) + matmul_t(give_b[0], p_b), outer)
+        given_near = along_z(matmul_t(give_a[0], p_a) + matmul_t(give_b[0], p_b), owners)
         give_side = behind(matmul_t(give_a[0], p_far_a) + matmul_t(give_b[0], p_far_b), token(given_near)[:, :1] if n_pool > 2 else token(given_near))
         give_far = matmul_t(give_a[1], p_all_a) + matmul_t(give_b[1], p_all_b)
         if nx == 2:
-            given = along_z(jnp.concatenate([give_side, give_far], axis=1), outer)
+            given = along_z(jnp.concatenate([give_side, give_far], axis=1), owners)
             given_side, given_far = given[:, :give_side.shape[1]], given[:, give_side.shape[1]:]
         else:
-            given_side, given_far = along_z(give_side, outer), along_z(give_far, outer)
+            given_side, given_far = along_z(give_side, owners), along_z(give_far, owners)
 
         p_squares = square_sum(p_all_a) + square_sum(p_all_b)
         sizes = [p_squares.shape[0], keep_a[0].shape[0], keep_a[1].shape[0]]
         squares = along_z(jnp.concatenate(
             [p_squares] + [square_sum(a) + square_sum(b) for a, b in zip(give_a, give_b)]
-        ), outer)
+        ), owners)
         pool_var = 1.0 + (p_squares + squares[:sizes[0]])
 
         def log_sums(group, given, offset):
@@ -201,9 +202,9 @@
         sums = sums + log_sums(1, given_far, sizes[0] + sizes[1])
 
         blocks = [sums[s * count:(s + 1) * count] for s in range(n_pool)]
-        own = blocks[0] + along_z(blocks[0], outer)
+        own = blocks[0] + along_z(blocks[0], owners)
         for s in range(1, n_pool):
-            own = own + (over_pool(blocks[s], -s) + over_pool(blocks[s], -s, 0, outer))
+            own = own + (over_pool(blocks[s], -s) + over_pool(blocks[s], -s, 0, owners))
         rows = [in_order([own if s == 0 else inner(own, s, 0), inner(own, s, 1)], core) for s in range(nx)]
         scores = in_order(rows, x)
         return jnp.where(z >= nz - 2, scores, along_z(scores, skip))

time: 154 us -> 157 us (1.019)
  starting transfers between devices: 35.5 us -> 56.3 us
  waiting for transfers between devices: 89.4 us -> 71.1 us
    ppermute x9, waiting for transfers between devices: 47.6 us -> 19.5 us  [along_z(): return lax.ppermute(value, 'tgt', pairs)]
    ppermute x9, starting transfers between devices: 13.2 us -> 35.1 us  [along_z(): return lax.ppermute(value, 'tgt', pairs)]
    ppermute x24, waiting for transfers between devices: 29.3 us -> 38.4 us  [inner(): return lax.ppermute(value, 'tgt', pairs)]
  transfers between devices with their start and end apart: 37 -> 37, of which waited for: 21 -> 18; matrix products, arithmetic and copies ran while one was open for 14% -> 14% of each run, Pallas kernels for 0% -> 0%
where the time goes in v7:
time: 157 us; the launch traced here: 156 us
  waiting for transfers between devices  71.1 us (45%)
  starting transfers between devices  56.3 us (36%)
  matrix products  15.5 us (10%)
  local copies, waits for them, and re-layouts  6.85 us (4%)
  other arithmetic  5.85 us (4%)
    ppermute x24, waiting for transfers between devices, inner(): return lax.ppermute(value, 'tgt', pairs)  38.4 us
    ppermute x9, starting transfers between devices, along_z(): return lax.ppermute(value, 'tgt', pairs)  35.1 us
    ppermute x9, waiting for transfers between devices, along_z(): return lax.ppermute(value, 'tgt', pairs)  19.5 us
    ppermute x24, starting transfers between devices, inner(): return lax.ppermute(value, 'tgt', pairs)  16.1 us
    ppermute x4, waiting for transfers between devices, over_pool(): return lax.ppermute(value, ('pool', 'tgt'), pairs)  13.2 us
    dot_general x16, matrix products, matmul(): lax.dot_general(a, b, (((1,), (0,)), ((), ())), preferred_element_type=F32)  10.8 us
    ppermute x4, starting transfers between devices, over_pool(): return lax.ppermute(value, ('pool', 'tgt'), pairs)  5.15 us
    dot_general x10, matrix products, matmul_t(): lax.dot_general(a, b, (((1,), (1,)), ((), ())), preferred_element_type=F32)  4.7 us
  transfers between devices with their start and end apart: 37, of which 18 were waited for; matrix products, arithmetic and copies ran while one was open for 14% of the time, Pallas kernels for 0%

profile of v7, /device:TPU:0, one launch (start us, length us, event | category | flops | bytes accessed | tf_op | source)
XLA Modules:
  0.0 156.3 jit_solution(5903823450573659469)
XLA Ops:
  0.0 2.0 %constant_dynamic-slice_fusion = bf16[256,1024]{1,0:T(8,128)(2,1)} fusion(bf16[256,4096]{1,0:T(8,128)(2,1)} %param.7, s32[]{:T(128)S(6)} %select_n.171), kind=kLoop, calls=%fused_computation.148 | loop fusion | bytes 1048580 | tf_op jit(solution)/shard_map/dynamic_slice | solution.py:110
  2.0 2.9 %collective-permute-start = (bf16[256,1024]{1,0:T(8,128)(2,1)}, bf16[256,1024]{1,0:T(8,128)(2,1)}, u32[]{:S(2)}, u32[]{:S(2)}) collective-permute-start(bf16[256,1024]{1,0:T(8,128)(2,1)} %constant_dynamic-slice_fusion), channel_id=1, source_target_pairs={{0,2},{1,3},{2,0},{3,1},{4,6},{5,7},{6,4},{7,5},{8,10},{9,11},{10,... | collective-permute-start | bytes 1572872 | tf_op jit(solution)/shard_map/ppermute | solution.py:57
  5.7 3.9 %gather_fusion = bf16[1024,256]{1,0:T(8,128)(2,1)S(1)} fusion(bf16[4096,256]{1,0:T(8,128)(2,1)S(1)} %copy-done, s32[1024]{0:T(1024)S(1)} %fusion.31), kind=kCustom, calls=%fused_computation | custom fusion | bytes 1052672 | tf_op jit(solution)/shard_map/gather | solution.py:97
  9.7 7.5 %collective-permute-done = bf16[256,1024]{1,0:T(8,128)(2,1)} collective-permute-done((bf16[256,1024]{1,0:T(8,128)(2,1)}, bf16[256,1024]{1,0:T(8,128)(2,1)}, u32[]{:S(2)}, u32[]{:S(2)}) %collective-permute-start) | collective-permute-done | bytes 524320 | tf_op jit(solution)/shard_map/ppermute | solution.py:57
  18.1 1.8 %collective-permute-start.1 = (bf16[512,256]{1,0:T(8,128)(2,1)S(1)}, bf16[512,256]{1,0:T(8,128)(2,1)S(1)}, u32[]{:S(2)}, u32[]{:S(2)}) collective-permute-start(bf16[512,256]{1,0:T(8,128)(2,1)S(1)} %get-tuple-element.28), channel_id=1, source_target_pairs={{0,2},{1,3},{2,0},{3,1},{4,6},{5,7},{6,4},{7,5},{8,10},{9,11},{10,... | collective-permute-start | bytes 786440 | tf_op jit(solution)/shard_map/ppermute | solution.py:57
  19.9 1.5 fusion.95
  22.0 4.8 %collective-permute-done.1 = bf16[512,256]{1,0:T(8,128)(2,1)S(1)} collective-permute-done((bf16[512,256]{1,0:T(8,128)(2,1)S(1)}, bf16[512,256]{1,0:T(8,128)(2,1)S(1)}, u32[]{:S(2)}, u32[]{:S(2)}) %collective-permute-start.1) | collective-permute-done | bytes 262176 | tf_op jit(solution)/shard_map/ppermute | solution.py:57
  26.7 1.5 fusion.96
  28.2 1.5 fusion.97
  31.5 4.4 %collective-permute-start.10 = (bf16[512,1024]{1,0:T(8,128)(2,1)S(1)}, bf16[512,1024]{1,0:T(8,128)(2,1)S(1)}, u32[]{:S(2)}, u32[]{:S(2)}) collective-permute-start(bf16[512,1024]{1,0:T(8,128)(2,1)S(1)} %add_convert_fusion.1), channel_id=1, source_target_pairs={{0,4},{1,5},{2,6},{3,7},{4,0},{5,1},{6,2},{7,3},{8,12},{9,13},{10,... | collective-permute-start | bytes 3145736 | tf_op jit(solution)/shard_map/ppermute | solution.py:63
  36.1 2.0 %collective-permute-start.6 = (bf16[256,1024]{1,0:T(8,128)(2,1)S(1)}, bf16[256,1024]{1,0:T(8,128)(2,1)S(1)}, u32[]{:S(2)}, u32[]{:S(2)}) collective-permute-start(bf16[256,1024]{1,0:T(8,128)(2,1)S(1)} %get-tuple-element.21), channel_id=1, source_target_pairs={{0,2},{1,3},{2,0},{3,1},{4,6},{5,7},{6,4},{7,5},{8,10},{9,11},{10,... | collective-permute-start | bytes 1572872 | tf_op jit(solution)/shard_map/ppermute | solution.py:57
  39.6 1.3 collective-permute-done.7
  41.8 17.9 %collective-permute-done.10 = bf16[512,1024]{1,0:T(8,128)(2,1)S(1)} collective-permute-done((bf16[512,1024]{1,0:T(8,128)(2,1)S(1)}, bf16[512,1024]{1,0:T(8,128)(2,1)S(1)}, u32[]{:S(2)}, u32[]{:S(2)}) %collective-permute-start.10) | collective-permute-done | bytes 1048608 | tf_op jit(solution)/shard_map/ppermute | solution.py:63
  59.8 1.8 %collective-permute-done.9 = bf16[256,1024]{1,0:T(8,128)(2,1)S(1)} collective-permute-done((bf16[256,1024]{1,0:T(8,128)(2,1)S(1)}, bf16[256,1024]{1,0:T(8,128)(2,1)S(1)}, u32[]{:S(2)}, u32[]{:S(2)}) %collective-permute-start.9) | collective-permute-done | bytes 524320 | tf_op jit(solution)/shard_map/ppermute | solution.py:57
  64.9 1.0 add_convert_fusion.2
  66.9 1.6 %collective-permute-start.15 = (bf16[256,1024]{1,0:T(8,128)(2,1)S(1)}, bf16[256,1024]{1,0:T(8,128)(2,1)S(1)}, u32[]{:S(2)}, u32[]{:S(2)}) collective-permute-start(bf16[256,1024]{1,0:T(8,128)(2,1)S(1)} %get-tuple-element.32), channel_id=1, source_target_pairs={{0,16},{1,17},{2,18},{3,19},{4,20},{5,21},{6,22},{7,23},{8,24},{9,... | collective-permute-start | bytes 1572872 | tf_op jit(solution)/shard_map/ppermute | solution.py:71
  68.5 0.9 collective-permute-start.19
  69.4 1.6 collective-permute-start.18
  71.5 9.7 %collective-permute-done.15 = bf16[256,1024]{1,0:T(8,128)(2,1)S(1)} collective-permute-done((bf16[256,1024]{1,0:T(8,128)(2,1)S(1)}, bf16[256,1024]{1,0:T(8,128)(2,1)S(1)}, u32[]{:S(2)}, u32[]{:S(2)}) %collective-permute-start.15) | collective-permute-done | bytes 524320 | tf_op jit(solution)/shard_map/ppermute | solution.py:71
  81.2 1.5 collective-permute-start.16
  83.5 11.2 %collective-permute-done.16 = bf16[256,1024]{1,0:T(8,128)(2,1)S(1)} collective-permute-done((bf16[256,1024]{1,0:T(8,128)(2,1)S(1)}, bf16[256,1024]{1,0:T(8,128)(2,1)S(1)}, u32[]{:S(2)}, u32[]{:S(2)}) %collective-permute-start.16) | collective-permute-done | bytes 524320 | tf_op jit(solution)/shard_map/ppermute | solution.py:57
  96.8 1.0 add_convert_fusion
  98.1 1.5 collective-permute-start.26
  99.6 1.5 collective-permute-start.23
  104.4 7.9 %collective-permute-done.26 = bf16[256,1024]{1,0:T(8,128)(2,1)S(1)} collective-permute-done((bf16[256,1024]{1,0:T(8,128)(2,1)S(1)}, bf16[256,1024]{1,0:T(8,128)(2,1)S(1)}, u32[]{:S(2)}, u32[]{:S(2)}) %collective-permute-start.26) | collective-permute-done | bytes 524320 | tf_op jit(solution)/shard_map/ppermute | solution.py:57
  112.3 1.2 collective-permute-done.23
  119.0 1.5 collective-permute-start.31
  122.6 1.5 collective-permute-done.32
  124.2 1.2 collective-permute-start.34
  126.1 1.8 %collective-permute-done.34 = f32[256]{0:T(256)S(1)} collective-permute-done((f32[256]{0:T(256)S(1)}, f32[256]{0:T(256)S(1)}, u32[]{:S(2)}, u32[]{:S(2)}) %collective-permute-start.34) | collective-permute-done | bytes 1056 | tf_op jit(solution)/shard_map/ppermute | solution.py:57
  128.4 25.6 %collective-permute-start.36 = (f32[1024]{0:T(1024)S(1)}, f32[1024]{0:T(1024)S(1)}, u32[]{:S(2)}, u32[]{:S(2)}) collective-permute-start(f32[1024]{0:T(1024)S(1)} %pad_maximum_fusion.4), channel_id=1, source_target_pairs={{0,8},{1,9},{2,10},{3,11},{4,12},{5,13},{6,14},{7,15},{8,0},{9,1},... | collective-permute-start | bytes 12296 | tf_op jit(solution)/shard_map/ppermute | solution.py:63
  154.1 1.6 %collective-permute-done.36 = f32[1024]{0:T(1024)S(1)} collective-permute-done((f32[1024]{0:T(1024)S(1)}, f32[1024]{0:T(1024)S(1)}, u32[]{:S(2)}, u32[]{:S(2)}) %collective-permute-start.36) | collective-permute-done | bytes 4128 | tf_op jit(solution)/shard_map/ppermute | solution.py:63
  (121 shorter events, 27.3 us)
Async XLA Ops:
  2.0 15.2 %collective-permute-start = (bf16[256,1024]{1,0:T(8,128)(2,1)}, bf16[256,1024]{1,0:T(8,128)(2,1)}, u32[]{:S(2)}, u32[]{:S(2)}) collective-permute-start(bf16[256,1024]{1,0:T(8,128)(2,1)} %constant_dynamic-slice_fusion), channel_id=1, source_target_pairs={{0,2},{1,3},{2,0},{3,1},{4,6},{5,7},{6,4},{7,5},{8,10},{9,11},{10,... | collective-permute-start | bytes 1572872 | tf_op jit(solution)/shard_map/ppermute | solution.py:57
  4.9 23.3 %collective-permute-start.3 = (bf16[256,1024]{1,0:T(8,128)(2,1)}, bf16[256,1024]{1,0:T(8,128)(2,1)}, u32[]{:S(2)}, u32[]{:S(2)}) collective-permute-start(bf16[256,1024]{1,0:T(8,128)(2,1)} %constant_dynamic-slice_fusion), channel_id=1, source_target_pairs={{0,1},{1,0},{2,3},{3,2},{4,5},{5,4},{6,7},{7,6},{8,9},{9,8},{10,11... | collective-permute-start | bytes 1572872 | tf_op jit(solution)/shard_map/ppermute | solution.py:57
  18.1 8.6 %collective-permute-start.1 = (bf16[512,256]{1,0:T(8,128)(2,1)S(1)}, bf16[512,256]{1,0:T(8,128)(2,1)S(1)}, u32[]{:S(2)}, u32[]{:S(2)}) collective-permute-start(bf16[512,256]{1,0:T(8,128)(2,1)S(1)} %get-tuple-element.28), channel_id=1, source_target_pairs={{0,2},{1,3},{2,0},{3,1},{4,6},{5,7},{6,4},{7,5},{8,10},{9,11},{10,... | collective-permute-start | bytes 786440 | tf_op jit(solution)/shard_map/ppermute | solution.py:57
  21.4 6.8 %collective-permute-start.2 = (bf16[512,256]{1,0:T(8,128)(2,1)S(1)}, bf16[512,256]{1,0:T(8,128)(2,1)S(1)}, u32[]{:S(2)}, u32[]{:S(2)}) collective-permute-start(bf16[512,256]{1,0:T(8,128)(2,1)S(1)} %get-tuple-element.27), channel_id=1, source_target_pairs={{0,1},{1,0},{2,3},{3,2},{4,5},{5,4},{6,7},{7,6},{8,9},{9,8},{10,11... | collective-permute-start | bytes 786440 | tf_op jit(solution)/shard_map/ppermute | solution.py:57
  21.5 8.8 %collective-permute-start.4 = (bf16[512,256]{1,0:T(8,128)(2,1)S(1)}, bf16[512,256]{1,0:T(8,128)(2,1)S(1)}, u32[]{:S(2)}, u32[]{:S(2)}) collective-permute-start(bf16[512,256]{1,0:T(8,128)(2,1)S(1)} %get-tuple-element.26), channel_id=1, source_target_pairs={{0,3},{1,2},{2,1},{3,0},{4,7},{5,6},{6,5},{7,4},{8,11},{9,10},{10,... | collective-permute-start | bytes 786440 | tf_op jit(solution)/shard_map/ppermute | solution.py:57
  21.9 8.4 %collective-permute-start.5 = (bf16[256,1024]{1,0:T(8,128)(2,1)}, bf16[256,1024]{1,0:T(8,128)(2,1)S(1)}, u32[]{:S(2)}, u32[]{:S(2)}) collective-permute-start(bf16[256,1024]{1,0:T(8,128)(2,1)} %collective-permute-done), channel_id=1, source_target_pairs={{0,1},{1,0},{2,3},{3,2},{4,5},{5,4},{6,7},{7,6},{8,9},{9,8},{10,11... | collective-permute-start | bytes 1572872 | tf_op jit(solution)/shard_map/ppermute | solution.py:57
  30.7 11.1 %collective-permute-start.11 = (bf16[512,1024]{1,0:T(8,128)(2,1)S(1)}, bf16[512,1024]{1,0:T(8,128)(2,1)S(1)}, u32[]{:S(2)}, u32[]{:S(2)}) collective-permute-start(bf16[512,1024]{1,0:T(8,128)(2,1)S(1)} %add_convert_fusion.1), channel_id=1, source_target_pairs={{0,0},{1,1},{2,2},{3,3},{4,8},{5,9},{6,10},{7,11},{8,4},{9,5},{10,... | collective-permute-start | bytes 3145736 | tf_op jit(solution)/shard_map/ppermute | solution.py:63
  31.5 28.3 %collective-permute-start.10 = (bf16[512,1024]{1,0:T(8,128)(2,1)S(1)}, bf16[512,1024]{1,0:T(8,128)(2,1)S(1)}, u32[]{:S(2)}, u32[]{:S(2)}) collective-permute-start(bf16[512,1024]{1,0:T(8,128)(2,1)S(1)} %add_convert_fusion.1), channel_id=1, source_target_pairs={{0,4},{1,5},{2,6},{3,7},{4,0},{5,1},{6,2},{7,3},{8,12},{9,13},{10,... | collective-permute-start | bytes 3145736 | tf_op jit(solution)/shard_map/ppermute | solution.py:63
  36.1 23.6 %collective-permute-start.6 = (bf16[256,1024]{1,0:T(8,128)(2,1)S(1)}, bf16[256,1024]{1,0:T(8,128)(2,1)S(1)}, u32[]{:S(2)}, u32[]{:S(2)}) collective-permute-start(bf16[256,1024]{1,0:T(8,128)(2,1)S(1)} %get-tuple-element.21), channel_id=1, source_target_pairs={{0,2},{1,3},{2,0},{3,1},{4,6},{5,7},{6,4},{7,5},{8,10},{9,11},{10,... | collective-permute-start | bytes 1572872 | tf_op jit(solution)/shard_map/ppermute | solution.py:57
  38.2 3.2 %collective-permute-start.8 = (bf16[256,1024]{1,0:T(8,128)(2,1)S(1)}, bf16[256,1024]{1,0:T(8,128)(2,1)S(1)}, u32[]{:S(2)}, u32[]{:S(2)}) collective-permute-start(bf16[256,1024]{1,0:T(8,128)(2,1)S(1)} %get-tuple-element.21), channel_id=1, source_target_pairs={{0,1},{1,0},{2,3},{3,2},{4,5},{5,4},{6,7},{7,6},{8,9},{9,8},{10,11... | collective-permute-start | bytes 1572872 | tf_op jit(solution)/shard_map/ppermute | solution.py:57
  38.2 2.7 %collective-permute-start.7 = (bf16[256,1024]{1,0:T(8,128)(2,1)S(1)}, bf16[256,1024]{1,0:T(8,128)(2,1)S(1)}, u32[]{:S(2)}, u32[]{:S(2)}) collective-permute-start(bf16[256,1024]{1,0:T(8,128)(2,1)S(1)} %get-tuple-element.22), channel_id=1, source_target_pairs={{0,1},{1,0},{2,3},{3,2},{4,5},{5,4},{6,7},{7,6},{8,9},{9,8},{10,11... | collective-permute-start | bytes 1572872 | tf_op jit(solution)/shard_map/ppermute | solution.py:57
  40.8 20.7 %collective-permute-start.9 = (bf16[256,1024]{1,0:T(8,128)(2,1)S(1)}, bf16[256,1024]{1,0:T(8,128)(2,1)S(1)}, u32[]{:S(2)}, u32[]{:S(2)}) collective-permute-start(bf16[256,1024]{1,0:T(8,128)(2,1)S(1)} %get-tuple-element.22), channel_id=1, source_target_pairs={{0,2},{1,3},{2,0},{3,1},{4,6},{5,7},{6,4},{7,5},{8,10},{9,11},{10,... | collective-permute-start | bytes 1572872 | tf_op jit(solution)/shard_map/ppermute | solution.py:57
  61.7 2.6 %collective-permute-start.12 = (bf16[256,1024]{1,0:T(8,128)(2,1)S(1)}, bf16[256,1024]{1,0:T(8,128)(2,1)S(1)}, u32[]{:S(2)}, u32[]{:S(2)}) collective-permute-start(bf16[256,1024]{1,0:T(8,128)(2,1)S(1)} %get-tuple-element.45), channel_id=1, source_target_pairs={{0,1},{1,0},{2,3},{3,2},{4,5},{5,4},{6,7},{7,6},{8,9},{9,8},{10,11... | collective-permute-start | bytes 1572872 | tf_op jit(solution)/shard_map/ppermute | solution.py:57
  65.9 17.5 %collective-permute-start.20 = (bf16[512,1024]{1,0:T(8,128)(2,1)S(1)}, bf16[512,1024]{1,0:T(8,128)(2,1)S(1)}, u32[]{:S(2)}, u32[]{:S(2)}) collective-permute-start(bf16[512,1024]{1,0:T(8,128)(2,1)S(1)} %get-tuple-element.19), channel_id=1, source_target_pairs={{0,0},{1,1},{2,2},{3,3},{4,4},{5,5},{6,6},{7,7},{8,12},{9,13},{10,... | collective-permute-start | bytes 3145736 | tf_op jit(solution)/shard_map/ppermute | solution.py:63
  66.6 4.8 %collective-permute-start.17 = (bf16[256,1024]{1,0:T(8,128)(2,1)S(1)}, bf16[256,1024]{1,0:T(8,128)(2,1)S(1)}, u32[]{:S(2)}, u32[]{:S(2)}) collective-permute-start(bf16[256,1024]{1,0:T(8,128)(2,1)S(1)} %slice_add_fusion), channel_id=1, source_target_pairs={{0,1},{1,0},{2,3},{3,2},{4,5},{5,4},{6,7},{7,6},{8,9},{9,8},{10,11... | collective-permute-start | bytes 1572872 | tf_op jit(solution)/shard_map/ppermute | solution.py:57
  66.9 14.3 %collective-permute-start.15 = (bf16[256,1024]{1,0:T(8,128)(2,1)S(1)}, bf16[256,1024]{1,0:T(8,128)(2,1)S(1)}, u32[]{:S(2)}, u32[]{:S(2)}) collective-permute-start(bf16[256,1024]{1,0:T(8,128)(2,1)S(1)} %get-tuple-element.32), channel_id=1, source_target_pairs={{0,16},{1,17},{2,18},{3,19},{4,20},{5,21},{6,22},{7,23},{8,24},{9,... | collective-permute-start | bytes 1572872 | tf_op jit(solution)/shard_map/ppermute | solution.py:71
  68.5 14.9 %collective-permute-start.19 = (bf16[512,1024]{1,0:T(8,128)(2,1)S(1)}, bf16[512,1024]{1,0:T(8,128)(2,1)S(1)}, u32[]{:S(2)}, u32[]{:S(2)}) collective-permute-start(bf16[512,1024]{1,0:T(8,128)(2,1)S(1)} %get-tuple-element.20), channel_id=1, source_target_pairs={{0,0},{1,1},{2,2},{3,3},{4,8},{5,9},{6,10},{7,11},{8,4},{9,5},{10,... | collective-permute-start | bytes 3145736 | tf_op jit(solution)/shard_map/ppermute | solution.py:63
  69.4 14.0 %collective-permute-start.18 = (bf16[256,1024]{1,0:T(8,128)(2,1)S(1)}, bf16[256,1024]{1,0:T(8,128)(2,1)S(1)}, u32[]{:S(2)}, u32[]{:S(2)}) collective-permute-start(bf16[256,1024]{1,0:T(8,128)(2,1)S(1)} %get-tuple-element.31), channel_id=1, source_target_pairs={{0,2},{1,3},{2,0},{3,1},{4,6},{5,7},{6,4},{7,5},{8,10},{9,11},{10,... | collective-permute-start | bytes 1572872 | tf_op jit(solution)/shard_map/ppermute | solution.py:57
  71.4 12.0 %collective-permute-start.14 = (bf16[256,1024]{1,0:T(8,128)(2,1)S(1)}, bf16[256,1024]{1,0:T(8,128)(2,1)S(1)}, u32[]{:S(2)}, u32[]{:S(2)}) collective-permute-start(bf16[256,1024]{1,0:T(8,128)(2,1)S(1)} %get-tuple-element.31), channel_id=1, source_target_pairs={{0,1},{1,0},{2,3},{3,2},{4,5},{5,4},{6,7},{7,6},{8,9},{9,8},{10,11... | collective-permute-start | bytes 1572872 | tf_op jit(solution)/shard_map/ppermute | solution.py:57
  81.2 13.4 %collective-permute-start.16 = (bf16[256,1024]{1,0:T(8,128)(2,1)S(1)}, bf16[256,1024]{1,0:T(8,128)(2,1)S(1)}, u32[]{:S(2)}, u32[]{:S(2)}) collective-permute-start(bf16[256,1024]{1,0:T(8,128)(2,1)S(1)} %slice_add_fusion), channel_id=1, source_target_pairs={{0,2},{1,3},{2,0},{3,1},{4,6},{5,7},{6,4},{7,5},{8,10},{9,11},{10,... | collective-permute-start | bytes 1572872 | tf_op jit(solution)/shard_map/ppermute | solution.py:57
  95.4 5.7 %collective-permute-start.25 = (bf16[256,1024]{1,0:T(8,128)(2,1)S(1)}, bf16[256,1024]{1,0:T(8,128)(2,1)S(1)}, u32[]{:S(2)}, u32[]{:S(2)}) collective-permute-start(bf16[256,1024]{1,0:T(8,128)(2,1)S(1)} %get-tuple-element.43), channel_id=1, source_target_pairs={{0,1},{1,0},{2,3},{3,2},{4,5},{5,4},{6,7},{7,6},{8,9},{9,8},{10,11... | collective-permute-start | bytes 1572872 | tf_op jit(solution)/shard_map/ppermute | solution.py:57
  97.9 4.6 %collective-permute-start.22 = (bf16[256,1024]{1,0:T(8,128)(2,1)S(1)}, bf16[256,1024]{1,0:T(8,128)(2,1)S(1)}, u32[]{:S(2)}, u32[]{:S(2)}) collective-permute-start(bf16[256,1024]{1,0:T(8,128)(2,1)S(1)} %get-tuple-element.30), channel_id=1, source_target_pairs={{0,1},{1,0},{2,3},{3,2},{4,5},{5,4},{6,7},{7,6},{8,9},{9,8},{10,11... | collective-permute-start | bytes 1572872 | tf_op jit(solution)/shard_map/ppermute | solution.py:57
  98.1 14.2 %collective-permute-start.26 = (bf16[256,1024]{1,0:T(8,128)(2,1)S(1)}, bf16[256,1024]{1,0:T(8,128)(2,1)S(1)}, u32[]{:S(2)}, u32[]{:S(2)}) collective-permute-start(bf16[256,1024]{1,0:T(8,128)(2,1)S(1)} %get-tuple-element.30), channel_id=1, source_target_pairs={{0,2},{1,3},{2,0},{3,1},{4,6},{5,7},{6,4},{7,5},{8,10},{9,11},{10,... | collective-permute-start | bytes 1572872 | tf_op jit(solution)/shard_map/ppermute | solution.py:57
  99.6 13.9 %collective-permute-start.23 = (bf16[256,1024]{1,0:T(8,128)(2,1)S(1)}, bf16[256,1024]{1,0:T(8,128)(2,1)S(1)}, u32[]{:S(2)}, u32[]{:S(2)}) collective-permute-start(bf16[256,1024]{1,0:T(8,128)(2,1)S(1)} %get-tuple-element.29), channel_id=1, source_target_pairs={{0,16},{1,17},{2,18},{3,19},{4,20},{5,21},{6,22},{7,23},{8,24},{9,... | collective-permute-start | bytes 1572872 | tf_op jit(solution)/shard_map/ppermute | solution.py:71
  103.7 10.4 %collective-permute-start.24 = (f32[256,256]{1,0:T(8,128)S(1)}, f32[256,256]{1,0:T(8,128)S(1)}, u32[]{:S(2)}, u32[]{:S(2)}) collective-permute-start(f32[256,256]{1,0:T(8,128)S(1)} %convolution_add_fusion.4), channel_id=1, source_target_pairs={{0,0},{1,1},{2,2},{3,3},{4,4},{5,5},{6,6},{7,7},{8,12},{9,13},{10,... | collective-permute-start | bytes 786440 | tf_op jit(solution)/shard_map/ppermute | solution.py:63
  115.1 2.4 %collective-permute-start.28 = (f32[256,768]{1,0:T(8,128)S(1)}, f32[256,768]{1,0:T(8,128)S(1)}, u32[]{:S(2)}, u32[]{:S(2)}) collective-permute-start(f32[256,768]{1,0:T(8,128)S(1)} %pad_maximum_fusion.2), channel_id=1, source_target_pairs={{0,0},{1,1},{2,2},{3,3},{4,4},{5,5},{6,6},{7,7},{8,12},{9,13},{10,... | collective-permute-start | bytes 2359304 | tf_op jit(solution)/shard_map/ppermute | solution.py:63
  119.0 3.6 %collective-permute-start.31 = (f32[256]{0:T(256)S(1)}, f32[256]{0:T(256)S(1)}, u32[]{:S(2)}, u32[]{:S(2)}) collective-permute-start(f32[256]{0:T(256)S(1)} %get-tuple-element.42), channel_id=1, source_target_pairs={{0,16},{1,17},{2,18},{3,19},{4,20},{5,21},{6,22},{7,23},{8,24},{9,... | collective-permute-start | bytes 3080 | tf_op jit(solution)/shard_map/ppermute | solution.py:71
  120.5 3.6 %collective-permute-start.32 = (f32[256]{0:T(256)S(1)}, f32[256]{0:T(256)S(1)}, u32[]{:S(2)}, u32[]{:S(2)}) collective-permute-start(f32[256]{0:T(256)S(1)} %get-tuple-element.42), channel_id=1, source_target_pairs={{0,16},{1,17},{2,18},{3,19},{4,20},{5,21},{6,22},{7,23},{8,28},{9,... | collective-permute-start | bytes 3080 | tf_op jit(solution)/shard_map/ppermute | solution.py:71
  121.1 3.0 %collective-permute-start.30 = (f32[256]{0:T(256)S(1)}, f32[256]{0:T(256)S(1)}, u32[]{:S(2)}, u32[]{:S(2)}) collective-permute-start(f32[256]{0:T(256)S(1)} %get-tuple-element.41), channel_id=1, source_target_pairs={{0,0},{1,1},{2,2},{3,3},{4,4},{5,5},{6,6},{7,7},{8,12},{9,13},{10,... | collective-permute-start | bytes 3080 | tf_op jit(solution)/shard_map/ppermute | solution.py:63
  124.2 3.6 %collective-permute-start.34 = (f32[256]{0:T(256)S(1)}, f32[256]{0:T(256)S(1)}, u32[]{:S(2)}, u32[]{:S(2)}) collective-permute-start(f32[256]{0:T(256)S(1)} %add_add_fusion.3), channel_id=1, source_target_pairs={{0,2},{1,3},{2,0},{3,1},{4,6},{5,7},{6,4},{7,5},{8,10},{9,11},{10,... | collective-permute-start | bytes 3080 | tf_op jit(solution)/shard_map/ppermute | solution.py:57
  125.4 3.0 %collective-permute-start.35 = (f32[256]{0:T(256)S(1)}, f32[256]{0:T(256)S(1)}, u32[]{:S(2)}, u32[]{:S(2)}) collective-permute-start(f32[256]{0:T(256)S(1)} %add_add_fusion.3), channel_id=1, source_target_pairs={{0,3},{1,2},{2,1},{3,0},{4,7},{5,6},{6,5},{7,4},{8,11},{9,10},{10,... | collective-permute-start | bytes 3080 | tf_op jit(solution)/shard_map/ppermute | solution.py:57
  128.4 27.2 %collective-permute-start.36 = (f32[1024]{0:T(1024)S(1)}, f32[1024]{0:T(1024)S(1)}, u32[]{:S(2)}, u32[]{:S(2)}) collective-permute-start(f32[1024]{0:T(1024)S(1)} %pad_maximum_fusion.4), channel_id=1, source_target_pairs={{0,8},{1,9},{2,10},{3,11},{4,12},{5,13},{6,14},{7,15},{8,0},{9,1},... | collective-permute-start | bytes 12296 | tf_op jit(solution)/shard_map/ppermute | solution.py:63
  (9 other events, 63.1 us)

commit v8 on v7

--- a/solution.py
+++ b/solution.py
@@ -58,7 +58,8 @@
 
     def along_z(value, to):
         pairs = [
-            (place(z, x, c), place(to[z], x, c)) for z in range(nz) for x in range(nx) for c in range(CORES)
+            (place(z, x, c), place(to[z], x, c ^ (to[z] == z)))
+            for z in range(nz) for x in range(nx) for c in range(CORES)
         ]
         return lax.ppermute(value, "tgt", pairs)
 

time: 157 us -> 149 us (0.949)
  starting transfers between devices: 56.3 us -> 46.7 us
  waiting for transfers between devices: 71.1 us -> 73.2 us
    ppermute x9, starting transfers between devices: 35.1 us -> 25.1 us  [along_z(): return lax.ppermute(value, 'tgt', pairs)]
  transfers between devices with their start and end apart: 37 -> 37, of which waited for: 18 -> 19; matrix products, arithmetic and copies ran while one was open for 14% -> 14% of each run, Pallas kernels for 0% -> 0%
where the time goes in v8:
time: 149 us
  waiting for transfers between devices  73.2 us (49%)
  starting transfers between devices  46.7 us (31%)
  matrix products  15.7 us (11%)
  local copies, waits for them, and re-layouts  6.85 us (5%)
  other arithmetic  5.84 us (4%)
    ppermute x24, waiting for transfers between devices, inner(): return lax.ppermute(value, 'tgt', pairs)  38.5 us
    ppermute x9, starting transfers between devices, along_z(): return lax.ppermute(value, 'tgt', pairs)  25.1 us
    ppermute x9, waiting for transfers between devices, along_z(): return lax.ppermute(value, 'tgt', pairs)  20.3 us
    ppermute x24, starting transfers between devices, inner(): return lax.ppermute(value, 'tgt', pairs)  16.4 us
    ppermute x4, waiting for transfers between devices, over_pool(): return lax.ppermute(value, ('pool', 'tgt'), pairs)  14.5 us
    dot_general x16, matrix products, matmul(): lax.dot_general(a, b, (((1,), (0,)), ((), ())), preferred_element_type=F32)  10.8 us
    ppermute x4, starting transfers between devices, over_pool(): return lax.ppermute(value, ('pool', 'tgt'), pairs)  5.2 us
    dot_general x10, matrix products, matmul_t(): lax.dot_general(a, b, (((1,), (1,)), ((), ())), preferred_element_type=F32)  4.88 us
  transfers between devices with their start and end apart: 37, of which 19 were waited for; matrix products, arithmetic and copies ran while one was open for 14% of the time, Pallas kernels for 0%

profile of v8, /device:TPU:0, one launch (start us, length us, event | category | flops | bytes accessed | tf_op | source)
XLA Modules:
  0.0 148.8 jit_solution(14641540182361748476)
XLA Ops:
  0.0 2.0 %constant_dynamic-slice_fusion = bf16[256,1024]{1,0:T(8,128)(2,1)} fusion(bf16[256,4096]{1,0:T(8,128)(2,1)} %param.7, s32[]{:T(128)S(6)} %select_n.171), kind=kLoop, calls=%fused_computation.148 | loop fusion | bytes 1048580 | tf_op jit(solution)/shard_map/dynamic_slice | solution.py:111
  2.0 2.9 %collective-permute-start = (bf16[256,1024]{1,0:T(8,128)(2,1)}, bf16[256,1024]{1,0:T(8,128)(2,1)}, u32[]{:S(2)}, u32[]{:S(2)}) collective-permute-start(bf16[256,1024]{1,0:T(8,128)(2,1)} %constant_dynamic-slice_fusion), channel_id=1, source_target_pairs={{0,2},{1,3},{2,0},{3,1},{4,6},{5,7},{6,4},{7,5},{8,10},{9,11},{10,... | collective-permute-start | bytes 1572872 | tf_op jit(solution)/shard_map/ppermute | solution.py:57
  5.7 3.9 %gather_fusion = bf16[1024,256]{1,0:T(8,128)(2,1)S(1)} fusion(bf16[4096,256]{1,0:T(8,128)(2,1)S(1)} %copy-done, s32[1024]{0:T(1024)S(1)} %fusion.31), kind=kCustom, calls=%fused_computation | custom fusion | bytes 1052672 | tf_op jit(solution)/shard_map/gather | solution.py:98
  9.7 7.5 %collective-permute-done = bf16[256,1024]{1,0:T(8,128)(2,1)} collective-permute-done((bf16[256,1024]{1,0:T(8,128)(2,1)}, bf16[256,1024]{1,0:T(8,128)(2,1)}, u32[]{:S(2)}, u32[]{:S(2)}) %collective-permute-start) | collective-permute-done | bytes 524320 | tf_op jit(solution)/shard_map/ppermute | solution.py:57
  18.1 1.8 %collective-permute-start.1 = (bf16[512,256]{1,0:T(8,128)(2,1)S(1)}, bf16[512,256]{1,0:T(8,128)(2,1)S(1)}, u32[]{:S(2)}, u32[]{:S(2)}) collective-permute-start(bf16[512,256]{1,0:T(8,128)(2,1)S(1)} %get-tuple-element.28), channel_id=1, source_target_pairs={{0,2},{1,3},{2,0},{3,1},{4,6},{5,7},{6,4},{7,5},{8,10},{9,11},{10,... | collective-permute-start | bytes 786440 | tf_op jit(solution)/shard_map/ppermute | solution.py:57
  19.9 1.5 fusion.95
  22.0 4.8 %collective-permute-done.1 = bf16[512,256]{1,0:T(8,128)(2,1)S(1)} collective-permute-done((bf16[512,256]{1,0:T(8,128)(2,1)S(1)}, bf16[512,256]{1,0:T(8,128)(2,1)S(1)}, u32[]{:S(2)}, u32[]{:S(2)}) %collective-permute-start.1) | collective-permute-done | bytes 262176 | tf_op jit(solution)/shard_map/ppermute | solution.py:57
  26.7 1.5 fusion.96
  28.2 1.5 fusion.97
  31.7 2.3 %collective-permute-start.10 = (bf16[512,1024]{1,0:T(8,128)(2,1)S(1)}, bf16[512,1024]{1,0:T(8,128)(2,1)S(1)}, u32[]{:S(2)}, u32[]{:S(2)}) collective-permute-start(bf16[512,1024]{1,0:T(8,128)(2,1)S(1)} %add_convert_fusion.1), channel_id=1, source_target_pairs={{0,4},{1,5},{2,6},{3,7},{4,0},{5,1},{6,2},{7,3},{8,12},{9,13},{10,... | collective-permute-start | bytes 3145736 | tf_op jit(solution)/shard_map/ppermute | solution.py:64
  34.2 1.9 %collective-permute-start.6 = (bf16[256,1024]{1,0:T(8,128)(2,1)S(1)}, bf16[256,1024]{1,0:T(8,128)(2,1)S(1)}, u32[]{:S(2)}, u32[]{:S(2)}) collective-permute-start(bf16[256,1024]{1,0:T(8,128)(2,1)S(1)} %get-tuple-element.21), channel_id=1, source_target_pairs={{0,2},{1,3},{2,0},{3,1},{4,6},{5,7},{6,4},{7,5},{8,10},{9,11},{10,... | collective-permute-start | bytes 1572872 | tf_op jit(solution)/shard_map/ppermute | solution.py:57
  37.5 1.3 collective-permute-done.7
  39.9 17.9 %collective-permute-done.10 = bf16[512,1024]{1,0:T(8,128)(2,1)S(1)} collective-permute-done((bf16[512,1024]{1,0:T(8,128)(2,1)S(1)}, bf16[512,1024]{1,0:T(8,128)(2,1)S(1)}, u32[]{:S(2)}, u32[]{:S(2)}) %collective-permute-start.10) | collective-permute-done | bytes 1048608 | tf_op jit(solution)/shard_map/ppermute | solution.py:64
  57.8 1.8 %collective-permute-done.9 = bf16[256,1024]{1,0:T(8,128)(2,1)S(1)} collective-permute-done((bf16[256,1024]{1,0:T(8,128)(2,1)S(1)}, bf16[256,1024]{1,0:T(8,128)(2,1)S(1)}, u32[]{:S(2)}, u32[]{:S(2)}) %collective-permute-start.9) | collective-permute-done | bytes 524320 | tf_op jit(solution)/shard_map/ppermute | solution.py:57
  63.0 1.0 add_convert_fusion.2
  64.7 1.6 %collective-permute-start.15 = (bf16[256,1024]{1,0:T(8,128)(2,1)S(1)}, bf16[256,1024]{1,0:T(8,128)(2,1)S(1)}, u32[]{:S(2)}, u32[]{:S(2)}) collective-permute-start(bf16[256,1024]{1,0:T(8,128)(2,1)S(1)} %get-tuple-element.32), channel_id=1, source_target_pairs={{0,16},{1,17},{2,18},{3,19},{4,20},{5,21},{6,22},{7,23},{8,24},{9,... | collective-permute-start | bytes 1572872 | tf_op jit(solution)/shard_map/ppermute | solution.py:72
  66.3 1.5 %collective-permute-start.18 = (bf16[256,1024]{1,0:T(8,128)(2,1)S(1)}, bf16[256,1024]{1,0:T(8,128)(2,1)S(1)}, u32[]{:S(2)}, u32[]{:S(2)}) collective-permute-start(bf16[256,1024]{1,0:T(8,128)(2,1)S(1)} %get-tuple-element.31), channel_id=1, source_target_pairs={{0,2},{1,3},{2,0},{3,1},{4,6},{5,7},{6,4},{7,5},{8,10},{9,11},{10,... | collective-permute-start | bytes 1572872 | tf_op jit(solution)/shard_map/ppermute | solution.py:57
  68.5 10.2 %collective-permute-done.15 = bf16[256,1024]{1,0:T(8,128)(2,1)S(1)} collective-permute-done((bf16[256,1024]{1,0:T(8,128)(2,1)S(1)}, bf16[256,1024]{1,0:T(8,128)(2,1)S(1)}, u32[]{:S(2)}, u32[]{:S(2)}) %collective-permute-start.15) | collective-permute-done | bytes 524320 | tf_op jit(solution)/shard_map/ppermute | solution.py:72
  78.7 1.5 collective-permute-start.16
  81.0 10.9 %collective-permute-done.16 = bf16[256,1024]{1,0:T(8,128)(2,1)S(1)} collective-permute-done((bf16[256,1024]{1,0:T(8,128)(2,1)S(1)}, bf16[256,1024]{1,0:T(8,128)(2,1)S(1)}, u32[]{:S(2)}, u32[]{:S(2)}) %collective-permute-start.16) | collective-permute-done | bytes 524320 | tf_op jit(solution)/shard_map/ppermute | solution.py:57
  94.0 1.0 add_convert_fusion
  95.3 1.5 %collective-permute-start.26 = (bf16[256,1024]{1,0:T(8,128)(2,1)S(1)}, bf16[256,1024]{1,0:T(8,128)(2,1)S(1)}, u32[]{:S(2)}, u32[]{:S(2)}) collective-permute-start(bf16[256,1024]{1,0:T(8,128)(2,1)S(1)} %get-tuple-element.30), channel_id=1, source_target_pairs={{0,2},{1,3},{2,0},{3,1},{4,6},{5,7},{6,4},{7,5},{8,10},{9,11},{10,... | collective-permute-start | bytes 1572872 | tf_op jit(solution)/shard_map/ppermute | solution.py:57
  96.8 1.5 %collective-permute-start.23 = (bf16[256,1024]{1,0:T(8,128)(2,1)S(1)}, bf16[256,1024]{1,0:T(8,128)(2,1)S(1)}, u32[]{:S(2)}, u32[]{:S(2)}) collective-permute-start(bf16[256,1024]{1,0:T(8,128)(2,1)S(1)} %get-tuple-element.29), channel_id=1, source_target_pairs={{0,16},{1,17},{2,18},{3,19},{4,20},{5,21},{6,22},{7,23},{8,24},{9,... | collective-permute-start | bytes 1572872 | tf_op jit(solution)/shard_map/ppermute | solution.py:72
  101.3 8.2 %collective-permute-done.26 = bf16[256,1024]{1,0:T(8,128)(2,1)S(1)} collective-permute-done((bf16[256,1024]{1,0:T(8,128)(2,1)S(1)}, bf16[256,1024]{1,0:T(8,128)(2,1)S(1)}, u32[]{:S(2)}, u32[]{:S(2)}) %collective-permute-start.26) | collective-permute-done | bytes 524320 | tf_op jit(solution)/shard_map/ppermute | solution.py:57
  109.5 1.2 collective-permute-done.23
  116.2 1.6 %collective-permute-start.31 = (f32[256]{0:T(256)S(1)}, f32[256]{0:T(256)S(1)}, u32[]{:S(2)}, u32[]{:S(2)}) collective-permute-start(f32[256]{0:T(256)S(1)} %get-tuple-element.42), channel_id=1, source_target_pairs={{0,16},{1,17},{2,18},{3,19},{4,20},{5,21},{6,22},{7,23},{8,24},{9,... | collective-permute-start | bytes 3080 | tf_op jit(solution)/shard_map/ppermute | solution.py:72
  118.3 1.5 %collective-permute-done.31 = f32[256]{0:T(256)S(1)} collective-permute-done((f32[256]{0:T(256)S(1)}, f32[256]{0:T(256)S(1)}, u32[]{:S(2)}, u32[]{:S(2)}) %collective-permute-start.31) | collective-permute-done | bytes 1056 | tf_op jit(solution)/shard_map/ppermute | solution.py:72
  119.8 1.5 %collective-permute-done.32 = f32[256]{0:T(256)S(1)} collective-permute-done((f32[256]{0:T(256)S(1)}, f32[256]{0:T(256)S(1)}, u32[]{:S(2)}, u32[]{:S(2)}) %collective-permute-start.32) | collective-permute-done | bytes 1056 | tf_op jit(solution)/shard_map/ppermute | solution.py:72
  121.4 1.2 collective-permute-start.34
  123.3 1.8 %collective-permute-done.34 = f32[256]{0:T(256)S(1)} collective-permute-done((f32[256]{0:T(256)S(1)}, f32[256]{0:T(256)S(1)}, u32[]{:S(2)}, u32[]{:S(2)}) %collective-permute-start.34) | collective-permute-done | bytes 1056 | tf_op jit(solution)/shard_map/ppermute | solution.py:57
  125.7 21.0 %collective-permute-start.36 = (f32[1024]{0:T(1024)S(1)}, f32[1024]{0:T(1024)S(1)}, u32[]{:S(2)}, u32[]{:S(2)}) collective-permute-start(f32[1024]{0:T(1024)S(1)} %pad_maximum_fusion.4), channel_id=1, source_target_pairs={{0,8},{1,9},{2,10},{3,11},{4,12},{5,13},{6,14},{7,15},{8,0},{9,1},... | collective-permute-start | bytes 12296 | tf_op jit(solution)/shard_map/ppermute | solution.py:64
  146.7 1.6 %collective-permute-done.36 = f32[1024]{0:T(1024)S(1)} collective-permute-done((f32[1024]{0:T(1024)S(1)}, f32[1024]{0:T(1024)S(1)}, u32[]{:S(2)}, u32[]{:S(2)}) %collective-permute-start.36) | collective-permute-done | bytes 4128 | tf_op jit(solution)/shard_map/ppermute | solution.py:64
  (121 shorter events, 25.5 us)
Async XLA Ops:
  2.0 15.2 %collective-permute-start = (bf16[256,1024]{1,0:T(8,128)(2,1)}, bf16[256,1024]{1,0:T(8,128)(2,1)}, u32[]{:S(2)}, u32[]{:S(2)}) collective-permute-start(bf16[256,1024]{1,0:T(8,128)(2,1)} %constant_dynamic-slice_fusion), channel_id=1, source_target_pairs={{0,2},{1,3},{2,0},{3,1},{4,6},{5,7},{6,4},{7,5},{8,10},{9,11},{10,... | collective-permute-start | bytes 1572872 | tf_op jit(solution)/shard_map/ppermute | solution.py:57
  4.9 23.3 %collective-permute-start.3 = (bf16[256,1024]{1,0:T(8,128)(2,1)}, bf16[256,1024]{1,0:T(8,128)(2,1)}, u32[]{:S(2)}, u32[]{:S(2)}) collective-permute-start(bf16[256,1024]{1,0:T(8,128)(2,1)} %constant_dynamic-slice_fusion), channel_id=1, source_target_pairs={{0,1},{1,0},{2,3},{3,2},{4,5},{5,4},{6,7},{7,6},{8,9},{9,8},{10,11... | collective-permute-start | bytes 1572872 | tf_op jit(solution)/shard_map/ppermute | solution.py:57
  18.1 8.6 %collective-permute-start.1 = (bf16[512,256]{1,0:T(8,128)(2,1)S(1)}, bf16[512,256]{1,0:T(8,128)(2,1)S(1)}, u32[]{:S(2)}, u32[]{:S(2)}) collective-permute-start(bf16[512,256]{1,0:T(8,128)(2,1)S(1)} %get-tuple-element.28), channel_id=1, source_target_pairs={{0,2},{1,3},{2,0},{3,1},{4,6},{5,7},{6,4},{7,5},{8,10},{9,11},{10,... | collective-permute-start | bytes 786440 | tf_op jit(solution)/shard_map/ppermute | solution.py:57
  21.4 6.8 %collective-permute-start.2 = (bf16[512,256]{1,0:T(8,128)(2,1)S(1)}, bf16[512,256]{1,0:T(8,128)(2,1)S(1)}, u32[]{:S(2)}, u32[]{:S(2)}) collective-permute-start(bf16[512,256]{1,0:T(8,128)(2,1)S(1)} %get-tuple-element.27), channel_id=1, source_target_pairs={{0,1},{1,0},{2,3},{3,2},{4,5},{5,4},{6,7},{7,6},{8,9},{9,8},{10,11... | collective-permute-start | bytes 786440 | tf_op jit(solution)/shard_map/ppermute | solution.py:57
  21.5 8.8 %collective-permute-start.4 = (bf16[512,256]{1,0:T(8,128)(2,1)S(1)}, bf16[512,256]{1,0:T(8,128)(2,1)S(1)}, u32[]{:S(2)}, u32[]{:S(2)}) collective-permute-start(bf16[512,256]{1,0:T(8,128)(2,1)S(1)} %get-tuple-element.26), channel_id=1, source_target_pairs={{0,3},{1,2},{2,1},{3,0},{4,7},{5,6},{6,5},{7,4},{8,11},{9,10},{10,... | collective-permute-start | bytes 786440 | tf_op jit(solution)/shard_map/ppermute | solution.py:57
  21.9 8.4 %collective-permute-start.5 = (bf16[256,1024]{1,0:T(8,128)(2,1)}, bf16[256,1024]{1,0:T(8,128)(2,1)S(1)}, u32[]{:S(2)}, u32[]{:S(2)}) collective-permute-start(bf16[256,1024]{1,0:T(8,128)(2,1)} %collective-permute-done), channel_id=1, source_target_pairs={{0,1},{1,0},{2,3},{3,2},{4,5},{5,4},{6,7},{7,6},{8,9},{9,8},{10,11... | collective-permute-start | bytes 1572872 | tf_op jit(solution)/shard_map/ppermute | solution.py:57
  30.7 9.1 %collective-permute-start.11 = (bf16[512,1024]{1,0:T(8,128)(2,1)S(1)}, bf16[512,1024]{1,0:T(8,128)(2,1)S(1)}, u32[]{:S(2)}, u32[]{:S(2)}) collective-permute-start(bf16[512,1024]{1,0:T(8,128)(2,1)S(1)} %add_convert_fusion.1), channel_id=1, source_target_pairs={{0,1},{1,0},{2,3},{3,2},{4,8},{5,9},{6,10},{7,11},{8,4},{9,5},{10,... | collective-permute-start | bytes 3145736 | tf_op jit(solution)/shard_map/ppermute | solution.py:64
  31.7 26.1 %collective-permute-start.10 = (bf16[512,1024]{1,0:T(8,128)(2,1)S(1)}, bf16[512,1024]{1,0:T(8,128)(2,1)S(1)}, u32[]{:S(2)}, u32[]{:S(2)}) collective-permute-start(bf16[512,1024]{1,0:T(8,128)(2,1)S(1)} %add_convert_fusion.1), channel_id=1, source_target_pairs={{0,4},{1,5},{2,6},{3,7},{4,0},{5,1},{6,2},{7,3},{8,12},{9,13},{10,... | collective-permute-start | bytes 3145736 | tf_op jit(solution)/shard_map/ppermute | solution.py:64
  34.2 23.6 %collective-permute-start.6 = (bf16[256,1024]{1,0:T(8,128)(2,1)S(1)}, bf16[256,1024]{1,0:T(8,128)(2,1)S(1)}, u32[]{:S(2)}, u32[]{:S(2)}) collective-permute-start(bf16[256,1024]{1,0:T(8,128)(2,1)S(1)} %get-tuple-element.21), channel_id=1, source_target_pairs={{0,2},{1,3},{2,0},{3,1},{4,6},{5,7},{6,4},{7,5},{8,10},{9,11},{10,... | collective-permute-start | bytes 1572872 | tf_op jit(solution)/shard_map/ppermute | solution.py:57
  36.1 3.3 %collective-permute-start.8 = (bf16[256,1024]{1,0:T(8,128)(2,1)S(1)}, bf16[256,1024]{1,0:T(8,128)(2,1)S(1)}, u32[]{:S(2)}, u32[]{:S(2)}) collective-permute-start(bf16[256,1024]{1,0:T(8,128)(2,1)S(1)} %get-tuple-element.21), channel_id=1, source_target_pairs={{0,1},{1,0},{2,3},{3,2},{4,5},{5,4},{6,7},{7,6},{8,9},{9,8},{10,11... | collective-permute-start | bytes 1572872 | tf_op jit(solution)/shard_map/ppermute | solution.py:57
  36.1 2.7 %collective-permute-start.7 = (bf16[256,1024]{1,0:T(8,128)(2,1)S(1)}, bf16[256,1024]{1,0:T(8,128)(2,1)S(1)}, u32[]{:S(2)}, u32[]{:S(2)}) collective-permute-start(bf16[256,1024]{1,0:T(8,128)(2,1)S(1)} %get-tuple-element.22), channel_id=1, source_target_pairs={{0,1},{1,0},{2,3},{3,2},{4,5},{5,4},{6,7},{7,6},{8,9},{9,8},{10,11... | collective-permute-start | bytes 1572872 | tf_op jit(solution)/shard_map/ppermute | solution.py:57
  38.8 20.8 %collective-permute-start.9 = (bf16[256,1024]{1,0:T(8,128)(2,1)S(1)}, bf16[256,1024]{1,0:T(8,128)(2,1)S(1)}, u32[]{:S(2)}, u32[]{:S(2)}) collective-permute-start(bf16[256,1024]{1,0:T(8,128)(2,1)S(1)} %get-tuple-element.22), channel_id=1, source_target_pairs={{0,2},{1,3},{2,0},{3,1},{4,6},{5,7},{6,4},{7,5},{8,10},{9,11},{10,... | collective-permute-start | bytes 1572872 | tf_op jit(solution)/shard_map/ppermute | solution.py:57
  59.8 2.6 %collective-permute-start.12 = (bf16[256,1024]{1,0:T(8,128)(2,1)S(1)}, bf16[256,1024]{1,0:T(8,128)(2,1)S(1)}, u32[]{:S(2)}, u32[]{:S(2)}) collective-permute-start(bf16[256,1024]{1,0:T(8,128)(2,1)S(1)} %get-tuple-element.45), channel_id=1, source_target_pairs={{0,1},{1,0},{2,3},{3,2},{4,5},{5,4},{6,7},{7,6},{8,9},{9,8},{10,11... | collective-permute-start | bytes 1572872 | tf_op jit(solution)/shard_map/ppermute | solution.py:57
  63.9 17.0 %collective-permute-start.20 = (bf16[512,1024]{1,0:T(8,128)(2,1)S(1)}, bf16[512,1024]{1,0:T(8,128)(2,1)S(1)}, u32[]{:S(2)}, u32[]{:S(2)}) collective-permute-start(bf16[512,1024]{1,0:T(8,128)(2,1)S(1)} %get-tuple-element.19), channel_id=1, source_target_pairs={{0,1},{1,0},{2,3},{3,2},{4,5},{5,4},{6,7},{7,6},{8,12},{9,13},{10,... | collective-permute-start | bytes 3145736 | tf_op jit(solution)/shard_map/ppermute | solution.py:64
  64.2 4.0 %collective-permute-start.17 = (bf16[256,1024]{1,0:T(8,128)(2,1)S(1)}, bf16[256,1024]{1,0:T(8,128)(2,1)S(1)}, u32[]{:S(2)}, u32[]{:S(2)}) collective-permute-start(bf16[256,1024]{1,0:T(8,128)(2,1)S(1)} %slice_add_fusion), channel_id=1, source_target_pairs={{0,1},{1,0},{2,3},{3,2},{4,5},{5,4},{6,7},{7,6},{8,9},{9,8},{10,11... | collective-permute-start | bytes 1572872 | tf_op jit(solution)/shard_map/ppermute | solution.py:57
  64.7 14.0 %collective-permute-start.15 = (bf16[256,1024]{1,0:T(8,128)(2,1)S(1)}, bf16[256,1024]{1,0:T(8,128)(2,1)S(1)}, u32[]{:S(2)}, u32[]{:S(2)}) collective-permute-start(bf16[256,1024]{1,0:T(8,128)(2,1)S(1)} %get-tuple-element.32), channel_id=1, source_target_pairs={{0,16},{1,17},{2,18},{3,19},{4,20},{5,21},{6,22},{7,23},{8,24},{9,... | collective-permute-start | bytes 1572872 | tf_op jit(solution)/shard_map/ppermute | solution.py:72
  66.3 14.7 %collective-permute-start.19 = (bf16[512,1024]{1,0:T(8,128)(2,1)S(1)}, bf16[512,1024]{1,0:T(8,128)(2,1)S(1)}, u32[]{:S(2)}, u32[]{:S(2)}) collective-permute-start(bf16[512,1024]{1,0:T(8,128)(2,1)S(1)} %get-tuple-element.20), channel_id=1, source_target_pairs={{0,1},{1,0},{2,3},{3,2},{4,8},{5,9},{6,10},{7,11},{8,4},{9,5},{10,... | collective-permute-start | bytes 3145736 | tf_op jit(solution)/shard_map/ppermute | solution.py:64
  66.3 14.7 %collective-permute-start.18 = (bf16[256,1024]{1,0:T(8,128)(2,1)S(1)}, bf16[256,1024]{1,0:T(8,128)(2,1)S(1)}, u32[]{:S(2)}, u32[]{:S(2)}) collective-permute-start(bf16[256,1024]{1,0:T(8,128)(2,1)S(1)} %get-tuple-element.31), channel_id=1, source_target_pairs={{0,2},{1,3},{2,0},{3,1},{4,6},{5,7},{6,4},{7,5},{8,10},{9,11},{10,... | collective-permute-start | bytes 1572872 | tf_op jit(solution)/shard_map/ppermute | solution.py:57
  68.2 12.8 %collective-permute-start.14 = (bf16[256,1024]{1,0:T(8,128)(2,1)S(1)}, bf16[256,1024]{1,0:T(8,128)(2,1)S(1)}, u32[]{:S(2)}, u32[]{:S(2)}) collective-permute-start(bf16[256,1024]{1,0:T(8,128)(2,1)S(1)} %get-tuple-element.31), channel_id=1, source_target_pairs={{0,1},{1,0},{2,3},{3,2},{4,5},{5,4},{6,7},{7,6},{8,9},{9,8},{10,11... | collective-permute-start | bytes 1572872 | tf_op jit(solution)/shard_map/ppermute | solution.py:57
  78.7 13.1 %collective-permute-start.16 = (bf16[256,1024]{1,0:T(8,128)(2,1)S(1)}, bf16[256,1024]{1,0:T(8,128)(2,1)S(1)}, u32[]{:S(2)}, u32[]{:S(2)}) collective-permute-start(bf16[256,1024]{1,0:T(8,128)(2,1)S(1)} %slice_add_fusion), channel_id=1, source_target_pairs={{0,2},{1,3},{2,0},{3,1},{4,6},{5,7},{6,4},{7,5},{8,10},{9,11},{10,... | collective-permute-start | bytes 1572872 | tf_op jit(solution)/shard_map/ppermute | solution.py:57
  92.6 5.7 %collective-permute-start.25 = (bf16[256,1024]{1,0:T(8,128)(2,1)S(1)}, bf16[256,1024]{1,0:T(8,128)(2,1)S(1)}, u32[]{:S(2)}, u32[]{:S(2)}) collective-permute-start(bf16[256,1024]{1,0:T(8,128)(2,1)S(1)} %get-tuple-element.43), channel_id=1, source_target_pairs={{0,1},{1,0},{2,3},{3,2},{4,5},{5,4},{6,7},{7,6},{8,9},{9,8},{10,11... | collective-permute-start | bytes 1572872 | tf_op jit(solution)/shard_map/ppermute | solution.py:57
  95.1 4.9 %collective-permute-start.22 = (bf16[256,1024]{1,0:T(8,128)(2,1)S(1)}, bf16[256,1024]{1,0:T(8,128)(2,1)S(1)}, u32[]{:S(2)}, u32[]{:S(2)}) collective-permute-start(bf16[256,1024]{1,0:T(8,128)(2,1)S(1)} %get-tuple-element.30), channel_id=1, source_target_pairs={{0,1},{1,0},{2,3},{3,2},{4,5},{5,4},{6,7},{7,6},{8,9},{9,8},{10,11... | collective-permute-start | bytes 1572872 | tf_op jit(solution)/shard_map/ppermute | solution.py:57
  95.3 14.2 %collective-permute-start.26 = (bf16[256,1024]{1,0:T(8,128)(2,1)S(1)}, bf16[256,1024]{1,0:T(8,128)(2,1)S(1)}, u32[]{:S(2)}, u32[]{:S(2)}) collective-permute-start(bf16[256,1024]{1,0:T(8,128)(2,1)S(1)} %get-tuple-element.30), channel_id=1, source_target_pairs={{0,2},{1,3},{2,0},{3,1},{4,6},{5,7},{6,4},{7,5},{8,10},{9,11},{10,... | collective-permute-start | bytes 1572872 | tf_op jit(solution)/shard_map/ppermute | solution.py:57
  96.8 13.9 %collective-permute-start.23 = (bf16[256,1024]{1,0:T(8,128)(2,1)S(1)}, bf16[256,1024]{1,0:T(8,128)(2,1)S(1)}, u32[]{:S(2)}, u32[]{:S(2)}) collective-permute-start(bf16[256,1024]{1,0:T(8,128)(2,1)S(1)} %get-tuple-element.29), channel_id=1, source_target_pairs={{0,16},{1,17},{2,18},{3,19},{4,20},{5,21},{6,22},{7,23},{8,24},{9,... | collective-permute-start | bytes 1572872 | tf_op jit(solution)/shard_map/ppermute | solution.py:72
  101.2 10.2 %collective-permute-start.24 = (f32[256,256]{1,0:T(8,128)S(1)}, f32[256,256]{1,0:T(8,128)S(1)}, u32[]{:S(2)}, u32[]{:S(2)}) collective-permute-start(f32[256,256]{1,0:T(8,128)S(1)} %convolution_add_fusion.4), channel_id=1, source_target_pairs={{0,1},{1,0},{2,3},{3,2},{4,5},{5,4},{6,7},{7,6},{8,12},{9,13},{10,... | collective-permute-start | bytes 786440 | tf_op jit(solution)/shard_map/ppermute | solution.py:64
  112.3 2.4 %collective-permute-start.28 = (f32[256,768]{1,0:T(8,128)S(1)}, f32[256,768]{1,0:T(8,128)S(1)}, u32[]{:S(2)}, u32[]{:S(2)}) collective-permute-start(f32[256,768]{1,0:T(8,128)S(1)} %pad_maximum_fusion.2), channel_id=1, source_target_pairs={{0,1},{1,0},{2,3},{3,2},{4,5},{5,4},{6,7},{7,6},{8,12},{9,13},{10,... | collective-permute-start | bytes 2359304 | tf_op jit(solution)/shard_map/ppermute | solution.py:64
  116.2 3.6 %collective-permute-start.31 = (f32[256]{0:T(256)S(1)}, f32[256]{0:T(256)S(1)}, u32[]{:S(2)}, u32[]{:S(2)}) collective-permute-start(f32[256]{0:T(256)S(1)} %get-tuple-element.42), channel_id=1, source_target_pairs={{0,16},{1,17},{2,18},{3,19},{4,20},{5,21},{6,22},{7,23},{8,24},{9,... | collective-permute-start | bytes 3080 | tf_op jit(solution)/shard_map/ppermute | solution.py:72
  117.8 3.6 %collective-permute-start.32 = (f32[256]{0:T(256)S(1)}, f32[256]{0:T(256)S(1)}, u32[]{:S(2)}, u32[]{:S(2)}) collective-permute-start(f32[256]{0:T(256)S(1)} %get-tuple-element.42), channel_id=1, source_target_pairs={{0,16},{1,17},{2,18},{3,19},{4,20},{5,21},{6,22},{7,23},{8,28},{9,... | collective-permute-start | bytes 3080 | tf_op jit(solution)/shard_map/ppermute | solution.py:72
  118.3 3.1 %collective-permute-start.30 = (f32[256]{0:T(256)S(1)}, f32[256]{0:T(256)S(1)}, u32[]{:S(2)}, u32[]{:S(2)}) collective-permute-start(f32[256]{0:T(256)S(1)} %get-tuple-element.41), channel_id=1, source_target_pairs={{0,1},{1,0},{2,3},{3,2},{4,5},{5,4},{6,7},{7,6},{8,12},{9,13},{10,... | collective-permute-start | bytes 3080 | tf_op jit(solution)/shard_map/ppermute | solution.py:64
  121.4 3.6 %collective-permute-start.34 = (f32[256]{0:T(256)S(1)}, f32[256]{0:T(256)S(1)}, u32[]{:S(2)}, u32[]{:S(2)}) collective-permute-start(f32[256]{0:T(256)S(1)} %add_add_fusion.3), channel_id=1, source_target_pairs={{0,2},{1,3},{2,0},{3,1},{4,6},{5,7},{6,4},{7,5},{8,10},{9,11},{10,... | collective-permute-start | bytes 3080 | tf_op jit(solution)/shard_map/ppermute | solution.py:57
  122.7 3.0 %collective-permute-start.35 = (f32[256]{0:T(256)S(1)}, f32[256]{0:T(256)S(1)}, u32[]{:S(2)}, u32[]{:S(2)}) collective-permute-start(f32[256]{0:T(256)S(1)} %add_add_fusion.3), channel_id=1, source_target_pairs={{0,3},{1,2},{2,1},{3,0},{4,7},{5,6},{6,5},{7,4},{8,11},{9,10},{10,... | collective-permute-start | bytes 3080 | tf_op jit(solution)/shard_map/ppermute | solution.py:57
  125.7 22.6 %collective-permute-start.36 = (f32[1024]{0:T(1024)S(1)}, f32[1024]{0:T(1024)S(1)}, u32[]{:S(2)}, u32[]{:S(2)}) collective-permute-start(f32[1024]{0:T(1024)S(1)} %pad_maximum_fusion.4), channel_id=1, source_target_pairs={{0,8},{1,9},{2,10},{3,11},{4,12},{5,13},{6,14},{7,15},{8,0},{9,1},... | collective-permute-start | bytes 12296 | tf_op jit(solution)/shard_map/ppermute | solution.py:64
  (9 other events, 57.1 us)

commit v9 on v8

--- a/solution.py
+++ b/solution.py
@@ -24,8 +24,8 @@
 
 
 def fence(first, second, others):
-    done = lax.optimization_barrier(token(first))
-    done = lax.optimization_barrier(token(second) + done)
+    done = lax.optimization_barrier(token(*first))
+    done = lax.optimization_barrier(token(*second) + done)
     return token(*others) + done
 
 
@@ -137,9 +137,10 @@
         step2 = along_z(first, middle)
         own2 = behind(factor_own([0, 0, 0, 0]), start)
         own3 = behind(factor_own([1, 1, 1, 2]), start)
-        flip2, flip3 = inner(own2, 0, 1), inner(own3, 0, 1)
+        own4 = behind(factor_own([3, 3, 3, 3]), start)
+        flip2, flip3, flip4 = inner(own2, 0, 1), inner(own3, 0, 1), inner(own4, 0, 1)
         moved2, moved3 = factor_x(own2), factor_x(own3)
-        done = fence(step2, step1, [flip2, flip3, *moved2, *moved3])
+        done = fence([step2, step1], [*moved2, *moved3], [flip2, flip3, flip4])
         moved2, moved3 = [behind(v, done) for v in moved2], [behind(v, done) for v in moved3]
         second = partial([own2] + moved2 + [flip2] + factor_flip(moved2))
         third = partial([own3] + moved3 + [flip3] + factor_flip(moved3))
@@ -148,17 +149,16 @@
         step3 = along_z(behind(second, start).astype(BF), owners)
         step4 = along_z((behind(second, start) + step1.astype(F32)).astype(BF), middle)
         white_a = (third + step1.astype(F32) + jnp.where(top, 0.0, step2.astype(F32)) + start).astype(BF)
-        own4 = behind(factor_own([3, 3, 3, 3]), start)
-        flip4, moved4 = inner(own4, 0, 1), factor_x(own4)
+        moved4 = factor_x(behind(own4, start))
         t_a, p_a = white_a[:count_t], white_a[count_t:]
-        t_flip_a = inner(t_a, 0, 1)
         t_moved_a = [inner(t_a, s, 0) for s in range(1, nx)]
         p_moved_a = [over_pool(p_a, s) for s in range(1, n_pool)]
-        done = fence(step3, step4, [flip4, *moved4, t_flip_a, *t_moved_a, *p_moved_a])
+        done = fence([step3, step4], [*moved4, *t_moved_a], p_moved_a)
 
         moved4 = [behind(v, done) for v in moved4]
         fourth = partial([own4] + moved4 + [flip4] + factor_flip(moved4))
         t_moved_a = [behind(v, done) for v in t_moved_a]
+        t_flip_a = inner(behind(t_a, done), 0, 1)
         white_b = (jnp.where(top, fourth, second + step3.astype(F32) + step4.astype(F32)) + done).astype(BF)
         t_b, p_b = white_b[:count_t], white_b[count_t:]
         t_moved_b = [inner(t_b, s, 0) for s in range(1, nx)]

time: 149 us -> 148 us (level)
  waiting for transfers between devices: 73.2 us -> 71.6 us
    ppermute x4, waiting for transfers between devices: 14.5 us -> 4.54 us  [over_pool(): return lax.ppermute(value, ('pool', 'tgt'), pairs)]
    ppermute x24, waiting for transfers between devices: 38.5 us -> 47.3 us  [inner(): return lax.ppermute(value, 'tgt', pairs)]
  transfers between devices with their start and end apart: 37 -> 37, of which waited for: 19 -> 19; matrix products, arithmetic and copies ran while one was open for 14% -> 15% of each run, Pallas kernels for 0% -> 0%
where the time goes in v9:
time: 148 us; the launch traced here: 147 us
  waiting for transfers between devices  71.6 us (48%)
  starting transfers between devices  46.7 us (32%)
  matrix products  15.6 us (11%)
  local copies, waits for them, and re-layouts  6.85 us (5%)
  other arithmetic  6.11 us (4%)
    ppermute x24, waiting for transfers between devices, inner(): return lax.ppermute(value, 'tgt', pairs)  47.3 us
    ppermute x9, starting transfers between devices, along_z(): return lax.ppermute(value, 'tgt', pairs)  25.7 us
    ppermute x9, waiting for transfers between devices, along_z(): return lax.ppermute(value, 'tgt', pairs)  19.7 us
    ppermute x24, starting transfers between devices, inner(): return lax.ppermute(value, 'tgt', pairs)  15.8 us
    dot_general x16, matrix products, matmul(): lax.dot_general(a, b, (((1,), (0,)), ((), ())), preferred_element_type=F32)  10.8 us
    ppermute x4, starting transfers between devices, over_pool(): return lax.ppermute(value, ('pool', 'tgt'), pairs)  5.14 us
    dot_general x10, matrix products, matmul_t(): lax.dot_general(a, b, (((1,), (1,)), ((), ())), preferred_element_type=F32)  4.7 us
    ppermute x4, waiting for transfers between devices, over_pool(): return lax.ppermute(value, ('pool', 'tgt'), pairs)  4.54 us
  transfers between devices with their start and end apart: 37, of which 19 were waited for; matrix products, arithmetic and copies ran while one was open for 15% of the time, Pallas kernels for 0%

profile of v9, /device:TPU:0, one launch (start us, length us, event | category | flops | bytes accessed | tf_op | source)
XLA Modules:
  0.0 147.3 jit_solution(17429138337802196254)
XLA Ops:
  0.0 2.0 %constant_dynamic-slice_fusion = bf16[256,1024]{1,0:T(8,128)(2,1)} fusion(bf16[256,4096]{1,0:T(8,128)(2,1)} %param.7, s32[]{:T(128)S(6)} %select_n.171), kind=kLoop, calls=%fused_computation.146 | loop fusion | bytes 1048580 | tf_op jit(solution)/shard_map/dynamic_slice | solution.py:111
  2.0 2.9 %collective-permute-start = (bf16[256,1024]{1,0:T(8,128)(2,1)}, bf16[256,1024]{1,0:T(8,128)(2,1)}, u32[]{:S(2)}, u32[]{:S(2)}) collective-permute-start(bf16[256,1024]{1,0:T(8,128)(2,1)} %constant_dynamic-slice_fusion), channel_id=1, source_target_pairs={{0,2},{1,3},{2,0},{3,1},{4,6},{5,7},{6,4},{7,5},{8,10},{9,11},{10,... | collective-permute-start | bytes 1572872 | tf_op jit(solution)/shard_map/ppermute | solution.py:57
  5.7 3.9 %gather_fusion = bf16[1024,256]{1,0:T(8,128)(2,1)S(1)} fusion(bf16[4096,256]{1,0:T(8,128)(2,1)S(1)} %copy-done, s32[1024]{0:T(1024)S(1)} %fusion.31), kind=kCustom, calls=%fused_computation | custom fusion | bytes 1052672 | tf_op jit(solution)/shard_map/gather | solution.py:98
  9.7 7.5 %collective-permute-done = bf16[256,1024]{1,0:T(8,128)(2,1)} collective-permute-done((bf16[256,1024]{1,0:T(8,128)(2,1)}, bf16[256,1024]{1,0:T(8,128)(2,1)}, u32[]{:S(2)}, u32[]{:S(2)}) %collective-permute-start) | collective-permute-done | bytes 524320 | tf_op jit(solution)/shard_map/ppermute | solution.py:57
  18.1 1.8 %collective-permute-start.1 = (bf16[512,256]{1,0:T(8,128)(2,1)S(1)}, bf16[512,256]{1,0:T(8,128)(2,1)S(1)}, u32[]{:S(2)}, u32[]{:S(2)}) collective-permute-start(bf16[512,256]{1,0:T(8,128)(2,1)S(1)} %get-tuple-element.29), channel_id=1, source_target_pairs={{0,2},{1,3},{2,0},{3,1},{4,6},{5,7},{6,4},{7,5},{8,10},{9,11},{10,... | collective-permute-start | bytes 786440 | tf_op jit(solution)/shard_map/ppermute | solution.py:57
  19.9 1.5 %fusion.92 = f32[512,1024]{1,0:T(8,128)S(1)} fusion(bf16[512,256]{1,0:T(8,128)(2,1)S(1)} %fusion.21, bf16[256,1024]{1,0:T(8,128)(2,1)} %constant_dynamic-slice_fusion), kind=kOutput, calls=%fused_computation.176 | convolution fusion | flops 268435456 | bytes 2883584 | tf_op jit(solution)/shard_map/dot_general | solution.py:13
  22.0 4.8 %collective-permute-done.1 = bf16[512,256]{1,0:T(8,128)(2,1)S(1)} collective-permute-done((bf16[512,256]{1,0:T(8,128)(2,1)S(1)}, bf16[512,256]{1,0:T(8,128)(2,1)S(1)}, u32[]{:S(2)}, u32[]{:S(2)}) %collective-permute-start.1) | collective-permute-done | bytes 262176 | tf_op jit(solution)/shard_map/ppermute | solution.py:57
  26.7 1.5 %fusion.93 = f32[512,1024]{1,0:T(8,128)S(1)} fusion(bf16[512,256]{1,0:T(8,128)(2,1)S(1)} %collective-permute-done.1, bf16[256,1024]{1,0:T(8,128)(2,1)} %collective-permute-done), kind=kOutput, calls=%fused_computation.177 | convolution fusion | flops 268435456 | bytes 2883584 | tf_op jit(solution)/shard_map/dot_general | solution.py:13
  28.2 1.5 %fusion.94 = f32[512,1024]{1,0:T(8,128)S(1)} fusion(bf16[512,256]{1,0:T(8,128)(2,1)S(1)} %collective-permute-done.2, bf16[256,1024]{1,0:T(8,128)(2,1)} %collective-permute-done.3), kind=kOutput, calls=%fused_computation.178 | convolution fusion | flops 268435456 | bytes 2883584 | tf_op jit(solution)/shard_map/dot_general | solution.py:13
  30.7 1.6 %collective-permute-start.12 = (bf16[512,1024]{1,0:T(8,128)(2,1)S(1)}, bf16[512,1024]{1,0:T(8,128)(2,1)S(1)}, u32[]{:S(2)}, u32[]{:S(2)}) collective-permute-start(bf16[512,1024]{1,0:T(8,128)(2,1)S(1)} %add_convert_fusion.1), channel_id=1, source_target_pairs={{0,4},{1,5},{2,6},{3,7},{4,0},{5,1},{6,2},{7,3},{8,12},{9,13},{10,... | collective-permute-start | bytes 3145736 | tf_op jit(solution)/shard_map/ppermute | solution.py:64
  33.3 1.6 %collective-permute-start.6 = (bf16[256,1024]{1,0:T(8,128)(2,1)S(1)}, bf16[256,1024]{1,0:T(8,128)(2,1)S(1)}, u32[]{:S(2)}, u32[]{:S(2)}) collective-permute-start(bf16[256,1024]{1,0:T(8,128)(2,1)S(1)} %get-tuple-element.22), channel_id=1, source_target_pairs={{0,2},{1,3},{2,0},{3,1},{4,6},{5,7},{6,4},{7,5},{8,10},{9,11},{10,... | collective-permute-start | bytes 1572872 | tf_op jit(solution)/shard_map/ppermute | solution.py:57
  36.2 1.3 collective-permute-done.7
  37.5 0.9 collective-permute-start.10
  39.3 17.4 %collective-permute-done.12 = bf16[512,1024]{1,0:T(8,128)(2,1)S(1)} collective-permute-done((bf16[512,1024]{1,0:T(8,128)(2,1)S(1)}, bf16[512,1024]{1,0:T(8,128)(2,1)S(1)}, u32[]{:S(2)}, u32[]{:S(2)}) %collective-permute-start.12) | collective-permute-done | bytes 1048608 | tf_op jit(solution)/shard_map/ppermute | solution.py:64
  56.8 1.7 %collective-permute-done.10 = bf16[256,1024]{1,0:T(8,128)(2,1)S(1)} collective-permute-done((bf16[256,1024]{1,0:T(8,128)(2,1)S(1)}, bf16[256,1024]{1,0:T(8,128)(2,1)S(1)}, u32[]{:S(2)}, u32[]{:S(2)}) %collective-permute-start.10) | collective-permute-done | bytes 524320 | tf_op jit(solution)/shard_map/ppermute | solution.py:57
  61.9 1.0 add_convert_fusion.2
  63.5 1.8 %collective-permute-start.17 = (bf16[256,1024]{1,0:T(8,128)(2,1)S(1)}, bf16[256,1024]{1,0:T(8,128)(2,1)S(1)}, u32[]{:S(2)}, u32[]{:S(2)}) collective-permute-start(bf16[256,1024]{1,0:T(8,128)(2,1)S(1)} %get-tuple-element.33), channel_id=1, source_target_pairs={{0,2},{1,3},{2,0},{3,1},{4,6},{5,7},{6,4},{7,5},{8,10},{9,11},{10,... | collective-permute-start | bytes 1572872 | tf_op jit(solution)/shard_map/ppermute | solution.py:57
  65.7 1.5 %collective-permute-start.15 = (bf16[256,1024]{1,0:T(8,128)(2,1)S(1)}, bf16[256,1024]{1,0:T(8,128)(2,1)S(1)}, u32[]{:S(2)}, u32[]{:S(2)}) collective-permute-start(bf16[256,1024]{1,0:T(8,128)(2,1)S(1)} %get-tuple-element.32), channel_id=1, source_target_pairs={{0,16},{1,17},{2,18},{3,19},{4,20},{5,21},{6,22},{7,23},{8,24},{9,... | collective-permute-start | bytes 1572872 | tf_op jit(solution)/shard_map/ppermute | solution.py:72
  67.7 10.6 %collective-permute-done.17 = bf16[256,1024]{1,0:T(8,128)(2,1)S(1)} collective-permute-done((bf16[256,1024]{1,0:T(8,128)(2,1)S(1)}, bf16[256,1024]{1,0:T(8,128)(2,1)S(1)}, u32[]{:S(2)}, u32[]{:S(2)}) %collective-permute-start.17) | collective-permute-done | bytes 524320 | tf_op jit(solution)/shard_map/ppermute | solution.py:57
  78.3 10.4 %collective-permute-done.16 = bf16[256,1024]{1,0:T(8,128)(2,1)S(1)} collective-permute-done((bf16[256,1024]{1,0:T(8,128)(2,1)S(1)}, bf16[256,1024]{1,0:T(8,128)(2,1)S(1)}, u32[]{:S(2)}, u32[]{:S(2)}) %collective-permute-start.16) | collective-permute-done | bytes 524320 | tf_op jit(solution)/shard_map/ppermute | solution.py:57
  90.9 1.0 add_convert_fusion
  92.5 1.7 %collective-permute-start.26 = (bf16[256,1024]{1,0:T(8,128)(2,1)S(1)}, bf16[256,1024]{1,0:T(8,128)(2,1)S(1)}, u32[]{:S(2)}, u32[]{:S(2)}) collective-permute-start(bf16[256,1024]{1,0:T(8,128)(2,1)S(1)} %get-tuple-element.31), channel_id=1, source_target_pairs={{0,2},{1,3},{2,0},{3,1},{4,6},{5,7},{6,4},{7,5},{8,10},{9,11},{10,... | collective-permute-start | bytes 1572872 | tf_op jit(solution)/shard_map/ppermute | solution.py:57
  94.2 1.5 %collective-permute-start.23 = (bf16[256,1024]{1,0:T(8,128)(2,1)S(1)}, bf16[256,1024]{1,0:T(8,128)(2,1)S(1)}, u32[]{:S(2)}, u32[]{:S(2)}) collective-permute-start(bf16[256,1024]{1,0:T(8,128)(2,1)S(1)} %get-tuple-element.30), channel_id=1, source_target_pairs={{0,16},{1,17},{2,18},{3,19},{4,20},{5,21},{6,22},{7,23},{8,24},{9,... | collective-permute-start | bytes 1572872 | tf_op jit(solution)/shard_map/ppermute | solution.py:72
  99.2 7.3 %collective-permute-done.26 = bf16[256,1024]{1,0:T(8,128)(2,1)S(1)} collective-permute-done((bf16[256,1024]{1,0:T(8,128)(2,1)S(1)}, bf16[256,1024]{1,0:T(8,128)(2,1)S(1)}, u32[]{:S(2)}, u32[]{:S(2)}) %collective-permute-start.26) | collective-permute-done | bytes 524320 | tf_op jit(solution)/shard_map/ppermute | solution.py:57
  106.4 1.5 collective-permute-done.23
  113.4 1.6 %collective-permute-start.31 = (f32[256]{0:T(256)S(1)}, f32[256]{0:T(256)S(1)}, u32[]{:S(2)}, u32[]{:S(2)}) collective-permute-start(f32[256]{0:T(256)S(1)} %get-tuple-element.43), channel_id=1, source_target_pairs={{0,16},{1,17},{2,18},{3,19},{4,20},{5,21},{6,22},{7,23},{8,24},{9,... | collective-permute-start | bytes 3080 | tf_op jit(solution)/shard_map/ppermute | solution.py:72
  115.5 1.5 %collective-permute-done.31 = f32[256]{0:T(256)S(1)} collective-permute-done((f32[256]{0:T(256)S(1)}, f32[256]{0:T(256)S(1)}, u32[]{:S(2)}, u32[]{:S(2)}) %collective-permute-start.31) | collective-permute-done | bytes 1056 | tf_op jit(solution)/shard_map/ppermute | solution.py:72
  117.0 1.5 %collective-permute-done.32 = f32[256]{0:T(256)S(1)} collective-permute-done((f32[256]{0:T(256)S(1)}, f32[256]{0:T(256)S(1)}, u32[]{:S(2)}, u32[]{:S(2)}) %collective-permute-start.32) | collective-permute-done | bytes 1056 | tf_op jit(solution)/shard_map/ppermute | solution.py:72
  118.6 1.2 collective-permute-start.34
  120.5 1.8 %collective-permute-done.34 = f32[256]{0:T(256)S(1)} collective-permute-done((f32[256]{0:T(256)S(1)}, f32[256]{0:T(256)S(1)}, u32[]{:S(2)}, u32[]{:S(2)}) %collective-permute-start.34) | collective-permute-done | bytes 1056 | tf_op jit(solution)/shard_map/ppermute | solution.py:57
  122.9 22.3 %collective-permute-start.36 = (f32[1024]{0:T(1024)S(1)}, f32[1024]{0:T(1024)S(1)}, u32[]{:S(2)}, u32[]{:S(2)}) collective-permute-start(f32[1024]{0:T(1024)S(1)} %pad_maximum_fusion.4), channel_id=1, source_target_pairs={{0,8},{1,9},{2,10},{3,11},{4,12},{5,13},{6,14},{7,15},{8,0},{9,1},... | collective-permute-start | bytes 12296 | tf_op jit(solution)/shard_map/ppermute | solution.py:64
  145.1 1.6 %collective-permute-done.36 = f32[1024]{0:T(1024)S(1)} collective-permute-done((f32[1024]{0:T(1024)S(1)}, f32[1024]{0:T(1024)S(1)}, u32[]{:S(2)}, u32[]{:S(2)}) %collective-permute-start.36) | collective-permute-done | bytes 4128 | tf_op jit(solution)/shard_map/ppermute | solution.py:64
  (121 shorter events, 25.0 us)
Async XLA Ops:
  2.0 15.2 %collective-permute-start = (bf16[256,1024]{1,0:T(8,128)(2,1)}, bf16[256,1024]{1,0:T(8,128)(2,1)}, u32[]{:S(2)}, u32[]{:S(2)}) collective-permute-start(bf16[256,1024]{1,0:T(8,128)(2,1)} %constant_dynamic-slice_fusion), channel_id=1, source_target_pairs={{0,2},{1,3},{2,0},{3,1},{4,6},{5,7},{6,4},{7,5},{8,10},{9,11},{10,... | collective-permute-start | bytes 1572872 | tf_op jit(solution)/shard_map/ppermute | solution.py:57
  4.9 23.3 %collective-permute-start.3 = (bf16[256,1024]{1,0:T(8,128)(2,1)}, bf16[256,1024]{1,0:T(8,128)(2,1)}, u32[]{:S(2)}, u32[]{:S(2)}) collective-permute-start(bf16[256,1024]{1,0:T(8,128)(2,1)} %constant_dynamic-slice_fusion), channel_id=1, source_target_pairs={{0,1},{1,0},{2,3},{3,2},{4,5},{5,4},{6,7},{7,6},{8,9},{9,8},{10,11... | collective-permute-start | bytes 1572872 | tf_op jit(solution)/shard_map/ppermute | solution.py:57
  18.1 8.6 %collective-permute-start.1 = (bf16[512,256]{1,0:T(8,128)(2,1)S(1)}, bf16[512,256]{1,0:T(8,128)(2,1)S(1)}, u32[]{:S(2)}, u32[]{:S(2)}) collective-permute-start(bf16[512,256]{1,0:T(8,128)(2,1)S(1)} %get-tuple-element.29), channel_id=1, source_target_pairs={{0,2},{1,3},{2,0},{3,1},{4,6},{5,7},{6,4},{7,5},{8,10},{9,11},{10,... | collective-permute-start | bytes 786440 | tf_op jit(solution)/shard_map/ppermute | solution.py:57
  21.4 6.8 %collective-permute-start.2 = (bf16[512,256]{1,0:T(8,128)(2,1)S(1)}, bf16[512,256]{1,0:T(8,128)(2,1)S(1)}, u32[]{:S(2)}, u32[]{:S(2)}) collective-permute-start(bf16[512,256]{1,0:T(8,128)(2,1)S(1)} %get-tuple-element.28), channel_id=1, source_target_pairs={{0,1},{1,0},{2,3},{3,2},{4,5},{5,4},{6,7},{7,6},{8,9},{9,8},{10,11... | collective-permute-start | bytes 786440 | tf_op jit(solution)/shard_map/ppermute | solution.py:57
  21.5 8.8 %collective-permute-start.4 = (bf16[512,256]{1,0:T(8,128)(2,1)S(1)}, bf16[512,256]{1,0:T(8,128)(2,1)S(1)}, u32[]{:S(2)}, u32[]{:S(2)}) collective-permute-start(bf16[512,256]{1,0:T(8,128)(2,1)S(1)} %get-tuple-element.27), channel_id=1, source_target_pairs={{0,3},{1,2},{2,1},{3,0},{4,7},{5,6},{6,5},{7,4},{8,11},{9,10},{10,... | collective-permute-start | bytes 786440 | tf_op jit(solution)/shard_map/ppermute | solution.py:57
  21.9 8.4 %collective-permute-start.5 = (bf16[256,1024]{1,0:T(8,128)(2,1)}, bf16[256,1024]{1,0:T(8,128)(2,1)S(1)}, u32[]{:S(2)}, u32[]{:S(2)}) collective-permute-start(bf16[256,1024]{1,0:T(8,128)(2,1)} %collective-permute-done), channel_id=1, source_target_pairs={{0,1},{1,0},{2,3},{3,2},{4,5},{5,4},{6,7},{7,6},{8,9},{9,8},{10,11... | collective-permute-start | bytes 1572872 | tf_op jit(solution)/shard_map/ppermute | solution.py:57
  30.7 26.0 %collective-permute-start.12 = (bf16[512,1024]{1,0:T(8,128)(2,1)S(1)}, bf16[512,1024]{1,0:T(8,128)(2,1)S(1)}, u32[]{:S(2)}, u32[]{:S(2)}) collective-permute-start(bf16[512,1024]{1,0:T(8,128)(2,1)S(1)} %add_convert_fusion.1), channel_id=1, source_target_pairs={{0,4},{1,5},{2,6},{3,7},{4,0},{5,1},{6,2},{7,3},{8,12},{9,13},{10,... | collective-permute-start | bytes 3145736 | tf_op jit(solution)/shard_map/ppermute | solution.py:64
  32.4 24.4 %collective-permute-start.11 = (bf16[512,1024]{1,0:T(8,128)(2,1)S(1)}, bf16[512,1024]{1,0:T(8,128)(2,1)S(1)}, u32[]{:S(2)}, u32[]{:S(2)}) collective-permute-start(bf16[512,1024]{1,0:T(8,128)(2,1)S(1)} %add_convert_fusion.1), channel_id=1, source_target_pairs={{0,1},{1,0},{2,3},{3,2},{4,8},{5,9},{6,10},{7,11},{8,4},{9,5},{10,... | collective-permute-start | bytes 3145736 | tf_op jit(solution)/shard_map/ppermute | solution.py:64
  33.3 23.5 %collective-permute-start.6 = (bf16[256,1024]{1,0:T(8,128)(2,1)S(1)}, bf16[256,1024]{1,0:T(8,128)(2,1)S(1)}, u32[]{:S(2)}, u32[]{:S(2)}) collective-permute-start(bf16[256,1024]{1,0:T(8,128)(2,1)S(1)} %get-tuple-element.22), channel_id=1, source_target_pairs={{0,2},{1,3},{2,0},{3,1},{4,6},{5,7},{6,4},{7,5},{8,10},{9,11},{10,... | collective-permute-start | bytes 1572872 | tf_op jit(solution)/shard_map/ppermute | solution.py:57
  34.8 4.0 %collective-permute-start.8 = (bf16[256,1024]{1,0:T(8,128)(2,1)S(1)}, bf16[256,1024]{1,0:T(8,128)(2,1)S(1)}, u32[]{:S(2)}, u32[]{:S(2)}) collective-permute-start(bf16[256,1024]{1,0:T(8,128)(2,1)S(1)} %get-tuple-element.22), channel_id=1, source_target_pairs={{0,1},{1,0},{2,3},{3,2},{4,5},{5,4},{6,7},{7,6},{8,9},{9,8},{10,11... | collective-permute-start | bytes 1572872 | tf_op jit(solution)/shard_map/ppermute | solution.py:57
  34.9 2.6 %collective-permute-start.7 = (bf16[256,1024]{1,0:T(8,128)(2,1)S(1)}, bf16[256,1024]{1,0:T(8,128)(2,1)S(1)}, u32[]{:S(2)}, u32[]{:S(2)}) collective-permute-start(bf16[256,1024]{1,0:T(8,128)(2,1)S(1)} %get-tuple-element.23), channel_id=1, source_target_pairs={{0,1},{1,0},{2,3},{3,2},{4,5},{5,4},{6,7},{7,6},{8,9},{9,8},{10,11... | collective-permute-start | bytes 1572872 | tf_op jit(solution)/shard_map/ppermute | solution.py:57
  37.5 21.0 %collective-permute-start.10 = (bf16[256,1024]{1,0:T(8,128)(2,1)S(1)}, bf16[256,1024]{1,0:T(8,128)(2,1)S(1)}, u32[]{:S(2)}, u32[]{:S(2)}) collective-permute-start(bf16[256,1024]{1,0:T(8,128)(2,1)S(1)} %get-tuple-element.23), channel_id=1, source_target_pairs={{0,2},{1,3},{2,0},{3,1},{4,6},{5,7},{6,4},{7,5},{8,10},{9,11},{10,... | collective-permute-start | bytes 1572872 | tf_op jit(solution)/shard_map/ppermute | solution.py:57
  38.8 19.7 %collective-permute-start.9 = (bf16[256,1024]{1,0:T(8,128)(2,1)S(1)}, bf16[256,1024]{1,0:T(8,128)(2,1)S(1)}, u32[]{:S(2)}, u32[]{:S(2)}) collective-permute-start(bf16[256,1024]{1,0:T(8,128)(2,1)S(1)} %get-tuple-element.21), channel_id=1, source_target_pairs={{0,1},{1,0},{2,3},{3,2},{4,5},{5,4},{6,7},{7,6},{8,9},{9,8},{10,11... | collective-permute-start | bytes 1572872 | tf_op jit(solution)/shard_map/ppermute | solution.py:57
  58.7 2.6 %collective-permute-start.13 = (bf16[256,1024]{1,0:T(8,128)(2,1)S(1)}, bf16[256,1024]{1,0:T(8,128)(2,1)S(1)}, u32[]{:S(2)}, u32[]{:S(2)}) collective-permute-start(bf16[256,1024]{1,0:T(8,128)(2,1)S(1)} %get-tuple-element.47), channel_id=1, source_target_pairs={{0,1},{1,0},{2,3},{3,2},{4,5},{5,4},{6,7},{7,6},{8,9},{9,8},{10,11... | collective-permute-start | bytes 1572872 | tf_op jit(solution)/shard_map/ppermute | solution.py:57
  62.9 4.8 %collective-permute-start.19 = (bf16[512,1024]{1,0:T(8,128)(2,1)S(1)}, bf16[512,1024]{1,0:T(8,128)(2,1)S(1)}, u32[]{:S(2)}, u32[]{:S(2)}) collective-permute-start(bf16[512,1024]{1,0:T(8,128)(2,1)S(1)} %get-tuple-element.20), channel_id=1, source_target_pairs={{0,1},{1,0},{2,3},{3,2},{4,8},{5,9},{6,10},{7,11},{8,4},{9,5},{10,... | collective-permute-start | bytes 3145736 | tf_op jit(solution)/shard_map/ppermute | solution.py:64
  63.1 4.6 %collective-permute-start.18 = (bf16[512,1024]{1,0:T(8,128)(2,1)S(1)}, bf16[512,1024]{1,0:T(8,128)(2,1)S(1)}, u32[]{:S(2)}, u32[]{:S(2)}) collective-permute-start(bf16[512,1024]{1,0:T(8,128)(2,1)S(1)} %get-tuple-element.19), channel_id=1, source_target_pairs={{0,1},{1,0},{2,3},{3,2},{4,5},{5,4},{6,7},{7,6},{8,12},{9,13},{10,... | collective-permute-start | bytes 3145736 | tf_op jit(solution)/shard_map/ppermute | solution.py:64
  63.5 14.8 %collective-permute-start.17 = (bf16[256,1024]{1,0:T(8,128)(2,1)S(1)}, bf16[256,1024]{1,0:T(8,128)(2,1)S(1)}, u32[]{:S(2)}, u32[]{:S(2)}) collective-permute-start(bf16[256,1024]{1,0:T(8,128)(2,1)S(1)} %get-tuple-element.33), channel_id=1, source_target_pairs={{0,2},{1,3},{2,0},{3,1},{4,6},{5,7},{6,4},{7,5},{8,10},{9,11},{10,... | collective-permute-start | bytes 1572872 | tf_op jit(solution)/shard_map/ppermute | solution.py:57
  65.4 23.4 %collective-permute-start.16 = (bf16[256,1024]{1,0:T(8,128)(2,1)S(1)}, bf16[256,1024]{1,0:T(8,128)(2,1)S(1)}, u32[]{:S(2)}, u32[]{:S(2)}) collective-permute-start(bf16[256,1024]{1,0:T(8,128)(2,1)S(1)} %broadcast_add_fusion.3), channel_id=1, source_target_pairs={{0,2},{1,3},{2,0},{3,1},{4,6},{5,7},{6,4},{7,5},{8,10},{9,11},{10,... | collective-permute-start | bytes 1572872 | tf_op jit(solution)/shard_map/ppermute | solution.py:57
  65.7 23.1 %collective-permute-start.15 = (bf16[256,1024]{1,0:T(8,128)(2,1)S(1)}, bf16[256,1024]{1,0:T(8,128)(2,1)S(1)}, u32[]{:S(2)}, u32[]{:S(2)}) collective-permute-start(bf16[256,1024]{1,0:T(8,128)(2,1)S(1)} %get-tuple-element.32), channel_id=1, source_target_pairs={{0,16},{1,17},{2,18},{3,19},{4,20},{5,21},{6,22},{7,23},{8,24},{9,... | collective-permute-start | bytes 1572872 | tf_op jit(solution)/shard_map/ppermute | solution.py:72
  89.8 6.0 %collective-permute-start.25 = (bf16[256,1024]{1,0:T(8,128)(2,1)S(1)}, bf16[256,1024]{1,0:T(8,128)(2,1)S(1)}, u32[]{:S(2)}, u32[]{:S(2)}) collective-permute-start(bf16[256,1024]{1,0:T(8,128)(2,1)S(1)} %get-tuple-element.46), channel_id=1, source_target_pairs={{0,1},{1,0},{2,3},{3,2},{4,5},{5,4},{6,7},{7,6},{8,9},{9,8},{10,11... | collective-permute-start | bytes 1572872 | tf_op jit(solution)/shard_map/ppermute | solution.py:57
  90.3 6.9 %collective-permute-start.20 = (bf16[256,1024]{1,0:T(8,128)(2,1)S(1)}, bf16[256,1024]{1,0:T(8,128)(2,1)S(1)}, u32[]{:S(2)}, u32[]{:S(2)}) collective-permute-start(bf16[256,1024]{1,0:T(8,128)(2,1)S(1)} %get-tuple-element.44), channel_id=1, source_target_pairs={{0,1},{1,0},{2,3},{3,2},{4,5},{5,4},{6,7},{7,6},{8,9},{9,8},{10,11... | collective-permute-start | bytes 1572872 | tf_op jit(solution)/shard_map/ppermute | solution.py:57
  92.0 5.9 %collective-permute-start.22 = (bf16[256,1024]{1,0:T(8,128)(2,1)S(1)}, bf16[256,1024]{1,0:T(8,128)(2,1)S(1)}, u32[]{:S(2)}, u32[]{:S(2)}) collective-permute-start(bf16[256,1024]{1,0:T(8,128)(2,1)S(1)} %get-tuple-element.31), channel_id=1, source_target_pairs={{0,1},{1,0},{2,3},{3,2},{4,5},{5,4},{6,7},{7,6},{8,9},{9,8},{10,11... | collective-permute-start | bytes 1572872 | tf_op jit(solution)/shard_map/ppermute | solution.py:57
  92.5 14.0 %collective-permute-start.26 = (bf16[256,1024]{1,0:T(8,128)(2,1)S(1)}, bf16[256,1024]{1,0:T(8,128)(2,1)S(1)}, u32[]{:S(2)}, u32[]{:S(2)}) collective-permute-start(bf16[256,1024]{1,0:T(8,128)(2,1)S(1)} %get-tuple-element.31), channel_id=1, source_target_pairs={{0,2},{1,3},{2,0},{3,1},{4,6},{5,7},{6,4},{7,5},{8,10},{9,11},{10,... | collective-permute-start | bytes 1572872 | tf_op jit(solution)/shard_map/ppermute | solution.py:57
  94.2 13.7 %collective-permute-start.23 = (bf16[256,1024]{1,0:T(8,128)(2,1)S(1)}, bf16[256,1024]{1,0:T(8,128)(2,1)S(1)}, u32[]{:S(2)}, u32[]{:S(2)}) collective-permute-start(bf16[256,1024]{1,0:T(8,128)(2,1)S(1)} %get-tuple-element.30), channel_id=1, source_target_pairs={{0,16},{1,17},{2,18},{3,19},{4,20},{5,21},{6,22},{7,23},{8,24},{9,... | collective-permute-start | bytes 1572872 | tf_op jit(solution)/shard_map/ppermute | solution.py:72
  99.1 9.5 %collective-permute-start.24 = (f32[256,256]{1,0:T(8,128)S(1)}, f32[256,256]{1,0:T(8,128)S(1)}, u32[]{:S(2)}, u32[]{:S(2)}) collective-permute-start(f32[256,256]{1,0:T(8,128)S(1)} %convolution_add_fusion.4), channel_id=1, source_target_pairs={{0,1},{1,0},{2,3},{3,2},{4,5},{5,4},{6,7},{7,6},{8,12},{9,13},{10,... | collective-permute-start | bytes 786440 | tf_op jit(solution)/shard_map/ppermute | solution.py:64
  106.4 2.5 %collective-permute-start.27 = (bf16[256,1024]{1,0:T(8,128)(2,1)S(1)}, bf16[256,1024]{1,0:T(8,128)(2,1)S(1)}, u32[]{:S(2)}, u32[]{:S(2)}) collective-permute-start(bf16[256,1024]{1,0:T(8,128)(2,1)S(1)} %collective-permute-done.26), channel_id=1, source_target_pairs={{0,1},{1,0},{2,3},{3,2},{4,5},{5,4},{6,7},{7,6},{8,9},{9,8},{10,11... | collective-permute-start | bytes 1572872 | tf_op jit(solution)/shard_map/ppermute | solution.py:57
  113.4 3.6 %collective-permute-start.31 = (f32[256]{0:T(256)S(1)}, f32[256]{0:T(256)S(1)}, u32[]{:S(2)}, u32[]{:S(2)}) collective-permute-start(f32[256]{0:T(256)S(1)} %get-tuple-element.43), channel_id=1, source_target_pairs={{0,16},{1,17},{2,18},{3,19},{4,20},{5,21},{6,22},{7,23},{8,24},{9,... | collective-permute-start | bytes 3080 | tf_op jit(solution)/shard_map/ppermute | solution.py:72
  115.0 3.6 %collective-permute-start.32 = (f32[256]{0:T(256)S(1)}, f32[256]{0:T(256)S(1)}, u32[]{:S(2)}, u32[]{:S(2)}) collective-permute-start(f32[256]{0:T(256)S(1)} %get-tuple-element.43), channel_id=1, source_target_pairs={{0,16},{1,17},{2,18},{3,19},{4,20},{5,21},{6,22},{7,23},{8,28},{9,... | collective-permute-start | bytes 3080 | tf_op jit(solution)/shard_map/ppermute | solution.py:72
  115.4 3.1 %collective-permute-start.30 = (f32[256]{0:T(256)S(1)}, f32[256]{0:T(256)S(1)}, u32[]{:S(2)}, u32[]{:S(2)}) collective-permute-start(f32[256]{0:T(256)S(1)} %get-tuple-element.42), channel_id=1, source_target_pairs={{0,1},{1,0},{2,3},{3,2},{4,5},{5,4},{6,7},{7,6},{8,12},{9,13},{10,... | collective-permute-start | bytes 3080 | tf_op jit(solution)/shard_map/ppermute | solution.py:64
  118.6 3.6 %collective-permute-start.34 = (f32[256]{0:T(256)S(1)}, f32[256]{0:T(256)S(1)}, u32[]{:S(2)}, u32[]{:S(2)}) collective-permute-start(f32[256]{0:T(256)S(1)} %add_add_fusion.3), channel_id=1, source_target_pairs={{0,2},{1,3},{2,0},{3,1},{4,6},{5,7},{6,4},{7,5},{8,10},{9,11},{10,... | collective-permute-start | bytes 3080 | tf_op jit(solution)/shard_map/ppermute | solution.py:57
  119.8 3.0 %collective-permute-start.35 = (f32[256]{0:T(256)S(1)}, f32[256]{0:T(256)S(1)}, u32[]{:S(2)}, u32[]{:S(2)}) collective-permute-start(f32[256]{0:T(256)S(1)} %add_add_fusion.3), channel_id=1, source_target_pairs={{0,3},{1,2},{2,1},{3,0},{4,7},{5,6},{6,5},{7,4},{8,11},{9,10},{10,... | collective-permute-start | bytes 3080 | tf_op jit(solution)/shard_map/ppermute | solution.py:57
  122.9 23.8 %collective-permute-start.36 = (f32[1024]{0:T(1024)S(1)}, f32[1024]{0:T(1024)S(1)}, u32[]{:S(2)}, u32[]{:S(2)}) collective-permute-start(f32[1024]{0:T(1024)S(1)} %pad_maximum_fusion.4), channel_id=1, source_target_pairs={{0,8},{1,9},{2,10},{3,11},{4,12},{5,13},{6,14},{7,15},{8,0},{9,1},... | collective-permute-start | bytes 12296 | tf_op jit(solution)/shard_map/ppermute | solution.py:64
  (9 other events, 57.6 us)

commit v10 on v9

--- a/solution.py
+++ b/solution.py
@@ -125,7 +125,7 @@
 
         order = [(s, 0) for s in range(nx)] + [(s, 1) for s in range(nx)]
 
-        own1 = factor_own([0, 1, 2, 1])
+        own1 = lax.optimization_barrier(factor_own([0, 1, 2, 1]))
         same1 = [own1] + factor_x(own1)
 
         done = token(*same1[1:])
@@ -177,13 +177,11 @@
         p_all_a, p_all_b = jnp.concatenate([p_a, p_far_a], axis=0), jnp.concatenate([p_b, p_far_b], axis=0)
 
         given_near = along_z(matmul_t(give_a[0], p_a) + matmul_t(give_b[0], p_b), owners)
-        give_side = behind(matmul_t(give_a[0], p_far_a) + matmul_t(give_b[0], p_far_b), token(given_near)[:, :1] if n_pool > 2 else token(given_near))
-        give_far = matmul_t(give_a[1], p_all_a) + matmul_t(give_b[1], p_all_b)
-        if nx == 2:
-            given = along_z(jnp.concatenate([give_side, give_far], axis=1), owners)
-            given_side, given_far = given[:, :give_side.shape[1]], given[:, give_side.shape[1]:]
-        else:
-            given_side, given_far = along_z(give_side, owners), along_z(give_far, owners)
+        swapped = token(given_near)
+        swapped = swapped if p_far_a.shape[0] == p_a.shape[0] else swapped[:, :1]
+        give_side = behind(matmul_t(give_a[0], p_far_a) + matmul_t(give_b[0], p_far_b), swapped)
+        given_side = along_z(give_side, owners)
+        given_far = along_z(matmul_t(give_a[1], p_all_a) + matmul_t(give_b[1], p_all_b), owners)
 
         p_squares = square_sum(p_all_a) + square_sum(p_all_b)
         sizes = [p_squares.shape[0], keep_a[0].shape[0], keep_a[1].shape[0]]

time: 148 us -> 147 us (level)
    ppermute x24, waiting for transfers between devices: 47.3 us -> 39.8 us  [inner(): return lax.ppermute(value, 'tgt', pairs)]
    ppermute x4, waiting for transfers between devices: 4.54 us -> 11.8 us  [over_pool(): return lax.ppermute(value, ('pool', 'tgt'), pairs)]
    ppermute x9 -> x10, starting transfers between devices: 25.7 us -> 25 us  [along_z(): return lax.ppermute(value, 'tgt', pairs)]
    ppermute x9 -> x10, waiting for transfers between devices: 19.7 us -> 19.8 us  [along_z(): return lax.ppermute(value, 'tgt', pairs)]
  transfers between devices with their start and end apart: 37 -> 38, of which waited for: 19 -> 19; matrix products, arithmetic and copies ran while one was open for 15% -> 16% of each run, Pallas kernels for 0% -> 0%
where the time goes in v10:
time: 147 us; the launch traced here: 146 us
  waiting for transfers between devices  71.4 us (49%)
  starting transfers between devices  46 us (31%)
  matrix products  15.5 us (11%)
  local copies, waits for them, and re-layouts  6.83 us (5%)
  other arithmetic  6.04 us (4%)
    ppermute x24, waiting for transfers between devices, inner(): return lax.ppermute(value, 'tgt', pairs)  39.8 us
    ppermute x10, starting transfers between devices, along_z(): return lax.ppermute(value, 'tgt', pairs)  25 us
    ppermute x10, waiting for transfers between devices, along_z(): return lax.ppermute(value, 'tgt', pairs)  19.8 us
    ppermute x24, starting transfers between devices, inner(): return lax.ppermute(value, 'tgt', pairs)  15.9 us
    ppermute x4, waiting for transfers between devices, over_pool(): return lax.ppermute(value, ('pool', 'tgt'), pairs)  11.8 us
    dot_general x16, matrix products, matmul(): lax.dot_general(a, b, (((1,), (0,)), ((), ())), preferred_element_type=F32)  10.8 us
    ppermute x4, starting transfers between devices, over_pool(): return lax.ppermute(value, ('pool', 'tgt'), pairs)  5.16 us
    dot_general x10, matrix products, matmul_t(): lax.dot_general(a, b, (((1,), (1,)), ((), ())), preferred_element_type=F32)  4.68 us
  transfers between devices with their start and end apart: 38, of which 19 were waited for; matrix products, arithmetic and copies ran while one was open for 16% of the time, Pallas kernels for 0%

profile of v10, /device:TPU:0, one launch (start us, length us, event | category | flops | bytes accessed | tf_op | source)
XLA Modules:
  0.0 146.3 jit_solution(14178999044866383831)
XLA Ops:
  0.0 2.0 %constant_dynamic-slice_fusion = bf16[256,1024]{1,0:T(8,128)(2,1)} fusion(bf16[256,4096]{1,0:T(8,128)(2,1)} %param.7, s32[]{:T(128)S(6)} %select_n.171), kind=kLoop, calls=%fused_computation.145 | loop fusion | bytes 1048580 | tf_op jit(solution)/shard_map/dynamic_slice | solution.py:111
  2.0 2.9 %collective-permute-start = (bf16[256,1024]{1,0:T(8,128)(2,1)}, bf16[256,1024]{1,0:T(8,128)(2,1)}, u32[]{:S(2)}, u32[]{:S(2)}) collective-permute-start(bf16[256,1024]{1,0:T(8,128)(2,1)} %constant_dynamic-slice_fusion), channel_id=1, source_target_pairs={{0,2},{1,3},{2,0},{3,1},{4,6},{5,7},{6,4},{7,5},{8,10},{9,11},{10,... | collective-permute-start | bytes 1572872 | tf_op jit(solution)/shard_map/ppermute | solution.py:57
  5.7 3.9 %gather_fusion = bf16[1024,256]{1,0:T(8,128)(2,1)S(1)} fusion(bf16[4096,256]{1,0:T(8,128)(2,1)S(1)} %copy-done, s32[1024]{0:T(1024)S(1)} %fusion.31), kind=kCustom, calls=%fused_computation | custom fusion | bytes 1052672 | tf_op jit(solution)/shard_map/gather | solution.py:98
  9.7 7.5 %collective-permute-done = bf16[256,1024]{1,0:T(8,128)(2,1)} collective-permute-done((bf16[256,1024]{1,0:T(8,128)(2,1)}, bf16[256,1024]{1,0:T(8,128)(2,1)}, u32[]{:S(2)}, u32[]{:S(2)}) %collective-permute-start) | collective-permute-done | bytes 524320 | tf_op jit(solution)/shard_map/ppermute | solution.py:57
  18.1 1.8 %collective-permute-start.1 = (bf16[512,256]{1,0:T(8,128)(2,1)S(1)}, bf16[512,256]{1,0:T(8,128)(2,1)S(1)}, u32[]{:S(2)}, u32[]{:S(2)}) collective-permute-start(bf16[512,256]{1,0:T(8,128)(2,1)S(1)} %get-tuple-element.29), channel_id=1, source_target_pairs={{0,2},{1,3},{2,0},{3,1},{4,6},{5,7},{6,4},{7,5},{8,10},{9,11},{10,... | collective-permute-start | bytes 786440 | tf_op jit(solution)/shard_map/ppermute | solution.py:57
  19.9 1.5 %fusion.92 = f32[512,1024]{1,0:T(8,128)S(1)} fusion(bf16[512,256]{1,0:T(8,128)(2,1)S(1)} %fusion.21, bf16[256,1024]{1,0:T(8,128)(2,1)} %constant_dynamic-slice_fusion), kind=kOutput, calls=%fused_computation.175 | convolution fusion | flops 268435456 | bytes 2883584 | tf_op jit(solution)/shard_map/dot_general | solution.py:13
  22.0 4.8 %collective-permute-done.1 = bf16[512,256]{1,0:T(8,128)(2,1)S(1)} collective-permute-done((bf16[512,256]{1,0:T(8,128)(2,1)S(1)}, bf16[512,256]{1,0:T(8,128)(2,1)S(1)}, u32[]{:S(2)}, u32[]{:S(2)}) %collective-permute-start.1) | collective-permute-done | bytes 262176 | tf_op jit(solution)/shard_map/ppermute | solution.py:57
  26.7 1.5 %fusion.93 = f32[512,1024]{1,0:T(8,128)S(1)} fusion(bf16[512,256]{1,0:T(8,128)(2,1)S(1)} %collective-permute-done.1, bf16[256,1024]{1,0:T(8,128)(2,1)} %collective-permute-done), kind=kOutput, calls=%fused_computation.176 | convolution fusion | flops 268435456 | bytes 2883584 | tf_op jit(solution)/shard_map/dot_general | solution.py:13
  28.2 1.5 %fusion.94 = f32[512,1024]{1,0:T(8,128)S(1)} fusion(bf16[512,256]{1,0:T(8,128)(2,1)S(1)} %collective-permute-done.2, bf16[256,1024]{1,0:T(8,128)(2,1)} %collective-permute-done.3), kind=kOutput, calls=%fused_computation.177 | convolution fusion | flops 268435456 | bytes 2883584 | tf_op jit(solution)/shard_map/dot_general | solution.py:13
  30.7 1.6 %collective-permute-start.12 = (bf16[512,1024]{1,0:T(8,128)(2,1)S(1)}, bf16[512,1024]{1,0:T(8,128)(2,1)S(1)}, u32[]{:S(2)}, u32[]{:S(2)}) collective-permute-start(bf16[512,1024]{1,0:T(8,128)(2,1)S(1)} %add_convert_fusion.1), channel_id=1, source_target_pairs={{0,4},{1,5},{2,6},{3,7},{4,0},{5,1},{6,2},{7,3},{8,12},{9,13},{10,... | collective-permute-start | bytes 3145736 | tf_op jit(solution)/shard_map/ppermute | solution.py:64
  33.3 1.6 %collective-permute-start.6 = (bf16[256,1024]{1,0:T(8,128)(2,1)S(1)}, bf16[256,1024]{1,0:T(8,128)(2,1)S(1)}, u32[]{:S(2)}, u32[]{:S(2)}) collective-permute-start(bf16[256,1024]{1,0:T(8,128)(2,1)S(1)} %get-tuple-element.22), channel_id=1, source_target_pairs={{0,2},{1,3},{2,0},{3,1},{4,6},{5,7},{6,4},{7,5},{8,10},{9,11},{10,... | collective-permute-start | bytes 1572872 | tf_op jit(solution)/shard_map/ppermute | solution.py:57
  36.2 1.3 collective-permute-done.7
  37.5 0.9 collective-permute-start.10
  39.4 17.4 %collective-permute-done.12 = bf16[512,1024]{1,0:T(8,128)(2,1)S(1)} collective-permute-done((bf16[512,1024]{1,0:T(8,128)(2,1)S(1)}, bf16[512,1024]{1,0:T(8,128)(2,1)S(1)}, u32[]{:S(2)}, u32[]{:S(2)}) %collective-permute-start.12) | collective-permute-done | bytes 1048608 | tf_op jit(solution)/shard_map/ppermute | solution.py:64
  56.8 1.7 %collective-permute-done.10 = bf16[256,1024]{1,0:T(8,128)(2,1)S(1)} collective-permute-done((bf16[256,1024]{1,0:T(8,128)(2,1)S(1)}, bf16[256,1024]{1,0:T(8,128)(2,1)S(1)}, u32[]{:S(2)}, u32[]{:S(2)}) %collective-permute-start.10) | collective-permute-done | bytes 524320 | tf_op jit(solution)/shard_map/ppermute | solution.py:57
  61.9 0.9 add_convert_fusion.2
  63.4 1.8 %collective-permute-start.17 = (bf16[256,1024]{1,0:T(8,128)(2,1)S(1)}, bf16[256,1024]{1,0:T(8,128)(2,1)S(1)}, u32[]{:S(2)}, u32[]{:S(2)}) collective-permute-start(bf16[256,1024]{1,0:T(8,128)(2,1)S(1)} %get-tuple-element.33), channel_id=1, source_target_pairs={{0,2},{1,3},{2,0},{3,1},{4,6},{5,7},{6,4},{7,5},{8,10},{9,11},{10,... | collective-permute-start | bytes 1572872 | tf_op jit(solution)/shard_map/ppermute | solution.py:57
  65.6 1.5 %collective-permute-start.15 = (bf16[256,1024]{1,0:T(8,128)(2,1)S(1)}, bf16[256,1024]{1,0:T(8,128)(2,1)S(1)}, u32[]{:S(2)}, u32[]{:S(2)}) collective-permute-start(bf16[256,1024]{1,0:T(8,128)(2,1)S(1)} %get-tuple-element.32), channel_id=1, source_target_pairs={{0,16},{1,17},{2,18},{3,19},{4,20},{5,21},{6,22},{7,23},{8,24},{9,... | collective-permute-start | bytes 1572872 | tf_op jit(solution)/shard_map/ppermute | solution.py:72
  67.6 10.6 %collective-permute-done.17 = bf16[256,1024]{1,0:T(8,128)(2,1)S(1)} collective-permute-done((bf16[256,1024]{1,0:T(8,128)(2,1)S(1)}, bf16[256,1024]{1,0:T(8,128)(2,1)S(1)}, u32[]{:S(2)}, u32[]{:S(2)}) %collective-permute-start.17) | collective-permute-done | bytes 524320 | tf_op jit(solution)/shard_map/ppermute | solution.py:57
  78.3 10.4 %collective-permute-done.16 = bf16[256,1024]{1,0:T(8,128)(2,1)S(1)} collective-permute-done((bf16[256,1024]{1,0:T(8,128)(2,1)S(1)}, bf16[256,1024]{1,0:T(8,128)(2,1)S(1)}, u32[]{:S(2)}, u32[]{:S(2)}) %collective-permute-start.16) | collective-permute-done | bytes 524320 | tf_op jit(solution)/shard_map/ppermute | solution.py:57
  90.9 1.0 add_convert_fusion
  92.4 1.7 %collective-permute-start.27 = (bf16[256,1024]{1,0:T(8,128)(2,1)S(1)}, bf16[256,1024]{1,0:T(8,128)(2,1)S(1)}, u32[]{:S(2)}, u32[]{:S(2)}) collective-permute-start(bf16[256,1024]{1,0:T(8,128)(2,1)S(1)} %get-tuple-element.31), channel_id=1, source_target_pairs={{0,2},{1,3},{2,0},{3,1},{4,6},{5,7},{6,4},{7,5},{8,10},{9,11},{10,... | collective-permute-start | bytes 1572872 | tf_op jit(solution)/shard_map/ppermute | solution.py:57
  94.2 1.5 %collective-permute-start.23 = (bf16[256,1024]{1,0:T(8,128)(2,1)S(1)}, bf16[256,1024]{1,0:T(8,128)(2,1)S(1)}, u32[]{:S(2)}, u32[]{:S(2)}) collective-permute-start(bf16[256,1024]{1,0:T(8,128)(2,1)S(1)} %get-tuple-element.30), channel_id=1, source_target_pairs={{0,16},{1,17},{2,18},{3,19},{4,20},{5,21},{6,22},{7,23},{8,24},{9,... | collective-permute-start | bytes 1572872 | tf_op jit(solution)/shard_map/ppermute | solution.py:72
  99.1 8.7 %collective-permute-done.23 = bf16[256,1024]{1,0:T(8,128)(2,1)S(1)} collective-permute-done((bf16[256,1024]{1,0:T(8,128)(2,1)S(1)}, bf16[256,1024]{1,0:T(8,128)(2,1)S(1)}, u32[]{:S(2)}, u32[]{:S(2)}) %collective-permute-start.23) | collective-permute-done | bytes 524320 | tf_op jit(solution)/shard_map/ppermute | solution.py:72
  112.1 0.7 fusion.14
  114.2 1.6 %collective-permute-start.32 = (f32[256]{0:T(256)S(1)}, f32[256]{0:T(256)S(1)}, u32[]{:S(2)}, u32[]{:S(2)}) collective-permute-start(f32[256]{0:T(256)S(1)} %get-tuple-element.43), channel_id=1, source_target_pairs={{0,16},{1,17},{2,18},{3,19},{4,20},{5,21},{6,22},{7,23},{8,24},{9,... | collective-permute-start | bytes 3080 | tf_op jit(solution)/shard_map/ppermute | solution.py:72
  116.4 1.5 %collective-permute-done.32 = f32[256]{0:T(256)S(1)} collective-permute-done((f32[256]{0:T(256)S(1)}, f32[256]{0:T(256)S(1)}, u32[]{:S(2)}, u32[]{:S(2)}) %collective-permute-start.32) | collective-permute-done | bytes 1056 | tf_op jit(solution)/shard_map/ppermute | solution.py:72
  117.9 1.5 %collective-permute-done.33 = f32[256]{0:T(256)S(1)} collective-permute-done((f32[256]{0:T(256)S(1)}, f32[256]{0:T(256)S(1)}, u32[]{:S(2)}, u32[]{:S(2)}) %collective-permute-start.33) | collective-permute-done | bytes 1056 | tf_op jit(solution)/shard_map/ppermute | solution.py:72
  119.9 1.5 %collective-permute-start.36 = (f32[256]{0:T(256)S(1)}, f32[256]{0:T(256)S(1)}, u32[]{:S(2)}, u32[]{:S(2)}) collective-permute-start(f32[256]{0:T(256)S(1)} %add_add_fusion.3), channel_id=1, source_target_pairs={{0,3},{1,2},{2,1},{3,0},{4,7},{5,6},{6,5},{7,4},{8,11},{9,10},{10,... | collective-permute-start | bytes 3080 | tf_op jit(solution)/shard_map/ppermute | solution.py:57
  121.4 1.8 %collective-permute-done.35 = f32[256]{0:T(256)S(1)} collective-permute-done((f32[256]{0:T(256)S(1)}, f32[256]{0:T(256)S(1)}, u32[]{:S(2)}, u32[]{:S(2)}) %collective-permute-start.35) | collective-permute-done | bytes 1056 | tf_op jit(solution)/shard_map/ppermute | solution.py:57
  123.2 20.9 %collective-permute-start.37 = (f32[1024]{0:T(1024)S(1)}, f32[1024]{0:T(1024)S(1)}, u32[]{:S(2)}, u32[]{:S(2)}) collective-permute-start(f32[1024]{0:T(1024)S(1)} %pad_maximum_fusion.3), channel_id=1, source_target_pairs={{0,8},{1,9},{2,10},{3,11},{4,12},{5,13},{6,14},{7,15},{8,0},{9,1},... | collective-permute-start | bytes 12296 | tf_op jit(solution)/shard_map/ppermute | solution.py:64
  144.1 1.6 %collective-permute-done.37 = f32[1024]{0:T(1024)S(1)} collective-permute-done((f32[1024]{0:T(1024)S(1)}, f32[1024]{0:T(1024)S(1)}, u32[]{:S(2)}, u32[]{:S(2)}) %collective-permute-start.37) | collective-permute-done | bytes 4128 | tf_op jit(solution)/shard_map/ppermute | solution.py:64
  (121 shorter events, 24.5 us)
Async XLA Ops:
  2.0 15.2 %collective-permute-start = (bf16[256,1024]{1,0:T(8,128)(2,1)}, bf16[256,1024]{1,0:T(8,128)(2,1)}, u32[]{:S(2)}, u32[]{:S(2)}) collective-permute-start(bf16[256,1024]{1,0:T(8,128)(2,1)} %constant_dynamic-slice_fusion), channel_id=1, source_target_pairs={{0,2},{1,3},{2,0},{3,1},{4,6},{5,7},{6,4},{7,5},{8,10},{9,11},{10,... | collective-permute-start | bytes 1572872 | tf_op jit(solution)/shard_map/ppermute | solution.py:57
  4.9 23.3 %collective-permute-start.3 = (bf16[256,1024]{1,0:T(8,128)(2,1)}, bf16[256,1024]{1,0:T(8,128)(2,1)}, u32[]{:S(2)}, u32[]{:S(2)}) collective-permute-start(bf16[256,1024]{1,0:T(8,128)(2,1)} %constant_dynamic-slice_fusion), channel_id=1, source_target_pairs={{0,1},{1,0},{2,3},{3,2},{4,5},{5,4},{6,7},{7,6},{8,9},{9,8},{10,11... | collective-permute-start | bytes 1572872 | tf_op jit(solution)/shard_map/ppermute | solution.py:57
  18.1 8.6 %collective-permute-start.1 = (bf16[512,256]{1,0:T(8,128)(2,1)S(1)}, bf16[512,256]{1,0:T(8,128)(2,1)S(1)}, u32[]{:S(2)}, u32[]{:S(2)}) collective-permute-start(bf16[512,256]{1,0:T(8,128)(2,1)S(1)} %get-tuple-element.29), channel_id=1, source_target_pairs={{0,2},{1,3},{2,0},{3,1},{4,6},{5,7},{6,4},{7,5},{8,10},{9,11},{10,... | collective-permute-start | bytes 786440 | tf_op jit(solution)/shard_map/ppermute | solution.py:57
  21.4 6.8 %collective-permute-start.2 = (bf16[512,256]{1,0:T(8,128)(2,1)S(1)}, bf16[512,256]{1,0:T(8,128)(2,1)S(1)}, u32[]{:S(2)}, u32[]{:S(2)}) collective-permute-start(bf16[512,256]{1,0:T(8,128)(2,1)S(1)} %get-tuple-element.28), channel_id=1, source_target_pairs={{0,1},{1,0},{2,3},{3,2},{4,5},{5,4},{6,7},{7,6},{8,9},{9,8},{10,11... | collective-permute-start | bytes 786440 | tf_op jit(solution)/shard_map/ppermute | solution.py:57
  21.5 8.7 %collective-permute-start.4 = (bf16[512,256]{1,0:T(8,128)(2,1)S(1)}, bf16[512,256]{1,0:T(8,128)(2,1)S(1)}, u32[]{:S(2)}, u32[]{:S(2)}) collective-permute-start(bf16[512,256]{1,0:T(8,128)(2,1)S(1)} %get-tuple-element.27), channel_id=1, source_target_pairs={{0,3},{1,2},{2,1},{3,0},{4,7},{5,6},{6,5},{7,4},{8,11},{9,10},{10,... | collective-permute-start | bytes 786440 | tf_op jit(solution)/shard_map/ppermute | solution.py:57
  21.9 8.4 %collective-permute-start.5 = (bf16[256,1024]{1,0:T(8,128)(2,1)}, bf16[256,1024]{1,0:T(8,128)(2,1)S(1)}, u32[]{:S(2)}, u32[]{:S(2)}) collective-permute-start(bf16[256,1024]{1,0:T(8,128)(2,1)} %collective-permute-done), channel_id=1, source_target_pairs={{0,1},{1,0},{2,3},{3,2},{4,5},{5,4},{6,7},{7,6},{8,9},{9,8},{10,11... | collective-permute-start | bytes 1572872 | tf_op jit(solution)/shard_map/ppermute | solution.py:57
  30.7 26.0 %collective-permute-start.12 = (bf16[512,1024]{1,0:T(8,128)(2,1)S(1)}, bf16[512,1024]{1,0:T(8,128)(2,1)S(1)}, u32[]{:S(2)}, u32[]{:S(2)}) collective-permute-start(bf16[512,1024]{1,0:T(8,128)(2,1)S(1)} %add_convert_fusion.1), channel_id=1, source_target_pairs={{0,4},{1,5},{2,6},{3,7},{4,0},{5,1},{6,2},{7,3},{8,12},{9,13},{10,... | collective-permute-start | bytes 3145736 | tf_op jit(solution)/shard_map/ppermute | solution.py:64
  32.4 24.4 %collective-permute-start.11 = (bf16[512,1024]{1,0:T(8,128)(2,1)S(1)}, bf16[512,1024]{1,0:T(8,128)(2,1)S(1)}, u32[]{:S(2)}, u32[]{:S(2)}) collective-permute-start(bf16[512,1024]{1,0:T(8,128)(2,1)S(1)} %add_convert_fusion.1), channel_id=1, source_target_pairs={{0,1},{1,0},{2,3},{3,2},{4,8},{5,9},{6,10},{7,11},{8,4},{9,5},{10,... | collective-permute-start | bytes 3145736 | tf_op jit(solution)/shard_map/ppermute | solution.py:64
  33.3 23.5 %collective-permute-start.6 = (bf16[256,1024]{1,0:T(8,128)(2,1)S(1)}, bf16[256,1024]{1,0:T(8,128)(2,1)S(1)}, u32[]{:S(2)}, u32[]{:S(2)}) collective-permute-start(bf16[256,1024]{1,0:T(8,128)(2,1)S(1)} %get-tuple-element.22), channel_id=1, source_target_pairs={{0,2},{1,3},{2,0},{3,1},{4,6},{5,7},{6,4},{7,5},{8,10},{9,11},{10,... | collective-permute-start | bytes 1572872 | tf_op jit(solution)/shard_map/ppermute | solution.py:57
  34.8 4.0 %collective-permute-start.8 = (bf16[256,1024]{1,0:T(8,128)(2,1)S(1)}, bf16[256,1024]{1,0:T(8,128)(2,1)S(1)}, u32[]{:S(2)}, u32[]{:S(2)}) collective-permute-start(bf16[256,1024]{1,0:T(8,128)(2,1)S(1)} %get-tuple-element.22), channel_id=1, source_target_pairs={{0,1},{1,0},{2,3},{3,2},{4,5},{5,4},{6,7},{7,6},{8,9},{9,8},{10,11... | collective-permute-start | bytes 1572872 | tf_op jit(solution)/shard_map/ppermute | solution.py:57
  34.9 2.6 %collective-permute-start.7 = (bf16[256,1024]{1,0:T(8,128)(2,1)S(1)}, bf16[256,1024]{1,0:T(8,128)(2,1)S(1)}, u32[]{:S(2)}, u32[]{:S(2)}) collective-permute-start(bf16[256,1024]{1,0:T(8,128)(2,1)S(1)} %get-tuple-element.23), channel_id=1, source_target_pairs={{0,1},{1,0},{2,3},{3,2},{4,5},{5,4},{6,7},{7,6},{8,9},{9,8},{10,11... | collective-permute-start | bytes 1572872 | tf_op jit(solution)/shard_map/ppermute | solution.py:57
  37.5 21.0 %collective-permute-start.10 = (bf16[256,1024]{1,0:T(8,128)(2,1)S(1)}, bf16[256,1024]{1,0:T(8,128)(2,1)S(1)}, u32[]{:S(2)}, u32[]{:S(2)}) collective-permute-start(bf16[256,1024]{1,0:T(8,128)(2,1)S(1)} %get-tuple-element.23), channel_id=1, source_target_pairs={{0,2},{1,3},{2,0},{3,1},{4,6},{5,7},{6,4},{7,5},{8,10},{9,11},{10,... | collective-permute-start | bytes 1572872 | tf_op jit(solution)/shard_map/ppermute | solution.py:57
  38.8 19.7 %collective-permute-start.9 = (bf16[256,1024]{1,0:T(8,128)(2,1)S(1)}, bf16[256,1024]{1,0:T(8,128)(2,1)S(1)}, u32[]{:S(2)}, u32[]{:S(2)}) collective-permute-start(bf16[256,1024]{1,0:T(8,128)(2,1)S(1)} %get-tuple-element.21), channel_id=1, source_target_pairs={{0,1},{1,0},{2,3},{3,2},{4,5},{5,4},{6,7},{7,6},{8,9},{9,8},{10,11... | collective-permute-start | bytes 1572872 | tf_op jit(solution)/shard_map/ppermute | solution.py:57
  58.7 2.6 %collective-permute-start.13 = (bf16[256,1024]{1,0:T(8,128)(2,1)S(1)}, bf16[256,1024]{1,0:T(8,128)(2,1)S(1)}, u32[]{:S(2)}, u32[]{:S(2)}) collective-permute-start(bf16[256,1024]{1,0:T(8,128)(2,1)S(1)} %get-tuple-element.47), channel_id=1, source_target_pairs={{0,1},{1,0},{2,3},{3,2},{4,5},{5,4},{6,7},{7,6},{8,9},{9,8},{10,11... | collective-permute-start | bytes 1572872 | tf_op jit(solution)/shard_map/ppermute | solution.py:57
  62.8 4.8 %collective-permute-start.19 = (bf16[512,1024]{1,0:T(8,128)(2,1)S(1)}, bf16[512,1024]{1,0:T(8,128)(2,1)S(1)}, u32[]{:S(2)}, u32[]{:S(2)}) collective-permute-start(bf16[512,1024]{1,0:T(8,128)(2,1)S(1)} %get-tuple-element.20), channel_id=1, source_target_pairs={{0,1},{1,0},{2,3},{3,2},{4,8},{5,9},{6,10},{7,11},{8,4},{9,5},{10,... | collective-permute-start | bytes 3145736 | tf_op jit(solution)/shard_map/ppermute | solution.py:64
  63.0 4.6 %collective-permute-start.18 = (bf16[512,1024]{1,0:T(8,128)(2,1)S(1)}, bf16[512,1024]{1,0:T(8,128)(2,1)S(1)}, u32[]{:S(2)}, u32[]{:S(2)}) collective-permute-start(bf16[512,1024]{1,0:T(8,128)(2,1)S(1)} %get-tuple-element.19), channel_id=1, source_target_pairs={{0,1},{1,0},{2,3},{3,2},{4,5},{5,4},{6,7},{7,6},{8,12},{9,13},{10,... | collective-permute-start | bytes 3145736 | tf_op jit(solution)/shard_map/ppermute | solution.py:64
  63.4 14.8 %collective-permute-start.17 = (bf16[256,1024]{1,0:T(8,128)(2,1)S(1)}, bf16[256,1024]{1,0:T(8,128)(2,1)S(1)}, u32[]{:S(2)}, u32[]{:S(2)}) collective-permute-start(bf16[256,1024]{1,0:T(8,128)(2,1)S(1)} %get-tuple-element.33), channel_id=1, source_target_pairs={{0,2},{1,3},{2,0},{3,1},{4,6},{5,7},{6,4},{7,5},{8,10},{9,11},{10,... | collective-permute-start | bytes 1572872 | tf_op jit(solution)/shard_map/ppermute | solution.py:57
  65.3 23.4 %collective-permute-start.16 = (bf16[256,1024]{1,0:T(8,128)(2,1)S(1)}, bf16[256,1024]{1,0:T(8,128)(2,1)S(1)}, u32[]{:S(2)}, u32[]{:S(2)}) collective-permute-start(bf16[256,1024]{1,0:T(8,128)(2,1)S(1)} %broadcast_add_fusion.3), channel_id=1, source_target_pairs={{0,2},{1,3},{2,0},{3,1},{4,6},{5,7},{6,4},{7,5},{8,10},{9,11},{10,... | collective-permute-start | bytes 1572872 | tf_op jit(solution)/shard_map/ppermute | solution.py:57
  65.6 23.1 %collective-permute-start.15 = (bf16[256,1024]{1,0:T(8,128)(2,1)S(1)}, bf16[256,1024]{1,0:T(8,128)(2,1)S(1)}, u32[]{:S(2)}, u32[]{:S(2)}) collective-permute-start(bf16[256,1024]{1,0:T(8,128)(2,1)S(1)} %get-tuple-element.32), channel_id=1, source_target_pairs={{0,16},{1,17},{2,18},{3,19},{4,20},{5,21},{6,22},{7,23},{8,24},{9,... | collective-permute-start | bytes 1572872 | tf_op jit(solution)/shard_map/ppermute | solution.py:72
  89.7 7.4 %collective-permute-start.20 = (bf16[256,1024]{1,0:T(8,128)(2,1)S(1)}, bf16[256,1024]{1,0:T(8,128)(2,1)S(1)}, u32[]{:S(2)}, u32[]{:S(2)}) collective-permute-start(bf16[256,1024]{1,0:T(8,128)(2,1)S(1)} %get-tuple-element.46), channel_id=1, source_target_pairs={{0,1},{1,0},{2,3},{3,2},{4,5},{5,4},{6,7},{7,6},{8,9},{9,8},{10,11... | collective-permute-start | bytes 1572872 | tf_op jit(solution)/shard_map/ppermute | solution.py:57
  90.3 5.4 %collective-permute-start.26 = (bf16[256,1024]{1,0:T(8,128)(2,1)S(1)}, bf16[256,1024]{1,0:T(8,128)(2,1)S(1)}, u32[]{:S(2)}, u32[]{:S(2)}) collective-permute-start(bf16[256,1024]{1,0:T(8,128)(2,1)S(1)} %get-tuple-element.44), channel_id=1, source_target_pairs={{0,1},{1,0},{2,3},{3,2},{4,5},{5,4},{6,7},{7,6},{8,9},{9,8},{10,11... | collective-permute-start | bytes 1572872 | tf_op jit(solution)/shard_map/ppermute | solution.py:57
  92.0 5.8 %collective-permute-start.22 = (bf16[256,1024]{1,0:T(8,128)(2,1)S(1)}, bf16[256,1024]{1,0:T(8,128)(2,1)S(1)}, u32[]{:S(2)}, u32[]{:S(2)}) collective-permute-start(bf16[256,1024]{1,0:T(8,128)(2,1)S(1)} %get-tuple-element.31), channel_id=1, source_target_pairs={{0,1},{1,0},{2,3},{3,2},{4,5},{5,4},{6,7},{7,6},{8,9},{9,8},{10,11... | collective-permute-start | bytes 1572872 | tf_op jit(solution)/shard_map/ppermute | solution.py:57
  92.4 15.9 %collective-permute-start.27 = (bf16[256,1024]{1,0:T(8,128)(2,1)S(1)}, bf16[256,1024]{1,0:T(8,128)(2,1)S(1)}, u32[]{:S(2)}, u32[]{:S(2)}) collective-permute-start(bf16[256,1024]{1,0:T(8,128)(2,1)S(1)} %get-tuple-element.31), channel_id=1, source_target_pairs={{0,2},{1,3},{2,0},{3,1},{4,6},{5,7},{6,4},{7,5},{8,10},{9,11},{10,... | collective-permute-start | bytes 1572872 | tf_op jit(solution)/shard_map/ppermute | solution.py:57
  94.2 13.7 %collective-permute-start.23 = (bf16[256,1024]{1,0:T(8,128)(2,1)S(1)}, bf16[256,1024]{1,0:T(8,128)(2,1)S(1)}, u32[]{:S(2)}, u32[]{:S(2)}) collective-permute-start(bf16[256,1024]{1,0:T(8,128)(2,1)S(1)} %get-tuple-element.30), channel_id=1, source_target_pairs={{0,16},{1,17},{2,18},{3,19},{4,20},{5,21},{6,22},{7,23},{8,24},{9,... | collective-permute-start | bytes 1572872 | tf_op jit(solution)/shard_map/ppermute | solution.py:72
  99.0 10.0 %collective-permute-start.24 = (f32[256,256]{1,0:T(8,128)S(1)}, f32[256,256]{1,0:T(8,128)S(1)}, u32[]{:S(2)}, u32[]{:S(2)}) collective-permute-start(f32[256,256]{1,0:T(8,128)S(1)} %convolution_add_fusion.4), channel_id=1, source_target_pairs={{0,1},{1,0},{2,3},{3,2},{4,5},{5,4},{6,7},{7,6},{8,12},{9,13},{10,... | collective-permute-start | bytes 786440 | tf_op jit(solution)/shard_map/ppermute | solution.py:64
  109.5 2.6 %collective-permute-start.25 = (f32[256,256]{1,0:T(8,128)S(1)}, f32[256,256]{1,0:T(8,128)S(1)}, u32[]{:S(2)}, u32[]{:S(2)}) collective-permute-start(f32[256,256]{1,0:T(8,128)S(1)} %fusion.16), channel_id=1, source_target_pairs={{0,1},{1,0},{2,3},{3,2},{4,5},{5,4},{6,7},{7,6},{8,12},{9,13},{10,... | collective-permute-start | bytes 786440 | tf_op jit(solution)/shard_map/ppermute | solution.py:64
  114.2 3.6 %collective-permute-start.32 = (f32[256]{0:T(256)S(1)}, f32[256]{0:T(256)S(1)}, u32[]{:S(2)}, u32[]{:S(2)}) collective-permute-start(f32[256]{0:T(256)S(1)} %get-tuple-element.43), channel_id=1, source_target_pairs={{0,16},{1,17},{2,18},{3,19},{4,20},{5,21},{6,22},{7,23},{8,24},{9,... | collective-permute-start | bytes 3080 | tf_op jit(solution)/shard_map/ppermute | solution.py:72
  115.8 3.6 %collective-permute-start.33 = (f32[256]{0:T(256)S(1)}, f32[256]{0:T(256)S(1)}, u32[]{:S(2)}, u32[]{:S(2)}) collective-permute-start(f32[256]{0:T(256)S(1)} %get-tuple-element.43), channel_id=1, source_target_pairs={{0,16},{1,17},{2,18},{3,19},{4,20},{5,21},{6,22},{7,23},{8,28},{9,... | collective-permute-start | bytes 3080 | tf_op jit(solution)/shard_map/ppermute | solution.py:72
  116.4 3.1 %collective-permute-start.31 = (f32[256]{0:T(256)S(1)}, f32[256]{0:T(256)S(1)}, u32[]{:S(2)}, u32[]{:S(2)}) collective-permute-start(f32[256]{0:T(256)S(1)} %get-tuple-element.42), channel_id=1, source_target_pairs={{0,1},{1,0},{2,3},{3,2},{4,5},{5,4},{6,7},{7,6},{8,12},{9,13},{10,... | collective-permute-start | bytes 3080 | tf_op jit(solution)/shard_map/ppermute | solution.py:64
  119.5 3.6 %collective-permute-start.35 = (f32[256]{0:T(256)S(1)}, f32[256]{0:T(256)S(1)}, u32[]{:S(2)}, u32[]{:S(2)}) collective-permute-start(f32[256]{0:T(256)S(1)} %add_add_fusion.3), channel_id=1, source_target_pairs={{0,2},{1,3},{2,0},{3,1},{4,6},{5,7},{6,4},{7,5},{8,10},{9,11},{10,... | collective-permute-start | bytes 3080 | tf_op jit(solution)/shard_map/ppermute | solution.py:57
  119.9 3.3 %collective-permute-start.36 = (f32[256]{0:T(256)S(1)}, f32[256]{0:T(256)S(1)}, u32[]{:S(2)}, u32[]{:S(2)}) collective-permute-start(f32[256]{0:T(256)S(1)} %add_add_fusion.3), channel_id=1, source_target_pairs={{0,3},{1,2},{2,1},{3,0},{4,7},{5,6},{6,5},{7,4},{8,11},{9,10},{10,... | collective-permute-start | bytes 3080 | tf_op jit(solution)/shard_map/ppermute | solution.py:57
  123.2 22.5 %collective-permute-start.37 = (f32[1024]{0:T(1024)S(1)}, f32[1024]{0:T(1024)S(1)}, u32[]{:S(2)}, u32[]{:S(2)}) collective-permute-start(f32[1024]{0:T(1024)S(1)} %pad_maximum_fusion.3), channel_id=1, source_target_pairs={{0,8},{1,9},{2,10},{3,11},{4,12},{5,13},{6,14},{7,15},{8,0},{9,1},... | collective-permute-start | bytes 12296 | tf_op jit(solution)/shard_map/ppermute | solution.py:64
  (10 other events, 56.7 us)

commit v11 on v10

--- a/solution.py
+++ b/solution.py
@@ -27,6 +27,12 @@
     done = lax.optimization_barrier(token(*first))
     done = lax.optimization_barrier(token(*second) + done)
     return token(*others) + done
+
+
+def chained(zeros, steps):
+    for _ in range(steps):
+        zeros = lax.optimization_barrier(jnp.minimum(jnp.abs(zeros), 0.0))
+    return zeros
 
 
 def behind(value, zeros):
@@ -126,10 +132,11 @@
         order = [(s, 0) for s in range(nx)] + [(s, 1) for s in range(nx)]
 
         own1 = lax.optimization_barrier(factor_own([0, 1, 2, 1]))
-        same1 = [own1] + factor_x(own1)
-
-        done = token(*same1[1:])
-        features = [inner(behind(rows_of(s, f), done), s, f) if s or f else rows_of(0, 0) for s, f in order]
+        moved1 = factor_x(own1)
+        arrived = chained(token(*moved1), 4)
+
+        features = [inner(rows_of(s, f), s, f) if s or f else rows_of(0, 0) for s, f in order]
+        same1 = [own1] + [behind(v, arrived) for v in moved1]
         first = partial(same1 + factor_flip(same1)).astype(BF)
 
         start = token(first)

time: 147 us -> 144 us (0.980)
  other arithmetic: 6.04 us -> 9.63 us
  matrix products: 15.5 us -> 13.5 us
  waiting for transfers between devices: 71.4 us -> 69.5 us
  local copies, waits for them, and re-layouts: 6.83 us -> 5.34 us
    dot_general x16, matrix products: 10.8 us -> 8.74 us  [matmul(): lax.dot_general(a, b, (((1,), (0,)), ((), ())), preferred_element_type=F32)]
    squeeze x1, other arithmetic: 0.03 us -> 2 us  [rows_of(): lax.dynamic_slice(rows, (lax.rem(x + s, nx), core ^ f, 0, 0), (1, 1, n_ro...]
    ppermute x24, waiting for transfers between devices: 39.8 us -> 38.3 us  [inner(): return lax.ppermute(value, 'tgt', pairs)]
where the time goes in v11:
time: 144 us; the launch traced here: 143 us
  waiting for transfers between devices  69.5 us (48%)
  starting transfers between devices  45 us (31%)
  matrix products  13.5 us (9%)
  other arithmetic  9.63 us (7%)
  local copies, waits for them, and re-layouts  5.34 us (4%)
    ppermute x24, waiting for transfers between devices, inner(): return lax.ppermute(value, 'tgt', pairs)  38.3 us
    ppermute x10, starting transfers between devices, along_z(): return lax.ppermute(value, 'tgt', pairs)  24.3 us
    ppermute x10, waiting for transfers between devices, along_z(): return lax.ppermute(value, 'tgt', pairs)  19.4 us
    ppermute x24, starting transfers between devices, inner(): return lax.ppermute(value, 'tgt', pairs)  15.5 us
    ppermute x4, waiting for transfers between devices, over_pool(): return lax.ppermute(value, ('pool', 'tgt'), pairs)  11.8 us
    dot_general x16, matrix products, matmul(): lax.dot_general(a, b, (((1,), (0,)), ((), ())), preferred_element_type=F32)  8.74 us
    ppermute x4, starting transfers between devices, over_pool(): return lax.ppermute(value, ('pool', 'tgt'), pairs)  5.14 us
    dot_general x10, matrix products, matmul_t(): lax.dot_general(a, b, (((1,), (1,)), ((), ())), preferred_element_type=F32)  4.71 us
  transfers between devices with their start and end apart: 38, of which 19 were waited for; matrix products, arithmetic and copies ran while one was open for 16% of the time, Pallas kernels for 0%

profile of v11, /device:TPU:0, one launch (start us, length us, event | category | flops | bytes accessed | tf_op | source)
XLA Modules:
  0.0 143.4 jit_solution(11585298207088862893)
XLA Ops:
  0.0 1.2 constant_dynamic-slice_fusion
  1.7 2.6 %collective-permute-start.1 = (bf16[256,1024]{1,0:T(8,128)(2,1)S(1)}, bf16[256,1024]{1,0:T(8,128)(2,1)}, u32[]{:S(2)}, u32[]{:S(2)}) collective-permute-start(bf16[256,1024]{1,0:T(8,128)(2,1)S(1)} %constant_dynamic-slice_fusion), channel_id=1, source_target_pairs={{0,2},{1,3},{2,0},{3,1},{4,6},{5,7},{6,4},{7,5},{8,10},{9,11},{10,... | collective-permute-start | bytes 1572872 | tf_op jit(solution)/shard_map/ppermute | solution.py:63
  5.0 3.9 %gather_fusion = bf16[1024,256]{1,0:T(8,128)(2,1)S(1)} fusion(bf16[4096,256]{1,0:T(8,128)(2,1)S(1)} %copy-done, s32[1024]{0:T(1024)S(1)} %fusion.28), kind=kCustom, calls=%fused_computation | custom fusion | bytes 1052672 | tf_op jit(solution)/shard_map/gather | solution.py:104
  9.0 2.0 %fusion.22 = (bf16[512,256]{1,0:T(8,128)(2,1)}, bf16[512,256]{1,0:T(8,128)(2,1)}, bf16[512,256]{1,0:T(8,128)(2,1)S(1)}, bf16[512,256]{1,0:T(8,128)(2,1)S(1)}) fusion(s32[]{:T(128)S(6)} %select_n.172, s32[]{:T(128)S(6)} %select_n.165, bf16[2,2,256,256]{3,2,1,0:T(8,128)(2,1)} %bitcast.52, bf16[2,2,256,256]{3,2,1,0:T(8,128)(2,1)S(1)} %bitcast.51, ...), kind=kLoop, calls=%fused_computation.66 | loop fusion | flops 2097152 | bytes 2097168 | tf_op jit(solution)/shard_map/squeeze | solution.py:114
  11.4 1.4 collective-permute-start.4
  13.3 3.9 %collective-permute-done.1 = bf16[256,1024]{1,0:T(8,128)(2,1)} collective-permute-done((bf16[256,1024]{1,0:T(8,128)(2,1)S(1)}, bf16[256,1024]{1,0:T(8,128)(2,1)}, u32[]{:S(2)}, u32[]{:S(2)}) %collective-permute-start.1) | collective-permute-done | bytes 524320 | tf_op jit(solution)/shard_map/ppermute | solution.py:63
  18.0 1.1 broadcast_add_fusion.6
  19.2 3.5 %collective-permute-done = bf16[512,256]{1,0:T(8,128)(2,1)S(1)} collective-permute-done((bf16[512,256]{1,0:T(8,128)(2,1)}, bf16[512,256]{1,0:T(8,128)(2,1)S(1)}, u32[]{:S(2)}, u32[]{:S(2)}) %collective-permute-start) | collective-permute-done | bytes 262176 | tf_op jit(solution)/shard_map/ppermute | solution.py:63
  23.2 1.5 %fusion.89 = f32[512,1024]{1,0:T(8,128)S(1)} fusion(bf16[512,256]{1,0:T(8,128)(2,1)S(1)} %collective-permute-done.2, bf16[256,1024]{1,0:T(8,128)(2,1)} %collective-permute-done.3), kind=kOutput, calls=%fused_computation.177 | convolution fusion | flops 268435456 | bytes 2883584 | tf_op jit(solution)/shard_map/dot_general | solution.py:13
  24.7 3.1 %collective-permute-done.4 = bf16[512,256]{1,0:T(8,128)(2,1)S(1)} collective-permute-done((bf16[512,256]{1,0:T(8,128)(2,1)S(1)}, bf16[512,256]{1,0:T(8,128)(2,1)S(1)}, u32[]{:S(2)}, u32[]{:S(2)}) %collective-permute-start.4) | collective-permute-done | bytes 262176 | tf_op jit(solution)/shard_map/ppermute | solution.py:63
  28.3 1.7 %collective-permute-start.12 = (bf16[512,1024]{1,0:T(8,128)(2,1)S(1)}, bf16[512,1024]{1,0:T(8,128)(2,1)S(1)}, u32[]{:S(2)}, u32[]{:S(2)}) collective-permute-start(bf16[512,1024]{1,0:T(8,128)(2,1)S(1)} %add_convert_fusion.1), channel_id=1, source_target_pairs={{0,4},{1,5},{2,6},{3,7},{4,0},{5,1},{6,2},{7,3},{8,12},{9,13},{10,... | collective-permute-start | bytes 3145736 | tf_op jit(solution)/shard_map/ppermute | solution.py:70
  30.4 1.6 %collective-permute-start.6 = (bf16[256,1024]{1,0:T(8,128)(2,1)S(1)}, bf16[256,1024]{1,0:T(8,128)(2,1)S(1)}, u32[]{:S(2)}, u32[]{:S(2)}) collective-permute-start(bf16[256,1024]{1,0:T(8,128)(2,1)S(1)} %get-tuple-element.22), channel_id=1, source_target_pairs={{0,2},{1,3},{2,0},{3,1},{4,6},{5,7},{6,4},{7,5},{8,10},{9,11},{10,... | collective-permute-start | bytes 1572872 | tf_op jit(solution)/shard_map/ppermute | solution.py:63
  33.4 1.3 collective-permute-done.7
  34.6 1.0 collective-permute-start.10
  36.7 17.0 %collective-permute-done.12 = bf16[512,1024]{1,0:T(8,128)(2,1)S(1)} collective-permute-done((bf16[512,1024]{1,0:T(8,128)(2,1)S(1)}, bf16[512,1024]{1,0:T(8,128)(2,1)S(1)}, u32[]{:S(2)}, u32[]{:S(2)}) %collective-permute-start.12) | collective-permute-done | bytes 1048608 | tf_op jit(solution)/shard_map/ppermute | solution.py:70
  53.7 2.4 %collective-permute-done.10 = bf16[256,1024]{1,0:T(8,128)(2,1)S(1)} collective-permute-done((bf16[256,1024]{1,0:T(8,128)(2,1)S(1)}, bf16[256,1024]{1,0:T(8,128)(2,1)S(1)}, u32[]{:S(2)}, u32[]{:S(2)}) %collective-permute-start.10) | collective-permute-done | bytes 524320 | tf_op jit(solution)/shard_map/ppermute | solution.py:63
  59.4 0.9 add_convert_fusion.2
  61.0 1.6 %collective-permute-start.17 = (bf16[256,1024]{1,0:T(8,128)(2,1)S(1)}, bf16[256,1024]{1,0:T(8,128)(2,1)S(1)}, u32[]{:S(2)}, u32[]{:S(2)}) collective-permute-start(bf16[256,1024]{1,0:T(8,128)(2,1)S(1)} %get-tuple-element.30), channel_id=1, source_target_pairs={{0,2},{1,3},{2,0},{3,1},{4,6},{5,7},{6,4},{7,5},{8,10},{9,11},{10,... | collective-permute-start | bytes 1572872 | tf_op jit(solution)/shard_map/ppermute | solution.py:63
  63.2 1.5 %collective-permute-start.15 = (bf16[256,1024]{1,0:T(8,128)(2,1)S(1)}, bf16[256,1024]{1,0:T(8,128)(2,1)S(1)}, u32[]{:S(2)}, u32[]{:S(2)}) collective-permute-start(bf16[256,1024]{1,0:T(8,128)(2,1)S(1)} %get-tuple-element.29), channel_id=1, source_target_pairs={{0,16},{1,17},{2,18},{3,19},{4,20},{5,21},{6,22},{7,23},{8,24},{9,... | collective-permute-start | bytes 1572872 | tf_op jit(solution)/shard_map/ppermute | solution.py:78
  65.2 10.6 %collective-permute-done.17 = bf16[256,1024]{1,0:T(8,128)(2,1)S(1)} collective-permute-done((bf16[256,1024]{1,0:T(8,128)(2,1)S(1)}, bf16[256,1024]{1,0:T(8,128)(2,1)S(1)}, u32[]{:S(2)}, u32[]{:S(2)}) %collective-permute-start.17) | collective-permute-done | bytes 524320 | tf_op jit(solution)/shard_map/ppermute | solution.py:63
  75.8 10.4 %collective-permute-done.16 = bf16[256,1024]{1,0:T(8,128)(2,1)S(1)} collective-permute-done((bf16[256,1024]{1,0:T(8,128)(2,1)S(1)}, bf16[256,1024]{1,0:T(8,128)(2,1)S(1)}, u32[]{:S(2)}, u32[]{:S(2)}) %collective-permute-start.16) | collective-permute-done | bytes 524320 | tf_op jit(solution)/shard_map/ppermute | solution.py:63
  88.4 1.0 add_convert_fusion
  89.9 1.5 %collective-permute-start.27 = (bf16[256,1024]{1,0:T(8,128)(2,1)S(1)}, bf16[256,1024]{1,0:T(8,128)(2,1)S(1)}, u32[]{:S(2)}, u32[]{:S(2)}) collective-permute-start(bf16[256,1024]{1,0:T(8,128)(2,1)S(1)} %get-tuple-element.28), channel_id=1, source_target_pairs={{0,2},{1,3},{2,0},{3,1},{4,6},{5,7},{6,4},{7,5},{8,10},{9,11},{10,... | collective-permute-start | bytes 1572872 | tf_op jit(solution)/shard_map/ppermute | solution.py:63
  91.4 1.5 %collective-permute-start.23 = (bf16[256,1024]{1,0:T(8,128)(2,1)S(1)}, bf16[256,1024]{1,0:T(8,128)(2,1)S(1)}, u32[]{:S(2)}, u32[]{:S(2)}) collective-permute-start(bf16[256,1024]{1,0:T(8,128)(2,1)S(1)} %get-tuple-element.27), channel_id=1, source_target_pairs={{0,16},{1,17},{2,18},{3,19},{4,20},{5,21},{6,22},{7,23},{8,24},{9,... | collective-permute-start | bytes 1572872 | tf_op jit(solution)/shard_map/ppermute | solution.py:78
  96.4 8.7 %collective-permute-done.23 = bf16[256,1024]{1,0:T(8,128)(2,1)S(1)} collective-permute-done((bf16[256,1024]{1,0:T(8,128)(2,1)S(1)}, bf16[256,1024]{1,0:T(8,128)(2,1)S(1)}, u32[]{:S(2)}, u32[]{:S(2)}) %collective-permute-start.23) | collective-permute-done | bytes 524320 | tf_op jit(solution)/shard_map/ppermute | solution.py:78
  111.5 1.6 %collective-permute-start.32 = (f32[256]{0:T(256)S(1)}, f32[256]{0:T(256)S(1)}, u32[]{:S(2)}, u32[]{:S(2)}) collective-permute-start(f32[256]{0:T(256)S(1)} %get-tuple-element.44), channel_id=1, source_target_pairs={{0,16},{1,17},{2,18},{3,19},{4,20},{5,21},{6,22},{7,23},{8,24},{9,... | collective-permute-start | bytes 3080 | tf_op jit(solution)/shard_map/ppermute | solution.py:78
  113.7 1.5 %collective-permute-done.32 = f32[256]{0:T(256)S(1)} collective-permute-done((f32[256]{0:T(256)S(1)}, f32[256]{0:T(256)S(1)}, u32[]{:S(2)}, u32[]{:S(2)}) %collective-permute-start.32) | collective-permute-done | bytes 1056 | tf_op jit(solution)/shard_map/ppermute | solution.py:78
  115.2 1.5 %collective-permute-done.33 = f32[256]{0:T(256)S(1)} collective-permute-done((f32[256]{0:T(256)S(1)}, f32[256]{0:T(256)S(1)}, u32[]{:S(2)}, u32[]{:S(2)}) %collective-permute-start.33) | collective-permute-done | bytes 1056 | tf_op jit(solution)/shard_map/ppermute | solution.py:78
  117.4 1.3 collective-permute-start.36
  118.7 1.8 %collective-permute-done.35 = f32[256]{0:T(256)S(1)} collective-permute-done((f32[256]{0:T(256)S(1)}, f32[256]{0:T(256)S(1)}, u32[]{:S(2)}, u32[]{:S(2)}) %collective-permute-start.35) | collective-permute-done | bytes 1056 | tf_op jit(solution)/shard_map/ppermute | solution.py:63
  120.5 20.7 %collective-permute-start.37 = (f32[1024]{0:T(1024)S(1)}, f32[1024]{0:T(1024)S(1)}, u32[]{:S(2)}, u32[]{:S(2)}) collective-permute-start(f32[1024]{0:T(1024)S(1)} %pad_maximum_fusion.3), channel_id=1, source_target_pairs={{0,8},{1,9},{2,10},{3,11},{4,12},{5,13},{6,14},{7,15},{8,0},{9,1},... | collective-permute-start | bytes 12296 | tf_op jit(solution)/shard_map/ppermute | solution.py:70
  141.2 1.6 %collective-permute-done.37 = f32[1024]{0:T(1024)S(1)} collective-permute-done((f32[1024]{0:T(1024)S(1)}, f32[1024]{0:T(1024)S(1)}, u32[]{:S(2)}, u32[]{:S(2)}) %collective-permute-start.37) | collective-permute-done | bytes 4128 | tf_op jit(solution)/shard_map/ppermute | solution.py:70
  (122 shorter events, 25.8 us)
Async XLA Ops:
  1.2 21.9 %collective-permute-start.3 = (bf16[256,1024]{1,0:T(8,128)(2,1)S(1)}, bf16[256,1024]{1,0:T(8,128)(2,1)}, u32[]{:S(2)}, u32[]{:S(2)}) collective-permute-start(bf16[256,1024]{1,0:T(8,128)(2,1)S(1)} %constant_dynamic-slice_fusion), channel_id=1, source_target_pairs={{0,1},{1,0},{2,3},{3,2},{4,5},{5,4},{6,7},{7,6},{8,9},{9,8},{10,11... | collective-permute-start | bytes 1572872 | tf_op jit(solution)/shard_map/ppermute | solution.py:63
  1.7 15.4 %collective-permute-start.1 = (bf16[256,1024]{1,0:T(8,128)(2,1)S(1)}, bf16[256,1024]{1,0:T(8,128)(2,1)}, u32[]{:S(2)}, u32[]{:S(2)}) collective-permute-start(bf16[256,1024]{1,0:T(8,128)(2,1)S(1)} %constant_dynamic-slice_fusion), channel_id=1, source_target_pairs={{0,2},{1,3},{2,0},{3,1},{4,6},{5,7},{6,4},{7,5},{8,10},{9,11},{10,... | collective-permute-start | bytes 1572872 | tf_op jit(solution)/shard_map/ppermute | solution.py:63
  11.0 12.2 %collective-permute-start.2 = (bf16[512,256]{1,0:T(8,128)(2,1)}, bf16[512,256]{1,0:T(8,128)(2,1)S(1)}, u32[]{:S(2)}, u32[]{:S(2)}) collective-permute-start(bf16[512,256]{1,0:T(8,128)(2,1)} %get-tuple-element.32), channel_id=1, source_target_pairs={{0,1},{1,0},{2,3},{3,2},{4,5},{5,4},{6,7},{7,6},{8,9},{9,8},{10,11... | collective-permute-start | bytes 786440 | tf_op jit(solution)/shard_map/ppermute | solution.py:63
  11.1 11.6 %collective-permute-start = (bf16[512,256]{1,0:T(8,128)(2,1)}, bf16[512,256]{1,0:T(8,128)(2,1)S(1)}, u32[]{:S(2)}, u32[]{:S(2)}) collective-permute-start(bf16[512,256]{1,0:T(8,128)(2,1)} %get-tuple-element.31), channel_id=1, source_target_pairs={{0,2},{1,3},{2,0},{3,1},{4,6},{5,7},{6,4},{7,5},{8,10},{9,11},{10,... | collective-permute-start | bytes 786440 | tf_op jit(solution)/shard_map/ppermute | solution.py:63
  11.4 16.4 %collective-permute-start.4 = (bf16[512,256]{1,0:T(8,128)(2,1)S(1)}, bf16[512,256]{1,0:T(8,128)(2,1)S(1)}, u32[]{:S(2)}, u32[]{:S(2)}) collective-permute-start(bf16[512,256]{1,0:T(8,128)(2,1)S(1)} %get-tuple-element.34), channel_id=1, source_target_pairs={{0,3},{1,2},{2,1},{3,0},{4,7},{5,6},{6,5},{7,4},{8,11},{9,10},{10,... | collective-permute-start | bytes 786440 | tf_op jit(solution)/shard_map/ppermute | solution.py:63
  19.1 8.7 %collective-permute-start.5 = (bf16[256,1024]{1,0:T(8,128)(2,1)S(1)}, bf16[256,1024]{1,0:T(8,128)(2,1)S(1)}, u32[]{:S(2)}, u32[]{:S(2)}) collective-permute-start(bf16[256,1024]{1,0:T(8,128)(2,1)S(1)} %broadcast_add_fusion.6), channel_id=1, source_target_pairs={{0,1},{1,0},{2,3},{3,2},{4,5},{5,4},{6,7},{7,6},{8,9},{9,8},{10,11... | collective-permute-start | bytes 1572872 | tf_op jit(solution)/shard_map/ppermute | solution.py:63
  28.3 25.3 %collective-permute-start.12 = (bf16[512,1024]{1,0:T(8,128)(2,1)S(1)}, bf16[512,1024]{1,0:T(8,128)(2,1)S(1)}, u32[]{:S(2)}, u32[]{:S(2)}) collective-permute-start(bf16[512,1024]{1,0:T(8,128)(2,1)S(1)} %add_convert_fusion.1), channel_id=1, source_target_pairs={{0,4},{1,5},{2,6},{3,7},{4,0},{5,1},{6,2},{7,3},{8,12},{9,13},{10,... | collective-permute-start | bytes 3145736 | tf_op jit(solution)/shard_map/ppermute | solution.py:70
  30.0 23.6 %collective-permute-start.11 = (bf16[512,1024]{1,0:T(8,128)(2,1)S(1)}, bf16[512,1024]{1,0:T(8,128)(2,1)S(1)}, u32[]{:S(2)}, u32[]{:S(2)}) collective-permute-start(bf16[512,1024]{1,0:T(8,128)(2,1)S(1)} %add_convert_fusion.1), channel_id=1, source_target_pairs={{0,1},{1,0},{2,3},{3,2},{4,8},{5,9},{6,10},{7,11},{8,4},{9,5},{10,... | collective-permute-start | bytes 3145736 | tf_op jit(solution)/shard_map/ppermute | solution.py:70
  30.4 23.2 %collective-permute-start.6 = (bf16[256,1024]{1,0:T(8,128)(2,1)S(1)}, bf16[256,1024]{1,0:T(8,128)(2,1)S(1)}, u32[]{:S(2)}, u32[]{:S(2)}) collective-permute-start(bf16[256,1024]{1,0:T(8,128)(2,1)S(1)} %get-tuple-element.22), channel_id=1, source_target_pairs={{0,2},{1,3},{2,0},{3,1},{4,6},{5,7},{6,4},{7,5},{8,10},{9,11},{10,... | collective-permute-start | bytes 1572872 | tf_op jit(solution)/shard_map/ppermute | solution.py:63
  32.0 4.2 %collective-permute-start.8 = (bf16[256,1024]{1,0:T(8,128)(2,1)S(1)}, bf16[256,1024]{1,0:T(8,128)(2,1)S(1)}, u32[]{:S(2)}, u32[]{:S(2)}) collective-permute-start(bf16[256,1024]{1,0:T(8,128)(2,1)S(1)} %get-tuple-element.22), channel_id=1, source_target_pairs={{0,1},{1,0},{2,3},{3,2},{4,5},{5,4},{6,7},{7,6},{8,9},{9,8},{10,11... | collective-permute-start | bytes 1572872 | tf_op jit(solution)/shard_map/ppermute | solution.py:63
  32.2 2.4 %collective-permute-start.7 = (bf16[256,1024]{1,0:T(8,128)(2,1)S(1)}, bf16[256,1024]{1,0:T(8,128)(2,1)S(1)}, u32[]{:S(2)}, u32[]{:S(2)}) collective-permute-start(bf16[256,1024]{1,0:T(8,128)(2,1)S(1)} %get-tuple-element.23), channel_id=1, source_target_pairs={{0,1},{1,0},{2,3},{3,2},{4,5},{5,4},{6,7},{7,6},{8,9},{9,8},{10,11... | collective-permute-start | bytes 1572872 | tf_op jit(solution)/shard_map/ppermute | solution.py:63
  34.6 21.4 %collective-permute-start.10 = (bf16[256,1024]{1,0:T(8,128)(2,1)S(1)}, bf16[256,1024]{1,0:T(8,128)(2,1)S(1)}, u32[]{:S(2)}, u32[]{:S(2)}) collective-permute-start(bf16[256,1024]{1,0:T(8,128)(2,1)S(1)} %get-tuple-element.23), channel_id=1, source_target_pairs={{0,2},{1,3},{2,0},{3,1},{4,6},{5,7},{6,4},{7,5},{8,10},{9,11},{10,... | collective-permute-start | bytes 1572872 | tf_op jit(solution)/shard_map/ppermute | solution.py:63
  36.1 19.9 %collective-permute-start.9 = (bf16[256,1024]{1,0:T(8,128)(2,1)S(1)}, bf16[256,1024]{1,0:T(8,128)(2,1)S(1)}, u32[]{:S(2)}, u32[]{:S(2)}) collective-permute-start(bf16[256,1024]{1,0:T(8,128)(2,1)S(1)} %get-tuple-element.21), channel_id=1, source_target_pairs={{0,1},{1,0},{2,3},{3,2},{4,5},{5,4},{6,7},{7,6},{8,9},{9,8},{10,11... | collective-permute-start | bytes 1572872 | tf_op jit(solution)/shard_map/ppermute | solution.py:63
  56.3 2.6 %collective-permute-start.13 = (bf16[256,1024]{1,0:T(8,128)(2,1)S(1)}, bf16[256,1024]{1,0:T(8,128)(2,1)S(1)}, u32[]{:S(2)}, u32[]{:S(2)}) collective-permute-start(bf16[256,1024]{1,0:T(8,128)(2,1)S(1)} %get-tuple-element.48), channel_id=1, source_target_pairs={{0,1},{1,0},{2,3},{3,2},{4,5},{5,4},{6,7},{7,6},{8,9},{9,8},{10,11... | collective-permute-start | bytes 1572872 | tf_op jit(solution)/shard_map/ppermute | solution.py:63
  60.3 4.8 %collective-permute-start.19 = (bf16[512,1024]{1,0:T(8,128)(2,1)S(1)}, bf16[512,1024]{1,0:T(8,128)(2,1)S(1)}, u32[]{:S(2)}, u32[]{:S(2)}) collective-permute-start(bf16[512,1024]{1,0:T(8,128)(2,1)S(1)} %get-tuple-element.20), channel_id=1, source_target_pairs={{0,1},{1,0},{2,3},{3,2},{4,8},{5,9},{6,10},{7,11},{8,4},{9,5},{10,... | collective-permute-start | bytes 3145736 | tf_op jit(solution)/shard_map/ppermute | solution.py:70
  60.6 4.6 %collective-permute-start.18 = (bf16[512,1024]{1,0:T(8,128)(2,1)S(1)}, bf16[512,1024]{1,0:T(8,128)(2,1)S(1)}, u32[]{:S(2)}, u32[]{:S(2)}) collective-permute-start(bf16[512,1024]{1,0:T(8,128)(2,1)S(1)} %get-tuple-element.19), channel_id=1, source_target_pairs={{0,1},{1,0},{2,3},{3,2},{4,5},{5,4},{6,7},{7,6},{8,12},{9,13},{10,... | collective-permute-start | bytes 3145736 | tf_op jit(solution)/shard_map/ppermute | solution.py:70
  61.0 14.8 %collective-permute-start.17 = (bf16[256,1024]{1,0:T(8,128)(2,1)S(1)}, bf16[256,1024]{1,0:T(8,128)(2,1)S(1)}, u32[]{:S(2)}, u32[]{:S(2)}) collective-permute-start(bf16[256,1024]{1,0:T(8,128)(2,1)S(1)} %get-tuple-element.30), channel_id=1, source_target_pairs={{0,2},{1,3},{2,0},{3,1},{4,6},{5,7},{6,4},{7,5},{8,10},{9,11},{10,... | collective-permute-start | bytes 1572872 | tf_op jit(solution)/shard_map/ppermute | solution.py:63
  62.6 23.7 %collective-permute-start.16 = (bf16[256,1024]{1,0:T(8,128)(2,1)S(1)}, bf16[256,1024]{1,0:T(8,128)(2,1)S(1)}, u32[]{:S(2)}, u32[]{:S(2)}) collective-permute-start(bf16[256,1024]{1,0:T(8,128)(2,1)S(1)} %broadcast_add_fusion.3), channel_id=1, source_target_pairs={{0,2},{1,3},{2,0},{3,1},{4,6},{5,7},{6,4},{7,5},{8,10},{9,11},{10,... | collective-permute-start | bytes 1572872 | tf_op jit(solution)/shard_map/ppermute | solution.py:63
  63.2 23.1 %collective-permute-start.15 = (bf16[256,1024]{1,0:T(8,128)(2,1)S(1)}, bf16[256,1024]{1,0:T(8,128)(2,1)S(1)}, u32[]{:S(2)}, u32[]{:S(2)}) collective-permute-start(bf16[256,1024]{1,0:T(8,128)(2,1)S(1)} %get-tuple-element.29), channel_id=1, source_target_pairs={{0,16},{1,17},{2,18},{3,19},{4,20},{5,21},{6,22},{7,23},{8,24},{9,... | collective-permute-start | bytes 1572872 | tf_op jit(solution)/shard_map/ppermute | solution.py:78
  87.3 7.1 %collective-permute-start.20 = (bf16[256,1024]{1,0:T(8,128)(2,1)S(1)}, bf16[256,1024]{1,0:T(8,128)(2,1)S(1)}, u32[]{:S(2)}, u32[]{:S(2)}) collective-permute-start(bf16[256,1024]{1,0:T(8,128)(2,1)S(1)} %get-tuple-element.47), channel_id=1, source_target_pairs={{0,1},{1,0},{2,3},{3,2},{4,5},{5,4},{6,7},{7,6},{8,9},{9,8},{10,11... | collective-permute-start | bytes 1572872 | tf_op jit(solution)/shard_map/ppermute | solution.py:63
  87.8 5.1 %collective-permute-start.26 = (bf16[256,1024]{1,0:T(8,128)(2,1)S(1)}, bf16[256,1024]{1,0:T(8,128)(2,1)S(1)}, u32[]{:S(2)}, u32[]{:S(2)}) collective-permute-start(bf16[256,1024]{1,0:T(8,128)(2,1)S(1)} %get-tuple-element.45), channel_id=1, source_target_pairs={{0,1},{1,0},{2,3},{3,2},{4,5},{5,4},{6,7},{7,6},{8,9},{9,8},{10,11... | collective-permute-start | bytes 1572872 | tf_op jit(solution)/shard_map/ppermute | solution.py:63
  89.5 5.6 %collective-permute-start.22 = (bf16[256,1024]{1,0:T(8,128)(2,1)S(1)}, bf16[256,1024]{1,0:T(8,128)(2,1)S(1)}, u32[]{:S(2)}, u32[]{:S(2)}) collective-permute-start(bf16[256,1024]{1,0:T(8,128)(2,1)S(1)} %get-tuple-element.28), channel_id=1, source_target_pairs={{0,1},{1,0},{2,3},{3,2},{4,5},{5,4},{6,7},{7,6},{8,9},{9,8},{10,11... | collective-permute-start | bytes 1572872 | tf_op jit(solution)/shard_map/ppermute | solution.py:63
  89.9 15.7 %collective-permute-start.27 = (bf16[256,1024]{1,0:T(8,128)(2,1)S(1)}, bf16[256,1024]{1,0:T(8,128)(2,1)S(1)}, u32[]{:S(2)}, u32[]{:S(2)}) collective-permute-start(bf16[256,1024]{1,0:T(8,128)(2,1)S(1)} %get-tuple-element.28), channel_id=1, source_target_pairs={{0,2},{1,3},{2,0},{3,1},{4,6},{5,7},{6,4},{7,5},{8,10},{9,11},{10,... | collective-permute-start | bytes 1572872 | tf_op jit(solution)/shard_map/ppermute | solution.py:63
  91.4 13.7 %collective-permute-start.23 = (bf16[256,1024]{1,0:T(8,128)(2,1)S(1)}, bf16[256,1024]{1,0:T(8,128)(2,1)S(1)}, u32[]{:S(2)}, u32[]{:S(2)}) collective-permute-start(bf16[256,1024]{1,0:T(8,128)(2,1)S(1)} %get-tuple-element.27), channel_id=1, source_target_pairs={{0,16},{1,17},{2,18},{3,19},{4,20},{5,21},{6,22},{7,23},{8,24},{9,... | collective-permute-start | bytes 1572872 | tf_op jit(solution)/shard_map/ppermute | solution.py:78
  96.3 10.1 %collective-permute-start.24 = (f32[256,256]{1,0:T(8,128)S(1)}, f32[256,256]{1,0:T(8,128)S(1)}, u32[]{:S(2)}, u32[]{:S(2)}) collective-permute-start(f32[256,256]{1,0:T(8,128)S(1)} %convolution_add_fusion.4), channel_id=1, source_target_pairs={{0,1},{1,0},{2,3},{3,2},{4,5},{5,4},{6,7},{7,6},{8,12},{9,13},{10,... | collective-permute-start | bytes 786440 | tf_op jit(solution)/shard_map/ppermute | solution.py:70
  106.8 2.7 %collective-permute-start.25 = (f32[256,256]{1,0:T(8,128)S(1)}, f32[256,256]{1,0:T(8,128)S(1)}, u32[]{:S(2)}, u32[]{:S(2)}) collective-permute-start(f32[256,256]{1,0:T(8,128)S(1)} %fusion.16), channel_id=1, source_target_pairs={{0,1},{1,0},{2,3},{3,2},{4,5},{5,4},{6,7},{7,6},{8,12},{9,13},{10,... | collective-permute-start | bytes 786440 | tf_op jit(solution)/shard_map/ppermute | solution.py:70
  111.5 3.6 %collective-permute-start.32 = (f32[256]{0:T(256)S(1)}, f32[256]{0:T(256)S(1)}, u32[]{:S(2)}, u32[]{:S(2)}) collective-permute-start(f32[256]{0:T(256)S(1)} %get-tuple-element.44), channel_id=1, source_target_pairs={{0,16},{1,17},{2,18},{3,19},{4,20},{5,21},{6,22},{7,23},{8,24},{9,... | collective-permute-start | bytes 3080 | tf_op jit(solution)/shard_map/ppermute | solution.py:78
  113.1 3.6 %collective-permute-start.33 = (f32[256]{0:T(256)S(1)}, f32[256]{0:T(256)S(1)}, u32[]{:S(2)}, u32[]{:S(2)}) collective-permute-start(f32[256]{0:T(256)S(1)} %get-tuple-element.44), channel_id=1, source_target_pairs={{0,16},{1,17},{2,18},{3,19},{4,20},{5,21},{6,22},{7,23},{8,28},{9,... | collective-permute-start | bytes 3080 | tf_op jit(solution)/shard_map/ppermute | solution.py:78
  113.7 3.1 %collective-permute-start.31 = (f32[256]{0:T(256)S(1)}, f32[256]{0:T(256)S(1)}, u32[]{:S(2)}, u32[]{:S(2)}) collective-permute-start(f32[256]{0:T(256)S(1)} %get-tuple-element.43), channel_id=1, source_target_pairs={{0,1},{1,0},{2,3},{3,2},{4,5},{5,4},{6,7},{7,6},{8,12},{9,13},{10,... | collective-permute-start | bytes 3080 | tf_op jit(solution)/shard_map/ppermute | solution.py:70
  116.8 3.6 %collective-permute-start.35 = (f32[256]{0:T(256)S(1)}, f32[256]{0:T(256)S(1)}, u32[]{:S(2)}, u32[]{:S(2)}) collective-permute-start(f32[256]{0:T(256)S(1)} %add_add_fusion.3), channel_id=1, source_target_pairs={{0,2},{1,3},{2,0},{3,1},{4,6},{5,7},{6,4},{7,5},{8,10},{9,11},{10,... | collective-permute-start | bytes 3080 | tf_op jit(solution)/shard_map/ppermute | solution.py:63
  117.4 3.0 %collective-permute-start.36 = (f32[256]{0:T(256)S(1)}, f32[256]{0:T(256)S(1)}, u32[]{:S(2)}, u32[]{:S(2)}) collective-permute-start(f32[256]{0:T(256)S(1)} %add_add_fusion.3), channel_id=1, source_target_pairs={{0,3},{1,2},{2,1},{3,0},{4,7},{5,6},{6,5},{7,4},{8,11},{9,10},{10,... | collective-permute-start | bytes 3080 | tf_op jit(solution)/shard_map/ppermute | solution.py:63
  120.5 22.3 %collective-permute-start.37 = (f32[1024]{0:T(1024)S(1)}, f32[1024]{0:T(1024)S(1)}, u32[]{:S(2)}, u32[]{:S(2)}) collective-permute-start(f32[1024]{0:T(1024)S(1)} %pad_maximum_fusion.3), channel_id=1, source_target_pairs={{0,8},{1,9},{2,10},{3,11},{4,12},{5,13},{6,14},{7,15},{8,0},{9,1},... | collective-permute-start | bytes 12296 | tf_op jit(solution)/shard_map/ppermute | solution.py:70
  (9 other events, 54.1 us)

commit v12 on v11

--- a/solution.py
+++ b/solution.py
@@ -160,10 +160,10 @@
         t_a, p_a = white_a[:count_t], white_a[count_t:]
         t_moved_a = [inner(t_a, s, 0) for s in range(1, nx)]
         p_moved_a = [over_pool(p_a, s) for s in range(1, n_pool)]
-        done = fence([step3, step4], [*moved4, *t_moved_a], p_moved_a)
-
-        moved4 = [behind(v, done) for v in moved4]
-        fourth = partial([own4] + moved4 + [flip4] + factor_flip(moved4))
+        far4 = factor_flip(moved4)
+        done = fence([step3, step4], [*t_moved_a, *p_moved_a], far4)
+
+        fourth = partial([own4] + moved4 + [flip4] + far4)
         t_moved_a = [behind(v, done) for v in t_moved_a]
         t_flip_a = inner(behind(t_a, done), 0, 1)
         white_b = (jnp.where(top, fourth, second + step3.astype(F32) + step4.astype(F32)) + done).astype(BF)

time: 144 us -> 144 us (level)
    ppermute x24, waiting for transfers between devices: 38.3 us -> 35.8 us  [inner(): return lax.ppermute(value, 'tgt', pairs)]
    ppermute x10, waiting for transfers between devices: 19.4 us -> 21.8 us  [along_z(): return lax.ppermute(value, 'tgt', pairs)]
  transfers between devices with their start and end apart: 38 -> 38, of which waited for: 19 -> 18; matrix products, arithmetic and copies ran while one was open for 16% -> 15% of each run, Pallas kernels for 0% -> 0%
where the time goes in v12:
time: 144 us
  waiting for transfers between devices  70.3 us (49%)
  starting transfers between devices  44.9 us (31%)
  matrix products  13.6 us (9%)
  other arithmetic  9.45 us (7%)
  local copies, waits for them, and re-layouts  5.34 us (4%)
    ppermute x24, waiting for transfers between devices, inner(): return lax.ppermute(value, 'tgt', pairs)  35.8 us
    ppermute x10, starting transfers between devices, along_z(): return lax.ppermute(value, 'tgt', pairs)  25.3 us
    ppermute x10, waiting for transfers between devices, along_z(): return lax.ppermute(value, 'tgt', pairs)  21.8 us
    ppermute x24, starting transfers between devices, inner(): return lax.ppermute(value, 'tgt', pairs)  14.4 us
    ppermute x4, waiting for transfers between devices, over_pool(): return lax.ppermute(value, ('pool', 'tgt'), pairs)  12.7 us
    dot_general x16, matrix products, matmul(): lax.dot_general(a, b, (((1,), (0,)), ((), ())), preferred_element_type=F32)  8.84 us
    ppermute x4, starting transfers between devices, over_pool(): return lax.ppermute(value, ('pool', 'tgt'), pairs)  5.21 us
    dot_general x10, matrix products, matmul_t(): lax.dot_general(a, b, (((1,), (1,)), ((), ())), preferred_element_type=F32)  4.72 us
  transfers between devices with their start and end apart: 38, of which 18 were waited for; matrix products, arithmetic and copies ran while one was open for 15% of the time, Pallas kernels for 0%

profile of v12, /device:TPU:0, one launch (start us, length us, event | category | flops | bytes accessed | tf_op | source)
XLA Modules:
  0.0 144.1 jit_solution(16713445733548789901)
XLA Ops:
  0.0 1.2 constant_dynamic-slice_fusion
  1.7 2.6 %collective-permute-start.1 = (bf16[256,1024]{1,0:T(8,128)(2,1)S(1)}, bf16[256,1024]{1,0:T(8,128)(2,1)}, u32[]{:S(2)}, u32[]{:S(2)}) collective-permute-start(bf16[256,1024]{1,0:T(8,128)(2,1)S(1)} %constant_dynamic-slice_fusion), channel_id=1, source_target_pairs={{0,2},{1,3},{2,0},{3,1},{4,6},{5,7},{6,4},{7,5},{8,10},{9,11},{10,... | collective-permute-start | bytes 1572872 | tf_op jit(solution)/shard_map/ppermute | solution.py:63
  5.0 3.9 %gather_fusion = bf16[1024,256]{1,0:T(8,128)(2,1)S(1)} fusion(bf16[4096,256]{1,0:T(8,128)(2,1)S(1)} %copy-done, s32[1024]{0:T(1024)S(1)} %fusion.28), kind=kCustom, calls=%fused_computation | custom fusion | bytes 1052672 | tf_op jit(solution)/shard_map/gather | solution.py:104
  9.0 2.0 %fusion.22 = (bf16[512,256]{1,0:T(8,128)(2,1)}, bf16[512,256]{1,0:T(8,128)(2,1)}, bf16[512,256]{1,0:T(8,128)(2,1)S(1)}, bf16[512,256]{1,0:T(8,128)(2,1)S(1)}) fusion(s32[]{:T(128)S(6)} %select_n.172, s32[]{:T(128)S(6)} %select_n.165, bf16[2,2,256,256]{3,2,1,0:T(8,128)(2,1)} %bitcast.52, bf16[2,2,256,256]{3,2,1,0:T(8,128)(2,1)S(1)} %bitcast.51, ...), kind=kLoop, calls=%fused_computation.66 | loop fusion | flops 2097152 | bytes 2097168 | tf_op jit(solution)/shard_map/squeeze | solution.py:114
  11.4 1.4 collective-permute-start.4
  13.3 3.9 %collective-permute-done.1 = bf16[256,1024]{1,0:T(8,128)(2,1)} collective-permute-done((bf16[256,1024]{1,0:T(8,128)(2,1)S(1)}, bf16[256,1024]{1,0:T(8,128)(2,1)}, u32[]{:S(2)}, u32[]{:S(2)}) %collective-permute-start.1) | collective-permute-done | bytes 524320 | tf_op jit(solution)/shard_map/ppermute | solution.py:63
  17.2 0.7 fusion.71
  18.0 1.1 broadcast_add_fusion.5
  19.2 3.5 %collective-permute-done = bf16[512,256]{1,0:T(8,128)(2,1)S(1)} collective-permute-done((bf16[512,256]{1,0:T(8,128)(2,1)}, bf16[512,256]{1,0:T(8,128)(2,1)S(1)}, u32[]{:S(2)}, u32[]{:S(2)}) %collective-permute-start) | collective-permute-done | bytes 262176 | tf_op jit(solution)/shard_map/ppermute | solution.py:63
  23.2 1.5 %fusion.89 = f32[512,1024]{1,0:T(8,128)S(1)} fusion(bf16[512,256]{1,0:T(8,128)(2,1)S(1)} %collective-permute-done.2, bf16[256,1024]{1,0:T(8,128)(2,1)} %collective-permute-done.3), kind=kOutput, calls=%fused_computation.176 | convolution fusion | flops 268435456 | bytes 2883584 | tf_op jit(solution)/shard_map/dot_general | solution.py:13
  24.7 3.1 %collective-permute-done.4 = bf16[512,256]{1,0:T(8,128)(2,1)S(1)} collective-permute-done((bf16[512,256]{1,0:T(8,128)(2,1)S(1)}, bf16[512,256]{1,0:T(8,128)(2,1)S(1)}, u32[]{:S(2)}, u32[]{:S(2)}) %collective-permute-start.4) | collective-permute-done | bytes 262176 | tf_op jit(solution)/shard_map/ppermute | solution.py:63
  29.4 1.9 %collective-permute-start.12 = (bf16[512,1024]{1,0:T(8,128)(2,1)S(1)}, bf16[512,1024]{1,0:T(8,128)(2,1)S(1)}, u32[]{:S(2)}, u32[]{:S(2)}) collective-permute-start(bf16[512,1024]{1,0:T(8,128)(2,1)S(1)} %add_convert_fusion.1), channel_id=1, source_target_pairs={{0,4},{1,5},{2,6},{3,7},{4,0},{5,1},{6,2},{7,3},{8,12},{9,13},{10,... | collective-permute-start | bytes 3145736 | tf_op jit(solution)/shard_map/ppermute | solution.py:70
  31.3 1.5 %collective-permute-start.6 = (bf16[256,1024]{1,0:T(8,128)(2,1)S(1)}, bf16[256,1024]{1,0:T(8,128)(2,1)S(1)}, u32[]{:S(2)}, u32[]{:S(2)}) collective-permute-start(bf16[256,1024]{1,0:T(8,128)(2,1)S(1)} %get-tuple-element.22), channel_id=1, source_target_pairs={{0,2},{1,3},{2,0},{3,1},{4,6},{5,7},{6,4},{7,5},{8,10},{9,11},{10,... | collective-permute-start | bytes 1572872 | tf_op jit(solution)/shard_map/ppermute | solution.py:63
  35.5 19.4 %collective-permute-done.12 = bf16[512,1024]{1,0:T(8,128)(2,1)S(1)} collective-permute-done((bf16[512,1024]{1,0:T(8,128)(2,1)S(1)}, bf16[512,1024]{1,0:T(8,128)(2,1)S(1)}, u32[]{:S(2)}, u32[]{:S(2)}) %collective-permute-start.12) | collective-permute-done | bytes 1048608 | tf_op jit(solution)/shard_map/ppermute | solution.py:70
  55.0 1.9 %collective-permute-done.10 = bf16[256,1024]{1,0:T(8,128)(2,1)S(1)} collective-permute-done((bf16[256,1024]{1,0:T(8,128)(2,1)S(1)}, bf16[256,1024]{1,0:T(8,128)(2,1)S(1)}, u32[]{:S(2)}, u32[]{:S(2)}) %collective-permute-start.10) | collective-permute-done | bytes 524320 | tf_op jit(solution)/shard_map/ppermute | solution.py:63
  60.3 0.9 add_convert_fusion.2
  61.8 1.6 %collective-permute-start.15 = (bf16[256,1024]{1,0:T(8,128)(2,1)S(1)}, bf16[256,1024]{1,0:T(8,128)(2,1)S(1)}, u32[]{:S(2)}, u32[]{:S(2)}) collective-permute-start(bf16[256,1024]{1,0:T(8,128)(2,1)S(1)} %broadcast_add_fusion.2), channel_id=1, source_target_pairs={{0,2},{1,3},{2,0},{3,1},{4,6},{5,7},{6,4},{7,5},{8,10},{9,11},{10,... | collective-permute-start | bytes 1572872 | tf_op jit(solution)/shard_map/ppermute | solution.py:63
  63.5 1.6 %collective-permute-start.18 = (bf16[256,1024]{1,0:T(8,128)(2,1)S(1)}, bf16[256,1024]{1,0:T(8,128)(2,1)S(1)}, u32[]{:S(2)}, u32[]{:S(2)}) collective-permute-start(bf16[256,1024]{1,0:T(8,128)(2,1)S(1)} %get-tuple-element.30), channel_id=1, source_target_pairs={{0,16},{1,17},{2,18},{3,19},{4,20},{5,21},{6,22},{7,23},{8,24},{9,... | collective-permute-start | bytes 1572872 | tf_op jit(solution)/shard_map/ppermute | solution.py:78
  66.0 10.6 %collective-permute-done.15 = bf16[256,1024]{1,0:T(8,128)(2,1)S(1)} collective-permute-done((bf16[256,1024]{1,0:T(8,128)(2,1)S(1)}, bf16[256,1024]{1,0:T(8,128)(2,1)S(1)}, u32[]{:S(2)}, u32[]{:S(2)}) %collective-permute-start.15) | collective-permute-done | bytes 524320 | tf_op jit(solution)/shard_map/ppermute | solution.py:63
  77.2 9.9 %collective-permute-done.17 = bf16[256,1024]{1,0:T(8,128)(2,1)S(1)} collective-permute-done((bf16[256,1024]{1,0:T(8,128)(2,1)S(1)}, bf16[256,1024]{1,0:T(8,128)(2,1)S(1)}, u32[]{:S(2)}, u32[]{:S(2)}) %collective-permute-start.17) | collective-permute-done | bytes 524320 | tf_op jit(solution)/shard_map/ppermute | solution.py:63
  87.2 1.0 add_convert_fusion
  89.2 1.6 %collective-permute-start.27 = (bf16[256,1024]{1,0:T(8,128)(2,1)S(1)}, bf16[256,1024]{1,0:T(8,128)(2,1)S(1)}, u32[]{:S(2)}, u32[]{:S(2)}) collective-permute-start(bf16[256,1024]{1,0:T(8,128)(2,1)S(1)} %get-tuple-element.28), channel_id=1, source_target_pairs={{0,2},{1,3},{2,0},{3,1},{4,6},{5,7},{6,4},{7,5},{8,10},{9,11},{10,... | collective-permute-start | bytes 1572872 | tf_op jit(solution)/shard_map/ppermute | solution.py:63
  90.8 1.5 %collective-permute-start.23 = (bf16[256,1024]{1,0:T(8,128)(2,1)S(1)}, bf16[256,1024]{1,0:T(8,128)(2,1)S(1)}, u32[]{:S(2)}, u32[]{:S(2)}) collective-permute-start(bf16[256,1024]{1,0:T(8,128)(2,1)S(1)} %get-tuple-element.27), channel_id=1, source_target_pairs={{0,16},{1,17},{2,18},{3,19},{4,20},{5,21},{6,22},{7,23},{8,24},{9,... | collective-permute-start | bytes 1572872 | tf_op jit(solution)/shard_map/ppermute | solution.py:78
  94.0 0.8 collective-permute-start.24
  94.8 9.6 %collective-permute-done.23 = bf16[256,1024]{1,0:T(8,128)(2,1)S(1)} collective-permute-done((bf16[256,1024]{1,0:T(8,128)(2,1)S(1)}, bf16[256,1024]{1,0:T(8,128)(2,1)S(1)}, u32[]{:S(2)}, u32[]{:S(2)}) %collective-permute-start.23) | collective-permute-done | bytes 524320 | tf_op jit(solution)/shard_map/ppermute | solution.py:78
  112.1 1.6 %collective-permute-start.32 = (f32[256]{0:T(256)S(1)}, f32[256]{0:T(256)S(1)}, u32[]{:S(2)}, u32[]{:S(2)}) collective-permute-start(f32[256]{0:T(256)S(1)} %get-tuple-element.44), channel_id=1, source_target_pairs={{0,16},{1,17},{2,18},{3,19},{4,20},{5,21},{6,22},{7,23},{8,24},{9,... | collective-permute-start | bytes 3080 | tf_op jit(solution)/shard_map/ppermute | solution.py:78
  114.2 1.5 %collective-permute-done.32 = f32[256]{0:T(256)S(1)} collective-permute-done((f32[256]{0:T(256)S(1)}, f32[256]{0:T(256)S(1)}, u32[]{:S(2)}, u32[]{:S(2)}) %collective-permute-start.32) | collective-permute-done | bytes 1056 | tf_op jit(solution)/shard_map/ppermute | solution.py:78
  115.8 1.5 %collective-permute-done.33 = f32[256]{0:T(256)S(1)} collective-permute-done((f32[256]{0:T(256)S(1)}, f32[256]{0:T(256)S(1)}, u32[]{:S(2)}, u32[]{:S(2)}) %collective-permute-start.33) | collective-permute-done | bytes 1056 | tf_op jit(solution)/shard_map/ppermute | solution.py:78
  118.0 1.2 collective-permute-start.36
  119.2 1.8 %collective-permute-done.35 = f32[256]{0:T(256)S(1)} collective-permute-done((f32[256]{0:T(256)S(1)}, f32[256]{0:T(256)S(1)}, u32[]{:S(2)}, u32[]{:S(2)}) %collective-permute-start.35) | collective-permute-done | bytes 1056 | tf_op jit(solution)/shard_map/ppermute | solution.py:63
  121.0 20.8 %collective-permute-start.37 = (f32[1024]{0:T(1024)S(1)}, f32[1024]{0:T(1024)S(1)}, u32[]{:S(2)}, u32[]{:S(2)}) collective-permute-start(f32[1024]{0:T(1024)S(1)} %pad_maximum_fusion.3), channel_id=1, source_target_pairs={{0,8},{1,9},{2,10},{3,11},{4,12},{5,13},{6,14},{7,15},{8,0},{9,1},... | collective-permute-start | bytes 12296 | tf_op jit(solution)/shard_map/ppermute | solution.py:70
  141.9 1.6 %collective-permute-done.37 = f32[1024]{0:T(1024)S(1)} collective-permute-done((f32[1024]{0:T(1024)S(1)}, f32[1024]{0:T(1024)S(1)}, u32[]{:S(2)}, u32[]{:S(2)}) %collective-permute-start.37) | collective-permute-done | bytes 4128 | tf_op jit(solution)/shard_map/ppermute | solution.py:70
  (122 shorter events, 24.7 us)
Async XLA Ops:
  1.2 21.9 %collective-permute-start.3 = (bf16[256,1024]{1,0:T(8,128)(2,1)S(1)}, bf16[256,1024]{1,0:T(8,128)(2,1)}, u32[]{:S(2)}, u32[]{:S(2)}) collective-permute-start(bf16[256,1024]{1,0:T(8,128)(2,1)S(1)} %constant_dynamic-slice_fusion), channel_id=1, source_target_pairs={{0,1},{1,0},{2,3},{3,2},{4,5},{5,4},{6,7},{7,6},{8,9},{9,8},{10,11... | collective-permute-start | bytes 1572872 | tf_op jit(solution)/shard_map/ppermute | solution.py:63
  1.7 15.4 %collective-permute-start.1 = (bf16[256,1024]{1,0:T(8,128)(2,1)S(1)}, bf16[256,1024]{1,0:T(8,128)(2,1)}, u32[]{:S(2)}, u32[]{:S(2)}) collective-permute-start(bf16[256,1024]{1,0:T(8,128)(2,1)S(1)} %constant_dynamic-slice_fusion), channel_id=1, source_target_pairs={{0,2},{1,3},{2,0},{3,1},{4,6},{5,7},{6,4},{7,5},{8,10},{9,11},{10,... | collective-permute-start | bytes 1572872 | tf_op jit(solution)/shard_map/ppermute | solution.py:63
  11.0 12.2 %collective-permute-start.2 = (bf16[512,256]{1,0:T(8,128)(2,1)}, bf16[512,256]{1,0:T(8,128)(2,1)S(1)}, u32[]{:S(2)}, u32[]{:S(2)}) collective-permute-start(bf16[512,256]{1,0:T(8,128)(2,1)} %get-tuple-element.32), channel_id=1, source_target_pairs={{0,1},{1,0},{2,3},{3,2},{4,5},{5,4},{6,7},{7,6},{8,9},{9,8},{10,11... | collective-permute-start | bytes 786440 | tf_op jit(solution)/shard_map/ppermute | solution.py:63
  11.1 11.6 %collective-permute-start = (bf16[512,256]{1,0:T(8,128)(2,1)}, bf16[512,256]{1,0:T(8,128)(2,1)S(1)}, u32[]{:S(2)}, u32[]{:S(2)}) collective-permute-start(bf16[512,256]{1,0:T(8,128)(2,1)} %get-tuple-element.31), channel_id=1, source_target_pairs={{0,2},{1,3},{2,0},{3,1},{4,6},{5,7},{6,4},{7,5},{8,10},{9,11},{10,... | collective-permute-start | bytes 786440 | tf_op jit(solution)/shard_map/ppermute | solution.py:63
  11.4 16.4 %collective-permute-start.4 = (bf16[512,256]{1,0:T(8,128)(2,1)S(1)}, bf16[512,256]{1,0:T(8,128)(2,1)S(1)}, u32[]{:S(2)}, u32[]{:S(2)}) collective-permute-start(bf16[512,256]{1,0:T(8,128)(2,1)S(1)} %get-tuple-element.34), channel_id=1, source_target_pairs={{0,3},{1,2},{2,1},{3,0},{4,7},{5,6},{6,5},{7,4},{8,11},{9,10},{10,... | collective-permute-start | bytes 786440 | tf_op jit(solution)/shard_map/ppermute | solution.py:63
  19.1 8.7 %collective-permute-start.5 = (bf16[256,1024]{1,0:T(8,128)(2,1)S(1)}, bf16[256,1024]{1,0:T(8,128)(2,1)S(1)}, u32[]{:S(2)}, u32[]{:S(2)}) collective-permute-start(bf16[256,1024]{1,0:T(8,128)(2,1)S(1)} %broadcast_add_fusion.5), channel_id=1, source_target_pairs={{0,1},{1,0},{2,3},{3,2},{4,5},{5,4},{6,7},{7,6},{8,9},{9,8},{10,11... | collective-permute-start | bytes 1572872 | tf_op jit(solution)/shard_map/ppermute | solution.py:63
  28.8 5.1 %collective-permute-start.7 = (bf16[256,1024]{1,0:T(8,128)(2,1)S(1)}, bf16[256,1024]{1,0:T(8,128)(2,1)S(1)}, u32[]{:S(2)}, u32[]{:S(2)}) collective-permute-start(bf16[256,1024]{1,0:T(8,128)(2,1)S(1)} %get-tuple-element.23), channel_id=1, source_target_pairs={{0,1},{1,0},{2,3},{3,2},{4,5},{5,4},{6,7},{7,6},{8,9},{9,8},{10,11... | collective-permute-start | bytes 1572872 | tf_op jit(solution)/shard_map/ppermute | solution.py:63
  29.4 25.5 %collective-permute-start.12 = (bf16[512,1024]{1,0:T(8,128)(2,1)S(1)}, bf16[512,1024]{1,0:T(8,128)(2,1)S(1)}, u32[]{:S(2)}, u32[]{:S(2)}) collective-permute-start(bf16[512,1024]{1,0:T(8,128)(2,1)S(1)} %add_convert_fusion.1), channel_id=1, source_target_pairs={{0,4},{1,5},{2,6},{3,7},{4,0},{5,1},{6,2},{7,3},{8,12},{9,13},{10,... | collective-permute-start | bytes 3145736 | tf_op jit(solution)/shard_map/ppermute | solution.py:70
  31.3 23.6 %collective-permute-start.11 = (bf16[512,1024]{1,0:T(8,128)(2,1)S(1)}, bf16[512,1024]{1,0:T(8,128)(2,1)S(1)}, u32[]{:S(2)}, u32[]{:S(2)}) collective-permute-start(bf16[512,1024]{1,0:T(8,128)(2,1)S(1)} %add_convert_fusion.1), channel_id=1, source_target_pairs={{0,1},{1,0},{2,3},{3,2},{4,8},{5,9},{6,10},{7,11},{8,4},{9,5},{10,... | collective-permute-start | bytes 3145736 | tf_op jit(solution)/shard_map/ppermute | solution.py:70
  31.3 23.7 %collective-permute-start.6 = (bf16[256,1024]{1,0:T(8,128)(2,1)S(1)}, bf16[256,1024]{1,0:T(8,128)(2,1)S(1)}, u32[]{:S(2)}, u32[]{:S(2)}) collective-permute-start(bf16[256,1024]{1,0:T(8,128)(2,1)S(1)} %get-tuple-element.22), channel_id=1, source_target_pairs={{0,2},{1,3},{2,0},{3,1},{4,6},{5,7},{6,4},{7,5},{8,10},{9,11},{10,... | collective-permute-start | bytes 1572872 | tf_op jit(solution)/shard_map/ppermute | solution.py:63
  33.9 23.0 %collective-permute-start.10 = (bf16[256,1024]{1,0:T(8,128)(2,1)S(1)}, bf16[256,1024]{1,0:T(8,128)(2,1)S(1)}, u32[]{:S(2)}, u32[]{:S(2)}) collective-permute-start(bf16[256,1024]{1,0:T(8,128)(2,1)S(1)} %get-tuple-element.23), channel_id=1, source_target_pairs={{0,2},{1,3},{2,0},{3,1},{4,6},{5,7},{6,4},{7,5},{8,10},{9,11},{10,... | collective-permute-start | bytes 1572872 | tf_op jit(solution)/shard_map/ppermute | solution.py:63
  35.0 21.9 %collective-permute-start.9 = (bf16[256,1024]{1,0:T(8,128)(2,1)S(1)}, bf16[256,1024]{1,0:T(8,128)(2,1)S(1)}, u32[]{:S(2)}, u32[]{:S(2)}) collective-permute-start(bf16[256,1024]{1,0:T(8,128)(2,1)S(1)} %get-tuple-element.21), channel_id=1, source_target_pairs={{0,1},{1,0},{2,3},{3,2},{4,5},{5,4},{6,7},{7,6},{8,9},{9,8},{10,11... | collective-permute-start | bytes 1572872 | tf_op jit(solution)/shard_map/ppermute | solution.py:63
  57.2 2.6 %collective-permute-start.13 = (bf16[256,1024]{1,0:T(8,128)(2,1)S(1)}, bf16[256,1024]{1,0:T(8,128)(2,1)S(1)}, u32[]{:S(2)}, u32[]{:S(2)}) collective-permute-start(bf16[256,1024]{1,0:T(8,128)(2,1)S(1)} %get-tuple-element.47), channel_id=1, source_target_pairs={{0,1},{1,0},{2,3},{3,2},{4,5},{5,4},{6,7},{7,6},{8,9},{9,8},{10,11... | collective-permute-start | bytes 1572872 | tf_op jit(solution)/shard_map/ppermute | solution.py:63
  61.2 15.9 %collective-permute-start.20 = (bf16[512,1024]{1,0:T(8,128)(2,1)S(1)}, bf16[512,1024]{1,0:T(8,128)(2,1)S(1)}, u32[]{:S(2)}, u32[]{:S(2)}) collective-permute-start(bf16[512,1024]{1,0:T(8,128)(2,1)S(1)} %get-tuple-element.20), channel_id=1, source_target_pairs={{0,1},{1,0},{2,3},{3,2},{4,8},{5,9},{6,10},{7,11},{8,4},{9,5},{10,... | collective-permute-start | bytes 3145736 | tf_op jit(solution)/shard_map/ppermute | solution.py:70
  61.4 15.7 %collective-permute-start.19 = (bf16[512,1024]{1,0:T(8,128)(2,1)S(1)}, bf16[512,1024]{1,0:T(8,128)(2,1)S(1)}, u32[]{:S(2)}, u32[]{:S(2)}) collective-permute-start(bf16[512,1024]{1,0:T(8,128)(2,1)S(1)} %get-tuple-element.19), channel_id=1, source_target_pairs={{0,1},{1,0},{2,3},{3,2},{4,5},{5,4},{6,7},{7,6},{8,12},{9,13},{10,... | collective-permute-start | bytes 3145736 | tf_op jit(solution)/shard_map/ppermute | solution.py:70
  61.8 14.8 %collective-permute-start.15 = (bf16[256,1024]{1,0:T(8,128)(2,1)S(1)}, bf16[256,1024]{1,0:T(8,128)(2,1)S(1)}, u32[]{:S(2)}, u32[]{:S(2)}) collective-permute-start(bf16[256,1024]{1,0:T(8,128)(2,1)S(1)} %broadcast_add_fusion.2), channel_id=1, source_target_pairs={{0,2},{1,3},{2,0},{3,1},{4,6},{5,7},{6,4},{7,5},{8,10},{9,11},{10,... | collective-permute-start | bytes 1572872 | tf_op jit(solution)/shard_map/ppermute | solution.py:63
  63.5 13.7 %collective-permute-start.18 = (bf16[256,1024]{1,0:T(8,128)(2,1)S(1)}, bf16[256,1024]{1,0:T(8,128)(2,1)S(1)}, u32[]{:S(2)}, u32[]{:S(2)}) collective-permute-start(bf16[256,1024]{1,0:T(8,128)(2,1)S(1)} %get-tuple-element.30), channel_id=1, source_target_pairs={{0,16},{1,17},{2,18},{3,19},{4,20},{5,21},{6,22},{7,23},{8,24},{9,... | collective-permute-start | bytes 1572872 | tf_op jit(solution)/shard_map/ppermute | solution.py:78
  65.1 22.0 %collective-permute-start.17 = (bf16[256,1024]{1,0:T(8,128)(2,1)S(1)}, bf16[256,1024]{1,0:T(8,128)(2,1)S(1)}, u32[]{:S(2)}, u32[]{:S(2)}) collective-permute-start(bf16[256,1024]{1,0:T(8,128)(2,1)S(1)} %get-tuple-element.29), channel_id=1, source_target_pairs={{0,2},{1,3},{2,0},{3,1},{4,6},{5,7},{6,4},{7,5},{8,10},{9,11},{10,... | collective-permute-start | bytes 1572872 | tf_op jit(solution)/shard_map/ppermute | solution.py:63
  76.7 10.5 %collective-permute-start.16 = (bf16[256,1024]{1,0:T(8,128)(2,1)S(1)}, bf16[256,1024]{1,0:T(8,128)(2,1)S(1)}, u32[]{:S(2)}, u32[]{:S(2)}) collective-permute-start(bf16[256,1024]{1,0:T(8,128)(2,1)S(1)} %collective-permute-done.15), channel_id=1, source_target_pairs={{0,1},{1,0},{2,3},{3,2},{4,5},{5,4},{6,7},{7,6},{8,9},{9,8},{10,11... | collective-permute-start | bytes 1572872 | tf_op jit(solution)/shard_map/ppermute | solution.py:63
  88.2 4.1 %collective-permute-start.22 = (bf16[256,1024]{1,0:T(8,128)(2,1)S(1)}, bf16[256,1024]{1,0:T(8,128)(2,1)S(1)}, u32[]{:S(2)}, u32[]{:S(2)}) collective-permute-start(bf16[256,1024]{1,0:T(8,128)(2,1)S(1)} %get-tuple-element.28), channel_id=1, source_target_pairs={{0,1},{1,0},{2,3},{3,2},{4,5},{5,4},{6,7},{7,6},{8,9},{9,8},{10,11... | collective-permute-start | bytes 1572872 | tf_op jit(solution)/shard_map/ppermute | solution.py:63
  88.4 4.4 %collective-permute-start.21 = (bf16[256,1024]{1,0:T(8,128)(2,1)S(1)}, bf16[256,1024]{1,0:T(8,128)(2,1)S(1)}, u32[]{:S(2)}, u32[]{:S(2)}) collective-permute-start(bf16[256,1024]{1,0:T(8,128)(2,1)S(1)} %get-tuple-element.46), channel_id=1, source_target_pairs={{0,1},{1,0},{2,3},{3,2},{4,5},{5,4},{6,7},{7,6},{8,9},{9,8},{10,11... | collective-permute-start | bytes 1572872 | tf_op jit(solution)/shard_map/ppermute | solution.py:63
  89.2 17.0 %collective-permute-start.27 = (bf16[256,1024]{1,0:T(8,128)(2,1)S(1)}, bf16[256,1024]{1,0:T(8,128)(2,1)S(1)}, u32[]{:S(2)}, u32[]{:S(2)}) collective-permute-start(bf16[256,1024]{1,0:T(8,128)(2,1)S(1)} %get-tuple-element.28), channel_id=1, source_target_pairs={{0,2},{1,3},{2,0},{3,1},{4,6},{5,7},{6,4},{7,5},{8,10},{9,11},{10,... | collective-permute-start | bytes 1572872 | tf_op jit(solution)/shard_map/ppermute | solution.py:63
  90.8 13.6 %collective-permute-start.23 = (bf16[256,1024]{1,0:T(8,128)(2,1)S(1)}, bf16[256,1024]{1,0:T(8,128)(2,1)S(1)}, u32[]{:S(2)}, u32[]{:S(2)}) collective-permute-start(bf16[256,1024]{1,0:T(8,128)(2,1)S(1)} %get-tuple-element.27), channel_id=1, source_target_pairs={{0,16},{1,17},{2,18},{3,19},{4,20},{5,21},{6,22},{7,23},{8,24},{9,... | collective-permute-start | bytes 1572872 | tf_op jit(solution)/shard_map/ppermute | solution.py:78
  92.3 12.6 %collective-permute-start.26 = (bf16[256,1024]{1,0:T(8,128)(2,1)S(1)}, bf16[256,1024]{1,0:T(8,128)(2,1)S(1)}, u32[]{:S(2)}, u32[]{:S(2)}) collective-permute-start(bf16[256,1024]{1,0:T(8,128)(2,1)S(1)} %get-tuple-element.45), channel_id=1, source_target_pairs={{0,1},{1,0},{2,3},{3,2},{4,5},{5,4},{6,7},{7,6},{8,9},{9,8},{10,11... | collective-permute-start | bytes 1572872 | tf_op jit(solution)/shard_map/ppermute | solution.py:63
  94.0 13.1 %collective-permute-start.24 = (f32[256,256]{1,0:T(8,128)S(1)}, f32[256,256]{1,0:T(8,128)S(1)}, u32[]{:S(2)}, u32[]{:S(2)}) collective-permute-start(f32[256,256]{1,0:T(8,128)S(1)} %convolution_add_fusion.4), channel_id=1, source_target_pairs={{0,1},{1,0},{2,3},{3,2},{4,5},{5,4},{6,7},{7,6},{8,12},{9,13},{10,... | collective-permute-start | bytes 786440 | tf_op jit(solution)/shard_map/ppermute | solution.py:70
  107.5 2.5 %collective-permute-start.25 = (f32[256,256]{1,0:T(8,128)S(1)}, f32[256,256]{1,0:T(8,128)S(1)}, u32[]{:S(2)}, u32[]{:S(2)}) collective-permute-start(f32[256,256]{1,0:T(8,128)S(1)} %fusion.16), channel_id=1, source_target_pairs={{0,1},{1,0},{2,3},{3,2},{4,5},{5,4},{6,7},{7,6},{8,12},{9,13},{10,... | collective-permute-start | bytes 786440 | tf_op jit(solution)/shard_map/ppermute | solution.py:70
  112.1 3.6 %collective-permute-start.32 = (f32[256]{0:T(256)S(1)}, f32[256]{0:T(256)S(1)}, u32[]{:S(2)}, u32[]{:S(2)}) collective-permute-start(f32[256]{0:T(256)S(1)} %get-tuple-element.44), channel_id=1, source_target_pairs={{0,16},{1,17},{2,18},{3,19},{4,20},{5,21},{6,22},{7,23},{8,24},{9,... | collective-permute-start | bytes 3080 | tf_op jit(solution)/shard_map/ppermute | solution.py:78
  113.7 3.6 %collective-permute-start.33 = (f32[256]{0:T(256)S(1)}, f32[256]{0:T(256)S(1)}, u32[]{:S(2)}, u32[]{:S(2)}) collective-permute-start(f32[256]{0:T(256)S(1)} %get-tuple-element.44), channel_id=1, source_target_pairs={{0,16},{1,17},{2,18},{3,19},{4,20},{5,21},{6,22},{7,23},{8,28},{9,... | collective-permute-start | bytes 3080 | tf_op jit(solution)/shard_map/ppermute | solution.py:78
  114.2 3.1 %collective-permute-start.31 = (f32[256]{0:T(256)S(1)}, f32[256]{0:T(256)S(1)}, u32[]{:S(2)}, u32[]{:S(2)}) collective-permute-start(f32[256]{0:T(256)S(1)} %get-tuple-element.43), channel_id=1, source_target_pairs={{0,1},{1,0},{2,3},{3,2},{4,5},{5,4},{6,7},{7,6},{8,12},{9,13},{10,... | collective-permute-start | bytes 3080 | tf_op jit(solution)/shard_map/ppermute | solution.py:70
  117.4 3.6 %collective-permute-start.35 = (f32[256]{0:T(256)S(1)}, f32[256]{0:T(256)S(1)}, u32[]{:S(2)}, u32[]{:S(2)}) collective-permute-start(f32[256]{0:T(256)S(1)} %add_add_fusion.3), channel_id=1, source_target_pairs={{0,2},{1,3},{2,0},{3,1},{4,6},{5,7},{6,4},{7,5},{8,10},{9,11},{10,... | collective-permute-start | bytes 3080 | tf_op jit(solution)/shard_map/ppermute | solution.py:63
  118.0 3.0 %collective-permute-start.36 = (f32[256]{0:T(256)S(1)}, f32[256]{0:T(256)S(1)}, u32[]{:S(2)}, u32[]{:S(2)}) collective-permute-start(f32[256]{0:T(256)S(1)} %add_add_fusion.3), channel_id=1, source_target_pairs={{0,3},{1,2},{2,1},{3,0},{4,7},{5,6},{6,5},{7,4},{8,11},{9,10},{10,... | collective-permute-start | bytes 3080 | tf_op jit(solution)/shard_map/ppermute | solution.py:63
  121.0 22.4 %collective-permute-start.37 = (f32[1024]{0:T(1024)S(1)}, f32[1024]{0:T(1024)S(1)}, u32[]{:S(2)}, u32[]{:S(2)}) collective-permute-start(f32[1024]{0:T(1024)S(1)} %pad_maximum_fusion.3), channel_id=1, source_target_pairs={{0,8},{1,9},{2,10},{3,11},{4,12},{5,13},{6,14},{7,15},{8,0},{9,1},... | collective-permute-start | bytes 12296 | tf_op jit(solution)/shard_map/ppermute | solution.py:70
  (9 other events, 52.7 us)

commit v13 on v12

--- a/solution.py
+++ b/solution.py
@@ -197,8 +197,10 @@
         ), owners)
         pool_var = 1.0 + (p_squares + squares[:sizes[0]])
 
+        hold = token(given_side)[:, :1]
+
         def log_sums(group, given, offset):
-            a, b = keep_a[group], keep_b[group]
+            a, b = behind(keep_a[group], hold), behind(keep_b[group], hold)
             target_var = 1.0 + (square_sum(a) + square_sum(b) + squares[offset:offset + sizes[1 + group]])
             cross = matmul_t(a, p_all_a) + matmul_t(b, p_all_b) + given
             ratio = jnp.square(cross) / (target_var[:, None] * pool_var[None, :])

time: 144 us -> 142 us (0.986)
  waiting for transfers between devices: 70.3 us -> 68.2 us
    ppermute x4, waiting for transfers between devices: 12.7 us -> 3.81 us  [over_pool(): return lax.ppermute(value, ('pool', 'tgt'), pairs)]
    ppermute x24, waiting for transfers between devices: 35.8 us -> 44.6 us  [inner(): return lax.ppermute(value, 'tgt', pairs)]
    ppermute x10, waiting for transfers between devices: 21.8 us -> 19.8 us  [along_z(): return lax.ppermute(value, 'tgt', pairs)]
    ppermute x10, starting transfers between devices: 25.3 us -> 23.8 us  [along_z(): return lax.ppermute(value, 'tgt', pairs)]
  transfers between devices with their start and end apart: 38 -> 38, of which waited for: 18 -> 18; matrix products, arithmetic and copies ran while one was open for 15% -> 16% of each run, Pallas kernels for 0% -> 0%
where the time goes in v13:
time: 142 us
  waiting for transfers between devices  68.2 us (48%)
  starting transfers between devices  43.5 us (31%)
  matrix products  13.7 us (10%)
  other arithmetic  9.38 us (7%)
  local copies, waits for them, and re-layouts  5.86 us (4%)
    ppermute x24, waiting for transfers between devices, inner(): return lax.ppermute(value, 'tgt', pairs)  44.6 us
    ppermute x10, starting transfers between devices, along_z(): return lax.ppermute(value, 'tgt', pairs)  23.8 us
    ppermute x10, waiting for transfers between devices, along_z(): return lax.ppermute(value, 'tgt', pairs)  19.8 us
    ppermute x24, starting transfers between devices, inner(): return lax.ppermute(value, 'tgt', pairs)  14.7 us
    dot_general x16, matrix products, matmul(): lax.dot_general(a, b, (((1,), (0,)), ((), ())), preferred_element_type=F32)  8.84 us
    ppermute x4, starting transfers between devices, over_pool(): return lax.ppermute(value, ('pool', 'tgt'), pairs)  5.07 us
    dot_general x10, matrix products, matmul_t(): lax.dot_general(a, b, (((1,), (1,)), ((), ())), preferred_element_type=F32)  4.89 us
    gather x1, local copies, waits for them, and re-layouts, body(): pool_rows = pool_table.at[local_index].get(mode='promise_in_bounds')  3.93 us
  transfers between devices with their start and end apart: 38, of which 18 were waited for; matrix products, arithmetic and copies ran while one was open for 16% of the time, Pallas kernels for 0%

profile of v13, /device:TPU:0, one launch (start us, length us, event | category | flops | bytes accessed | tf_op | source)
XLA Modules:
  0.0 141.9 jit_solution(13107460658592727127)
XLA Ops:
  0.0 1.2 constant_dynamic-slice_fusion
  1.2 3.0 %collective-permute-start.1 = (bf16[256,1024]{1,0:T(8,128)(2,1)S(1)}, bf16[256,1024]{1,0:T(8,128)(2,1)}, u32[]{:S(2)}, u32[]{:S(2)}) collective-permute-start(bf16[256,1024]{1,0:T(8,128)(2,1)S(1)} %constant_dynamic-slice_fusion), channel_id=1, source_target_pairs={{0,2},{1,3},{2,0},{3,1},{4,6},{5,7},{6,4},{7,5},{8,10},{9,11},{10,... | collective-permute-start | bytes 1572872 | tf_op jit(solution)/shard_map/ppermute | solution.py:63
  4.9 3.9 %gather_fusion = bf16[1024,256]{1,0:T(8,128)(2,1)S(1)} fusion(bf16[4096,256]{1,0:T(8,128)(2,1)S(1)} %copy-done, s32[1024]{0:T(1024)S(1)} %fusion.28), kind=kCustom, calls=%fused_computation | custom fusion | bytes 1052672 | tf_op jit(solution)/shard_map/gather | solution.py:104
  8.9 1.9 %fusion.22 = (bf16[512,256]{1,0:T(8,128)(2,1)}, bf16[512,256]{1,0:T(8,128)(2,1)S(1)}, bf16[512,256]{1,0:T(8,128)(2,1)S(1)}, bf16[512,256]{1,0:T(8,128)(2,1)S(1)}) fusion(s32[]{:T(128)S(6)} %select_n.172, s32[]{:T(128)S(6)} %select_n.165, bf16[2,2,256,256]{3,2,1,0:T(8,128)(2,1)} %bitcast.54, bf16[2,2,256,256]{3,2,1,0:T(8,128)(2,1)S(1)} %bitcast.53, ...), kind=kLoop, calls=%fused_computation.66 | loop fusion | flops 2097152 | bytes 2097168 | tf_op jit(solution)/shard_map/squeeze | solution.py:114
  11.3 1.6 %collective-permute-start.4 = (bf16[512,256]{1,0:T(8,128)(2,1)S(1)}, bf16[512,256]{1,0:T(8,128)(2,1)S(1)}, u32[]{:S(2)}, u32[]{:S(2)}) collective-permute-start(bf16[512,256]{1,0:T(8,128)(2,1)S(1)} %get-tuple-element.32), channel_id=1, source_target_pairs={{0,3},{1,2},{2,1},{3,0},{4,7},{5,6},{6,5},{7,4},{8,11},{9,10},{10,... | collective-permute-start | bytes 786440 | tf_op jit(solution)/shard_map/ppermute | solution.py:63
  13.3 3.8 %collective-permute-done.1 = bf16[256,1024]{1,0:T(8,128)(2,1)} collective-permute-done((bf16[256,1024]{1,0:T(8,128)(2,1)S(1)}, bf16[256,1024]{1,0:T(8,128)(2,1)}, u32[]{:S(2)}, u32[]{:S(2)}) %collective-permute-start.1) | collective-permute-done | bytes 524320 | tf_op jit(solution)/shard_map/ppermute | solution.py:63
  17.9 1.1 broadcast_add_fusion.5
  19.1 3.5 %collective-permute-done = bf16[512,256]{1,0:T(8,128)(2,1)S(1)} collective-permute-done((bf16[512,256]{1,0:T(8,128)(2,1)}, bf16[512,256]{1,0:T(8,128)(2,1)S(1)}, u32[]{:S(2)}, u32[]{:S(2)}) %collective-permute-start) | collective-permute-done | bytes 262176 | tf_op jit(solution)/shard_map/ppermute | solution.py:63
  23.1 1.5 %fusion.89 = f32[512,1024]{1,0:T(8,128)S(1)} fusion(bf16[512,256]{1,0:T(8,128)(2,1)S(1)} %collective-permute-done.2, bf16[256,1024]{1,0:T(8,128)(2,1)} %collective-permute-done.3), kind=kOutput, calls=%fused_computation.176 | convolution fusion | flops 268435456 | bytes 2883584 | tf_op jit(solution)/shard_map/dot_general | solution.py:13
  24.6 2.1 %collective-permute-done.4 = bf16[512,256]{1,0:T(8,128)(2,1)S(1)} collective-permute-done((bf16[512,256]{1,0:T(8,128)(2,1)S(1)}, bf16[512,256]{1,0:T(8,128)(2,1)S(1)}, u32[]{:S(2)}, u32[]{:S(2)}) %collective-permute-start.4) | collective-permute-done | bytes 262176 | tf_op jit(solution)/shard_map/ppermute | solution.py:63
  27.9 2.6 %collective-permute-start.12 = (bf16[512,1024]{1,0:T(8,128)(2,1)S(1)}, bf16[512,1024]{1,0:T(8,128)(2,1)S(1)}, u32[]{:S(2)}, u32[]{:S(2)}) collective-permute-start(bf16[512,1024]{1,0:T(8,128)(2,1)S(1)} %add_convert_fusion.1), channel_id=1, source_target_pairs={{0,4},{1,5},{2,6},{3,7},{4,0},{5,1},{6,2},{7,3},{8,12},{9,13},{10,... | collective-permute-start | bytes 3145736 | tf_op jit(solution)/shard_map/ppermute | solution.py:70
  30.9 1.4 collective-permute-start.10
  34.1 0.8 collective-permute-done.8
  36.6 17.7 %collective-permute-done.12 = bf16[512,1024]{1,0:T(8,128)(2,1)S(1)} collective-permute-done((bf16[512,1024]{1,0:T(8,128)(2,1)S(1)}, bf16[512,1024]{1,0:T(8,128)(2,1)S(1)}, u32[]{:S(2)}, u32[]{:S(2)}) %collective-permute-start.12) | collective-permute-done | bytes 1048608 | tf_op jit(solution)/shard_map/ppermute | solution.py:70
  54.3 1.9 %collective-permute-done.6 = bf16[256,1024]{1,0:T(8,128)(2,1)S(1)} collective-permute-done((bf16[256,1024]{1,0:T(8,128)(2,1)S(1)}, bf16[256,1024]{1,0:T(8,128)(2,1)S(1)}, u32[]{:S(2)}, u32[]{:S(2)}) %collective-permute-start.6) | collective-permute-done | bytes 524320 | tf_op jit(solution)/shard_map/ppermute | solution.py:63
  59.6 0.9 add_convert_fusion.2
  61.1 1.6 %collective-permute-start.15 = (bf16[256,1024]{1,0:T(8,128)(2,1)S(1)}, bf16[256,1024]{1,0:T(8,128)(2,1)S(1)}, u32[]{:S(2)}, u32[]{:S(2)}) collective-permute-start(bf16[256,1024]{1,0:T(8,128)(2,1)S(1)} %broadcast_add_fusion.2), channel_id=1, source_target_pairs={{0,2},{1,3},{2,0},{3,1},{4,6},{5,7},{6,4},{7,5},{8,10},{9,11},{10,... | collective-permute-start | bytes 1572872 | tf_op jit(solution)/shard_map/ppermute | solution.py:63
  63.4 1.5 %collective-permute-start.18 = (bf16[256,1024]{1,0:T(8,128)(2,1)S(1)}, bf16[256,1024]{1,0:T(8,128)(2,1)S(1)}, u32[]{:S(2)}, u32[]{:S(2)}) collective-permute-start(bf16[256,1024]{1,0:T(8,128)(2,1)S(1)} %get-tuple-element.28), channel_id=1, source_target_pairs={{0,16},{1,17},{2,18},{3,19},{4,20},{5,21},{6,22},{7,23},{8,24},{9,... | collective-permute-start | bytes 1572872 | tf_op jit(solution)/shard_map/ppermute | solution.py:78
  65.3 10.6 %collective-permute-done.15 = bf16[256,1024]{1,0:T(8,128)(2,1)S(1)} collective-permute-done((bf16[256,1024]{1,0:T(8,128)(2,1)S(1)}, bf16[256,1024]{1,0:T(8,128)(2,1)S(1)}, u32[]{:S(2)}, u32[]{:S(2)}) %collective-permute-start.15) | collective-permute-done | bytes 524320 | tf_op jit(solution)/shard_map/ppermute | solution.py:63
  76.5 9.9 %collective-permute-done.17 = bf16[256,1024]{1,0:T(8,128)(2,1)S(1)} collective-permute-done((bf16[256,1024]{1,0:T(8,128)(2,1)S(1)}, bf16[256,1024]{1,0:T(8,128)(2,1)S(1)}, u32[]{:S(2)}, u32[]{:S(2)}) %collective-permute-start.17) | collective-permute-done | bytes 524320 | tf_op jit(solution)/shard_map/ppermute | solution.py:63
  86.5 1.0 add_convert_fusion
  88.6 1.6 %collective-permute-start.27 = (bf16[256,1024]{1,0:T(8,128)(2,1)S(1)}, bf16[256,1024]{1,0:T(8,128)(2,1)S(1)}, u32[]{:S(2)}, u32[]{:S(2)}) collective-permute-start(bf16[256,1024]{1,0:T(8,128)(2,1)S(1)} %get-tuple-element.26), channel_id=1, source_target_pairs={{0,2},{1,3},{2,0},{3,1},{4,6},{5,7},{6,4},{7,5},{8,10},{9,11},{10,... | collective-permute-start | bytes 1572872 | tf_op jit(solution)/shard_map/ppermute | solution.py:63
  90.1 1.5 %collective-permute-start.23 = (bf16[256,1024]{1,0:T(8,128)(2,1)S(1)}, bf16[256,1024]{1,0:T(8,128)(2,1)S(1)}, u32[]{:S(2)}, u32[]{:S(2)}) collective-permute-start(bf16[256,1024]{1,0:T(8,128)(2,1)S(1)} %get-tuple-element.25), channel_id=1, source_target_pairs={{0,16},{1,17},{2,18},{3,19},{4,20},{5,21},{6,22},{7,23},{8,24},{9,... | collective-permute-start | bytes 1572872 | tf_op jit(solution)/shard_map/ppermute | solution.py:78
  93.5 9.0 %collective-permute-done.27 = bf16[256,1024]{1,0:T(8,128)(2,1)S(1)} collective-permute-done((bf16[256,1024]{1,0:T(8,128)(2,1)S(1)}, bf16[256,1024]{1,0:T(8,128)(2,1)S(1)}, u32[]{:S(2)}, u32[]{:S(2)}) %collective-permute-start.27) | collective-permute-done | bytes 524320 | tf_op jit(solution)/shard_map/ppermute | solution.py:63
  112.4 1.5 %collective-permute-start.32 = (f32[256]{0:T(256)S(1)}, f32[256]{0:T(256)S(1)}, u32[]{:S(2)}, u32[]{:S(2)}) collective-permute-start(f32[256]{0:T(256)S(1)} %get-tuple-element.42), channel_id=1, source_target_pairs={{0,16},{1,17},{2,18},{3,19},{4,20},{5,21},{6,22},{7,23},{8,24},{9,... | collective-permute-start | bytes 3080 | tf_op jit(solution)/shard_map/ppermute | solution.py:78
  114.4 1.5 %collective-permute-done.32 = f32[256]{0:T(256)S(1)} collective-permute-done((f32[256]{0:T(256)S(1)}, f32[256]{0:T(256)S(1)}, u32[]{:S(2)}, u32[]{:S(2)}) %collective-permute-start.32) | collective-permute-done | bytes 1056 | tf_op jit(solution)/shard_map/ppermute | solution.py:78
  116.0 1.5 %collective-permute-done.33 = f32[256]{0:T(256)S(1)} collective-permute-done((f32[256]{0:T(256)S(1)}, f32[256]{0:T(256)S(1)}, u32[]{:S(2)}, u32[]{:S(2)}) %collective-permute-start.33) | collective-permute-done | bytes 1056 | tf_op jit(solution)/shard_map/ppermute | solution.py:78
  117.5 1.0 collective-permute-start.35
  118.5 0.9 collective-permute-start.36
  119.4 1.8 %collective-permute-done.35 = f32[256]{0:T(256)S(1)} collective-permute-done((f32[256]{0:T(256)S(1)}, f32[256]{0:T(256)S(1)}, u32[]{:S(2)}, u32[]{:S(2)}) %collective-permute-start.35) | collective-permute-done | bytes 1056 | tf_op jit(solution)/shard_map/ppermute | solution.py:63
  121.5 18.2 %collective-permute-start.37 = (f32[1024]{0:T(1024)S(1)}, f32[1024]{0:T(1024)S(1)}, u32[]{:S(2)}, u32[]{:S(2)}) collective-permute-start(f32[1024]{0:T(1024)S(1)} %pad_maximum_fusion.3), channel_id=1, source_target_pairs={{0,8},{1,9},{2,10},{3,11},{4,12},{5,13},{6,14},{7,15},{8,0},{9,1},... | collective-permute-start | bytes 12296 | tf_op jit(solution)/shard_map/ppermute | solution.py:70
  139.7 1.6 %collective-permute-done.37 = f32[1024]{0:T(1024)S(1)} collective-permute-done((f32[1024]{0:T(1024)S(1)}, f32[1024]{0:T(1024)S(1)}, u32[]{:S(2)}, u32[]{:S(2)}) %collective-permute-start.37) | collective-permute-done | bytes 4128 | tf_op jit(solution)/shard_map/ppermute | solution.py:70
  (124 shorter events, 27.0 us)
Async XLA Ops:
  1.2 15.9 %collective-permute-start.1 = (bf16[256,1024]{1,0:T(8,128)(2,1)S(1)}, bf16[256,1024]{1,0:T(8,128)(2,1)}, u32[]{:S(2)}, u32[]{:S(2)}) collective-permute-start(bf16[256,1024]{1,0:T(8,128)(2,1)S(1)} %constant_dynamic-slice_fusion), channel_id=1, source_target_pairs={{0,2},{1,3},{2,0},{3,1},{4,6},{5,7},{6,4},{7,5},{8,10},{9,11},{10,... | collective-permute-start | bytes 1572872 | tf_op jit(solution)/shard_map/ppermute | solution.py:63
  4.2 18.8 %collective-permute-start.3 = (bf16[256,1024]{1,0:T(8,128)(2,1)S(1)}, bf16[256,1024]{1,0:T(8,128)(2,1)}, u32[]{:S(2)}, u32[]{:S(2)}) collective-permute-start(bf16[256,1024]{1,0:T(8,128)(2,1)S(1)} %constant_dynamic-slice_fusion), channel_id=1, source_target_pairs={{0,1},{1,0},{2,3},{3,2},{4,5},{5,4},{6,7},{7,6},{8,9},{9,8},{10,11... | collective-permute-start | bytes 1572872 | tf_op jit(solution)/shard_map/ppermute | solution.py:63
  10.8 11.8 %collective-permute-start = (bf16[512,256]{1,0:T(8,128)(2,1)}, bf16[512,256]{1,0:T(8,128)(2,1)S(1)}, u32[]{:S(2)}, u32[]{:S(2)}) collective-permute-start(bf16[512,256]{1,0:T(8,128)(2,1)} %get-tuple-element.29), channel_id=1, source_target_pairs={{0,2},{1,3},{2,0},{3,1},{4,6},{5,7},{6,4},{7,5},{8,10},{9,11},{10,... | collective-permute-start | bytes 786440 | tf_op jit(solution)/shard_map/ppermute | solution.py:63
  10.9 12.2 %collective-permute-start.2 = (bf16[512,256]{1,0:T(8,128)(2,1)S(1)}, bf16[512,256]{1,0:T(8,128)(2,1)S(1)}, u32[]{:S(2)}, u32[]{:S(2)}) collective-permute-start(bf16[512,256]{1,0:T(8,128)(2,1)S(1)} %get-tuple-element.30), channel_id=1, source_target_pairs={{0,1},{1,0},{2,3},{3,2},{4,5},{5,4},{6,7},{7,6},{8,9},{9,8},{10,11... | collective-permute-start | bytes 786440 | tf_op jit(solution)/shard_map/ppermute | solution.py:63
  11.3 15.4 %collective-permute-start.4 = (bf16[512,256]{1,0:T(8,128)(2,1)S(1)}, bf16[512,256]{1,0:T(8,128)(2,1)S(1)}, u32[]{:S(2)}, u32[]{:S(2)}) collective-permute-start(bf16[512,256]{1,0:T(8,128)(2,1)S(1)} %get-tuple-element.32), channel_id=1, source_target_pairs={{0,3},{1,2},{2,1},{3,0},{4,7},{5,6},{6,5},{7,4},{8,11},{9,10},{10,... | collective-permute-start | bytes 786440 | tf_op jit(solution)/shard_map/ppermute | solution.py:63
  19.0 7.7 %collective-permute-start.5 = (bf16[256,1024]{1,0:T(8,128)(2,1)S(1)}, bf16[256,1024]{1,0:T(8,128)(2,1)S(1)}, u32[]{:S(2)}, u32[]{:S(2)}) collective-permute-start(bf16[256,1024]{1,0:T(8,128)(2,1)S(1)} %broadcast_add_fusion.5), channel_id=1, source_target_pairs={{0,1},{1,0},{2,3},{3,2},{4,5},{5,4},{6,7},{7,6},{8,9},{9,8},{10,11... | collective-permute-start | bytes 1572872 | tf_op jit(solution)/shard_map/ppermute | solution.py:63
  27.2 9.4 %collective-permute-start.11 = (bf16[512,1024]{1,0:T(8,128)(2,1)S(1)}, bf16[512,1024]{1,0:T(8,128)(2,1)S(1)}, u32[]{:S(2)}, u32[]{:S(2)}) collective-permute-start(bf16[512,1024]{1,0:T(8,128)(2,1)S(1)} %add_convert_fusion.1), channel_id=1, source_target_pairs={{0,1},{1,0},{2,3},{3,2},{4,8},{5,9},{6,10},{7,11},{8,4},{9,5},{10,... | collective-permute-start | bytes 3145736 | tf_op jit(solution)/shard_map/ppermute | solution.py:70
  27.9 26.4 %collective-permute-start.12 = (bf16[512,1024]{1,0:T(8,128)(2,1)S(1)}, bf16[512,1024]{1,0:T(8,128)(2,1)S(1)}, u32[]{:S(2)}, u32[]{:S(2)}) collective-permute-start(bf16[512,1024]{1,0:T(8,128)(2,1)S(1)} %add_convert_fusion.1), channel_id=1, source_target_pairs={{0,4},{1,5},{2,6},{3,7},{4,0},{5,1},{6,2},{7,3},{8,12},{9,13},{10,... | collective-permute-start | bytes 3145736 | tf_op jit(solution)/shard_map/ppermute | solution.py:70
  30.9 23.5 %collective-permute-start.10 = (bf16[256,1024]{1,0:T(8,128)(2,1)S(1)}, bf16[256,1024]{1,0:T(8,128)(2,1)S(1)}, u32[]{:S(2)}, u32[]{:S(2)}) collective-permute-start(bf16[256,1024]{1,0:T(8,128)(2,1)S(1)} %get-tuple-element.23), channel_id=1, source_target_pairs={{0,2},{1,3},{2,0},{3,1},{4,6},{5,7},{6,4},{7,5},{8,10},{9,11},{10,... | collective-permute-start | bytes 1572872 | tf_op jit(solution)/shard_map/ppermute | solution.py:63
  32.3 3.8 %collective-permute-start.7 = (bf16[256,1024]{1,0:T(8,128)(2,1)S(1)}, bf16[256,1024]{1,0:T(8,128)(2,1)S(1)}, u32[]{:S(2)}, u32[]{:S(2)}) collective-permute-start(bf16[256,1024]{1,0:T(8,128)(2,1)S(1)} %get-tuple-element.23), channel_id=1, source_target_pairs={{0,1},{1,0},{2,3},{3,2},{4,5},{5,4},{6,7},{7,6},{8,9},{9,8},{10,11... | collective-permute-start | bytes 1572872 | tf_op jit(solution)/shard_map/ppermute | solution.py:63
  32.4 2.5 %collective-permute-start.8 = (bf16[256,1024]{1,0:T(8,128)(2,1)S(1)}, bf16[256,1024]{1,0:T(8,128)(2,1)S(1)}, u32[]{:S(2)}, u32[]{:S(2)}) collective-permute-start(bf16[256,1024]{1,0:T(8,128)(2,1)S(1)} %get-tuple-element.22), channel_id=1, source_target_pairs={{0,1},{1,0},{2,3},{3,2},{4,5},{5,4},{6,7},{7,6},{8,9},{9,8},{10,11... | collective-permute-start | bytes 1572872 | tf_op jit(solution)/shard_map/ppermute | solution.py:63
  34.9 21.3 %collective-permute-start.6 = (bf16[256,1024]{1,0:T(8,128)(2,1)S(1)}, bf16[256,1024]{1,0:T(8,128)(2,1)S(1)}, u32[]{:S(2)}, u32[]{:S(2)}) collective-permute-start(bf16[256,1024]{1,0:T(8,128)(2,1)S(1)} %get-tuple-element.22), channel_id=1, source_target_pairs={{0,2},{1,3},{2,0},{3,1},{4,6},{5,7},{6,4},{7,5},{8,10},{9,11},{10,... | collective-permute-start | bytes 1572872 | tf_op jit(solution)/shard_map/ppermute | solution.py:63
  36.1 20.2 %collective-permute-start.9 = (bf16[256,1024]{1,0:T(8,128)(2,1)S(1)}, bf16[256,1024]{1,0:T(8,128)(2,1)S(1)}, u32[]{:S(2)}, u32[]{:S(2)}) collective-permute-start(bf16[256,1024]{1,0:T(8,128)(2,1)S(1)} %get-tuple-element.21), channel_id=1, source_target_pairs={{0,1},{1,0},{2,3},{3,2},{4,5},{5,4},{6,7},{7,6},{8,9},{9,8},{10,11... | collective-permute-start | bytes 1572872 | tf_op jit(solution)/shard_map/ppermute | solution.py:63
  56.5 2.6 %collective-permute-start.14 = (bf16[256,1024]{1,0:T(8,128)(2,1)S(1)}, bf16[256,1024]{1,0:T(8,128)(2,1)S(1)}, u32[]{:S(2)}, u32[]{:S(2)}) collective-permute-start(bf16[256,1024]{1,0:T(8,128)(2,1)S(1)} %get-tuple-element.46), channel_id=1, source_target_pairs={{0,1},{1,0},{2,3},{3,2},{4,5},{5,4},{6,7},{7,6},{8,9},{9,8},{10,11... | collective-permute-start | bytes 1572872 | tf_op jit(solution)/shard_map/ppermute | solution.py:63
  60.5 15.9 %collective-permute-start.19 = (bf16[512,1024]{1,0:T(8,128)(2,1)S(1)}, bf16[512,1024]{1,0:T(8,128)(2,1)S(1)}, u32[]{:S(2)}, u32[]{:S(2)}) collective-permute-start(bf16[512,1024]{1,0:T(8,128)(2,1)S(1)} %get-tuple-element.19), channel_id=1, source_target_pairs={{0,1},{1,0},{2,3},{3,2},{4,5},{5,4},{6,7},{7,6},{8,12},{9,13},{10,... | collective-permute-start | bytes 3145736 | tf_op jit(solution)/shard_map/ppermute | solution.py:70
  60.7 15.7 %collective-permute-start.20 = (bf16[512,1024]{1,0:T(8,128)(2,1)S(1)}, bf16[512,1024]{1,0:T(8,128)(2,1)S(1)}, u32[]{:S(2)}, u32[]{:S(2)}) collective-permute-start(bf16[512,1024]{1,0:T(8,128)(2,1)S(1)} %get-tuple-element.20), channel_id=1, source_target_pairs={{0,1},{1,0},{2,3},{3,2},{4,8},{5,9},{6,10},{7,11},{8,4},{9,5},{10,... | collective-permute-start | bytes 3145736 | tf_op jit(solution)/shard_map/ppermute | solution.py:70
  61.1 14.8 %collective-permute-start.15 = (bf16[256,1024]{1,0:T(8,128)(2,1)S(1)}, bf16[256,1024]{1,0:T(8,128)(2,1)S(1)}, u32[]{:S(2)}, u32[]{:S(2)}) collective-permute-start(bf16[256,1024]{1,0:T(8,128)(2,1)S(1)} %broadcast_add_fusion.2), channel_id=1, source_target_pairs={{0,2},{1,3},{2,0},{3,1},{4,6},{5,7},{6,4},{7,5},{8,10},{9,11},{10,... | collective-permute-start | bytes 1572872 | tf_op jit(solution)/shard_map/ppermute | solution.py:63
  62.8 23.6 %collective-permute-start.17 = (bf16[256,1024]{1,0:T(8,128)(2,1)S(1)}, bf16[256,1024]{1,0:T(8,128)(2,1)S(1)}, u32[]{:S(2)}, u32[]{:S(2)}) collective-permute-start(bf16[256,1024]{1,0:T(8,128)(2,1)S(1)} %get-tuple-element.27), channel_id=1, source_target_pairs={{0,2},{1,3},{2,0},{3,1},{4,6},{5,7},{6,4},{7,5},{8,10},{9,11},{10,... | collective-permute-start | bytes 1572872 | tf_op jit(solution)/shard_map/ppermute | solution.py:63
  63.4 23.0 %collective-permute-start.18 = (bf16[256,1024]{1,0:T(8,128)(2,1)S(1)}, bf16[256,1024]{1,0:T(8,128)(2,1)S(1)}, u32[]{:S(2)}, u32[]{:S(2)}) collective-permute-start(bf16[256,1024]{1,0:T(8,128)(2,1)S(1)} %get-tuple-element.28), channel_id=1, source_target_pairs={{0,16},{1,17},{2,18},{3,19},{4,20},{5,21},{6,22},{7,23},{8,24},{9,... | collective-permute-start | bytes 1572872 | tf_op jit(solution)/shard_map/ppermute | solution.py:78
  76.0 10.5 %collective-permute-start.16 = (bf16[256,1024]{1,0:T(8,128)(2,1)S(1)}, bf16[256,1024]{1,0:T(8,128)(2,1)S(1)}, u32[]{:S(2)}, u32[]{:S(2)}) collective-permute-start(bf16[256,1024]{1,0:T(8,128)(2,1)S(1)} %collective-permute-done.15), channel_id=1, source_target_pairs={{0,1},{1,0},{2,3},{3,2},{4,5},{5,4},{6,7},{7,6},{8,9},{9,8},{10,11... | collective-permute-start | bytes 1572872 | tf_op jit(solution)/shard_map/ppermute | solution.py:63
  87.6 4.1 %collective-permute-start.22 = (bf16[256,1024]{1,0:T(8,128)(2,1)S(1)}, bf16[256,1024]{1,0:T(8,128)(2,1)S(1)}, u32[]{:S(2)}, u32[]{:S(2)}) collective-permute-start(bf16[256,1024]{1,0:T(8,128)(2,1)S(1)} %get-tuple-element.26), channel_id=1, source_target_pairs={{0,1},{1,0},{2,3},{3,2},{4,5},{5,4},{6,7},{7,6},{8,9},{9,8},{10,11... | collective-permute-start | bytes 1572872 | tf_op jit(solution)/shard_map/ppermute | solution.py:63
  87.7 4.2 %collective-permute-start.21 = (bf16[256,1024]{1,0:T(8,128)(2,1)S(1)}, bf16[256,1024]{1,0:T(8,128)(2,1)S(1)}, u32[]{:S(2)}, u32[]{:S(2)}) collective-permute-start(bf16[256,1024]{1,0:T(8,128)(2,1)S(1)} %get-tuple-element.44), channel_id=1, source_target_pairs={{0,1},{1,0},{2,3},{3,2},{4,5},{5,4},{6,7},{7,6},{8,9},{9,8},{10,11... | collective-permute-start | bytes 1572872 | tf_op jit(solution)/shard_map/ppermute | solution.py:63
  88.6 13.9 %collective-permute-start.27 = (bf16[256,1024]{1,0:T(8,128)(2,1)S(1)}, bf16[256,1024]{1,0:T(8,128)(2,1)S(1)}, u32[]{:S(2)}, u32[]{:S(2)}) collective-permute-start(bf16[256,1024]{1,0:T(8,128)(2,1)S(1)} %get-tuple-element.26), channel_id=1, source_target_pairs={{0,2},{1,3},{2,0},{3,1},{4,6},{5,7},{6,4},{7,5},{8,10},{9,11},{10,... | collective-permute-start | bytes 1572872 | tf_op jit(solution)/shard_map/ppermute | solution.py:63
  90.1 13.6 %collective-permute-start.23 = (bf16[256,1024]{1,0:T(8,128)(2,1)S(1)}, bf16[256,1024]{1,0:T(8,128)(2,1)S(1)}, u32[]{:S(2)}, u32[]{:S(2)}) collective-permute-start(bf16[256,1024]{1,0:T(8,128)(2,1)S(1)} %get-tuple-element.25), channel_id=1, source_target_pairs={{0,16},{1,17},{2,18},{3,19},{4,20},{5,21},{6,22},{7,23},{8,24},{9,... | collective-permute-start | bytes 1572872 | tf_op jit(solution)/shard_map/ppermute | solution.py:78
  91.6 10.8 %collective-permute-start.26 = (bf16[256,1024]{1,0:T(8,128)(2,1)S(1)}, bf16[256,1024]{1,0:T(8,128)(2,1)S(1)}, u32[]{:S(2)}, u32[]{:S(2)}) collective-permute-start(bf16[256,1024]{1,0:T(8,128)(2,1)S(1)} %get-tuple-element.43), channel_id=1, source_target_pairs={{0,1},{1,0},{2,3},{3,2},{4,5},{5,4},{6,7},{7,6},{8,9},{9,8},{10,11... | collective-permute-start | bytes 1572872 | tf_op jit(solution)/shard_map/ppermute | solution.py:63
  92.9 11.6 %collective-permute-start.24 = (f32[256,256]{1,0:T(8,128)S(1)}, f32[256,256]{1,0:T(8,128)S(1)}, u32[]{:S(2)}, u32[]{:S(2)}) collective-permute-start(f32[256,256]{1,0:T(8,128)S(1)} %convolution_add_fusion.3), channel_id=1, source_target_pairs={{0,1},{1,0},{2,3},{3,2},{4,5},{5,4},{6,7},{7,6},{8,12},{9,13},{10,... | collective-permute-start | bytes 786440 | tf_op jit(solution)/shard_map/ppermute | solution.py:70
  105.4 5.8 %collective-permute-start.30 = (f32[256,512]{1,0:T(8,128)S(1)}, f32[256,512]{1,0:T(8,128)S(1)}, u32[]{:S(2)}, u32[]{:S(2)}) collective-permute-start(f32[256,512]{1,0:T(8,128)S(1)} %convolution_add_fusion), channel_id=1, source_target_pairs={{0,1},{1,0},{2,3},{3,2},{4,5},{5,4},{6,7},{7,6},{8,12},{9,13},{10,... | collective-permute-start | bytes 1572872 | tf_op jit(solution)/shard_map/ppermute | solution.py:70
  112.4 3.6 %collective-permute-start.32 = (f32[256]{0:T(256)S(1)}, f32[256]{0:T(256)S(1)}, u32[]{:S(2)}, u32[]{:S(2)}) collective-permute-start(f32[256]{0:T(256)S(1)} %get-tuple-element.42), channel_id=1, source_target_pairs={{0,16},{1,17},{2,18},{3,19},{4,20},{5,21},{6,22},{7,23},{8,24},{9,... | collective-permute-start | bytes 3080 | tf_op jit(solution)/shard_map/ppermute | solution.py:78
  113.9 3.6 %collective-permute-start.33 = (f32[256]{0:T(256)S(1)}, f32[256]{0:T(256)S(1)}, u32[]{:S(2)}, u32[]{:S(2)}) collective-permute-start(f32[256]{0:T(256)S(1)} %get-tuple-element.42), channel_id=1, source_target_pairs={{0,16},{1,17},{2,18},{3,19},{4,20},{5,21},{6,22},{7,23},{8,28},{9,... | collective-permute-start | bytes 3080 | tf_op jit(solution)/shard_map/ppermute | solution.py:78
  117.5 3.6 %collective-permute-start.35 = (f32[256]{0:T(256)S(1)}, f32[256]{0:T(256)S(1)}, u32[]{:S(2)}, u32[]{:S(2)}) collective-permute-start(f32[256]{0:T(256)S(1)} %add_add_fusion.3), channel_id=1, source_target_pairs={{0,2},{1,3},{2,0},{3,1},{4,6},{5,7},{6,4},{7,5},{8,10},{9,11},{10,... | collective-permute-start | bytes 3080 | tf_op jit(solution)/shard_map/ppermute | solution.py:63
  118.5 3.0 %collective-permute-start.36 = (f32[256]{0:T(256)S(1)}, f32[256]{0:T(256)S(1)}, u32[]{:S(2)}, u32[]{:S(2)}) collective-permute-start(f32[256]{0:T(256)S(1)} %add_add_fusion.3), channel_id=1, source_target_pairs={{0,3},{1,2},{2,1},{3,0},{4,7},{5,6},{6,5},{7,4},{8,11},{9,10},{10,... | collective-permute-start | bytes 3080 | tf_op jit(solution)/shard_map/ppermute | solution.py:63
  121.5 19.8 %collective-permute-start.37 = (f32[1024]{0:T(1024)S(1)}, f32[1024]{0:T(1024)S(1)}, u32[]{:S(2)}, u32[]{:S(2)}) collective-permute-start(f32[1024]{0:T(1024)S(1)} %pad_maximum_fusion.3), channel_id=1, source_target_pairs={{0,8},{1,9},{2,10},{3,11},{4,12},{5,13},{6,14},{7,15},{8,0},{9,1},... | collective-permute-start | bytes 12296 | tf_op jit(solution)/shard_map/ppermute | solution.py:70
  (9 other events, 53.6 us)

commit v14 on v13

--- a/solution.py
+++ b/solution.py
@@ -147,9 +147,10 @@
         own4 = behind(factor_own([3, 3, 3, 3]), start)
         flip2, flip3, flip4 = inner(own2, 0, 1), inner(own3, 0, 1), inner(own4, 0, 1)
         moved2, moved3 = factor_x(own2), factor_x(own3)
-        done = fence([step2, step1], [*moved2, *moved3], [flip2, flip3, flip4])
-        moved2, moved3 = [behind(v, done) for v in moved2], [behind(v, done) for v in moved3]
-        second = partial([own2] + moved2 + [flip2] + factor_flip(moved2))
+        far2 = factor_flip(moved2)
+        done = fence([step2, step1], moved3, [flip2, flip3, flip4, *far2])
+        moved3 = [behind(v, done) for v in moved3]
+        second = partial([own2] + moved2 + [flip2] + far2)
         third = partial([own3] + moved3 + [flip3] + factor_flip(moved3))
 
         start = token(second, third) + done

time: 142 us -> 144 us (1.014)
  waiting for transfers between devices: 68.2 us -> 70.1 us
    ppermute x24, waiting for transfers between devices: 44.6 us -> 64.2 us  [inner(): return lax.ppermute(value, 'tgt', pairs)]
    ppermute x10, waiting for transfers between devices: 19.8 us -> 2.08 us  [along_z(): return lax.ppermute(value, 'tgt', pairs)]
  transfers between devices with their start and end apart: 38 -> 38, of which waited for: 18 -> 17; matrix products, arithmetic and copies ran while one was open for 16% -> 16% of each run, Pallas kernels for 0% -> 0%
where the time goes in v14:
time: 144 us
  waiting for transfers between devices  70.1 us (49%)
  starting transfers between devices  43.5 us (30%)
  matrix products  13.8 us (10%)
  other arithmetic  9.35 us (6%)
  local copies, waits for them, and re-layouts  5.86 us (4%)
    ppermute x24, waiting for transfers between devices, inner(): return lax.ppermute(value, 'tgt', pairs)  64.2 us
    ppermute x10, starting transfers between devices, along_z(): return lax.ppermute(value, 'tgt', pairs)  23.7 us
    ppermute x24, starting transfers between devices, inner(): return lax.ppermute(value, 'tgt', pairs)  14.8 us
    dot_general x16, matrix products, matmul(): lax.dot_general(a, b, (((1,), (0,)), ((), ())), preferred_element_type=F32)  8.87 us
    ppermute x4, starting transfers between devices, over_pool(): return lax.ppermute(value, ('pool', 'tgt'), pairs)  5.07 us
    dot_general x10, matrix products, matmul_t(): lax.dot_general(a, b, (((1,), (1,)), ((), ())), preferred_element_type=F32)  4.91 us
    gather x1, local copies, waits for them, and re-layouts, body(): pool_rows = pool_table.at[local_index].get(mode='promise_in_bounds')  3.93 us
    ppermute x4, waiting for transfers between devices, over_pool(): return lax.ppermute(value, ('pool', 'tgt'), pairs)  3.83 us
  transfers between devices with their start and end apart: 38, of which 17 were waited for; matrix products, arithmetic and copies ran while one was open for 16% of the time, Pallas kernels for 0%

profile of v14, /device:TPU:0, one launch (start us, length us, event | category | flops | bytes accessed | tf_op | source)
XLA Modules:
  0.0 143.8 jit_solution(14901424208824031160)
XLA Ops:
  0.0 1.2 constant_dynamic-slice_fusion
  1.2 3.0 %collective-permute-start.1 = (bf16[256,1024]{1,0:T(8,128)(2,1)S(1)}, bf16[256,1024]{1,0:T(8,128)(2,1)}, u32[]{:S(2)}, u32[]{:S(2)}) collective-permute-start(bf16[256,1024]{1,0:T(8,128)(2,1)S(1)} %constant_dynamic-slice_fusion), channel_id=1, source_target_pairs={{0,2},{1,3},{2,0},{3,1},{4,6},{5,7},{6,4},{7,5},{8,10},{9,11},{10,... | collective-permute-start | bytes 1572872 | tf_op jit(solution)/shard_map/ppermute | solution.py:63
  4.9 3.9 %gather_fusion = bf16[1024,256]{1,0:T(8,128)(2,1)S(1)} fusion(bf16[4096,256]{1,0:T(8,128)(2,1)S(1)} %copy-done, s32[1024]{0:T(1024)S(1)} %fusion.28), kind=kCustom, calls=%fused_computation | custom fusion | bytes 1052672 | tf_op jit(solution)/shard_map/gather | solution.py:104
  8.9 1.9 %fusion.22 = (bf16[512,256]{1,0:T(8,128)(2,1)}, bf16[512,256]{1,0:T(8,128)(2,1)S(1)}, bf16[512,256]{1,0:T(8,128)(2,1)S(1)}, bf16[512,256]{1,0:T(8,128)(2,1)S(1)}) fusion(s32[]{:T(128)S(6)} %select_n.172, s32[]{:T(128)S(6)} %select_n.165, bf16[2,2,256,256]{3,2,1,0:T(8,128)(2,1)} %bitcast.54, bf16[2,2,256,256]{3,2,1,0:T(8,128)(2,1)S(1)} %bitcast.53, ...), kind=kLoop, calls=%fused_computation.66 | loop fusion | flops 2097152 | bytes 2097168 | tf_op jit(solution)/shard_map/squeeze | solution.py:114
  11.3 1.6 %collective-permute-start.4 = (bf16[512,256]{1,0:T(8,128)(2,1)S(1)}, bf16[512,256]{1,0:T(8,128)(2,1)S(1)}, u32[]{:S(2)}, u32[]{:S(2)}) collective-permute-start(bf16[512,256]{1,0:T(8,128)(2,1)S(1)} %get-tuple-element.32), channel_id=1, source_target_pairs={{0,3},{1,2},{2,1},{3,0},{4,7},{5,6},{6,5},{7,4},{8,11},{9,10},{10,... | collective-permute-start | bytes 786440 | tf_op jit(solution)/shard_map/ppermute | solution.py:63
  13.3 3.7 %collective-permute-done.1 = bf16[256,1024]{1,0:T(8,128)(2,1)} collective-permute-done((bf16[256,1024]{1,0:T(8,128)(2,1)S(1)}, bf16[256,1024]{1,0:T(8,128)(2,1)}, u32[]{:S(2)}, u32[]{:S(2)}) %collective-permute-start.1) | collective-permute-done | bytes 524320 | tf_op jit(solution)/shard_map/ppermute | solution.py:63
  17.9 1.1 broadcast_add_fusion.4
  19.1 3.5 %collective-permute-done = bf16[512,256]{1,0:T(8,128)(2,1)S(1)} collective-permute-done((bf16[512,256]{1,0:T(8,128)(2,1)}, bf16[512,256]{1,0:T(8,128)(2,1)S(1)}, u32[]{:S(2)}, u32[]{:S(2)}) %collective-permute-start) | collective-permute-done | bytes 262176 | tf_op jit(solution)/shard_map/ppermute | solution.py:63
  23.1 1.5 %fusion.89 = f32[512,1024]{1,0:T(8,128)S(1)} fusion(bf16[512,256]{1,0:T(8,128)(2,1)S(1)} %collective-permute-done.2, bf16[256,1024]{1,0:T(8,128)(2,1)} %collective-permute-done.3), kind=kOutput, calls=%fused_computation.175 | convolution fusion | flops 268435456 | bytes 2883584 | tf_op jit(solution)/shard_map/dot_general | solution.py:13
  24.6 2.1 %collective-permute-done.4 = bf16[512,256]{1,0:T(8,128)(2,1)S(1)} collective-permute-done((bf16[512,256]{1,0:T(8,128)(2,1)S(1)}, bf16[512,256]{1,0:T(8,128)(2,1)S(1)}, u32[]{:S(2)}, u32[]{:S(2)}) %collective-permute-start.4) | collective-permute-done | bytes 262176 | tf_op jit(solution)/shard_map/ppermute | solution.py:63
  27.9 2.6 %collective-permute-start.13 = (bf16[512,1024]{1,0:T(8,128)(2,1)S(1)}, bf16[512,1024]{1,0:T(8,128)(2,1)S(1)}, u32[]{:S(2)}, u32[]{:S(2)}) collective-permute-start(bf16[512,1024]{1,0:T(8,128)(2,1)S(1)} %add_convert_fusion.1), channel_id=1, source_target_pairs={{0,4},{1,5},{2,6},{3,7},{4,0},{5,1},{6,2},{7,3},{8,12},{9,13},{10,... | collective-permute-start | bytes 3145736 | tf_op jit(solution)/shard_map/ppermute | solution.py:70
  30.9 1.4 collective-permute-start.6
  35.1 21.1 %collective-permute-done.10 = bf16[256,1024]{1,0:T(8,128)(2,1)S(1)} collective-permute-done((bf16[256,1024]{1,0:T(8,128)(2,1)S(1)}, bf16[256,1024]{1,0:T(8,128)(2,1)S(1)}, u32[]{:S(2)}, u32[]{:S(2)}) %collective-permute-start.10) | collective-permute-done | bytes 524320 | tf_op jit(solution)/shard_map/ppermute | solution.py:63
  58.2 0.7 collective-permute-done.11
  61.5 0.9 add_convert_fusion.2
  63.0 1.6 %collective-permute-start.15 = (bf16[256,1024]{1,0:T(8,128)(2,1)S(1)}, bf16[256,1024]{1,0:T(8,128)(2,1)S(1)}, u32[]{:S(2)}, u32[]{:S(2)}) collective-permute-start(bf16[256,1024]{1,0:T(8,128)(2,1)S(1)} %broadcast_add_fusion.2), channel_id=1, source_target_pairs={{0,2},{1,3},{2,0},{3,1},{4,6},{5,7},{6,4},{7,5},{8,10},{9,11},{10,... | collective-permute-start | bytes 1572872 | tf_op jit(solution)/shard_map/ppermute | solution.py:63
  65.3 1.5 %collective-permute-start.18 = (bf16[256,1024]{1,0:T(8,128)(2,1)S(1)}, bf16[256,1024]{1,0:T(8,128)(2,1)S(1)}, u32[]{:S(2)}, u32[]{:S(2)}) collective-permute-start(bf16[256,1024]{1,0:T(8,128)(2,1)S(1)} %get-tuple-element.28), channel_id=1, source_target_pairs={{0,16},{1,17},{2,18},{3,19},{4,20},{5,21},{6,22},{7,23},{8,24},{9,... | collective-permute-start | bytes 1572872 | tf_op jit(solution)/shard_map/ppermute | solution.py:78
  67.2 10.6 %collective-permute-done.15 = bf16[256,1024]{1,0:T(8,128)(2,1)S(1)} collective-permute-done((bf16[256,1024]{1,0:T(8,128)(2,1)S(1)}, bf16[256,1024]{1,0:T(8,128)(2,1)S(1)}, u32[]{:S(2)}, u32[]{:S(2)}) %collective-permute-start.15) | collective-permute-done | bytes 524320 | tf_op jit(solution)/shard_map/ppermute | solution.py:63
  78.3 10.1 %collective-permute-done.17 = bf16[256,1024]{1,0:T(8,128)(2,1)S(1)} collective-permute-done((bf16[256,1024]{1,0:T(8,128)(2,1)S(1)}, bf16[256,1024]{1,0:T(8,128)(2,1)S(1)}, u32[]{:S(2)}, u32[]{:S(2)}) %collective-permute-start.17) | collective-permute-done | bytes 524320 | tf_op jit(solution)/shard_map/ppermute | solution.py:63
  88.5 1.0 add_convert_fusion
  90.6 1.6 %collective-permute-start.27 = (bf16[256,1024]{1,0:T(8,128)(2,1)S(1)}, bf16[256,1024]{1,0:T(8,128)(2,1)S(1)}, u32[]{:S(2)}, u32[]{:S(2)}) collective-permute-start(bf16[256,1024]{1,0:T(8,128)(2,1)S(1)} %get-tuple-element.26), channel_id=1, source_target_pairs={{0,2},{1,3},{2,0},{3,1},{4,6},{5,7},{6,4},{7,5},{8,10},{9,11},{10,... | collective-permute-start | bytes 1572872 | tf_op jit(solution)/shard_map/ppermute | solution.py:63
  92.1 1.5 %collective-permute-start.23 = (bf16[256,1024]{1,0:T(8,128)(2,1)S(1)}, bf16[256,1024]{1,0:T(8,128)(2,1)S(1)}, u32[]{:S(2)}, u32[]{:S(2)}) collective-permute-start(bf16[256,1024]{1,0:T(8,128)(2,1)S(1)} %get-tuple-element.25), channel_id=1, source_target_pairs={{0,16},{1,17},{2,18},{3,19},{4,20},{5,21},{6,22},{7,23},{8,24},{9,... | collective-permute-start | bytes 1572872 | tf_op jit(solution)/shard_map/ppermute | solution.py:78
  95.5 9.0 %collective-permute-done.27 = bf16[256,1024]{1,0:T(8,128)(2,1)S(1)} collective-permute-done((bf16[256,1024]{1,0:T(8,128)(2,1)S(1)}, bf16[256,1024]{1,0:T(8,128)(2,1)S(1)}, u32[]{:S(2)}, u32[]{:S(2)}) %collective-permute-start.27) | collective-permute-done | bytes 524320 | tf_op jit(solution)/shard_map/ppermute | solution.py:63
  105.0 0.7 collective-permute-done.23
  114.4 1.5 %collective-permute-start.32 = (f32[256]{0:T(256)S(1)}, f32[256]{0:T(256)S(1)}, u32[]{:S(2)}, u32[]{:S(2)}) collective-permute-start(f32[256]{0:T(256)S(1)} %get-tuple-element.42), channel_id=1, source_target_pairs={{0,16},{1,17},{2,18},{3,19},{4,20},{5,21},{6,22},{7,23},{8,24},{9,... | collective-permute-start | bytes 3080 | tf_op jit(solution)/shard_map/ppermute | solution.py:78
  116.5 1.5 %collective-permute-done.32 = f32[256]{0:T(256)S(1)} collective-permute-done((f32[256]{0:T(256)S(1)}, f32[256]{0:T(256)S(1)}, u32[]{:S(2)}, u32[]{:S(2)}) %collective-permute-start.32) | collective-permute-done | bytes 1056 | tf_op jit(solution)/shard_map/ppermute | solution.py:78
  118.0 1.5 %collective-permute-done.33 = f32[256]{0:T(256)S(1)} collective-permute-done((f32[256]{0:T(256)S(1)}, f32[256]{0:T(256)S(1)}, u32[]{:S(2)}, u32[]{:S(2)}) %collective-permute-start.33) | collective-permute-done | bytes 1056 | tf_op jit(solution)/shard_map/ppermute | solution.py:78
  119.6 1.0 collective-permute-start.35
  120.6 0.9 collective-permute-start.36
  121.5 1.8 %collective-permute-done.35 = f32[256]{0:T(256)S(1)} collective-permute-done((f32[256]{0:T(256)S(1)}, f32[256]{0:T(256)S(1)}, u32[]{:S(2)}, u32[]{:S(2)}) %collective-permute-start.35) | collective-permute-done | bytes 1056 | tf_op jit(solution)/shard_map/ppermute | solution.py:63
  123.6 18.0 %collective-permute-start.37 = (f32[1024]{0:T(1024)S(1)}, f32[1024]{0:T(1024)S(1)}, u32[]{:S(2)}, u32[]{:S(2)}) collective-permute-start(f32[1024]{0:T(1024)S(1)} %pad_maximum_fusion.3), channel_id=1, source_target_pairs={{0,8},{1,9},{2,10},{3,11},{4,12},{5,13},{6,14},{7,15},{8,0},{9,1},... | collective-permute-start | bytes 12296 | tf_op jit(solution)/shard_map/ppermute | solution.py:70
  141.6 1.6 %collective-permute-done.37 = f32[1024]{0:T(1024)S(1)} collective-permute-done((f32[1024]{0:T(1024)S(1)}, f32[1024]{0:T(1024)S(1)}, u32[]{:S(2)}, u32[]{:S(2)}) %collective-permute-start.37) | collective-permute-done | bytes 4128 | tf_op jit(solution)/shard_map/ppermute | solution.py:70
  (124 shorter events, 26.7 us)
Async XLA Ops:
  1.2 15.9 %collective-permute-start.1 = (bf16[256,1024]{1,0:T(8,128)(2,1)S(1)}, bf16[256,1024]{1,0:T(8,128)(2,1)}, u32[]{:S(2)}, u32[]{:S(2)}) collective-permute-start(bf16[256,1024]{1,0:T(8,128)(2,1)S(1)} %constant_dynamic-slice_fusion), channel_id=1, source_target_pairs={{0,2},{1,3},{2,0},{3,1},{4,6},{5,7},{6,4},{7,5},{8,10},{9,11},{10,... | collective-permute-start | bytes 1572872 | tf_op jit(solution)/shard_map/ppermute | solution.py:63
  4.2 18.8 %collective-permute-start.3 = (bf16[256,1024]{1,0:T(8,128)(2,1)S(1)}, bf16[256,1024]{1,0:T(8,128)(2,1)}, u32[]{:S(2)}, u32[]{:S(2)}) collective-permute-start(bf16[256,1024]{1,0:T(8,128)(2,1)S(1)} %constant_dynamic-slice_fusion), channel_id=1, source_target_pairs={{0,1},{1,0},{2,3},{3,2},{4,5},{5,4},{6,7},{7,6},{8,9},{9,8},{10,11... | collective-permute-start | bytes 1572872 | tf_op jit(solution)/shard_map/ppermute | solution.py:63
  10.8 11.8 %collective-permute-start = (bf16[512,256]{1,0:T(8,128)(2,1)}, bf16[512,256]{1,0:T(8,128)(2,1)S(1)}, u32[]{:S(2)}, u32[]{:S(2)}) collective-permute-start(bf16[512,256]{1,0:T(8,128)(2,1)} %get-tuple-element.29), channel_id=1, source_target_pairs={{0,2},{1,3},{2,0},{3,1},{4,6},{5,7},{6,4},{7,5},{8,10},{9,11},{10,... | collective-permute-start | bytes 786440 | tf_op jit(solution)/shard_map/ppermute | solution.py:63
  10.9 12.2 %collective-permute-start.2 = (bf16[512,256]{1,0:T(8,128)(2,1)S(1)}, bf16[512,256]{1,0:T(8,128)(2,1)S(1)}, u32[]{:S(2)}, u32[]{:S(2)}) collective-permute-start(bf16[512,256]{1,0:T(8,128)(2,1)S(1)} %get-tuple-element.30), channel_id=1, source_target_pairs={{0,1},{1,0},{2,3},{3,2},{4,5},{5,4},{6,7},{7,6},{8,9},{9,8},{10,11... | collective-permute-start | bytes 786440 | tf_op jit(solution)/shard_map/ppermute | solution.py:63
  11.3 15.4 %collective-permute-start.4 = (bf16[512,256]{1,0:T(8,128)(2,1)S(1)}, bf16[512,256]{1,0:T(8,128)(2,1)S(1)}, u32[]{:S(2)}, u32[]{:S(2)}) collective-permute-start(bf16[512,256]{1,0:T(8,128)(2,1)S(1)} %get-tuple-element.32), channel_id=1, source_target_pairs={{0,3},{1,2},{2,1},{3,0},{4,7},{5,6},{6,5},{7,4},{8,11},{9,10},{10,... | collective-permute-start | bytes 786440 | tf_op jit(solution)/shard_map/ppermute | solution.py:63
  19.0 7.7 %collective-permute-start.5 = (bf16[256,1024]{1,0:T(8,128)(2,1)S(1)}, bf16[256,1024]{1,0:T(8,128)(2,1)S(1)}, u32[]{:S(2)}, u32[]{:S(2)}) collective-permute-start(bf16[256,1024]{1,0:T(8,128)(2,1)S(1)} %broadcast_add_fusion.4), channel_id=1, source_target_pairs={{0,1},{1,0},{2,3},{3,2},{4,5},{5,4},{6,7},{7,6},{8,9},{9,8},{10,11... | collective-permute-start | bytes 1572872 | tf_op jit(solution)/shard_map/ppermute | solution.py:63
  27.3 30.5 %collective-permute-start.12 = (bf16[512,1024]{1,0:T(8,128)(2,1)S(1)}, bf16[512,1024]{1,0:T(8,128)(2,1)S(1)}, u32[]{:S(2)}, u32[]{:S(2)}) collective-permute-start(bf16[512,1024]{1,0:T(8,128)(2,1)S(1)} %add_convert_fusion.1), channel_id=1, source_target_pairs={{0,1},{1,0},{2,3},{3,2},{4,8},{5,9},{6,10},{7,11},{8,4},{9,5},{10,... | collective-permute-start | bytes 3145736 | tf_op jit(solution)/shard_map/ppermute | solution.py:70
  27.9 29.9 %collective-permute-start.13 = (bf16[512,1024]{1,0:T(8,128)(2,1)S(1)}, bf16[512,1024]{1,0:T(8,128)(2,1)S(1)}, u32[]{:S(2)}, u32[]{:S(2)}) collective-permute-start(bf16[512,1024]{1,0:T(8,128)(2,1)S(1)} %add_convert_fusion.1), channel_id=1, source_target_pairs={{0,4},{1,5},{2,6},{3,7},{4,0},{5,1},{6,2},{7,3},{8,12},{9,13},{10,... | collective-permute-start | bytes 3145736 | tf_op jit(solution)/shard_map/ppermute | solution.py:70
  30.9 26.9 %collective-permute-start.6 = (bf16[256,1024]{1,0:T(8,128)(2,1)S(1)}, bf16[256,1024]{1,0:T(8,128)(2,1)S(1)}, u32[]{:S(2)}, u32[]{:S(2)}) collective-permute-start(bf16[256,1024]{1,0:T(8,128)(2,1)S(1)} %get-tuple-element.22), channel_id=1, source_target_pairs={{0,2},{1,3},{2,0},{3,1},{4,6},{5,7},{6,4},{7,5},{8,10},{9,11},{10,... | collective-permute-start | bytes 1572872 | tf_op jit(solution)/shard_map/ppermute | solution.py:63
  32.9 23.4 %collective-permute-start.10 = (bf16[256,1024]{1,0:T(8,128)(2,1)S(1)}, bf16[256,1024]{1,0:T(8,128)(2,1)S(1)}, u32[]{:S(2)}, u32[]{:S(2)}) collective-permute-start(bf16[256,1024]{1,0:T(8,128)(2,1)S(1)} %get-tuple-element.23), channel_id=1, source_target_pairs={{0,2},{1,3},{2,0},{3,1},{4,6},{5,7},{6,4},{7,5},{8,10},{9,11},{10,... | collective-permute-start | bytes 1572872 | tf_op jit(solution)/shard_map/ppermute | solution.py:63
  34.4 22.3 %collective-permute-start.7 = (bf16[256,1024]{1,0:T(8,128)(2,1)S(1)}, bf16[256,1024]{1,0:T(8,128)(2,1)S(1)}, u32[]{:S(2)}, u32[]{:S(2)}) collective-permute-start(bf16[256,1024]{1,0:T(8,128)(2,1)S(1)} %get-tuple-element.23), channel_id=1, source_target_pairs={{0,1},{1,0},{2,3},{3,2},{4,5},{5,4},{6,7},{7,6},{8,9},{9,8},{10,11... | collective-permute-start | bytes 1572872 | tf_op jit(solution)/shard_map/ppermute | solution.py:63
  56.7 2.2 %collective-permute-start.11 = (bf16[256,1024]{1,0:T(8,128)(2,1)S(1)}, bf16[256,1024]{1,0:T(8,128)(2,1)S(1)}, u32[]{:S(2)}, u32[]{:S(2)}) collective-permute-start(bf16[256,1024]{1,0:T(8,128)(2,1)S(1)} %collective-permute-done.10), channel_id=1, source_target_pairs={{0,1},{1,0},{2,3},{3,2},{4,5},{5,4},{6,7},{7,6},{8,9},{9,8},{10,11... | collective-permute-start | bytes 1572872 | tf_op jit(solution)/shard_map/ppermute | solution.py:63
  62.4 15.9 %collective-permute-start.19 = (bf16[512,1024]{1,0:T(8,128)(2,1)S(1)}, bf16[512,1024]{1,0:T(8,128)(2,1)S(1)}, u32[]{:S(2)}, u32[]{:S(2)}) collective-permute-start(bf16[512,1024]{1,0:T(8,128)(2,1)S(1)} %get-tuple-element.19), channel_id=1, source_target_pairs={{0,1},{1,0},{2,3},{3,2},{4,5},{5,4},{6,7},{7,6},{8,12},{9,13},{10,... | collective-permute-start | bytes 3145736 | tf_op jit(solution)/shard_map/ppermute | solution.py:70
  62.8 15.6 %collective-permute-start.20 = (bf16[512,1024]{1,0:T(8,128)(2,1)S(1)}, bf16[512,1024]{1,0:T(8,128)(2,1)S(1)}, u32[]{:S(2)}, u32[]{:S(2)}) collective-permute-start(bf16[512,1024]{1,0:T(8,128)(2,1)S(1)} %get-tuple-element.20), channel_id=1, source_target_pairs={{0,1},{1,0},{2,3},{3,2},{4,8},{5,9},{6,10},{7,11},{8,4},{9,5},{10,... | collective-permute-start | bytes 3145736 | tf_op jit(solution)/shard_map/ppermute | solution.py:70
  63.0 14.8 %collective-permute-start.15 = (bf16[256,1024]{1,0:T(8,128)(2,1)S(1)}, bf16[256,1024]{1,0:T(8,128)(2,1)S(1)}, u32[]{:S(2)}, u32[]{:S(2)}) collective-permute-start(bf16[256,1024]{1,0:T(8,128)(2,1)S(1)} %broadcast_add_fusion.2), channel_id=1, source_target_pairs={{0,2},{1,3},{2,0},{3,1},{4,6},{5,7},{6,4},{7,5},{8,10},{9,11},{10,... | collective-permute-start | bytes 1572872 | tf_op jit(solution)/shard_map/ppermute | solution.py:63
  64.7 23.8 %collective-permute-start.17 = (bf16[256,1024]{1,0:T(8,128)(2,1)S(1)}, bf16[256,1024]{1,0:T(8,128)(2,1)S(1)}, u32[]{:S(2)}, u32[]{:S(2)}) collective-permute-start(bf16[256,1024]{1,0:T(8,128)(2,1)S(1)} %get-tuple-element.27), channel_id=1, source_target_pairs={{0,2},{1,3},{2,0},{3,1},{4,6},{5,7},{6,4},{7,5},{8,10},{9,11},{10,... | collective-permute-start | bytes 1572872 | tf_op jit(solution)/shard_map/ppermute | solution.py:63
  65.3 23.2 %collective-permute-start.18 = (bf16[256,1024]{1,0:T(8,128)(2,1)S(1)}, bf16[256,1024]{1,0:T(8,128)(2,1)S(1)}, u32[]{:S(2)}, u32[]{:S(2)}) collective-permute-start(bf16[256,1024]{1,0:T(8,128)(2,1)S(1)} %get-tuple-element.28), channel_id=1, source_target_pairs={{0,16},{1,17},{2,18},{3,19},{4,20},{5,21},{6,22},{7,23},{8,24},{9,... | collective-permute-start | bytes 1572872 | tf_op jit(solution)/shard_map/ppermute | solution.py:78
  77.8 10.6 %collective-permute-start.16 = (bf16[256,1024]{1,0:T(8,128)(2,1)S(1)}, bf16[256,1024]{1,0:T(8,128)(2,1)S(1)}, u32[]{:S(2)}, u32[]{:S(2)}) collective-permute-start(bf16[256,1024]{1,0:T(8,128)(2,1)S(1)} %collective-permute-done.15), channel_id=1, source_target_pairs={{0,1},{1,0},{2,3},{3,2},{4,5},{5,4},{6,7},{7,6},{8,9},{9,8},{10,11... | collective-permute-start | bytes 1572872 | tf_op jit(solution)/shard_map/ppermute | solution.py:63
  89.6 4.1 %collective-permute-start.22 = (bf16[256,1024]{1,0:T(8,128)(2,1)S(1)}, bf16[256,1024]{1,0:T(8,128)(2,1)S(1)}, u32[]{:S(2)}, u32[]{:S(2)}) collective-permute-start(bf16[256,1024]{1,0:T(8,128)(2,1)S(1)} %get-tuple-element.26), channel_id=1, source_target_pairs={{0,1},{1,0},{2,3},{3,2},{4,5},{5,4},{6,7},{7,6},{8,9},{9,8},{10,11... | collective-permute-start | bytes 1572872 | tf_op jit(solution)/shard_map/ppermute | solution.py:63
  89.7 4.2 %collective-permute-start.21 = (bf16[256,1024]{1,0:T(8,128)(2,1)S(1)}, bf16[256,1024]{1,0:T(8,128)(2,1)S(1)}, u32[]{:S(2)}, u32[]{:S(2)}) collective-permute-start(bf16[256,1024]{1,0:T(8,128)(2,1)S(1)} %get-tuple-element.44), channel_id=1, source_target_pairs={{0,1},{1,0},{2,3},{3,2},{4,5},{5,4},{6,7},{7,6},{8,9},{9,8},{10,11... | collective-permute-start | bytes 1572872 | tf_op jit(solution)/shard_map/ppermute | solution.py:63
  90.6 13.9 %collective-permute-start.27 = (bf16[256,1024]{1,0:T(8,128)(2,1)S(1)}, bf16[256,1024]{1,0:T(8,128)(2,1)S(1)}, u32[]{:S(2)}, u32[]{:S(2)}) collective-permute-start(bf16[256,1024]{1,0:T(8,128)(2,1)S(1)} %get-tuple-element.26), channel_id=1, source_target_pairs={{0,2},{1,3},{2,0},{3,1},{4,6},{5,7},{6,4},{7,5},{8,10},{9,11},{10,... | collective-permute-start | bytes 1572872 | tf_op jit(solution)/shard_map/ppermute | solution.py:63
  92.1 13.6 %collective-permute-start.23 = (bf16[256,1024]{1,0:T(8,128)(2,1)S(1)}, bf16[256,1024]{1,0:T(8,128)(2,1)S(1)}, u32[]{:S(2)}, u32[]{:S(2)}) collective-permute-start(bf16[256,1024]{1,0:T(8,128)(2,1)S(1)} %get-tuple-element.25), channel_id=1, source_target_pairs={{0,16},{1,17},{2,18},{3,19},{4,20},{5,21},{6,22},{7,23},{8,24},{9,... | collective-permute-start | bytes 1572872 | tf_op jit(solution)/shard_map/ppermute | solution.py:78
  93.7 10.8 %collective-permute-start.26 = (bf16[256,1024]{1,0:T(8,128)(2,1)S(1)}, bf16[256,1024]{1,0:T(8,128)(2,1)S(1)}, u32[]{:S(2)}, u32[]{:S(2)}) collective-permute-start(bf16[256,1024]{1,0:T(8,128)(2,1)S(1)} %get-tuple-element.43), channel_id=1, source_target_pairs={{0,1},{1,0},{2,3},{3,2},{4,5},{5,4},{6,7},{7,6},{8,9},{9,8},{10,11... | collective-permute-start | bytes 1572872 | tf_op jit(solution)/shard_map/ppermute | solution.py:63
  94.9 11.6 %collective-permute-start.24 = (f32[256,256]{1,0:T(8,128)S(1)}, f32[256,256]{1,0:T(8,128)S(1)}, u32[]{:S(2)}, u32[]{:S(2)}) collective-permute-start(f32[256,256]{1,0:T(8,128)S(1)} %convolution_add_fusion.3), channel_id=1, source_target_pairs={{0,1},{1,0},{2,3},{3,2},{4,5},{5,4},{6,7},{7,6},{8,12},{9,13},{10,... | collective-permute-start | bytes 786440 | tf_op jit(solution)/shard_map/ppermute | solution.py:70
  104.5 2.5 %collective-permute-start.28 = (bf16[256,1024]{1,0:T(8,128)(2,1)S(1)}, bf16[256,1024]{1,0:T(8,128)(2,1)S(1)}, u32[]{:S(2)}, u32[]{:S(2)}) collective-permute-start(bf16[256,1024]{1,0:T(8,128)(2,1)S(1)} %collective-permute-done.27), channel_id=1, source_target_pairs={{0,1},{1,0},{2,3},{3,2},{4,5},{5,4},{6,7},{7,6},{8,9},{9,8},{10,11... | collective-permute-start | bytes 1572872 | tf_op jit(solution)/shard_map/ppermute | solution.py:63
  107.5 5.8 %collective-permute-start.30 = (f32[256,512]{1,0:T(8,128)S(1)}, f32[256,512]{1,0:T(8,128)S(1)}, u32[]{:S(2)}, u32[]{:S(2)}) collective-permute-start(f32[256,512]{1,0:T(8,128)S(1)} %convolution_add_fusion), channel_id=1, source_target_pairs={{0,1},{1,0},{2,3},{3,2},{4,5},{5,4},{6,7},{7,6},{8,12},{9,13},{10,... | collective-permute-start | bytes 1572872 | tf_op jit(solution)/shard_map/ppermute | solution.py:70
  114.0 2.5 %collective-permute-start.31 = (f32[256]{0:T(256)S(1)}, f32[256]{0:T(256)S(1)}, u32[]{:S(2)}, u32[]{:S(2)}) collective-permute-start(f32[256]{0:T(256)S(1)} %get-tuple-element.41), channel_id=1, source_target_pairs={{0,1},{1,0},{2,3},{3,2},{4,5},{5,4},{6,7},{7,6},{8,12},{9,13},{10,... | collective-permute-start | bytes 3080 | tf_op jit(solution)/shard_map/ppermute | solution.py:70
  114.4 3.6 %collective-permute-start.32 = (f32[256]{0:T(256)S(1)}, f32[256]{0:T(256)S(1)}, u32[]{:S(2)}, u32[]{:S(2)}) collective-permute-start(f32[256]{0:T(256)S(1)} %get-tuple-element.42), channel_id=1, source_target_pairs={{0,16},{1,17},{2,18},{3,19},{4,20},{5,21},{6,22},{7,23},{8,24},{9,... | collective-permute-start | bytes 3080 | tf_op jit(solution)/shard_map/ppermute | solution.py:78
  116.0 3.6 %collective-permute-start.33 = (f32[256]{0:T(256)S(1)}, f32[256]{0:T(256)S(1)}, u32[]{:S(2)}, u32[]{:S(2)}) collective-permute-start(f32[256]{0:T(256)S(1)} %get-tuple-element.42), channel_id=1, source_target_pairs={{0,16},{1,17},{2,18},{3,19},{4,20},{5,21},{6,22},{7,23},{8,28},{9,... | collective-permute-start | bytes 3080 | tf_op jit(solution)/shard_map/ppermute | solution.py:78
  119.6 3.6 %collective-permute-start.35 = (f32[256]{0:T(256)S(1)}, f32[256]{0:T(256)S(1)}, u32[]{:S(2)}, u32[]{:S(2)}) collective-permute-start(f32[256]{0:T(256)S(1)} %add_add_fusion.3), channel_id=1, source_target_pairs={{0,2},{1,3},{2,0},{3,1},{4,6},{5,7},{6,4},{7,5},{8,10},{9,11},{10,... | collective-permute-start | bytes 3080 | tf_op jit(solution)/shard_map/ppermute | solution.py:63
  120.6 3.0 %collective-permute-start.36 = (f32[256]{0:T(256)S(1)}, f32[256]{0:T(256)S(1)}, u32[]{:S(2)}, u32[]{:S(2)}) collective-permute-start(f32[256]{0:T(256)S(1)} %add_add_fusion.3), channel_id=1, source_target_pairs={{0,3},{1,2},{2,1},{3,0},{4,7},{5,6},{6,5},{7,4},{8,11},{9,10},{10,... | collective-permute-start | bytes 3080 | tf_op jit(solution)/shard_map/ppermute | solution.py:63
  123.6 19.6 %collective-permute-start.37 = (f32[1024]{0:T(1024)S(1)}, f32[1024]{0:T(1024)S(1)}, u32[]{:S(2)}, u32[]{:S(2)}) collective-permute-start(f32[1024]{0:T(1024)S(1)} %pad_maximum_fusion.3), channel_id=1, source_target_pairs={{0,8},{1,9},{2,10},{3,11},{4,12},{5,13},{6,14},{7,15},{8,0},{9,1},... | collective-permute-start | bytes 12296 | tf_op jit(solution)/shard_map/ppermute | solution.py:70
  (9 other events, 52.6 us)
